TPU v7x, 32 devices: a whole 2x2x4 slice. The times are simulated.
32 devices in a mesh: fibre: 8 (over z, core), rest: 4 (over y, x).
Axes of the slice: x: 2, y: 2, z: 4, core: 2. Of those that a mesh axis runs over, the one named last changes fastest.
Arguments:
- slab: float32 [672, 65536], P('fibre', 'rest'), may hold values from -6 to 6
- start_basis: float32 [672, 96], replicated, may hold values from -6 to 6
Outputs:
- factor: float32 [672, 96], replicated
- core: float32 [96, 65536], P('fibre', 'rest')
All inputs are finite; a program needn't handle non-finite values.
Results may differ from a plain program's by a relative error of at most 0.00023.
Values sent between devices are 32-bit elements; how exact they have to be, the bound alone decides.
No kernel may reach another device: no remote copies, remote signals or barrier semaphores. Data moves between devices by JAX's collectives and lax.ppermute only.
A program may use at most 64 MiB of HBM per device.

v0:
```python
import jax
import jax.numpy as jnp
from jax import lax
from jax.sharding import PartitionSpec as P

ITERS = 3


def orthonormal(image, small):
    lower = jnp.linalg.cholesky(small)
    return lax.linalg.triangular_solve(lower, image, left_side=False, lower=True, transpose_a=True)


def shards(slab, start_basis):
    hp = lax.Precision.HIGHEST
    fibres = lax.all_to_all(slab, "fibre", split_axis=1, concat_axis=0, tiled=True)
    partial_gram = jnp.dot(fibres, fibres.T, precision=hp, preferred_element_type=jnp.float32)
    own_rows = slab.shape[0]
    first_row = lax.axis_index("fibre") * own_rows
    basis = start_basis
    gram = lax.psum(partial_gram, ("fibre", "rest"))
    for step in range(ITERS):
        image = jnp.dot(gram, basis, precision=hp, preferred_element_type=jnp.float32)
        small = jnp.dot(image.T, image, precision=hp, preferred_element_type=jnp.float32)
        basis = orthonormal(image, small)
    own_basis = lax.dynamic_slice_in_dim(basis, first_row, own_rows, 0)
    core = lax.psum_scatter(
        jnp.dot(own_basis.T, slab, precision=hp, preferred_element_type=jnp.float32),
        "fibre",
        scatter_dimension=0,
        tiled=True,
    )
    return (basis, core)


def solution(mesh):
    return jax.shard_map(
        shards,
        mesh=mesh,
        in_specs=(P("fibre", "rest"), P()),
        out_specs=(P(), P("fibre", "rest")),
        check_vma=False,
    )
```

profile of v0, /device:TPU:1, one launch (start us, length us, event | category | flops | bytes accessed | tf_op | source)
XLA Modules:
  0.0 530.5 jit_solution(12924450988103902975)
XLA Ops:
  7.2 6.5 %copy.15 = f32[11,8,8,2048]{3,2,1,0:T(8,128)S(1)} copy(f32[11,8,8,2048]{3,1,2,0:T(8,128)} %bitcast.58) | data formatting | bytes 11534336
  13.7 0.7 slice.7
  14.4 3.2 copy.11
  17.6 133.3 %all_to_all.19 = f32[84,8,2048]{2,0,1:T(8,128)} all-to-all(f32[84,8,2048]{2,0,1:T(8,128)S(1)} %copy.11), channel_id=1, replica_groups=mesh['fibre'=8,'rest'=4] {'fibre'}, dimensions={1} | all-to-all | bytes 11010048 | tf_op jit(solution)/shard_map/all_to_all | solution.py:16
  150.8 5.7 %all_to_all.17 = f32[672,2048]{1,0:T(8,128)} reshape(f32[8,84,2048]{2,1,0:T(8,128)} %bitcast.59) | data formatting | bytes 11010048 | tf_op jit(solution)/shard_map/all_to_all | solution.py:16
  156.5 17.6 %fusion.17 = f32[672,672]{1,0:T(8,128)} fusion(f32[672,2048]{1,0:T(8,128)} %all_to_all.17), kind=kOutput, calls=%fused_computation.32 | convolution fusion | flops 11098128384 | bytes 7311360 | tf_op jit(solution)/shard_map/dot_general | solution.py:17
  174.2 131.9 %all-reduce.4.cloned.1.call-done = f32[672,672]{1,0:T(8,128)} async-done(((f32[672,672]{1,0:T(8,128)}), f32[672,672]{1,0:T(8,128)}) %all-reduce.4.cloned.1.call-update) | async-done | bytes 1806352 | tf_op jit(solution)/shard_map/psum | solution.py:21
  306.1 3.7 fusion.18
  310.3 8.8 %cholesky.59 = f32[96,96]{1,0:T(8,128)S(1)} custom-call(f32[96,96]{1,0:T(8,128)S(1)} %fusion.9), custom_call_target="Cholesky" | custom-call | tf_op jit(solution)/shard_map/jit(cholesky)/cholesky | solution.py:10
  319.1 0.6 compare_reduce_fusion.2
  319.7 0.7 fusion.1
  320.4 7.4 %custom-call.7 = f32[1,96,96]{1,2,0:T(8,128)S(1)} custom-call(f32[1,96,96]{2,1,0:T(8,128)S(1)} %fusion.1), custom_call_target="InvertDiagBlocksLowerTriangular" | custom-call | tf_op jit(solution)/shard_map/triangular_solve/custom-call.0 | solution.py:11
  327.7 0.4 convolution_bitcast_fusion.2
  328.2 2.0 fusion.20
  330.7 8.8 %cholesky.70 = f32[96,96]{1,0:T(8,128)S(1)} custom-call(f32[96,96]{1,0:T(8,128)S(1)} %fusion.7), custom_call_target="Cholesky" | custom-call | tf_op jit(solution)/shard_map/jit(cholesky)/cholesky | solution.py:10
  339.5 0.6 compare_reduce_fusion.1
  340.1 0.7 fusion.2
  340.8 7.4 %custom-call.8 = f32[1,96,96]{1,2,0:T(8,128)S(1)} custom-call(f32[1,96,96]{2,1,0:T(8,128)S(1)} %fusion.2), custom_call_target="InvertDiagBlocksLowerTriangular" | custom-call | tf_op jit(solution)/shard_map/triangular_solve/custom-call.0 | solution.py:11
  348.6 2.2 fusion.22
  351.3 8.8 %cholesky.81 = f32[96,96]{1,0:T(8,128)S(1)} custom-call(f32[96,96]{1,0:T(8,128)S(1)} %fusion.5), custom_call_target="Cholesky" | custom-call | tf_op jit(solution)/shard_map/jit(cholesky)/cholesky | solution.py:10
  360.1 0.6 compare_reduce_fusion
  360.8 0.7 fusion.3
  361.5 7.4 %custom-call.9 = f32[1,96,96]{1,2,0:T(8,128)S(1)} custom-call(f32[1,96,96]{2,1,0:T(8,128)S(1)} %fusion.3), custom_call_target="InvertDiagBlocksLowerTriangular" | custom-call | tf_op jit(solution)/shard_map/triangular_solve/custom-call.0 | solution.py:11
  369.3 0.7 copy-done.2
  370.0 9.0 %fusion.14 = f32[96,16384]{1,0:T(8,128)} fusion(f32[84,16384]{1,0:T(8,128)} %param.5, f32[672,96]{0,1:T(8,128)S(1)} %convolution_bitcast_fusion, s32[]{:T(128)S(6)} %select_n.6), kind=kOutput, calls=%fused_computation.25 | convolution fusion | flops 1585446912 | bytes 11845636 | tf_op jit(solution)/shard_map/dot_general | solution.py:28
  379.0 84.9 %fusion = f32[16,16384]{1,0:T(8,128)S(1)} fusion(f32[96,16384]{1,0:T(8,128)} %fusion.14), kind=kCustom, calls=%all-reduce-scatter | all-reduce-scatter fusion | flops 2097153 | bytes 7340544
  463.9 4.4 collective-permute-start
  468.4 3.0 collective-permute-start.1
  471.5 0.6 dynamic-slice.4
  472.7 29.8 %collective-permute-done.1 = f32[12,16384]{1,0:T(8,128)} collective-permute-done((f32[12,16384]{1,0:T(8,128)S(1)}, f32[12,16384]{1,0:T(8,128)}, u32[]{:S(2)}, u32[]{:S(2)}) %collective-permute-start.1) | collective-permute-done | bytes 786464
  502.5 18.2 %concatenate = f32[44,16384]{1,0:T(8,128)} concatenate(f32[12,16384]{1,0:T(8,128)} %collective-permute-done.1, f32[16,16384]{1,0:T(8,128)S(1)} %collective-permute-done, f32[16,16384]{1,0:T(8,128)S(1)} %fusion), dimensions={0} | concatenate | bytes 5767168
  520.8 2.5 constant_dynamic-slice_fusion
  (25 shorter events, 2.6 us)
Async XLA Ops:
  7.2 298.9 %copy-start = (f32[672,96]{0,1:T(8,128)S(1)}, f32[672,96]{0,1:T(8,128)}, u32[]{:S(2)}) copy-start(f32[672,96]{0,1:T(8,128)} %param.6) | copy-start | bytes 774148
  7.2 298.9 %all-reduce.4.cloned.1.call-start = ((), (), s32[]{:S(2)}) async-start(), calls=%async_computation.1 | async-start | bytes 4128768 | tf_op jit(solution)/shard_map/psum | solution.py:21
  306.1 22.1 %copy-start.1 = (f32[672,672]{1,0:T(8,128)S(1)}, f32[672,672]{1,0:T(8,128)}, u32[]{:S(2)}) copy-start(f32[672,672]{1,0:T(8,128)} %all-reduce.4.cloned.1.call-done) | copy-start | bytes 5419012
  369.3 0.7 copy-start.2
  379.0 92.5 %copy-start.3 = (u32[32]{0:T(128)S(1)}, u32[32]{0:T(128)}, u32[]{:S(2)}) copy-start(u32[32]{0:T(128)} %constant.44) | copy-start | bytes 388
  463.9 38.6 %collective-permute-start = (f32[16,16384]{1,0:T(8,128)S(1)}, f32[16,16384]{1,0:T(8,128)S(1)}, u32[]{:S(2)}, u32[]{:S(2)}) collective-permute-start(f32[16,16384]{1,0:T(8,128)S(1)} %fusion), channel_id=1, source_target_pairs={{0,4},{4,8},{8,12},{12,16},{16,20},{20,24},{24,28},{1,5},{5,9},{9,... | collective-permute-start | bytes 3145736
  468.4 34.1 %collective-permute-start.1 = (f32[12,16384]{1,0:T(8,128)S(1)}, f32[12,16384]{1,0:T(8,128)}, u32[]{:S(2)}, u32[]{:S(2)}) collective-permute-start(f32[12,16384]{1,0:T(8,128)S(1)} %slice.6), channel_id=1, source_target_pairs={{0,8},{4,12},{8,16},{12,20},{16,24},{20,28},{1,9},{5,13},{9,17},{1... | collective-permute-start | bytes 2359304
Sparse Core Ops, SparseCore 0:
  174.3 131.7 all-reduce.3
where the time goes:
time: 537 us; the launch traced here: 531 us
  blocking collectives  218 us (41%)
  waiting for transfers between devices  162 us (30%)
  other arithmetic  52.4 us (10%)
  local copies, waits for them, and re-layouts  38.3 us (7%)
  matrix products  37 us (7%)
  between operations  15.4 us (3%)
  starting transfers between devices  7.45 us (1%)
    all_to_all x1, blocking collectives, shards(): lax.all_to_all(slab, 'fibre', split_axis=1, concat_axis=0, tiled=True)  133 us
    psum x1, waiting for transfers between devices, shards(): gram = lax.psum(partial_gram, ('fibre', 'rest'))  132 us
    unnamed x1, blocking collectives  84.9 us
    unnamed x3, waiting for transfers between devices  29.9 us
    unnamed x13, local copies, waits for them, and re-layouts  28.6 us
    another operation x9, other arithmetic, orthonormal(): lower = jnp.linalg.cholesky(small)  28.4 us
    another operation x6, other arithmetic, orthonormal(): lax.linalg.triangular_solve(lower, image, left_side=False, lower=True, tr...  24 us
    dot_general x1, matrix products, shards(): jnp.dot(fibres, fibres.T, precision=hp, preferred_element_type=jnp.float32)  17.6 us
  transfers between devices with their start and end apart: 3, of which 2 were waited for; matrix products, arithmetic and copies ran while one was open for 0% of the time, Pallas kernels for 0%

commit v1 on v0

v1 whole, which is shorter than its diff:
```python
import jax
import jax.numpy as jnp
from jax import lax
from jax.sharding import PartitionSpec as P

ITERS = 3
HIGH = lax.Precision.HIGH
HIGHEST = lax.Precision.HIGHEST


def orthonormal(image, small):
    lower = jnp.linalg.cholesky(small)
    return lax.linalg.triangular_solve(lower, image, left_side=False, lower=True, transpose_a=True)


def swap(x, axis, size, bits):
    return lax.ppermute(x, axis, [(i, i ^ bits) for i in range(size)])


def in_order(core, mine, other, axis):
    return jnp.where(core == 0, jnp.concatenate([mine, other], axis), jnp.concatenate([other, mine], axis))


def pack(gram):
    h = gram.shape[0] // 2
    upper = lax.broadcasted_iota(jnp.int32, (h, h), 0) <= lax.broadcasted_iota(jnp.int32, (h, h), 1)
    low = gram[h:, h:]
    tri = jnp.where(upper, gram[:h, :h], low)
    eye = lax.broadcasted_iota(jnp.int32, (h, h), 0) == lax.broadcasted_iota(jnp.int32, (h, h), 1)
    diag = jnp.sum(jnp.where(eye, low, 0.0), axis=0, keepdims=True)
    return jnp.concatenate([gram[:h, h:], tri, diag], 0)


def unpack(packed, n):
    h = n // 2
    row = lax.broadcasted_iota(jnp.int32, (h, h), 0)
    col = lax.broadcasted_iota(jnp.int32, (h, h), 1)
    cross, tri, diag = packed[:h], packed[h : 2 * h], packed[2 * h : 2 * h + 1]
    top = jnp.where(row <= col, tri, tri.T)
    low = jnp.where(row > col, tri, jnp.where(row == col, diag, tri.T))
    return jnp.concatenate([jnp.concatenate([top, cross], 1), jnp.concatenate([cross.T, low], 1)], 0)


def sum_everywhere(packed, fibre, rest):
    f, r = lax.axis_index("fibre"), lax.axis_index("rest")
    core = f % 2
    piece = -(-packed.shape[0] // (2 * rest * 8)) * 8
    half = piece * rest
    padded = jnp.pad(packed, ((0, 2 * half - packed.shape[0]), (0, 0)))
    width = packed.shape[1]
    mine = lax.dynamic_slice(padded, (core * half, 0), (half, width))
    theirs = lax.dynamic_slice(padded, ((1 - core) * half, 0), (half, width))
    mine = mine + swap(theirs, "fibre", fibre, 1)
    total = lax.dynamic_slice(mine, (r * piece, 0), (piece, width))
    for bits in range(1, rest):
        part = lax.dynamic_slice(mine, ((r ^ bits) * piece, 0), (piece, width))
        total = total + swap(part, "rest", rest, bits)
    terms = [total] + [swap(total, "fibre", fibre, 2 * bits) for bits in range(1, fibre // 2)]
    while len(terms) > 1:
        terms = [terms[i] + terms[i + 1] for i in range(0, len(terms), 2)]
    total = terms[0]
    out = jnp.zeros((rest, piece, width), jnp.float32)
    for bits in range(rest):
        got = swap(total, "rest", rest, bits) if bits else total
        out = lax.dynamic_update_slice(out, got[None], (r ^ bits, 0, 0))
    out = out.reshape(half, width)
    return in_order(core, out, swap(out, "fibre", fibre, 1), 0)


def shards(fibre, rest, slab, start_basis):
    rows, cols = slab.shape
    zs = fibre // 2
    f = lax.axis_index("fibre")
    z, core = f // 2, f % 2
    half = cols // 2
    part = half // zs
    chunks = [(0, part * 3 // 4), (part * 3 // 4, part // 4)]
    order = list(range(zs - 1, -1, -1))
    gram = 0.0
    fibres = []
    for start, width in chunks:
        whole = jnp.zeros((zs, 2 * rows, width), jnp.float32)
        for bits in order:
            at = (z ^ bits) * part + start
            mine = lax.dynamic_slice(slab, (0, core * half + at), (rows, width))
            theirs = lax.dynamic_slice(slab, (0, (1 - core) * half + at), (rows, width))
            block = in_order(core, mine, swap(theirs, "fibre", fibre, 1), 0)
            if bits:
                block = swap(block, "fibre", fibre, 2 * bits)
            whole = lax.dynamic_update_slice(whole, block[None], (z ^ bits, 0, 0))
        whole = whole.reshape(zs * 2 * rows, width)
        fibres.append(whole)
        gram = gram + jnp.dot(whole, whole.T, precision=HIGH, preferred_element_type=jnp.float32)
    n = gram.shape[0]
    gram = unpack(sum_everywhere(pack(gram), fibre, rest), n)
    basis = start_basis
    for step in range(ITERS):
        image = jnp.dot(gram, basis, precision=HIGHEST, preferred_element_type=jnp.float32)
        small = jnp.dot(image.T, image, precision=HIGHEST, preferred_element_type=jnp.float32)
        basis = orthonormal(image, small)
    rank = basis.shape[1]
    own = rank // fibre
    out = jnp.zeros((own, cols), jnp.float32)
    for (start, width), whole in zip(chunks, fibres):
        share = jnp.dot(basis.T, whole, precision=HIGH, preferred_element_type=jnp.float32)
        for bits in order:
            block = lax.dynamic_slice(share, ((z ^ bits) * 2 * own, 0), (2 * own, width))
            if bits:
                block = swap(block, "fibre", fibre, 2 * bits)
            mine = lax.dynamic_slice(block, (core * own, 0), (own, width))
            theirs = lax.dynamic_slice(block, ((1 - core) * own, 0), (own, width))
            other = swap(theirs, "fibre", fibre, 1)
            at = (z ^ bits) * part + start
            out = lax.dynamic_update_slice(out, mine, (0, core * half + at))
            out = lax.dynamic_update_slice(out, other, (0, (1 - core) * half + at))
    return (basis, out)


def solution(mesh):
    fibre, rest = mesh.shape["fibre"], mesh.shape["rest"]
    return jax.shard_map(
        lambda slab, start_basis: shards(fibre, rest, slab, start_basis),
        mesh=mesh,
        in_specs=(P("fibre", "rest"), P()),
        out_specs=(P(), P("fibre", "rest")),
        check_vma=False,
    )
```

time: 537 us -> 316 us (0.59); the launches traced: 531 us -> 315 us
  blocking collectives: 218 us -> 0 us
  starting transfers between devices: 7.45 us -> 71.1 us
  waiting for transfers between devices: 162 us -> 132 us
  matrix products: 37 us -> 22.1 us
  between operations: 15.4 us -> 1.31 us
  local copies, waits for them, and re-layouts: 38.3 us -> 24.5 us
  other arithmetic: 52.4 us -> 64 us
    all_to_all x1 -> x0, blocking collectives: 133 us -> none  [shards(): lax.all_to_all(slab, 'fibre', split_axis=1, concat_axis=0, tiled=True)]
    ppermute x0 -> x39, waiting for transfers between devices: none -> 132 us  [swap(): return lax.ppermute(x, axis, [(i, i ^ bits) for i in range(size)])]
    psum x1 -> x0, waiting for transfers between devices: 132 us -> none  [shards(): gram = lax.psum(partial_gram, ('fibre', 'rest'))]
    unnamed x1 -> x0, blocking collectives: 84.9 us -> none
    ppermute x0 -> x39, starting transfers between devices: none -> 71.1 us  [swap(): return lax.ppermute(x, axis, [(i, i ^ bits) for i in range(size)])]
    unnamed x3 -> x0, waiting for transfers between devices: 29.9 us -> none
    unnamed x13 -> x10, local copies, waits for them, and re-layouts: 28.6 us -> 0.03 us
    dot_general x8 -> x10, matrix products: 35.7 us -> 20.8 us  [the longest x3 8.37 us: shards(): jnp.dot(gram, basis, precision=HIGHEST, preferred_element_type=jnp.float32)]
  transfers between devices with their start and end apart: 3 -> 39, of which waited for: 2 -> 25; matrix products, arithmetic and copies ran while one was open for 0% -> 5% of each run, Pallas kernels for 0% -> 0%
where the time goes in v1:
time: 316 us; the launch traced here: 315 us
  waiting for transfers between devices  132 us (42%)
  starting transfers between devices  71.1 us (22%)
  other arithmetic  64 us (20%)
  local copies, waits for them, and re-layouts  24.5 us (8%)
  matrix products  22.1 us (7%)
    ppermute x39, waiting for transfers between devices, swap(): return lax.ppermute(x, axis, [(i, i ^ bits) for i in range(size)])  132 us
    ppermute x39, starting transfers between devices, swap(): return lax.ppermute(x, axis, [(i, i ^ bits) for i in range(size)])  71.1 us
    another operation x9, other arithmetic, orthonormal(): lower = jnp.linalg.cholesky(small)  28.4 us
    another operation x6, other arithmetic, orthonormal(): lax.linalg.triangular_solve(lower, image, left_side=False, lower=True, tr...  24 us
    dot_general x3, matrix products, shards(): jnp.dot(gram, basis, precision=HIGHEST, preferred_element_type=jnp.float32)  8.37 us
    select_n x7, other arithmetic, in_order(): jnp.where(core == 0, jnp.concatenate([mine, other], axis), jnp.concatenat...  7.84 us
    dot_general x2, matrix products, shards(): jnp.dot(whole, whole.T, precision=HIGH, preferred_element_type=jnp.float32)  7.03 us
  transfers between devices with their start and end apart: 39, of which 25 were waited for; matrix products, arithmetic and copies ran while one was open for 5% of the time, Pallas kernels for 0%

profile of v1, /device:TPU:1, one launch (start us, length us, event | category | flops | bytes accessed | tf_op | source)
XLA Modules:
  0.0 315.1 jit_solution(2219610316208842416)
XLA Ops:
  0.7 2.3 dynamic-slice_bitcast_fusion.1
  3.1 3.7 %dynamic-slice_bitcast_fusion = (f32[1,84,1536]{2,1,0:T(8,128)S(1)}, f32[84,1536]{1,0:T(8,128)}, f32[84,1536]{1,0:T(8,128)}, f32[84,1536]{1,0:T(8,128)S(1)}, f32...) fusion(f32[84,16384]{1,0:T(8,128)} %param.5, s32[]{:T(128)S(6)} %select_n.269, ...), kind=kLoop, calls=%fused_computation.17 | loop fusion | bytes 8257568 | tf_op jit(solution)/shard_map/concatenate | solution.py:21
  11.1 3.7 %collective-permute-start.10 = (f32[168,512]{1,0:T(8,128)S(1)}, f32[168,512]{1,0:T(8,128)S(1)}, u32[]{:S(2)}, u32[]{:S(2)}) collective-permute-start(f32[168,512]{1,0:T(8,128)S(1)} %maximum_select_fusion.6), channel_id=1, source_target_pairs={{0,16},{4,20},{8,24},{12,28},{16,0},{20,4},{24,8},{28,12},{1,17},{... | collective-permute-start | bytes 1032200 | tf_op jit(solution)/shard_map/ppermute | solution.py:17
  20.4 11.1 %collective-permute-done.8 = f32[168,512]{1,0:T(8,128)S(1)} collective-permute-done((f32[168,512]{1,0:T(8,128)S(1)}, f32[168,512]{1,0:T(8,128)S(1)}, u32[]{:S(2)}, u32[]{:S(2)}) %collective-permute-start.8) | collective-permute-done | bytes 344096 | tf_op jit(solution)/shard_map/ppermute | solution.py:17
  31.4 2.2 collective-permute-start.1
  33.8 4.1 %collective-permute-done.10 = f32[168,512]{1,0:T(8,128)S(1)} collective-permute-done((f32[168,512]{1,0:T(8,128)S(1)}, f32[168,512]{1,0:T(8,128)S(1)}, u32[]{:S(2)}, u32[]{:S(2)}) %collective-permute-start.10) | collective-permute-done | bytes 344096 | tf_op jit(solution)/shard_map/ppermute | solution.py:17
  37.9 32.4 %collective-permute-start.3 = (f32[168,1536]{1,0:T(8,128)S(1)}, f32[168,1536]{1,0:T(8,128)S(1)}, u32[]{:S(2)}, u32[]{:S(2)}) collective-permute-start(f32[168,1536]{1,0:T(8,128)S(1)} %maximum_select_fusion.1), channel_id=1, source_target_pairs={{0,16},{4,20},{8,24},{12,28},{16,0},{20,4},{24,8},{28,12},{1,17},{... | collective-permute-start | bytes 3096584 | tf_op jit(solution)/shard_map/ppermute | solution.py:17
  73.3 63.7 %collective-permute-done.3 = f32[168,1536]{1,0:T(8,128)S(1)} collective-permute-done((f32[168,1536]{1,0:T(8,128)S(1)}, f32[168,1536]{1,0:T(8,128)S(1)}, u32[]{:S(2)}, u32[]{:S(2)}) %collective-permute-start.3) | collective-permute-done | bytes 1032224 | tf_op jit(solution)/shard_map/ppermute | solution.py:17
  137.5 5.2 %convolution_add_fusion = f32[672,672]{0,1:T(8,128)S(1)} fusion(f32[672,672]{0,1:T(8,128)S(1)} %fusion.23, f32[672,1536]{1,0:T(8,128)S(1)} %bitcast.85), kind=kOutput, calls=%fused_computation.1 | convolution fusion | flops 4162249728 | bytes 7741440 | tf_op jit(solution)/shard_map/dot_general | solution.py:93
  150.5 2.9 collective-permute-done.15
  154.3 3.8 %collective-permute-done.17 = f32[88,336]{0,1:T(8,128)S(1)} collective-permute-done((f32[88,336]{0,1:T(8,128)S(1)}, f32[88,336]{0,1:T(8,128)S(1)}, u32[]{:S(2)}, u32[]{:S(2)}) %collective-permute-start.17) | collective-permute-done | bytes 118304 | tf_op jit(solution)/shard_map/ppermute | solution.py:17
  158.3 2.6 collective-permute-start.19
  161.8 3.7 %collective-permute-done.18 = f32[88,336]{0,1:T(8,128)S(1)} collective-permute-done((f32[88,336]{0,1:T(8,128)S(1)}, f32[88,336]{0,1:T(8,128)S(1)}, u32[]{:S(2)}, u32[]{:S(2)}) %collective-permute-start.18) | collective-permute-done | bytes 118304 | tf_op jit(solution)/shard_map/ppermute | solution.py:17
  165.5 5.8 %collective-permute-done.20 = f32[88,336]{0,1:T(8,128)S(1)} collective-permute-done((f32[88,336]{0,1:T(8,128)S(1)}, f32[88,336]{0,1:T(8,128)S(1)}, u32[]{:S(2)}, u32[]{:S(2)}) %collective-permute-start.20) | collective-permute-done | bytes 118304 | tf_op jit(solution)/shard_map/ppermute | solution.py:17
  175.8 3.4 %collective-permute-done.22 = f32[88,336]{0,1:T(8,128)S(1)} collective-permute-done((f32[88,336]{0,1:T(8,128)S(1)}, f32[88,336]{0,1:T(8,128)S(1)}, u32[]{:S(2)}, u32[]{:S(2)}) %collective-permute-start.22) | collective-permute-done | bytes 118304 | tf_op jit(solution)/shard_map/ppermute | solution.py:17
  179.8 5.0 %collective-permute-start.24 = (f32[352,336]{0,1:T(8,128)S(1)}, f32[352,336]{0,1:T(8,128)}, u32[]{:S(2)}, u32[]{:S(2)}) collective-permute-start(f32[352,336]{0,1:T(8,128)S(1)} %copy.17), channel_id=1, source_target_pairs={{0,4},{4,0},{8,12},{12,8},{16,20},{20,16},{24,28},{28,24},{1,5},{5... | collective-permute-start | bytes 1419272 | tf_op jit(solution)/shard_map/ppermute | solution.py:17
  194.2 3.0 fusion.4
  197.8 8.8 %cholesky.59 = f32[96,96]{1,0:T(8,128)S(1)} custom-call(f32[96,96]{1,0:T(8,128)S(1)} %fusion.14), custom_call_target="Cholesky" | custom-call | tf_op jit(solution)/shard_map/jit(cholesky)/cholesky | solution.py:12
  207.9 7.4 %custom-call.7 = f32[1,96,96]{1,2,0:T(8,128)S(1)} custom-call(f32[1,96,96]{2,1,0:T(8,128)S(1)} %fusion.6), custom_call_target="InvertDiagBlocksLowerTriangular" | custom-call | tf_op jit(solution)/shard_map/triangular_solve/custom-call.0 | solution.py:13
  215.7 2.7 fusion.3
  218.9 8.8 %cholesky.70 = f32[96,96]{1,0:T(8,128)S(1)} custom-call(f32[96,96]{1,0:T(8,128)S(1)} %fusion.12), custom_call_target="Cholesky" | custom-call | tf_op jit(solution)/shard_map/jit(cholesky)/cholesky | solution.py:12
  229.0 7.4 %custom-call.8 = f32[1,96,96]{1,2,0:T(8,128)S(1)} custom-call(f32[1,96,96]{2,1,0:T(8,128)S(1)} %fusion.7), custom_call_target="InvertDiagBlocksLowerTriangular" | custom-call | tf_op jit(solution)/shard_map/triangular_solve/custom-call.0 | solution.py:13
  236.8 2.7 fusion.2
  240.0 8.8 %cholesky.81 = f32[96,96]{1,0:T(8,128)S(1)} custom-call(f32[96,96]{1,0:T(8,128)S(1)} %fusion.10), custom_call_target="Cholesky" | custom-call | tf_op jit(solution)/shard_map/jit(cholesky)/cholesky | solution.py:12
  250.1 7.4 %custom-call.9 = f32[1,96,96]{1,2,0:T(8,128)S(1)} custom-call(f32[1,96,96]{2,1,0:T(8,128)S(1)} %fusion.8), custom_call_target="InvertDiagBlocksLowerTriangular" | custom-call | tf_op jit(solution)/shard_map/triangular_solve/custom-call.0 | solution.py:13
  258.0 3.7 %fusion.27 = f32[96,1536]{1,0:T(8,128)S(1)} fusion(f32[672,96]{0,1:T(8,128)S(1)} %convolution_bitcast_fusion, f32[672,1536]{1,0:T(8,128)} %bitcast.86), kind=kOutput, calls=%fused_computation.128 | convolution fusion | flops 594542592 | bytes 4976640 | tf_op jit(solution)/shard_map/dot_general | solution.py:105
  263.8 4.9 %collective-permute-done.25 = f32[24,1536]{1,0:T(8,128)S(1)} collective-permute-done((f32[24,1536]{1,0:T(8,128)S(1)}, f32[24,1536]{1,0:T(8,128)S(1)}, u32[]{:S(2)}, u32[]{:S(2)}) %collective-permute-start.25) | collective-permute-done | bytes 147488 | tf_op jit(solution)/shard_map/ppermute | solution.py:17
  271.6 4.1 %collective-permute-start.27 = (f32[24,1536]{1,0:T(8,128)S(1)}, f32[24,1536]{1,0:T(8,128)S(1)}, u32[]{:S(2)}, u32[]{:S(2)}) collective-permute-start(f32[24,1536]{1,0:T(8,128)S(1)} %get-tuple-element.30), channel_id=1, source_target_pairs={{0,16},{4,20},{8,24},{12,28},{16,0},{20,4},{24,8},{28,12},{1,17},{... | collective-permute-start | bytes 442376 | tf_op jit(solution)/shard_map/ppermute | solution.py:17
  276.4 6.7 %collective-permute-done.27 = f32[24,1536]{1,0:T(8,128)S(1)} collective-permute-done((f32[24,1536]{1,0:T(8,128)S(1)}, f32[24,1536]{1,0:T(8,128)S(1)}, u32[]{:S(2)}, u32[]{:S(2)}) %collective-permute-start.27) | collective-permute-done | bytes 147488 | tf_op jit(solution)/shard_map/ppermute | solution.py:17
  286.0 3.9 %collective-permute-done.29 = f32[24,1536]{1,0:T(8,128)S(1)} collective-permute-done((f32[24,1536]{1,0:T(8,128)S(1)}, f32[24,1536]{1,0:T(8,128)S(1)}, u32[]{:S(2)}, u32[]{:S(2)}) %collective-permute-start.29) | collective-permute-done | bytes 147488 | tf_op jit(solution)/shard_map/ppermute | solution.py:17
  296.0 2.8 collective-permute-done.32
  302.2 2.8 collective-permute-done.34
  (151 shorter events, 72.5 us)
Async XLA Ops:
  3.0 4.8 %collective-permute-start.9 = (f32[84,512]{1,0:T(8,128)}, f32[84,512]{1,0:T(8,128)}, u32[]{:S(2)}, u32[]{:S(2)}) collective-permute-start(f32[84,512]{1,0:T(8,128)} %get-tuple-element.15), channel_id=1, source_target_pairs={{0,4},{4,0},{8,12},{12,8},{16,20},{20,16},{24,28},{28,24},{1,5},{5... | collective-permute-start | bytes 516104 | tf_op jit(solution)/shard_map/ppermute | solution.py:17
  6.8 4.3 %collective-permute-start = (f32[84,1536]{1,0:T(8,128)}, f32[84,1536]{1,0:T(8,128)}, u32[]{:S(2)}, u32[]{:S(2)}) collective-permute-start(f32[84,1536]{1,0:T(8,128)} %get-tuple-element.10), channel_id=1, source_target_pairs={{0,4},{4,0},{8,12},{12,8},{16,20},{20,16},{24,28},{28,24},{1,5},{5... | collective-permute-start | bytes 1548296 | tf_op jit(solution)/shard_map/ppermute | solution.py:17
  7.3 8.9 %collective-permute-start.2 = (f32[84,1536]{1,0:T(8,128)}, f32[84,1536]{1,0:T(8,128)}, u32[]{:S(2)}, u32[]{:S(2)}) collective-permute-start(f32[84,1536]{1,0:T(8,128)} %get-tuple-element.8), channel_id=1, source_target_pairs={{0,4},{4,0},{8,12},{12,8},{16,20},{20,16},{24,28},{28,24},{1,5},{5... | collective-permute-start | bytes 1548296 | tf_op jit(solution)/shard_map/ppermute | solution.py:17
  7.7 11.0 %collective-permute-start.4 = (f32[84,1536]{1,0:T(8,128)}, f32[84,1536]{1,0:T(8,128)}, u32[]{:S(2)}, u32[]{:S(2)}) collective-permute-start(f32[84,1536]{1,0:T(8,128)} %get-tuple-element.6), channel_id=1, source_target_pairs={{0,4},{4,0},{8,12},{12,8},{16,20},{20,16},{24,28},{28,24},{1,5},{5... | collective-permute-start | bytes 1548296 | tf_op jit(solution)/shard_map/ppermute | solution.py:17
  7.8 3.0 collective-permute-start.11
  9.4 127.9 %collective-permute-start.6 = (f32[84,1536]{1,0:T(8,128)}, f32[84,1536]{1,0:T(8,128)S(1)}, u32[]{:S(2)}, u32[]{:S(2)}) collective-permute-start(f32[84,1536]{1,0:T(8,128)} %get-tuple-element.5), channel_id=1, source_target_pairs={{0,4},{4,0},{8,12},{12,8},{16,20},{20,16},{24,28},{28,24},{1,5},{5... | collective-permute-start | bytes 1548296 | tf_op jit(solution)/shard_map/ppermute | solution.py:17
  10.8 59.9 %collective-permute-start.13 = (f32[84,512]{1,0:T(8,128)S(1)}, f32[84,512]{1,0:T(8,128)S(1)}, u32[]{:S(2)}, u32[]{:S(2)}) collective-permute-start(f32[84,512]{1,0:T(8,128)S(1)} %get-tuple-element.19), channel_id=1, source_target_pairs={{0,4},{4,0},{8,12},{12,8},{16,20},{20,16},{24,28},{28,24},{1,5},{5... | collective-permute-start | bytes 516104 | tf_op jit(solution)/shard_map/ppermute | solution.py:17
  11.1 26.8 %collective-permute-start.10 = (f32[168,512]{1,0:T(8,128)S(1)}, f32[168,512]{1,0:T(8,128)S(1)}, u32[]{:S(2)}, u32[]{:S(2)}) collective-permute-start(f32[168,512]{1,0:T(8,128)S(1)} %maximum_select_fusion.6), channel_id=1, source_target_pairs={{0,16},{4,20},{8,24},{12,28},{16,0},{20,4},{24,8},{28,12},{1,17},{... | collective-permute-start | bytes 1032200 | tf_op jit(solution)/shard_map/ppermute | solution.py:17
  16.2 15.2 %collective-permute-start.8 = (f32[168,512]{1,0:T(8,128)S(1)}, f32[168,512]{1,0:T(8,128)S(1)}, u32[]{:S(2)}, u32[]{:S(2)}) collective-permute-start(f32[168,512]{1,0:T(8,128)S(1)} %maximum_select_fusion.5), channel_id=1, source_target_pairs={{0,24},{4,28},{8,16},{12,20},{16,8},{20,12},{24,0},{28,4},{1,25},{... | collective-permute-start | bytes 1032200 | tf_op jit(solution)/shard_map/ppermute | solution.py:17
  18.7 51.7 %collective-permute-start.12 = (f32[168,512]{1,0:T(8,128)S(1)}, f32[168,512]{1,0:T(8,128)S(1)}, u32[]{:S(2)}, u32[]{:S(2)}) collective-permute-start(f32[168,512]{1,0:T(8,128)S(1)} %maximum_select_fusion.7), channel_id=1, source_target_pairs={{0,8},{4,12},{8,0},{12,4},{16,24},{20,28},{24,16},{28,20},{1,9},{5... | collective-permute-start | bytes 1032200 | tf_op jit(solution)/shard_map/ppermute | solution.py:17
  31.4 41.3 %collective-permute-start.1 = (f32[168,1536]{1,0:T(8,128)S(1)}, f32[168,1536]{1,0:T(8,128)S(1)}, u32[]{:S(2)}, u32[]{:S(2)}) collective-permute-start(f32[168,1536]{1,0:T(8,128)S(1)} %maximum_select_fusion), channel_id=1, source_target_pairs={{0,24},{4,28},{8,16},{12,20},{16,8},{20,12},{24,0},{28,4},{1,25},{... | collective-permute-start | bytes 3096584 | tf_op jit(solution)/shard_map/ppermute | solution.py:17
  37.9 99.1 %collective-permute-start.3 = (f32[168,1536]{1,0:T(8,128)S(1)}, f32[168,1536]{1,0:T(8,128)S(1)}, u32[]{:S(2)}, u32[]{:S(2)}) collective-permute-start(f32[168,1536]{1,0:T(8,128)S(1)} %maximum_select_fusion.1), channel_id=1, source_target_pairs={{0,16},{4,20},{8,24},{12,28},{16,0},{20,4},{24,8},{28,12},{1,17},{... | collective-permute-start | bytes 3096584 | tf_op jit(solution)/shard_map/ppermute | solution.py:17
  70.4 66.8 %collective-permute-start.5 = (f32[168,1536]{1,0:T(8,128)S(1)}, f32[168,1536]{1,0:T(8,128)S(1)}, u32[]{:S(2)}, u32[]{:S(2)}) collective-permute-start(f32[168,1536]{1,0:T(8,128)S(1)} %maximum_select_fusion.2), channel_id=1, source_target_pairs={{0,8},{4,12},{8,0},{12,4},{16,24},{20,28},{24,16},{28,20},{1,9},{5... | collective-permute-start | bytes 3096584 | tf_op jit(solution)/shard_map/ppermute | solution.py:17
  143.6 2.7 collective-permute-start.14
  147.7 5.7 %collective-permute-start.15 = (f32[88,336]{0,1:T(8,128)S(1)}, f32[88,336]{0,1:T(8,128)S(1)}, u32[]{:S(2)}, u32[]{:S(2)}) collective-permute-start(f32[88,336]{0,1:T(8,128)S(1)} %get-tuple-element.32), channel_id=1, source_target_pairs={{0,1},{1,0},{2,3},{3,2},{4,5},{5,4},{6,7},{7,6},{8,9},{9,8},{10,11... | collective-permute-start | bytes 354824 | tf_op jit(solution)/shard_map/ppermute | solution.py:17
  149.0 5.3 %collective-permute-start.16 = (f32[88,336]{0,1:T(8,128)S(1)}, f32[88,336]{0,1:T(8,128)S(1)}, u32[]{:S(2)}, u32[]{:S(2)}) collective-permute-start(f32[88,336]{0,1:T(8,128)S(1)} %get-tuple-element.34), channel_id=1, source_target_pairs={{0,2},{1,3},{2,0},{3,1},{4,6},{5,7},{6,4},{7,5},{8,10},{9,11},{10,... | collective-permute-start | bytes 354824 | tf_op jit(solution)/shard_map/ppermute | solution.py:17
  150.3 7.8 %collective-permute-start.17 = (f32[88,336]{0,1:T(8,128)S(1)}, f32[88,336]{0,1:T(8,128)S(1)}, u32[]{:S(2)}, u32[]{:S(2)}) collective-permute-start(f32[88,336]{0,1:T(8,128)S(1)} %get-tuple-element.33), channel_id=1, source_target_pairs={{0,3},{1,2},{2,1},{3,0},{4,7},{5,6},{6,5},{7,4},{8,11},{9,10},{10,... | collective-permute-start | bytes 354824 | tf_op jit(solution)/shard_map/ppermute | solution.py:17
  158.2 7.3 %collective-permute-start.18 = (f32[88,336]{0,1:T(8,128)S(1)}, f32[88,336]{0,1:T(8,128)S(1)}, u32[]{:S(2)}, u32[]{:S(2)}) collective-permute-start(f32[88,336]{0,1:T(8,128)S(1)} %add_add_fusion.1), channel_id=1, source_target_pairs={{0,8},{4,12},{8,0},{12,4},{16,24},{20,28},{24,16},{28,20},{1,9},{5... | collective-permute-start | bytes 354824 | tf_op jit(solution)/shard_map/ppermute | solution.py:17
  158.3 7.2 %collective-permute-start.19 = (f32[88,336]{0,1:T(8,128)S(1)}, f32[88,336]{0,1:T(8,128)S(1)}, u32[]{:S(2)}, u32[]{:S(2)}) collective-permute-start(f32[88,336]{0,1:T(8,128)S(1)} %add_add_fusion.1), channel_id=1, source_target_pairs={{0,16},{4,20},{8,24},{12,28},{16,0},{20,4},{24,8},{28,12},{1,17},{... | collective-permute-start | bytes 354824 | tf_op jit(solution)/shard_map/ppermute | solution.py:17
  160.9 10.4 %collective-permute-start.20 = (f32[88,336]{0,1:T(8,128)S(1)}, f32[88,336]{0,1:T(8,128)S(1)}, u32[]{:S(2)}, u32[]{:S(2)}) collective-permute-start(f32[88,336]{0,1:T(8,128)S(1)} %add_add_fusion.1), channel_id=1, source_target_pairs={{0,24},{4,28},{8,16},{12,20},{16,8},{20,12},{24,0},{28,4},{1,25},{... | collective-permute-start | bytes 354824 | tf_op jit(solution)/shard_map/ppermute | solution.py:17
  171.4 4.3 %collective-permute-start.21 = (f32[88,336]{0,1:T(8,128)S(1)}, f32[88,336]{0,1:T(8,128)S(1)}, u32[]{:S(2)}, u32[]{:S(2)}) collective-permute-start(f32[88,336]{0,1:T(8,128)S(1)} %add_add_fusion), channel_id=1, source_target_pairs={{0,1},{1,0},{2,3},{3,2},{4,5},{5,4},{6,7},{7,6},{8,9},{9,8},{10,11... | collective-permute-start | bytes 354824 | tf_op jit(solution)/shard_map/ppermute | solution.py:17
  172.8 6.4 %collective-permute-start.22 = (f32[88,336]{0,1:T(8,128)S(1)}, f32[88,336]{0,1:T(8,128)S(1)}, u32[]{:S(2)}, u32[]{:S(2)}) collective-permute-start(f32[88,336]{0,1:T(8,128)S(1)} %add_add_fusion), channel_id=1, source_target_pairs={{0,2},{1,3},{2,0},{3,1},{4,6},{5,7},{6,4},{7,5},{8,10},{9,11},{10,... | collective-permute-start | bytes 354824 | tf_op jit(solution)/shard_map/ppermute | solution.py:17
  172.8 6.5 %collective-permute-start.23 = (f32[88,336]{0,1:T(8,128)S(1)}, f32[88,336]{0,1:T(8,128)S(1)}, u32[]{:S(2)}, u32[]{:S(2)}) collective-permute-start(f32[88,336]{0,1:T(8,128)S(1)} %add_add_fusion), channel_id=1, source_target_pairs={{0,3},{1,2},{2,1},{3,0},{4,7},{5,6},{6,5},{7,4},{8,11},{9,10},{10,... | collective-permute-start | bytes 354824 | tf_op jit(solution)/shard_map/ppermute | solution.py:17
  179.8 6.6 %collective-permute-start.24 = (f32[352,336]{0,1:T(8,128)S(1)}, f32[352,336]{0,1:T(8,128)}, u32[]{:S(2)}, u32[]{:S(2)}) collective-permute-start(f32[352,336]{0,1:T(8,128)S(1)} %copy.17), channel_id=1, source_target_pairs={{0,4},{4,0},{8,12},{12,8},{16,20},{20,16},{24,28},{28,24},{1,5},{5... | collective-permute-start | bytes 1419272 | tf_op jit(solution)/shard_map/ppermute | solution.py:17
  261.7 6.9 %collective-permute-start.25 = (f32[24,1536]{1,0:T(8,128)S(1)}, f32[24,1536]{1,0:T(8,128)S(1)}, u32[]{:S(2)}, u32[]{:S(2)}) collective-permute-start(f32[24,1536]{1,0:T(8,128)S(1)} %get-tuple-element.31), channel_id=1, source_target_pairs={{0,24},{4,28},{8,16},{12,20},{16,8},{20,12},{24,0},{28,4},{1,25},{... | collective-permute-start | bytes 442376 | tf_op jit(solution)/shard_map/ppermute | solution.py:17
  270.3 5.4 %collective-permute-start.26 = (f32[12,1536]{1,0:T(8,128)S(1)}, f32[12,1536]{1,0:T(8,128)S(1)}, u32[]{:S(2)}, u32[]{:S(2)}) collective-permute-start(f32[12,1536]{1,0:T(8,128)S(1)} %get-tuple-element.44), channel_id=1, source_target_pairs={{0,4},{4,0},{8,12},{12,8},{16,20},{20,16},{24,28},{28,24},{1,5},{5... | collective-permute-start | bytes 221192 | tf_op jit(solution)/shard_map/ppermute | solution.py:17
  271.6 11.5 %collective-permute-start.27 = (f32[24,1536]{1,0:T(8,128)S(1)}, f32[24,1536]{1,0:T(8,128)S(1)}, u32[]{:S(2)}, u32[]{:S(2)}) collective-permute-start(f32[24,1536]{1,0:T(8,128)S(1)} %get-tuple-element.30), channel_id=1, source_target_pairs={{0,16},{4,20},{8,24},{12,28},{16,0},{20,4},{24,8},{28,12},{1,17},{... | collective-permute-start | bytes 442376 | tf_op jit(solution)/shard_map/ppermute | solution.py:17
  284.4 5.5 %collective-permute-start.29 = (f32[24,1536]{1,0:T(8,128)S(1)}, f32[24,1536]{1,0:T(8,128)S(1)}, u32[]{:S(2)}, u32[]{:S(2)}) collective-permute-start(f32[24,1536]{1,0:T(8,128)S(1)} %get-tuple-element.29), channel_id=1, source_target_pairs={{0,8},{4,12},{8,0},{12,4},{16,24},{20,28},{24,16},{28,20},{1,9},{5... | collective-permute-start | bytes 442376 | tf_op jit(solution)/shard_map/ppermute | solution.py:17
  294.0 4.8 %collective-permute-start.32 = (f32[24,512]{1,0:T(8,128)S(1)}, f32[24,512]{1,0:T(8,128)S(1)}, u32[]{:S(2)}, u32[]{:S(2)}) collective-permute-start(f32[24,512]{1,0:T(8,128)S(1)} %get-tuple-element.39), channel_id=1, source_target_pairs={{0,24},{4,28},{8,16},{12,20},{16,8},{20,12},{24,0},{28,4},{1,25},{... | collective-permute-start | bytes 147464 | tf_op jit(solution)/shard_map/ppermute | solution.py:17
  299.4 2.2 collective-permute-start.33
  300.7 4.3 %collective-permute-start.34 = (f32[24,512]{1,0:T(8,128)S(1)}, f32[24,512]{1,0:T(8,128)S(1)}, u32[]{:S(2)}, u32[]{:S(2)}) collective-permute-start(f32[24,512]{1,0:T(8,128)S(1)} %get-tuple-element.38), channel_id=1, source_target_pairs={{0,16},{4,20},{8,24},{12,28},{16,0},{20,4},{24,8},{28,12},{1,17},{... | collective-permute-start | bytes 147464 | tf_op jit(solution)/shard_map/ppermute | solution.py:17
  306.4 3.4 %collective-permute-start.36 = (f32[24,512]{1,0:T(8,128)S(1)}, f32[24,512]{1,0:T(8,128)S(1)}, u32[]{:S(2)}, u32[]{:S(2)}) collective-permute-start(f32[24,512]{1,0:T(8,128)S(1)} %get-tuple-element.37), channel_id=1, source_target_pairs={{0,8},{4,12},{8,0},{12,4},{16,24},{20,28},{24,16},{28,20},{1,9},{5... | collective-permute-start | bytes 147464 | tf_op jit(solution)/shard_map/ppermute | solution.py:17
  (12 other events, 286.8 us)

commit v2 on v1

--- a/solution.py
+++ b/solution.py
@@ -1,16 +1,15 @@
+import functools
+
 import jax
 import jax.numpy as jnp
 from jax import lax
+from jax.experimental import pallas as pl
+from jax.experimental.pallas import tpu as pltpu
 from jax.sharding import PartitionSpec as P
 
 ITERS = 3
 HIGH = lax.Precision.HIGH
 HIGHEST = lax.Precision.HIGHEST
-
-
-def orthonormal(image, small):
-    lower = jnp.linalg.cholesky(small)
-    return lax.linalg.triangular_solve(lower, image, left_side=False, lower=True, transpose_a=True)
 
 
 def swap(x, axis, size, bits):
@@ -67,6 +66,85 @@
     return in_order(core, out, swap(out, "fibre", fibre, 1), 0)
 
 
+def lower_inverse(small):
+    n = small.shape[0]
+    lanes = 128
+    full = (8, lanes)
+    col = lax.broadcasted_iota(jnp.int32, full, 1)
+    row = lax.broadcasted_iota(jnp.int32, full, 0)
+    left = [small[8 * i : 8 * i + 8, :] for i in range(n // 8)]
+    right = [(col == row + 8 * i).astype(jnp.float32) for i in range(n // 8)]
+    done = []
+    for p in range(n // 8):
+        at = 8 * p
+        d = {(a, b): jnp.broadcast_to(left[p][a : a + 1, at + b : at + b + 1], full) for a in range(8) for b in range(a + 1)}
+        low, inv_diag = {}, []
+        for b in range(8):
+            r = lax.rsqrt(d[b, b])
+            inv_diag.append(r)
+            for a in range(b + 1, 8):
+                low[a, b] = d[a, b] * r
+            for a in range(b + 1, 8):
+                for c in range(b + 1, a + 1):
+                    d[a, c] = d[a, c] - low[a, b] * low[c, b]
+        inv = {}
+        for b in range(8):
+            inv[b, b] = inv_diag[b]
+            for a in range(b + 1, 8):
+                s = low[a, b] * inv[b, b]
+                for k in range(b + 1, a):
+                    s = s + low[a, k] * inv[k, b]
+                inv[a, b] = -s * inv_diag[a]
+        lrow = [jnp.broadcast_to(left[p][k : k + 1, :], full) for k in range(8)]
+        rrow = [jnp.broadcast_to(right[p][k : k + 1, :], full) for k in range(8)]
+        y, v = [], []
+        for m in range(8):
+            ym, vm = inv[m, 0] * lrow[0], inv[m, 0] * rrow[0]
+            for k in range(1, m + 1):
+                ym, vm = ym + inv[m, k] * lrow[k], vm + inv[m, k] * rrow[k]
+            y.append(ym)
+            v.append(vm)
+        out = v[0]
+        for m in range(1, 8):
+            out = jnp.where(row == m, v[m], out)
+        done.append(out)
+        for i in range(p + 1, n // 8):
+            c = [jnp.broadcast_to(left[i][:, at + k : at + k + 1], full) for k in range(8)]
+            li, ri = left[i], right[i]
+            for m in range(8):
+                f = inv[m, 0] * c[0]
+                for k in range(1, m + 1):
+                    f = f + inv[m, k] * c[k]
+                li = li - f * y[m]
+                ri = ri - f * v[m]
+            left[i], right[i] = li, ri
+    return jnp.concatenate(done, 0)
+
+
+def iterations_kernel(iters, gram_ref, start_ref, factor_ref):
+    def times(a, b, dims):
+        return lax.dot_general(a, b, (dims, ((), ())), precision=HIGHEST, preferred_element_type=jnp.float32)
+
+    image = times(gram_ref[...], start_ref[...], ((1,), (0,)))
+    for step in range(iters):
+        small = times(image, image, ((0,), (0,)))
+        inverse = lower_inverse(jnp.pad(small, ((0, 0), (0, 128 - small.shape[1]))))[:, : small.shape[1]]
+        if step < iters - 1:
+            image = times(times(gram_ref[...], image, ((1,), (0,))), inverse, ((1,), (1,)))
+        else:
+            factor_ref[...] = times(image, inverse, ((1,), (1,)))
+
+def iterations(gram, start, iters=3):
+    return pl.pallas_call(
+        functools.partial(iterations_kernel, iters),
+        out_shape=jax.ShapeDtypeStruct(start.shape, jnp.float32),
+        in_specs=[pl.BlockSpec(memory_space=pltpu.VMEM)] * 2,
+        out_specs=pl.BlockSpec(memory_space=pltpu.VMEM),
+        compiler_params=pltpu.CompilerParams(vmem_limit_bytes=32 * 2**20),
+        name="iterations",
+    )(gram, start)
+
+
 def shards(fibre, rest, slab, start_basis):
     rows, cols = slab.shape
     zs = fibre // 2
@@ -74,17 +152,21 @@
     z, core = f // 2, f % 2
     half = cols // 2
     part = half // zs
-    chunks = [(0, part * 3 // 4), (part * 3 // 4, part // 4)]
+    unit = part // 8
+    chunks = [(0, unit), (unit, 5 * unit), (6 * unit, 2 * unit)]
     order = list(range(zs - 1, -1, -1))
     gram = 0.0
     fibres = []
     for start, width in chunks:
-        whole = jnp.zeros((zs, 2 * rows, width), jnp.float32)
+        blocks = []
         for bits in order:
             at = (z ^ bits) * part + start
             mine = lax.dynamic_slice(slab, (0, core * half + at), (rows, width))
             theirs = lax.dynamic_slice(slab, (0, (1 - core) * half + at), (rows, width))
-            block = in_order(core, mine, swap(theirs, "fibre", fibre, 1), 0)
+            blocks.append(in_order(core, mine, swap(theirs, "fibre", fibre, 1), 0))
+        slab, blocks = lax.optimization_barrier((slab, blocks))
+        whole = jnp.zeros((zs, 2 * rows, width), jnp.float32)
+        for bits, block in zip(order, blocks):
             if bits:
                 block = swap(block, "fibre", fibre, 2 * bits)
             whole = lax.dynamic_update_slice(whole, block[None], (z ^ bits, 0, 0))
@@ -93,27 +175,24 @@
         gram = gram + jnp.dot(whole, whole.T, precision=HIGH, preferred_element_type=jnp.float32)
     n = gram.shape[0]
     gram = unpack(sum_everywhere(pack(gram), fibre, rest), n)
-    basis = start_basis
-    for step in range(ITERS):
-        image = jnp.dot(gram, basis, precision=HIGHEST, preferred_element_type=jnp.float32)
-        small = jnp.dot(image.T, image, precision=HIGHEST, preferred_element_type=jnp.float32)
-        basis = orthonormal(image, small)
+    basis = iterations(gram, start_basis, ITERS)
     rank = basis.shape[1]
     own = rank // fibre
-    out = jnp.zeros((own, cols), jnp.float32)
-    for (start, width), whole in zip(chunks, fibres):
-        share = jnp.dot(basis.T, whole, precision=HIGH, preferred_element_type=jnp.float32)
-        for bits in order:
-            block = lax.dynamic_slice(share, ((z ^ bits) * 2 * own, 0), (2 * own, width))
-            if bits:
-                block = swap(block, "fibre", fibre, 2 * bits)
-            mine = lax.dynamic_slice(block, (core * own, 0), (own, width))
-            theirs = lax.dynamic_slice(block, ((1 - core) * own, 0), (own, width))
-            other = swap(theirs, "fibre", fibre, 1)
-            at = (z ^ bits) * part + start
-            out = lax.dynamic_update_slice(out, mine, (0, core * half + at))
-            out = lax.dynamic_update_slice(out, other, (0, (1 - core) * half + at))
-    return (basis, out)
+    rows_of = [lax.dynamic_slice(basis.T, ((z ^ bits) * 2 * own, 0), (2 * own, n)) for bits in range(zs)]
+    rows_of = jnp.concatenate(rows_of, 0)
+    share = [jnp.dot(rows_of, whole, precision=HIGH, preferred_element_type=jnp.float32) for whole in fibres]
+    share = jnp.concatenate(share, 1)
+    arrived = jnp.zeros((zs, 2 * own, part), jnp.float32)
+    for bits in order:
+        block = share[2 * own * bits : 2 * own * (bits + 1)]
+        if bits:
+            block = swap(block, "fibre", fibre, 2 * bits)
+        arrived = lax.dynamic_update_slice(arrived, block[None], (z ^ bits, 0, 0))
+    mine = lax.dynamic_slice(arrived, (0, core * own, 0), (zs, own, part))
+    theirs = lax.dynamic_slice(arrived, (0, (1 - core) * own, 0), (zs, own, part))
+    theirs = theirs.transpose(1, 0, 2).reshape(own, half)
+    mine = mine.transpose(1, 0, 2).reshape(own, half)
+    return (basis, in_order(core, mine, swap(theirs, "fibre", fibre, 1), 1))
 
 
 def solution(mesh):

time: 316 us -> 247 us (0.78)
  other arithmetic: 64 us -> 8.89 us
  waiting for transfers between devices: 132 us -> 96.2 us
  starting transfers between devices: 71.1 us -> 90.1 us
  Pallas kernels: 0 us -> 18 us
  matrix products: 22.1 us -> 9.68 us
    another operation x15 -> x0, other arithmetic: 52.4 us -> none  [the longest x9 28.4 us: orthonormal(): lower = jnp.linalg.cholesky(small)]
    ppermute x39 -> x36, waiting for transfers between devices: 132 us -> 96.2 us  [swap(): return lax.ppermute(x, axis, [(i, i ^ bits) for i in range(size)])]
    ppermute x39 -> x36, starting transfers between devices: 71.1 us -> 90.1 us  [swap(): return lax.ppermute(x, axis, [(i, i ^ bits) for i in range(size)])]
    pallas_call x0 -> x1, Pallas kernels: none -> 18 us  [iterations(): pl.pallas_call(functools.partial(iterations_kernel, iters), out_shape=jax...]
    dot_general x8 -> x3, matrix products: 13.8 us -> 2.22 us  [shards(): jnp.dot(rows_of, whole, precision=HIGH, preferred_element_type=jnp.float32)]
    concatenate x2 -> x0, local copies, waits for them, and re-layouts: 5.99 us -> none  [in_order(): jnp.concatenate([mine, other], axis)]
    select_n x7 -> x14, other arithmetic: 7.84 us -> 1.88 us  [in_order(): jnp.where(core == 0, jnp.concatenate([mine, other], axis), jnp.concatenat...]
    unnamed x10 -> x16, local copies, waits for them, and re-layouts: 0.03 us -> 5.23 us
  transfers between devices with their start and end apart: 39 -> 36, of which waited for: 25 -> 25; matrix products, arithmetic and copies ran while one was open for 5% -> 4% of each run, Pallas kernels for 0% -> 0%
where the time goes in v2:
time: 247 us; the launch traced here: 246 us
  waiting for transfers between devices  96.2 us (39%)
  starting transfers between devices  90.1 us (36%)
  local copies, waits for them, and re-layouts  22.1 us (9%)
  Pallas kernels  18 us (7%)
  matrix products  9.68 us (4%)
  other arithmetic  8.89 us (4%)
    ppermute x36, waiting for transfers between devices, swap(): return lax.ppermute(x, axis, [(i, i ^ bits) for i in range(size)])  96.2 us
    ppermute x36, starting transfers between devices, swap(): return lax.ppermute(x, axis, [(i, i ^ bits) for i in range(size)])  90.1 us
    pallas_call x1, Pallas kernels, iterations(): pl.pallas_call(functools.partial(iterations_kernel, iters), out_shape=jax...  18 us
    dot_general x3, matrix products, shards(): jnp.dot(whole, whole.T, precision=HIGH, preferred_element_type=jnp.float32)  7.46 us
    unnamed x16, local copies, waits for them, and re-layouts  5.23 us
    dynamic_slice x3, local copies, waits for them, and re-layouts, shards(): mine = lax.dynamic_slice(slab, (0, core * half + at), (rows, width))  5.01 us
  transfers between devices with their start and end apart: 36, of which 25 were waited for; matrix products, arithmetic and copies ran while one was open for 4% of the time, Pallas kernels for 0%

profile of v2, /device:TPU:1, one launch (start us, length us, event | category | flops | bytes accessed | tf_op | source)
XLA Modules:
  0.0 246.2 jit_solution(8223225097533600223)
XLA Ops:
  4.0 4.7 %collective-permute-start.4 = (f32[168,256]{1,0:T(8,128)S(1)}, f32[168,256]{1,0:T(8,128)S(1)}, u32[]{:S(2)}, u32[]{:S(2)}) collective-permute-start(f32[168,256]{1,0:T(8,128)S(1)} %maximum_select_fusion.10), channel_id=1, source_target_pairs={{0,24},{4,28},{8,16},{12,20},{16,8},{20,12},{24,0},{28,4},{1,25},{... | collective-permute-start | bytes 516104 | tf_op jit(solution)/shard_map/ppermute | solution.py:16
  8.8 2.2 constant_dynamic-slice_fusion.13
  13.4 3.9 %collective-permute-start.5 = (f32[168,256]{1,0:T(8,128)S(1)}, f32[168,256]{1,0:T(8,128)S(1)}, u32[]{:S(2)}, u32[]{:S(2)}) collective-permute-start(f32[168,256]{1,0:T(8,128)S(1)} %maximum_select_fusion.11), channel_id=1, source_target_pairs={{0,16},{4,20},{8,24},{12,28},{16,0},{20,4},{24,8},{28,12},{1,17},{... | collective-permute-start | bytes 516104 | tf_op jit(solution)/shard_map/ppermute | solution.py:16
  17.3 7.4 %collective-permute-done.5 = f32[168,256]{1,0:T(8,128)S(1)} collective-permute-done((f32[168,256]{1,0:T(8,128)S(1)}, f32[168,256]{1,0:T(8,128)S(1)}, u32[]{:S(2)}, u32[]{:S(2)}) %collective-permute-start.5) | collective-permute-done | bytes 172064 | tf_op jit(solution)/shard_map/ppermute | solution.py:16
  26.8 1.6 collective-permute-start.17
  29.0 2.8 %collective-permute-start.15 = (f32[84,512]{1,0:T(8,128)S(1)}, f32[84,512]{1,0:T(8,128)S(1)}, u32[]{:S(2)}, u32[]{:S(2)}) collective-permute-start(f32[84,512]{1,0:T(8,128)S(1)} %get-tuple-element.40), channel_id=1, source_target_pairs={{0,4},{4,0},{8,12},{12,8},{16,20},{20,16},{24,28},{28,24},{1,5},{5... | collective-permute-start | bytes 516104 | tf_op jit(solution)/shard_map/ppermute | solution.py:16
  36.0 1.8 collective-permute-start.11
  39.6 5.0 %collective-permute-done.18 = f32[168,512]{1,0:T(8,128)S(1)} collective-permute-done((f32[168,512]{1,0:T(8,128)S(1)}, f32[168,512]{1,0:T(8,128)S(1)}, u32[]{:S(2)}, u32[]{:S(2)}) %collective-permute-start.18) | collective-permute-done | bytes 344096 | tf_op jit(solution)/shard_map/ppermute | solution.py:16
  44.6 49.6 %collective-permute-start.20 = (f32[168,512]{1,0:T(8,128)S(1)}, f32[168,512]{1,0:T(8,128)S(1)}, u32[]{:S(2)}, u32[]{:S(2)}) collective-permute-start(f32[168,512]{1,0:T(8,128)S(1)} %maximum_select_fusion.8), channel_id=1, source_target_pairs={{0,8},{4,12},{8,0},{12,4},{16,24},{20,28},{24,16},{28,20},{1,9},{5... | collective-permute-start | bytes 1032200 | tf_op jit(solution)/shard_map/ppermute | solution.py:16
  94.4 6.9 %collective-permute-done.19 = f32[168,512]{1,0:T(8,128)S(1)} collective-permute-done((f32[168,512]{1,0:T(8,128)S(1)}, f32[168,512]{1,0:T(8,128)S(1)}, u32[]{:S(2)}, u32[]{:S(2)}) %collective-permute-start.19) | collective-permute-done | bytes 344096 | tf_op jit(solution)/shard_map/ppermute | solution.py:16
  101.4 10.9 %collective-permute-done.20 = f32[168,512]{1,0:T(8,128)S(1)} collective-permute-done((f32[168,512]{1,0:T(8,128)S(1)}, f32[168,512]{1,0:T(8,128)S(1)}, u32[]{:S(2)}, u32[]{:S(2)}) %collective-permute-start.20) | collective-permute-done | bytes 344096 | tf_op jit(solution)/shard_map/ppermute | solution.py:16
  112.6 25.6 %collective-permute-done.12 = f32[168,1280]{1,0:T(8,128)S(1)} collective-permute-done((f32[168,1280]{1,0:T(8,128)S(1)}, f32[168,1280]{1,0:T(8,128)S(1)}, u32[]{:S(2)}, u32[]{:S(2)}) %collective-permute-start.12) | collective-permute-done | bytes 860192 | tf_op jit(solution)/shard_map/ppermute | solution.py:16
  138.4 4.4 %fusion.3 = f32[672,672]{1,0:T(8,128)S(1)} fusion(f32[672,1280]{1,0:T(8,128)S(1)} %bitcast.81), kind=kOutput, calls=%fused_computation.90 | convolution fusion | flops 3468165120 | bytes 5246976 | tf_op jit(solution)/shard_map/dot_general | solution.py:175
  142.9 2.0 add_add_fusion
  146.1 2.1 copy.16
  149.2 1.9 collective-permute-done.21
  151.1 2.2 copy.17
  158.0 2.1 collective-permute-done.22
  161.0 2.9 %collective-permute-done.24 = f32[88,336]{1,0:T(8,128)S(1)} collective-permute-done((f32[88,336]{1,0:T(8,128)S(1)}, f32[88,336]{1,0:T(8,128)S(1)}, u32[]{:S(2)}, u32[]{:S(2)}) %collective-permute-start.24) | collective-permute-done | bytes 118304 | tf_op jit(solution)/shard_map/ppermute | solution.py:16
  164.9 1.7 collective-permute-start.26
  166.6 1.9 collective-permute-start.27
  168.5 2.4 collective-permute-done.25
  170.8 4.4 %collective-permute-done.27 = f32[88,336]{1,0:T(8,128)S(1)} collective-permute-done((f32[88,336]{1,0:T(8,128)S(1)}, f32[88,336]{1,0:T(8,128)S(1)}, u32[]{:S(2)}, u32[]{:S(2)}) %collective-permute-start.27) | collective-permute-done | bytes 118304 | tf_op jit(solution)/shard_map/ppermute | solution.py:16
  179.2 2.5 %collective-permute-done.29 = f32[88,336]{1,0:T(8,128)S(1)} collective-permute-done((f32[88,336]{1,0:T(8,128)S(1)}, f32[88,336]{1,0:T(8,128)S(1)}, u32[]{:S(2)}, u32[]{:S(2)}) %collective-permute-start.29) | collective-permute-done | bytes 118304 | tf_op jit(solution)/shard_map/ppermute | solution.py:16
  182.0 5.6 %collective-permute-start.31 = (f32[352,336]{0,1:T(8,128)S(1)}, f32[352,336]{0,1:T(8,128)}, u32[]{:S(2)}, u32[]{:S(2)}) collective-permute-start(f32[352,336]{0,1:T(8,128)S(1)} %copy.18), channel_id=1, source_target_pairs={{0,4},{4,0},{8,12},{12,8},{16,20},{20,16},{24,28},{28,24},{1,5},{5... | collective-permute-start | bytes 1419272 | tf_op jit(solution)/shard_map/ppermute | solution.py:16
  191.9 2.4 bitcast_select_fusion.1
  195.3 1.8 maximum_maximum_fusion.gram_ref
  197.1 18.0 %iterations.1 = f32[672,96]{1,0:T(8,128)S(1)} custom-call(f32[672,672]{1,0:T(8,128)S(1)} %maximum_maximum_fusion.gram_ref, f32[672,96]{1,0:T(8,128)S(1)} %copy.23.start_ref), custom_call_target="tpu_custom_call" | custom-call | tf_op jit(solution)/shard_map/iterations/pallas_call | solution.py:138
  220.5 1.9 collective-permute-start.33
  222.8 4.2 %collective-permute-done.32 = f32[24,2048]{1,0:T(8,128)S(1)} collective-permute-done((f32[24,2048]{1,0:T(8,128)S(1)}, f32[24,2048]{1,0:T(8,128)S(1)}, u32[]{:S(2)}, u32[]{:S(2)}) %collective-permute-start.32) | collective-permute-done | bytes 196640 | tf_op jit(solution)/shard_map/ppermute | solution.py:16
  227.1 13.2 %collective-permute-done.33 = f32[24,2048]{1,0:T(8,128)S(1)} collective-permute-done((f32[24,2048]{1,0:T(8,128)S(1)}, f32[24,2048]{1,0:T(8,128)S(1)}, u32[]{:S(2)}, u32[]{:S(2)}) %collective-permute-start.33) | collective-permute-done | bytes 196640 | tf_op jit(solution)/shard_map/ppermute | solution.py:16
  240.9 1.6 dynamic_update_slice.79
  (129 shorter events, 43.4 us)
Async XLA Ops:
  4.0 9.4 %collective-permute-start.4 = (f32[168,256]{1,0:T(8,128)S(1)}, f32[168,256]{1,0:T(8,128)S(1)}, u32[]{:S(2)}, u32[]{:S(2)}) collective-permute-start(f32[168,256]{1,0:T(8,128)S(1)} %maximum_select_fusion.10), channel_id=1, source_target_pairs={{0,24},{4,28},{8,16},{12,20},{16,8},{20,12},{24,0},{28,4},{1,25},{... | collective-permute-start | bytes 516104 | tf_op jit(solution)/shard_map/ppermute | solution.py:16
  11.0 13.8 %collective-permute-start.10 = (f32[84,1280]{1,0:T(8,128)S(1)}, f32[84,1280]{1,0:T(8,128)S(1)}, u32[]{:S(2)}, u32[]{:S(2)}) collective-permute-start(f32[84,1280]{1,0:T(8,128)S(1)} %get-tuple-element.45), channel_id=1, source_target_pairs={{0,4},{4,0},{8,12},{12,8},{16,20},{20,16},{24,28},{28,24},{1,5},{5... | collective-permute-start | bytes 1290248 | tf_op jit(solution)/shard_map/ppermute | solution.py:16
  11.5 13.4 %collective-permute-start.9 = (f32[84,1280]{1,0:T(8,128)S(1)}, f32[84,1280]{1,0:T(8,128)S(1)}, u32[]{:S(2)}, u32[]{:S(2)}) collective-permute-start(f32[84,1280]{1,0:T(8,128)S(1)} %get-tuple-element.46), channel_id=1, source_target_pairs={{0,4},{4,0},{8,12},{12,8},{16,20},{20,16},{24,28},{28,24},{1,5},{5... | collective-permute-start | bytes 1290248 | tf_op jit(solution)/shard_map/ppermute | solution.py:16
  11.5 13.5 %collective-permute-start.8 = (f32[84,1280]{1,0:T(8,128)S(1)}, f32[84,1280]{1,0:T(8,128)S(1)}, u32[]{:S(2)}, u32[]{:S(2)}) collective-permute-start(f32[84,1280]{1,0:T(8,128)S(1)} %get-tuple-element.48), channel_id=1, source_target_pairs={{0,4},{4,0},{8,12},{12,8},{16,20},{20,16},{24,28},{28,24},{1,5},{5... | collective-permute-start | bytes 1290248 | tf_op jit(solution)/shard_map/ppermute | solution.py:16
  12.0 13.2 %collective-permute-start.7 = (f32[84,1280]{1,0:T(8,128)S(1)}, f32[84,1280]{1,0:T(8,128)S(1)}, u32[]{:S(2)}, u32[]{:S(2)}) collective-permute-start(f32[84,1280]{1,0:T(8,128)S(1)} %get-tuple-element.50), channel_id=1, source_target_pairs={{0,4},{4,0},{8,12},{12,8},{16,20},{20,16},{24,28},{28,24},{1,5},{5... | collective-permute-start | bytes 1290248 | tf_op jit(solution)/shard_map/ppermute | solution.py:16
  13.4 11.3 %collective-permute-start.5 = (f32[168,256]{1,0:T(8,128)S(1)}, f32[168,256]{1,0:T(8,128)S(1)}, u32[]{:S(2)}, u32[]{:S(2)}) collective-permute-start(f32[168,256]{1,0:T(8,128)S(1)} %maximum_select_fusion.11), channel_id=1, source_target_pairs={{0,16},{4,20},{8,24},{12,28},{16,0},{20,4},{24,8},{28,12},{1,17},{... | collective-permute-start | bytes 516104 | tf_op jit(solution)/shard_map/ppermute | solution.py:16
  24.8 4.3 %collective-permute-start.6 = (f32[168,256]{1,0:T(8,128)S(1)}, f32[168,256]{1,0:T(8,128)S(1)}, u32[]{:S(2)}, u32[]{:S(2)}) collective-permute-start(f32[168,256]{1,0:T(8,128)S(1)} %maximum_select_fusion.12), channel_id=1, source_target_pairs={{0,8},{4,12},{8,0},{12,4},{16,24},{20,28},{24,16},{28,20},{1,9},{5... | collective-permute-start | bytes 516104 | tf_op jit(solution)/shard_map/ppermute | solution.py:16
  26.8 5.1 %collective-permute-start.17 = (f32[84,512]{1,0:T(8,128)S(1)}, f32[84,512]{1,0:T(8,128)S(1)}, u32[]{:S(2)}, u32[]{:S(2)}) collective-permute-start(f32[84,512]{1,0:T(8,128)S(1)} %get-tuple-element.37), channel_id=1, source_target_pairs={{0,4},{4,0},{8,12},{12,8},{16,20},{20,16},{24,28},{28,24},{1,5},{5... | collective-permute-start | bytes 516104 | tf_op jit(solution)/shard_map/ppermute | solution.py:16
  28.4 3.5 %collective-permute-start.16 = (f32[84,512]{1,0:T(8,128)S(1)}, f32[84,512]{1,0:T(8,128)S(1)}, u32[]{:S(2)}, u32[]{:S(2)}) collective-permute-start(f32[84,512]{1,0:T(8,128)S(1)} %get-tuple-element.38), channel_id=1, source_target_pairs={{0,4},{4,0},{8,12},{12,8},{16,20},{20,16},{24,28},{28,24},{1,5},{5... | collective-permute-start | bytes 516104 | tf_op jit(solution)/shard_map/ppermute | solution.py:16
  29.0 3.8 %collective-permute-start.15 = (f32[84,512]{1,0:T(8,128)S(1)}, f32[84,512]{1,0:T(8,128)S(1)}, u32[]{:S(2)}, u32[]{:S(2)}) collective-permute-start(f32[84,512]{1,0:T(8,128)S(1)} %get-tuple-element.40), channel_id=1, source_target_pairs={{0,4},{4,0},{8,12},{12,8},{16,20},{20,16},{24,28},{28,24},{1,5},{5... | collective-permute-start | bytes 516104 | tf_op jit(solution)/shard_map/ppermute | solution.py:16
  31.8 1.4 collective-permute-start.14
  33.2 11.3 %collective-permute-start.18 = (f32[168,512]{1,0:T(8,128)S(1)}, f32[168,512]{1,0:T(8,128)S(1)}, u32[]{:S(2)}, u32[]{:S(2)}) collective-permute-start(f32[168,512]{1,0:T(8,128)S(1)} %maximum_select_fusion.6), channel_id=1, source_target_pairs={{0,24},{4,28},{8,16},{12,20},{16,8},{20,12},{24,0},{28,4},{1,25},{... | collective-permute-start | bytes 1032200 | tf_op jit(solution)/shard_map/ppermute | solution.py:16
  34.9 66.5 %collective-permute-start.19 = (f32[168,512]{1,0:T(8,128)S(1)}, f32[168,512]{1,0:T(8,128)S(1)}, u32[]{:S(2)}, u32[]{:S(2)}) collective-permute-start(f32[168,512]{1,0:T(8,128)S(1)} %maximum_select_fusion.7), channel_id=1, source_target_pairs={{0,16},{4,20},{8,24},{12,28},{16,0},{20,4},{24,8},{28,12},{1,17},{... | collective-permute-start | bytes 1032200 | tf_op jit(solution)/shard_map/ppermute | solution.py:16
  36.0 76.3 %collective-permute-start.11 = (f32[168,1280]{1,0:T(8,128)S(1)}, f32[168,1280]{1,0:T(8,128)S(1)}, u32[]{:S(2)}, u32[]{:S(2)}) collective-permute-start(f32[168,1280]{1,0:T(8,128)S(1)} %maximum_select_fusion.2), channel_id=1, source_target_pairs={{0,24},{4,28},{8,16},{12,20},{16,8},{20,12},{24,0},{28,4},{1,25},{... | collective-permute-start | bytes 2580488 | tf_op jit(solution)/shard_map/ppermute | solution.py:16
  37.8 100.4 %collective-permute-start.12 = (f32[168,1280]{1,0:T(8,128)S(1)}, f32[168,1280]{1,0:T(8,128)S(1)}, u32[]{:S(2)}, u32[]{:S(2)}) collective-permute-start(f32[168,1280]{1,0:T(8,128)S(1)} %maximum_select_fusion.3), channel_id=1, source_target_pairs={{0,16},{4,20},{8,24},{12,28},{16,0},{20,4},{24,8},{28,12},{1,17},{... | collective-permute-start | bytes 2580488 | tf_op jit(solution)/shard_map/ppermute | solution.py:16
  39.2 99.0 %collective-permute-start.13 = (f32[168,1280]{1,0:T(8,128)S(1)}, f32[168,1280]{1,0:T(8,128)S(1)}, u32[]{:S(2)}, u32[]{:S(2)}) collective-permute-start(f32[168,1280]{1,0:T(8,128)S(1)} %maximum_select_fusion.4), channel_id=1, source_target_pairs={{0,8},{4,12},{8,0},{12,4},{16,24},{20,28},{24,16},{28,20},{1,9},{5... | collective-permute-start | bytes 2580488 | tf_op jit(solution)/shard_map/ppermute | solution.py:16
  44.6 67.6 %collective-permute-start.20 = (f32[168,512]{1,0:T(8,128)S(1)}, f32[168,512]{1,0:T(8,128)S(1)}, u32[]{:S(2)}, u32[]{:S(2)}) collective-permute-start(f32[168,512]{1,0:T(8,128)S(1)} %maximum_select_fusion.8), channel_id=1, source_target_pairs={{0,8},{4,12},{8,0},{12,4},{16,24},{20,28},{24,16},{28,20},{1,9},{5... | collective-permute-start | bytes 1032200 | tf_op jit(solution)/shard_map/ppermute | solution.py:16
  148.2 2.9 %collective-permute-start.21 = (f32[352,336]{0,1:T(8,128)}, f32[352,336]{0,1:T(8,128)}, u32[]{:S(2)}, u32[]{:S(2)}) collective-permute-start(f32[352,336]{0,1:T(8,128)} %copy.16), channel_id=1, source_target_pairs={{0,4},{4,0},{8,12},{12,8},{16,20},{20,16},{24,28},{28,24},{1,5},{5... | collective-permute-start | bytes 1419272 | tf_op jit(solution)/shard_map/ppermute | solution.py:16
  155.3 4.9 %collective-permute-start.22 = (f32[88,336]{1,0:T(8,128)S(1)}, f32[88,336]{1,0:T(8,128)S(1)}, u32[]{:S(2)}, u32[]{:S(2)}) collective-permute-start(f32[88,336]{1,0:T(8,128)S(1)} %get-tuple-element.73), channel_id=1, source_target_pairs={{0,1},{1,0},{2,3},{3,2},{4,5},{5,4},{6,7},{7,6},{8,9},{9,8},{10,11... | collective-permute-start | bytes 354824 | tf_op jit(solution)/shard_map/ppermute | solution.py:16
  156.6 4.5 %collective-permute-start.23 = (f32[88,336]{1,0:T(8,128)S(1)}, f32[88,336]{1,0:T(8,128)S(1)}, u32[]{:S(2)}, u32[]{:S(2)}) collective-permute-start(f32[88,336]{1,0:T(8,128)S(1)} %get-tuple-element.75), channel_id=1, source_target_pairs={{0,2},{1,3},{2,0},{3,1},{4,6},{5,7},{6,4},{7,5},{8,10},{9,11},{10,... | collective-permute-start | bytes 354824 | tf_op jit(solution)/shard_map/ppermute | solution.py:16
  157.8 6.1 %collective-permute-start.24 = (f32[88,336]{1,0:T(8,128)S(1)}, f32[88,336]{1,0:T(8,128)S(1)}, u32[]{:S(2)}, u32[]{:S(2)}) collective-permute-start(f32[88,336]{1,0:T(8,128)S(1)} %get-tuple-element.74), channel_id=1, source_target_pairs={{0,3},{1,2},{2,1},{3,0},{4,7},{5,6},{6,5},{7,4},{8,11},{9,10},{10,... | collective-permute-start | bytes 354824 | tf_op jit(solution)/shard_map/ppermute | solution.py:16
  164.8 6.0 %collective-permute-start.25 = (f32[88,336]{1,0:T(8,128)S(1)}, f32[88,336]{1,0:T(8,128)S(1)}, u32[]{:S(2)}, u32[]{:S(2)}) collective-permute-start(f32[88,336]{1,0:T(8,128)S(1)} %add_add_fusion.2), channel_id=1, source_target_pairs={{0,8},{4,12},{8,0},{12,4},{16,24},{20,28},{24,16},{28,20},{1,9},{5... | collective-permute-start | bytes 354824 | tf_op jit(solution)/shard_map/ppermute | solution.py:16
  164.9 5.9 %collective-permute-start.26 = (f32[88,336]{1,0:T(8,128)S(1)}, f32[88,336]{1,0:T(8,128)S(1)}, u32[]{:S(2)}, u32[]{:S(2)}) collective-permute-start(f32[88,336]{1,0:T(8,128)S(1)} %add_add_fusion.2), channel_id=1, source_target_pairs={{0,16},{4,20},{8,24},{12,28},{16,0},{20,4},{24,8},{28,12},{1,17},{... | collective-permute-start | bytes 354824 | tf_op jit(solution)/shard_map/ppermute | solution.py:16
  166.6 8.6 %collective-permute-start.27 = (f32[88,336]{1,0:T(8,128)S(1)}, f32[88,336]{1,0:T(8,128)S(1)}, u32[]{:S(2)}, u32[]{:S(2)}) collective-permute-start(f32[88,336]{1,0:T(8,128)S(1)} %add_add_fusion.2), channel_id=1, source_target_pairs={{0,24},{4,28},{8,16},{12,20},{16,8},{20,12},{24,0},{28,4},{1,25},{... | collective-permute-start | bytes 354824 | tf_op jit(solution)/shard_map/ppermute | solution.py:16
  175.3 3.9 %collective-permute-start.28 = (f32[88,336]{1,0:T(8,128)S(1)}, f32[88,336]{1,0:T(8,128)S(1)}, u32[]{:S(2)}, u32[]{:S(2)}) collective-permute-start(f32[88,336]{1,0:T(8,128)S(1)} %get-tuple-element.35), channel_id=1, source_target_pairs={{0,1},{1,0},{2,3},{3,2},{4,5},{5,4},{6,7},{7,6},{8,9},{9,8},{10,11... | collective-permute-start | bytes 354824 | tf_op jit(solution)/shard_map/ppermute | solution.py:16
  176.5 5.3 %collective-permute-start.29 = (f32[88,336]{1,0:T(8,128)S(1)}, f32[88,336]{1,0:T(8,128)S(1)}, u32[]{:S(2)}, u32[]{:S(2)}) collective-permute-start(f32[88,336]{1,0:T(8,128)S(1)} %get-tuple-element.35), channel_id=1, source_target_pairs={{0,2},{1,3},{2,0},{3,1},{4,6},{5,7},{6,4},{7,5},{8,10},{9,11},{10,... | collective-permute-start | bytes 354824 | tf_op jit(solution)/shard_map/ppermute | solution.py:16
  176.9 4.9 %collective-permute-start.30 = (f32[88,336]{1,0:T(8,128)S(1)}, f32[88,336]{1,0:T(8,128)S(1)}, u32[]{:S(2)}, u32[]{:S(2)}) collective-permute-start(f32[88,336]{1,0:T(8,128)S(1)} %get-tuple-element.35), channel_id=1, source_target_pairs={{0,3},{1,2},{2,1},{3,0},{4,7},{5,6},{6,5},{7,4},{8,11},{9,10},{10,... | collective-permute-start | bytes 354824 | tf_op jit(solution)/shard_map/ppermute | solution.py:16
  182.0 7.3 %collective-permute-start.31 = (f32[352,336]{0,1:T(8,128)S(1)}, f32[352,336]{0,1:T(8,128)}, u32[]{:S(2)}, u32[]{:S(2)}) collective-permute-start(f32[352,336]{0,1:T(8,128)S(1)} %copy.18), channel_id=1, source_target_pairs={{0,4},{4,0},{8,12},{12,8},{16,20},{20,16},{24,28},{28,24},{1,5},{5... | collective-permute-start | bytes 1419272 | tf_op jit(solution)/shard_map/ppermute | solution.py:16
  219.0 8.0 %collective-permute-start.32 = (f32[24,2048]{1,0:T(8,128)S(1)}, f32[24,2048]{1,0:T(8,128)S(1)}, u32[]{:S(2)}, u32[]{:S(2)}) collective-permute-start(f32[24,2048]{1,0:T(8,128)S(1)} %get-tuple-element.72), channel_id=1, source_target_pairs={{0,24},{4,28},{8,16},{12,20},{16,8},{20,12},{24,0},{28,4},{1,25},{... | collective-permute-start | bytes 589832 | tf_op jit(solution)/shard_map/ppermute | solution.py:16
  220.5 19.9 %collective-permute-start.33 = (f32[24,2048]{1,0:T(8,128)S(1)}, f32[24,2048]{1,0:T(8,128)S(1)}, u32[]{:S(2)}, u32[]{:S(2)}) collective-permute-start(f32[24,2048]{1,0:T(8,128)S(1)} %get-tuple-element.71), channel_id=1, source_target_pairs={{0,16},{4,20},{8,24},{12,28},{16,0},{20,4},{24,8},{28,12},{1,17},{... | collective-permute-start | bytes 589832 | tf_op jit(solution)/shard_map/ppermute | solution.py:16
  222.4 18.0 %collective-permute-start.34 = (f32[24,2048]{1,0:T(8,128)S(1)}, f32[24,2048]{1,0:T(8,128)S(1)}, u32[]{:S(2)}, u32[]{:S(2)}) collective-permute-start(f32[24,2048]{1,0:T(8,128)S(1)} %get-tuple-element.70), channel_id=1, source_target_pairs={{0,8},{4,12},{8,0},{12,4},{16,24},{20,28},{24,16},{28,20},{1,9},{5... | collective-permute-start | bytes 589832 | tf_op jit(solution)/shard_map/ppermute | solution.py:16
  243.0 2.1 collective-permute-start.35
  (9 other events, 14.6 us)

commit v3 on v2

--- a/solution.py
+++ b/solution.py
@@ -20,50 +20,61 @@
     return jnp.where(core == 0, jnp.concatenate([mine, other], axis), jnp.concatenate([other, mine], axis))
 
 
-def pack(gram):
-    h = gram.shape[0] // 2
-    upper = lax.broadcasted_iota(jnp.int32, (h, h), 0) <= lax.broadcasted_iota(jnp.int32, (h, h), 1)
-    low = gram[h:, h:]
-    tri = jnp.where(upper, gram[:h, :h], low)
-    eye = lax.broadcasted_iota(jnp.int32, (h, h), 0) == lax.broadcasted_iota(jnp.int32, (h, h), 1)
-    diag = jnp.sum(jnp.where(eye, low, 0.0), axis=0, keepdims=True)
-    return jnp.concatenate([gram[:h, h:], tri, diag], 0)
-
-
-def unpack(packed, n):
-    h = n // 2
-    row = lax.broadcasted_iota(jnp.int32, (h, h), 0)
-    col = lax.broadcasted_iota(jnp.int32, (h, h), 1)
-    cross, tri, diag = packed[:h], packed[h : 2 * h], packed[2 * h : 2 * h + 1]
-    top = jnp.where(row <= col, tri, tri.T)
-    low = jnp.where(row > col, tri, jnp.where(row == col, diag, tri.T))
-    return jnp.concatenate([jnp.concatenate([top, cross], 1), jnp.concatenate([cross.T, low], 1)], 0)
-
-
-def sum_everywhere(packed, fibre, rest):
-    f, r = lax.axis_index("fibre"), lax.axis_index("rest")
-    core = f % 2
-    piece = -(-packed.shape[0] // (2 * rest * 8)) * 8
-    half = piece * rest
-    padded = jnp.pad(packed, ((0, 2 * half - packed.shape[0]), (0, 0)))
-    width = packed.shape[1]
-    mine = lax.dynamic_slice(padded, (core * half, 0), (half, width))
-    theirs = lax.dynamic_slice(padded, ((1 - core) * half, 0), (half, width))
-    mine = mine + swap(theirs, "fibre", fibre, 1)
-    total = lax.dynamic_slice(mine, (r * piece, 0), (piece, width))
-    for bits in range(1, rest):
-        part = lax.dynamic_slice(mine, ((r ^ bits) * piece, 0), (piece, width))
-        total = total + swap(part, "rest", rest, bits)
-    terms = [total] + [swap(total, "fibre", fibre, 2 * bits) for bits in range(1, fibre // 2)]
-    while len(terms) > 1:
-        terms = [terms[i] + terms[i + 1] for i in range(0, len(terms), 2)]
-    total = terms[0]
-    out = jnp.zeros((rest, piece, width), jnp.float32)
-    for bits in range(rest):
-        got = swap(total, "rest", rest, bits) if bits else total
-        out = lax.dynamic_update_slice(out, got[None], (r ^ bits, 0, 0))
-    out = out.reshape(half, width)
-    return in_order(core, out, swap(out, "fibre", fibre, 1), 0)
+def split(x):
+    high = x.astype(jnp.bfloat16)
+    return high, (x - high.astype(jnp.float32)).astype(jnp.bfloat16)
+
+
+def layout(n):
+    places, at, strip = [], 0, n % 128
+    for j in range(n // 128):
+        places.append((at, 128 * (j + 1), at + 128 * (j + 1)))
+        at += 128 * (j + 1) + strip
+    return places, at, at + strip
+
+
+def pack_kernel(core_ref, whole_ref, gram_ref, mine_ref, theirs_ref, packed):
+    n = whole_ref.shape[0]
+    places, corner, size = layout(n)
+    edge = n // 128 * 128
+    high, low = split(whole_ref[...])
+
+    def block(r0, r1, c0, c1):
+        def times(a, b):
+            return lax.dot_general(a, b, (((1,), (1,)), ((), ())), preferred_element_type=jnp.float32)
+
+        total = times(high[r0:r1], low[c0:c1]) + times(low[r0:r1], high[c0:c1]) + times(high[r0:r1], high[c0:c1])
+        return total + gram_ref[r0:r1, c0:c1]
+
+    for start in range(0, edge, 256):
+        stop = min(start + 256, edge)
+        upper = block(0, stop, start, stop)
+        for j in range(start // 128, stop // 128):
+            at, rows, _ = places[j]
+            packed[at : at + rows, :] = upper[:rows, 128 * j - start : 128 * j - start + 128]
+    if n > edge:
+        strip = block(edge, n, 0, n)
+        for j, (_, _, at) in enumerate(places):
+            packed[at : at + n - edge, :] = strip[:, 128 * j : 128 * j + 128]
+        packed[corner:size, :] = jnp.pad(strip[:, edge:], ((0, 0), (0, 128 - (n - edge))))
+    half = size // 2
+    core = core_ref[0]
+    mine_ref[...] = packed[pl.ds(pl.multiple_of(core * half, 8), half), :]
+    theirs_ref[...] = packed[pl.ds(pl.multiple_of((1 - core) * half, 8), half), :]
+
+
+def pack(core, whole, gram):
+    size = layout(whole.shape[0])[2]
+    half = jax.ShapeDtypeStruct((size // 2, 128), jnp.float32)
+    return pl.pallas_call(
+        pack_kernel,
+        out_shape=(half, half),
+        in_specs=[pl.BlockSpec(memory_space=pltpu.SMEM)] + [pl.BlockSpec(memory_space=pltpu.VMEM)] * 2,
+        out_specs=[pl.BlockSpec(memory_space=pltpu.VMEM)] * 2,
+        scratch_shapes=[pltpu.VMEM((size, 128), jnp.float32)],
+        compiler_params=pltpu.CompilerParams(vmem_limit_bytes=32 * 2**20),
+        name="gram_pack",
+    )(core.reshape(1), whole, gram)
 
 
 def lower_inverse(small):
@@ -121,28 +132,71 @@
     return jnp.concatenate(done, 0)
 
 
-def iterations_kernel(iters, gram_ref, start_ref, factor_ref):
+def iterations_kernel(iters, core_ref, mine_ref, other_ref, start_ref, factor_ref, packed, gram):
     def times(a, b, dims):
         return lax.dot_general(a, b, (dims, ((), ())), precision=HIGHEST, preferred_element_type=jnp.float32)
 
-    image = times(gram_ref[...], start_ref[...], ((1,), (0,)))
+    n = gram.shape[0]
+    places, corner, size = layout(n)
+    edge = n // 128 * 128
+    half = size // 2
+    core = core_ref[0]
+    packed[pl.ds(pl.multiple_of(core * half, 8), half), :] = mine_ref[...]
+    packed[pl.ds(pl.multiple_of((1 - core) * half, 8), half), :] = other_ref[...]
+    for j, (at, rows, strip) in enumerate(places):
+        cols = slice(128 * j, 128 * j + 128)
+        gram[:rows, cols] = packed[at : at + rows, :]
+        for i in range(j):
+            gram[cols, 128 * i : 128 * i + 128] = packed[at + 128 * i : at + 128 * i + 128, :].T
+        if n > edge:
+            gram[edge:, cols] = packed[strip : strip + n - edge, :]
+            gram[cols, edge:] = packed[strip : strip + n - edge, :].T
+    if n > edge:
+        gram[edge:, edge:] = packed[corner:size, : n - edge]
+
+    image = times(gram[...], start_ref[...], ((1,), (0,)))
     for step in range(iters):
         small = times(image, image, ((0,), (0,)))
         inverse = lower_inverse(jnp.pad(small, ((0, 0), (0, 128 - small.shape[1]))))[:, : small.shape[1]]
         if step < iters - 1:
-            image = times(times(gram_ref[...], image, ((1,), (0,))), inverse, ((1,), (1,)))
+            image = times(times(gram[...], image, ((1,), (0,))), inverse, ((1,), (1,)))
         else:
             factor_ref[...] = times(image, inverse, ((1,), (1,)))
 
-def iterations(gram, start, iters=3):
+
+def iterations(core, mine, other, start, iters):
+    n = start.shape[0]
     return pl.pallas_call(
         functools.partial(iterations_kernel, iters),
         out_shape=jax.ShapeDtypeStruct(start.shape, jnp.float32),
-        in_specs=[pl.BlockSpec(memory_space=pltpu.VMEM)] * 2,
+        in_specs=[pl.BlockSpec(memory_space=pltpu.SMEM)] + [pl.BlockSpec(memory_space=pltpu.VMEM)] * 3,
         out_specs=pl.BlockSpec(memory_space=pltpu.VMEM),
+        scratch_shapes=[pltpu.VMEM((layout(n)[2], 128), jnp.float32), pltpu.VMEM((n, n), jnp.float32)],
         compiler_params=pltpu.CompilerParams(vmem_limit_bytes=32 * 2**20),
         name="iterations",
-    )(gram, start)
+    )(core.reshape(1), mine, other, start)
+
+
+def sum_everywhere(mine, theirs, fibre, rest):
+    r = lax.axis_index("rest")
+    half, width = mine.shape
+    piece = -(-half // (8 * rest)) * 8
+    mine = mine + swap(theirs, "fibre", fibre, 1)
+    mine = jnp.pad(mine, ((0, piece * rest - half), (0, 0)))
+    total = lax.dynamic_slice(mine, (r * piece, 0), (piece, width))
+    for bits in range(1, rest):
+        part = lax.dynamic_slice(mine, ((r ^ bits) * piece, 0), (piece, width))
+        total = total + swap(part, "rest", rest, bits)
+    terms = [total] + [swap(total, "fibre", fibre, 2 * bits) for bits in range(1, fibre // 2)]
+    while len(terms) > 1:
+        terms = [terms[i] + terms[i + 1] for i in range(0, len(terms), 2)]
+    total = terms[0]
+    out = jnp.zeros((rest, piece, width), jnp.float32)
+    for bits in range(rest):
+        got = swap(total, "rest", rest, bits) if bits else total
+        out = lax.dynamic_update_slice(out, got[None], (r ^ bits, 0, 0))
+    out = out.reshape(rest * piece, width)[:half]
+    return out, swap(out, "fibre", fibre, 1)
 
 
 def shards(fibre, rest, slab, start_basis):
@@ -152,30 +206,28 @@
     z, core = f // 2, f % 2
     half = cols // 2
     part = half // zs
-    unit = part // 8
-    chunks = [(0, unit), (unit, 5 * unit), (6 * unit, 2 * unit)]
+    chunks = [(0, part * 3 // 4), (part * 3 // 4, part // 4)]
     order = list(range(zs - 1, -1, -1))
-    gram = 0.0
     fibres = []
+    before = [None] * zs
     for start, width in chunks:
-        blocks = []
+        whole = jnp.zeros((zs, 2 * rows, width), jnp.float32)
         for bits in order:
             at = (z ^ bits) * part + start
             mine = lax.dynamic_slice(slab, (0, core * half + at), (rows, width))
             theirs = lax.dynamic_slice(slab, (0, (1 - core) * half + at), (rows, width))
-            blocks.append(in_order(core, mine, swap(theirs, "fibre", fibre, 1), 0))
-        slab, blocks = lax.optimization_barrier((slab, blocks))
-        whole = jnp.zeros((zs, 2 * rows, width), jnp.float32)
-        for bits, block in zip(order, blocks):
+            block = in_order(core, mine, swap(theirs, "fibre", fibre, 1), 0)
+            slab, block = lax.optimization_barrier((slab, block))
             if bits:
-                block = swap(block, "fibre", fibre, 2 * bits)
+                if before[bits] is not None:
+                    block, before[bits] = lax.optimization_barrier((block, before[bits]))
+                block = before[bits] = swap(block, "fibre", fibre, 2 * bits)
             whole = lax.dynamic_update_slice(whole, block[None], (z ^ bits, 0, 0))
-        whole = whole.reshape(zs * 2 * rows, width)
-        fibres.append(whole)
-        gram = gram + jnp.dot(whole, whole.T, precision=HIGH, preferred_element_type=jnp.float32)
-    n = gram.shape[0]
-    gram = unpack(sum_everywhere(pack(gram), fibre, rest), n)
-    basis = iterations(gram, start_basis, ITERS)
+        fibres.append(whole.reshape(zs * 2 * rows, width))
+    n = zs * 2 * rows
+    gram = jnp.dot(fibres[0], fibres[0].T, precision=HIGH, preferred_element_type=jnp.float32)
+    mine, other = sum_everywhere(*pack(core, fibres[1], gram), fibre, rest)
+    basis = iterations(core, mine, other, start_basis, ITERS)
     rank = basis.shape[1]
     own = rank // fibre
     rows_of = [lax.dynamic_slice(basis.T, ((z ^ bits) * 2 * own, 0), (2 * own, n)) for bits in range(zs)]

time: 247 us -> 231 us (0.935)
  starting transfers between devices: 90.1 us -> 47.7 us
  waiting for transfers between devices: 96.2 us -> 132 us
  local copies, waits for them, and re-layouts: 22.1 us -> 17.3 us
  other arithmetic: 8.89 us -> 5.29 us
  matrix products: 9.68 us -> 7.13 us
    ppermute x36 -> x29, starting transfers between devices: 90.1 us -> 47.7 us  [swap(): return lax.ppermute(x, axis, [(i, i ^ bits) for i in range(size)])]
    ppermute x36 -> x29, waiting for transfers between devices: 96.2 us -> 132 us  [swap(): return lax.ppermute(x, axis, [(i, i ^ bits) for i in range(size)])]
    dynamic_slice x3 -> x8, local copies, waits for them, and re-layouts: 5.01 us -> 9.98 us  [shards(): mine = lax.dynamic_slice(slab, (0, core * half + at), (rows, width))]
    ppermute x2 -> x0, local copies, waits for them, and re-layouts: 3.49 us -> none  [swap(): return lax.ppermute(x, axis, [(i, i ^ bits) for i in range(size)])]
    unnamed x16 -> x12, local copies, waits for them, and re-layouts: 5.23 us -> 1.84 us
    dynamic_slice x2 -> x0, local copies, waits for them, and re-layouts: 2.9 us -> none  [sum_everywhere(): theirs = lax.dynamic_slice(padded, ((1 - core) * half, 0), (half, width))]
    select_n x14 -> x9, other arithmetic: 1.88 us -> 4.76 us  [in_order(): jnp.where(core == 0, jnp.concatenate([mine, other], axis), jnp.concatenat...]
    dot_general x3 -> x1, matrix products: 7.46 us -> 5.14 us  [shards(): jnp.dot(fibres[0], fibres[0].T, precision=HIGH, preferred_element_type=jn...]
  transfers between devices with their start and end apart: 36 -> 29, of which waited for: 25 -> 20; matrix products, arithmetic and copies ran while one was open for 4% -> 7% of each run, Pallas kernels for 0% -> 0%
where the time goes in v3:
time: 231 us
  waiting for transfers between devices  132 us (57%)
  starting transfers between devices  47.7 us (21%)
  Pallas kernels  20.2 us (9%)
  local copies, waits for them, and re-layouts  17.3 us (7%)
  matrix products  7.13 us (3%)
  other arithmetic  5.29 us (2%)
    ppermute x29, waiting for transfers between devices, swap(): return lax.ppermute(x, axis, [(i, i ^ bits) for i in range(size)])  132 us
    ppermute x29, starting transfers between devices, swap(): return lax.ppermute(x, axis, [(i, i ^ bits) for i in range(size)])  47.7 us
    pallas_call x1, Pallas kernels, iterations(): pl.pallas_call(functools.partial(iterations_kernel, iters), out_shape=jax...  18.3 us
    dynamic_slice x8, local copies, waits for them, and re-layouts, shards(): mine = lax.dynamic_slice(slab, (0, core * half + at), (rows, width))  9.98 us
    dot_general x1, matrix products, shards(): jnp.dot(fibres[0], fibres[0].T, precision=HIGH, preferred_element_type=jn...  5.14 us
    select_n x9, other arithmetic, in_order(): jnp.where(core == 0, jnp.concatenate([mine, other], axis), jnp.concatenat...  4.76 us
  transfers between devices with their start and end apart: 29, of which 20 were waited for; matrix products, arithmetic and copies ran while one was open for 7% of the time, Pallas kernels for 0%

profile of v3, /device:TPU:1, one launch (start us, length us, event | category | flops | bytes accessed | tf_op | source)
XLA Modules:
  0.0 230.8 jit_solution(92168908040155483)
XLA Ops:
  2.1 1.9 collective-permute-done
  5.6 1.8 collective-permute-done.1
  10.0 1.8 collective-permute-done.2
  14.4 4.7 %collective-permute-start.5 = (f32[168,1536]{1,0:T(8,128)S(1)}, f32[168,1536]{1,0:T(8,128)}, u32[]{:S(2)}, u32[]{:S(2)}) collective-permute-start(f32[168,1536]{1,0:T(8,128)S(1)} %maximum_select_fusion.1), channel_id=1, source_target_pairs={{0,24},{4,28},{8,16},{12,20},{16,8},{20,12},{24,0},{28,4},{1,25},{... | collective-permute-start | bytes 3096584 | tf_op jit(solution)/shard_map/ppermute | solution.py:16
  19.2 1.7 constant_dynamic-slice_fusion.10
  26.0 16.3 %collective-permute-done.5 = f32[168,1536]{1,0:T(8,128)} collective-permute-done((f32[168,1536]{1,0:T(8,128)S(1)}, f32[168,1536]{1,0:T(8,128)}, u32[]{:S(2)}, u32[]{:S(2)}) %collective-permute-start.5) | collective-permute-done | bytes 1032224 | tf_op jit(solution)/shard_map/ppermute | solution.py:16
  44.1 3.1 %collective-permute-start.6 = (f32[168,512]{1,0:T(8,128)S(1)}, f32[168,512]{1,0:T(8,128)S(1)}, u32[]{:S(2)}, u32[]{:S(2)}) collective-permute-start(f32[168,512]{1,0:T(8,128)S(1)} %maximum_select_fusion.5), channel_id=1, source_target_pairs={{0,24},{4,28},{8,16},{12,20},{16,8},{20,12},{24,0},{28,4},{1,25},{... | collective-permute-start | bytes 1032200 | tf_op jit(solution)/shard_map/ppermute | solution.py:16
  48.3 1.9 collective-permute-start.10
  50.2 64.5 %collective-permute-done.8 = f32[168,1536]{1,0:T(8,128)S(1)} collective-permute-done((f32[168,1536]{1,0:T(8,128)}, f32[168,1536]{1,0:T(8,128)S(1)}, u32[]{:S(2)}, u32[]{:S(2)}) %collective-permute-start.8) | collective-permute-done | bytes 1032224 | tf_op jit(solution)/shard_map/ppermute | solution.py:16
  116.0 1.6 collective-permute-start.13
  118.1 5.1 %fusion.4.gram_ref = f32[672,672]{1,0:T(8,128)S(1)} fusion(f32[672,1536]{1,0:T(8,128)S(1)} %bitcast.64), kind=kOutput, calls=%fused_computation.63 | convolution fusion | flops 4161798144 | bytes 5935104 | tf_op jit(solution)/shard_map/dot_general | solution.py:228
  123.2 12.2 %collective-permute-start.12 = (f32[168,512]{1,0:T(8,128)S(1)}, f32[168,512]{1,0:T(8,128)S(1)}, u32[]{:S(2)}, u32[]{:S(2)}) collective-permute-start(f32[168,512]{1,0:T(8,128)S(1)} %maximum_select_fusion.7), channel_id=1, source_target_pairs={{0,8},{4,12},{8,0},{12,4},{16,24},{20,28},{24,16},{28,20},{1,9},{5... | collective-permute-start | bytes 1032200 | tf_op jit(solution)/shard_map/ppermute | solution.py:16
  135.5 1.4 collective-permute-done.9
  136.9 6.9 %collective-permute-done.12 = f32[168,512]{1,0:T(8,128)S(1)} collective-permute-done((f32[168,512]{1,0:T(8,128)S(1)}, f32[168,512]{1,0:T(8,128)S(1)}, u32[]{:S(2)}, u32[]{:S(2)}) %collective-permute-start.12) | collective-permute-done | bytes 344096 | tf_op jit(solution)/shard_map/ppermute | solution.py:16
  143.9 1.9 gram_pack.1
  145.8 1.5 collective-permute-start.14
  147.2 1.6 collective-permute-done.14
  151.6 2.1 collective-permute-done.15
  154.7 2.9 %collective-permute-done.17 = f32[264,128]{1,0:T(8,128)S(1)} collective-permute-done((f32[264,128]{1,0:T(8,128)S(1)}, f32[264,128]{1,0:T(8,128)S(1)}, u32[]{:S(2)}, u32[]{:S(2)}) %collective-permute-start.17) | collective-permute-done | bytes 135200 | tf_op jit(solution)/shard_map/ppermute | solution.py:16
  158.4 1.7 collective-permute-start.19
  161.5 2.4 %collective-permute-done.19 = f32[264,128]{1,0:T(8,128)S(1)} collective-permute-done((f32[264,128]{1,0:T(8,128)S(1)}, f32[264,128]{1,0:T(8,128)S(1)}, u32[]{:S(2)}, u32[]{:S(2)}) %collective-permute-start.19) | collective-permute-done | bytes 135200 | tf_op jit(solution)/shard_map/ppermute | solution.py:16
  163.9 4.2 %collective-permute-done.20 = f32[264,128]{1,0:T(8,128)S(1)} collective-permute-done((f32[264,128]{1,0:T(8,128)S(1)}, f32[264,128]{1,0:T(8,128)S(1)}, u32[]{:S(2)}, u32[]{:S(2)}) %collective-permute-start.20) | collective-permute-done | bytes 135200 | tf_op jit(solution)/shard_map/ppermute | solution.py:16
  168.2 1.7 collective-permute-start.21
  172.4 2.9 %collective-permute-done.22 = f32[264,128]{1,0:T(8,128)S(1)} collective-permute-done((f32[264,128]{1,0:T(8,128)S(1)}, f32[264,128]{1,0:T(8,128)S(1)}, u32[]{:S(2)}, u32[]{:S(2)}) %collective-permute-start.22) | collective-permute-done | bytes 135200 | tf_op jit(solution)/shard_map/ppermute | solution.py:16
  175.3 5.5 %collective-permute-start.24 = (f32[1056,128]{1,0:T(8,128)S(1)}, f32[1056,128]{1,0:T(8,128)S(1)}, u32[]{:S(2)}, u32[]{:S(2)}) collective-permute-start(f32[1056,128]{1,0:T(8,128)S(1)} %bitcast.62), channel_id=1, source_target_pairs={{0,4},{4,0},{8,12},{12,8},{16,20},{20,16},{24,28},{28,24},{1,5},{5... | collective-permute-start | bytes 1622024 | tf_op jit(solution)/shard_map/ppermute | solution.py:16
  181.0 1.4 collective-permute-done.24.other_ref
  182.4 18.3 %iterations.1 = f32[672,96]{1,0:T(8,128)S(1)} custom-call(s32[1]{0:T(128)} %bitcast.core_ref, f32[1056,128]{1,0:T(8,128)S(1)} %bitcast.63, f32[1056,128]{1,0:T(8,128)S(1)} %collective-permute-done.24.other_ref, f32[672,96]{1,0:T(8,128)S(1)} %copy.4.start_ref), custom_call_target="tpu_custom_call" | custom-call | tf_op jit(solution)/shard_map/iterations/pallas_call | solution.py:169
  201.5 1.4 fusion.5
  203.6 2.1 collective-permute-start.25
  207.4 4.2 %collective-permute-done.25 = f32[24,2048]{1,0:T(8,128)S(1)} collective-permute-done((f32[24,2048]{1,0:T(8,128)S(1)}, f32[24,2048]{1,0:T(8,128)S(1)}, u32[]{:S(2)}, u32[]{:S(2)}) %collective-permute-start.25) | collective-permute-done | bytes 196640 | tf_op jit(solution)/shard_map/ppermute | solution.py:16
  211.7 13.3 %collective-permute-done.26 = f32[24,2048]{1,0:T(8,128)S(1)} collective-permute-done((f32[24,2048]{1,0:T(8,128)S(1)}, f32[24,2048]{1,0:T(8,128)S(1)}, u32[]{:S(2)}, u32[]{:S(2)}) %collective-permute-start.26) | collective-permute-done | bytes 196640 | tf_op jit(solution)/shard_map/ppermute | solution.py:16
  225.5 1.6 dynamic_update_slice.63
  (89 shorter events, 34.1 us)
Async XLA Ops:
  2.0 2.0 collective-permute-start
  5.4 2.0 collective-permute-start.1
  9.8 2.0 collective-permute-start.2
  14.2 4.9 %collective-permute-start.3 = (f32[84,1536]{1,0:T(8,128)S(1)}, f32[84,1536]{1,0:T(8,128)S(1)}, u32[]{:S(2)}, u32[]{:S(2)}) collective-permute-start(f32[84,1536]{1,0:T(8,128)S(1)} %get-tuple-element.55), channel_id=1, source_target_pairs={{0,4},{4,0},{8,12},{12,8},{16,20},{20,16},{24,28},{28,24},{1,5},{5... | collective-permute-start | bytes 1548296 | tf_op jit(solution)/shard_map/ppermute | solution.py:16
  14.4 27.9 %collective-permute-start.5 = (f32[168,1536]{1,0:T(8,128)S(1)}, f32[168,1536]{1,0:T(8,128)}, u32[]{:S(2)}, u32[]{:S(2)}) collective-permute-start(f32[168,1536]{1,0:T(8,128)S(1)} %maximum_select_fusion.1), channel_id=1, source_target_pairs={{0,24},{4,28},{8,16},{12,20},{16,8},{20,12},{24,0},{28,4},{1,25},{... | collective-permute-start | bytes 3096584 | tf_op jit(solution)/shard_map/ppermute | solution.py:16
  20.9 2.2 collective-permute-start.4
  21.3 93.4 %collective-permute-start.8 = (f32[168,1536]{1,0:T(8,128)}, f32[168,1536]{1,0:T(8,128)S(1)}, u32[]{:S(2)}, u32[]{:S(2)}) collective-permute-start(f32[168,1536]{1,0:T(8,128)} %maximum_select_fusion.2), channel_id=1, source_target_pairs={{0,16},{4,20},{8,24},{12,28},{16,0},{20,4},{24,8},{28,12},{1,17},{... | collective-permute-start | bytes 3096584 | tf_op jit(solution)/shard_map/ppermute | solution.py:16
  21.8 96.0 %collective-permute-start.11 = (f32[168,1536]{1,0:T(8,128)}, f32[168,1536]{1,0:T(8,128)S(1)}, u32[]{:S(2)}, u32[]{:S(2)}) collective-permute-start(f32[168,1536]{1,0:T(8,128)} %maximum_select_fusion.3), channel_id=1, source_target_pairs={{0,8},{4,12},{8,0},{12,4},{16,24},{20,28},{24,16},{28,20},{1,9},{5... | collective-permute-start | bytes 3096584 | tf_op jit(solution)/shard_map/ppermute | solution.py:16
  25.2 22.0 %collective-permute-start.7 = (f32[84,512]{1,0:T(8,128)S(1)}, f32[84,512]{1,0:T(8,128)S(1)}, u32[]{:S(2)}, u32[]{:S(2)}) collective-permute-start(f32[84,512]{1,0:T(8,128)S(1)} %get-tuple-element.51), channel_id=1, source_target_pairs={{0,4},{4,0},{8,12},{12,8},{16,20},{20,16},{24,28},{28,24},{1,5},{5... | collective-permute-start | bytes 516104 | tf_op jit(solution)/shard_map/ppermute | solution.py:16
  44.1 73.5 %collective-permute-start.6 = (f32[168,512]{1,0:T(8,128)S(1)}, f32[168,512]{1,0:T(8,128)S(1)}, u32[]{:S(2)}, u32[]{:S(2)}) collective-permute-start(f32[168,512]{1,0:T(8,128)S(1)} %maximum_select_fusion.5), channel_id=1, source_target_pairs={{0,24},{4,28},{8,16},{12,20},{16,8},{20,12},{24,0},{28,4},{1,25},{... | collective-permute-start | bytes 1032200 | tf_op jit(solution)/shard_map/ppermute | solution.py:16
  48.3 66.6 %collective-permute-start.10 = (f32[84,512]{1,0:T(8,128)S(1)}, f32[84,512]{1,0:T(8,128)S(1)}, u32[]{:S(2)}, u32[]{:S(2)}) collective-permute-start(f32[84,512]{1,0:T(8,128)S(1)} %get-tuple-element.49), channel_id=1, source_target_pairs={{0,4},{4,0},{8,12},{12,8},{16,20},{20,16},{24,28},{28,24},{1,5},{5... | collective-permute-start | bytes 516104 | tf_op jit(solution)/shard_map/ppermute | solution.py:16
  114.9 22.0 %collective-permute-start.9 = (f32[168,512]{1,0:T(8,128)S(1)}, f32[168,512]{1,0:T(8,128)S(1)}, u32[]{:S(2)}, u32[]{:S(2)}) collective-permute-start(f32[168,512]{1,0:T(8,128)S(1)} %maximum_select_fusion.6), channel_id=1, source_target_pairs={{0,16},{4,20},{8,24},{12,28},{16,0},{20,4},{24,8},{28,12},{1,17},{... | collective-permute-start | bytes 1032200 | tf_op jit(solution)/shard_map/ppermute | solution.py:16
  116.0 19.4 %collective-permute-start.13 = (f32[84,512]{1,0:T(8,128)S(1)}, f32[84,512]{1,0:T(8,128)S(1)}, u32[]{:S(2)}, u32[]{:S(2)}) collective-permute-start(f32[84,512]{1,0:T(8,128)S(1)} %get-tuple-element.47), channel_id=1, source_target_pairs={{0,4},{4,0},{8,12},{12,8},{16,20},{20,16},{24,28},{28,24},{1,5},{5... | collective-permute-start | bytes 516104 | tf_op jit(solution)/shard_map/ppermute | solution.py:16
  118.1 5.2 %copy-start = (f32[4,168,1536]{2,1,0:T(8,128)}, f32[4,168,1536]{2,1,0:T(8,128)S(1)}, u32[]{:S(2)}) copy-start(f32[4,168,1536]{2,1,0:T(8,128)S(1)} %bitcast_dynamic-update-slice_fusion) | copy-start | bytes 12386308
  123.2 20.5 %collective-permute-start.12 = (f32[168,512]{1,0:T(8,128)S(1)}, f32[168,512]{1,0:T(8,128)S(1)}, u32[]{:S(2)}, u32[]{:S(2)}) collective-permute-start(f32[168,512]{1,0:T(8,128)S(1)} %maximum_select_fusion.7), channel_id=1, source_target_pairs={{0,8},{4,12},{8,0},{12,4},{16,24},{20,28},{24,16},{28,20},{1,9},{5... | collective-permute-start | bytes 1032200 | tf_op jit(solution)/shard_map/ppermute | solution.py:16
  143.8 37.0 %copy-start.2 = (f32[672,96]{0,1:T(8,128)S(1)}, f32[672,96]{0,1:T(8,128)}, u32[]{:S(2)}) copy-start(f32[672,96]{0,1:T(8,128)} %param.3) | copy-start | bytes 774148
  145.8 3.1 %collective-permute-start.14 = (f32[1056,128]{1,0:T(8,128)S(1)}, f32[1056,128]{1,0:T(8,128)S(1)}, u32[]{:S(2)}, u32[]{:S(2)}) collective-permute-start(f32[1056,128]{1,0:T(8,128)S(1)} %get-tuple-element.41), channel_id=1, source_target_pairs={{0,4},{4,0},{8,12},{12,8},{16,20},{20,16},{24,28},{28,24},{1,5},{5... | collective-permute-start | bytes 1622024 | tf_op jit(solution)/shard_map/ppermute | solution.py:16
  148.9 4.9 %collective-permute-start.15 = (f32[264,128]{1,0:T(8,128)S(1)}, f32[264,128]{1,0:T(8,128)S(1)}, u32[]{:S(2)}, u32[]{:S(2)}) collective-permute-start(f32[264,128]{1,0:T(8,128)S(1)} %get-tuple-element.68), channel_id=1, source_target_pairs={{0,1},{1,0},{2,3},{3,2},{4,5},{5,4},{6,7},{7,6},{8,9},{9,8},{10,11... | collective-permute-start | bytes 405512 | tf_op jit(solution)/shard_map/ppermute | solution.py:16
  150.2 4.5 %collective-permute-start.16 = (f32[264,128]{1,0:T(8,128)S(1)}, f32[264,128]{1,0:T(8,128)S(1)}, u32[]{:S(2)}, u32[]{:S(2)}) collective-permute-start(f32[264,128]{1,0:T(8,128)S(1)} %get-tuple-element.70), channel_id=1, source_target_pairs={{0,2},{1,3},{2,0},{3,1},{4,6},{5,7},{6,4},{7,5},{8,10},{9,11},{10,... | collective-permute-start | bytes 405512 | tf_op jit(solution)/shard_map/ppermute | solution.py:16
  151.4 6.1 %collective-permute-start.17 = (f32[264,128]{1,0:T(8,128)S(1)}, f32[264,128]{1,0:T(8,128)S(1)}, u32[]{:S(2)}, u32[]{:S(2)}) collective-permute-start(f32[264,128]{1,0:T(8,128)S(1)} %get-tuple-element.69), channel_id=1, source_target_pairs={{0,3},{1,2},{2,1},{3,0},{4,7},{5,6},{6,5},{7,4},{8,11},{9,10},{10,... | collective-permute-start | bytes 405512 | tf_op jit(solution)/shard_map/ppermute | solution.py:16
  157.6 3.9 %collective-permute-start.18 = (f32[264,128]{1,0:T(8,128)S(1)}, f32[264,128]{1,0:T(8,128)S(1)}, u32[]{:S(2)}, u32[]{:S(2)}) collective-permute-start(f32[264,128]{1,0:T(8,128)S(1)} %add_add_fusion.1), channel_id=1, source_target_pairs={{0,8},{4,12},{8,0},{12,4},{16,24},{20,28},{24,16},{28,20},{1,9},{5... | collective-permute-start | bytes 405512 | tf_op jit(solution)/shard_map/ppermute | solution.py:16
  158.4 5.6 %collective-permute-start.19 = (f32[264,128]{1,0:T(8,128)S(1)}, f32[264,128]{1,0:T(8,128)S(1)}, u32[]{:S(2)}, u32[]{:S(2)}) collective-permute-start(f32[264,128]{1,0:T(8,128)S(1)} %add_add_fusion.1), channel_id=1, source_target_pairs={{0,16},{4,20},{8,24},{12,28},{16,0},{20,4},{24,8},{28,12},{1,17},{... | collective-permute-start | bytes 405512 | tf_op jit(solution)/shard_map/ppermute | solution.py:16
  160.1 8.0 %collective-permute-start.20 = (f32[264,128]{1,0:T(8,128)S(1)}, f32[264,128]{1,0:T(8,128)S(1)}, u32[]{:S(2)}, u32[]{:S(2)}) collective-permute-start(f32[264,128]{1,0:T(8,128)S(1)} %add_add_fusion.1), channel_id=1, source_target_pairs={{0,24},{4,28},{8,16},{12,20},{16,8},{20,12},{24,0},{28,4},{1,25},{... | collective-permute-start | bytes 405512 | tf_op jit(solution)/shard_map/ppermute | solution.py:16
  168.2 4.1 %collective-permute-start.21 = (f32[264,128]{1,0:T(8,128)S(1)}, f32[264,128]{1,0:T(8,128)S(1)}, u32[]{:S(2)}, u32[]{:S(2)}) collective-permute-start(f32[264,128]{1,0:T(8,128)S(1)} %get-tuple-element.45), channel_id=1, source_target_pairs={{0,1},{1,0},{2,3},{3,2},{4,5},{5,4},{6,7},{7,6},{8,9},{9,8},{10,11... | collective-permute-start | bytes 405512 | tf_op jit(solution)/shard_map/ppermute | solution.py:16
  169.9 5.3 %collective-permute-start.22 = (f32[264,128]{1,0:T(8,128)S(1)}, f32[264,128]{1,0:T(8,128)S(1)}, u32[]{:S(2)}, u32[]{:S(2)}) collective-permute-start(f32[264,128]{1,0:T(8,128)S(1)} %get-tuple-element.45), channel_id=1, source_target_pairs={{0,2},{1,3},{2,0},{3,1},{4,6},{5,7},{6,4},{7,5},{8,10},{9,11},{10,... | collective-permute-start | bytes 405512 | tf_op jit(solution)/shard_map/ppermute | solution.py:16
  170.0 5.3 %collective-permute-start.23 = (f32[264,128]{1,0:T(8,128)S(1)}, f32[264,128]{1,0:T(8,128)S(1)}, u32[]{:S(2)}, u32[]{:S(2)}) collective-permute-start(f32[264,128]{1,0:T(8,128)S(1)} %get-tuple-element.45), channel_id=1, source_target_pairs={{0,3},{1,2},{2,1},{3,0},{4,7},{5,6},{6,5},{7,4},{8,11},{9,10},{10,... | collective-permute-start | bytes 405512 | tf_op jit(solution)/shard_map/ppermute | solution.py:16
  175.3 7.1 %collective-permute-start.24 = (f32[1056,128]{1,0:T(8,128)S(1)}, f32[1056,128]{1,0:T(8,128)S(1)}, u32[]{:S(2)}, u32[]{:S(2)}) collective-permute-start(f32[1056,128]{1,0:T(8,128)S(1)} %bitcast.62), channel_id=1, source_target_pairs={{0,4},{4,0},{8,12},{12,8},{16,20},{20,16},{24,28},{28,24},{1,5},{5... | collective-permute-start | bytes 1622024 | tf_op jit(solution)/shard_map/ppermute | solution.py:16
  181.0 20.5 %copy-start.1 = (f32[4,168,1536]{2,1,0:T(8,128)S(1)}, f32[4,168,1536]{2,1,0:T(8,128)}, u32[]{:S(2)}) copy-start(f32[4,168,1536]{2,1,0:T(8,128)} %copy-done) | copy-start | bytes 12386308
  203.6 8.0 %collective-permute-start.25 = (f32[24,2048]{1,0:T(8,128)S(1)}, f32[24,2048]{1,0:T(8,128)S(1)}, u32[]{:S(2)}, u32[]{:S(2)}) collective-permute-start(f32[24,2048]{1,0:T(8,128)S(1)} %get-tuple-element.65), channel_id=1, source_target_pairs={{0,24},{4,28},{8,16},{12,20},{16,8},{20,12},{24,0},{28,4},{1,25},{... | collective-permute-start | bytes 589832 | tf_op jit(solution)/shard_map/ppermute | solution.py:16
  205.7 19.3 %collective-permute-start.26 = (f32[24,2048]{1,0:T(8,128)S(1)}, f32[24,2048]{1,0:T(8,128)S(1)}, u32[]{:S(2)}, u32[]{:S(2)}) collective-permute-start(f32[24,2048]{1,0:T(8,128)S(1)} %get-tuple-element.66), channel_id=1, source_target_pairs={{0,16},{4,20},{8,24},{12,28},{16,0},{20,4},{24,8},{28,12},{1,17},{... | collective-permute-start | bytes 589832 | tf_op jit(solution)/shard_map/ppermute | solution.py:16
  207.0 18.0 %collective-permute-start.27 = (f32[24,2048]{1,0:T(8,128)S(1)}, f32[24,2048]{1,0:T(8,128)S(1)}, u32[]{:S(2)}, u32[]{:S(2)}) collective-permute-start(f32[24,2048]{1,0:T(8,128)S(1)} %get-tuple-element.67), channel_id=1, source_target_pairs={{0,8},{4,12},{8,0},{12,4},{16,24},{20,28},{24,16},{28,20},{1,9},{5... | collective-permute-start | bytes 589832 | tf_op jit(solution)/shard_map/ppermute | solution.py:16
  227.6 2.1 collective-permute-start.28

commit v4 on v3

--- a/solution.py
+++ b/solution.py
@@ -20,6 +20,50 @@
     return jnp.where(core == 0, jnp.concatenate([mine, other], axis), jnp.concatenate([other, mine], axis))
 
 
+def prepare_kernel(chunks, place_ref, slab_ref, got_ref, *refs):
+    outs, own, sems = refs[:-2], refs[-2], refs[-1]
+    zs, rows, part = own.shape
+    z, core = place_ref[0], place_ref[1]
+
+    def fetch(bits):
+        at = pl.multiple_of(core * (zs * part) + (z ^ bits) * part, 128)
+        return pltpu.make_async_copy(slab_ref.at[:, pl.ds(at, part)], own.at[bits], sems.at[bits])
+
+    for bits in reversed(range(zs)):
+        fetch(bits).start()
+    for bits in reversed(range(zs)):
+        fetch(bits).wait()
+        for c, (start, width) in enumerate(chunks):
+            out = outs[c * zs + bits]
+            at = pl.multiple_of((z ^ bits) * part + start, 128)
+
+            @pl.when(core == 0)
+            def _():
+                out[:rows, :] = own[bits, :, start : start + width]
+                out[rows:, :] = got_ref[:, pl.ds(at, width)]
+
+            @pl.when(core == 1)
+            def _():
+                out[:rows, :] = got_ref[:, pl.ds(at, width)]
+                out[rows:, :] = own[bits, :, start : start + width]
+
+
+def prepare(place, slab, got, zs, chunks):
+    rows, half = got.shape
+    vmem = pl.BlockSpec(memory_space=pltpu.VMEM)
+    outs = [jax.ShapeDtypeStruct((2 * rows, width), jnp.float32) for _, width in chunks for _ in range(zs)]
+    outs = pl.pallas_call(
+        functools.partial(prepare_kernel, chunks),
+        out_shape=outs,
+        in_specs=[pl.BlockSpec(memory_space=pltpu.SMEM), pl.BlockSpec(memory_space=pl.ANY), vmem],
+        out_specs=[vmem] * len(outs),
+        scratch_shapes=[pltpu.VMEM((zs, rows, half // zs), jnp.float32), pltpu.SemaphoreType.DMA((zs,))],
+        compiler_params=pltpu.CompilerParams(vmem_limit_bytes=40 * 2**20),
+        name="prepare",
+    )(place, slab, got)
+    return [outs[c * zs : (c + 1) * zs] for c in range(len(chunks))]
+
+
 def split(x):
     high = x.astype(jnp.bfloat16)
     return high, (x - high.astype(jnp.float32)).astype(jnp.bfloat16)
@@ -33,8 +77,13 @@
     return places, at, at + strip
 
 
-def pack_kernel(core_ref, whole_ref, gram_ref, mine_ref, theirs_ref, packed):
+def pack_kernel(zs, place_ref, gram_ref, *refs):
+    blocks, (mine_ref, theirs_ref, whole_ref, packed) = refs[:zs], refs[zs:]
     n = whole_ref.shape[0]
+    deep = n // zs
+    z, core = place_ref[0], place_ref[1]
+    for bits in range(zs):
+        whole_ref[pl.ds(pl.multiple_of((z ^ bits) * deep, 8), deep), :] = blocks[bits][...]
     places, corner, size = layout(n)
     edge = n // 128 * 128
     high, low = split(whole_ref[...])
@@ -58,23 +107,24 @@
             packed[at : at + n - edge, :] = strip[:, 128 * j : 128 * j + 128]
         packed[corner:size, :] = jnp.pad(strip[:, edge:], ((0, 0), (0, 128 - (n - edge))))
     half = size // 2
-    core = core_ref[0]
     mine_ref[...] = packed[pl.ds(pl.multiple_of(core * half, 8), half), :]
     theirs_ref[...] = packed[pl.ds(pl.multiple_of((1 - core) * half, 8), half), :]
 
 
-def pack(core, whole, gram):
-    size = layout(whole.shape[0])[2]
+def pack(place, gram, blocks):
+    n = gram.shape[0]
+    size = layout(n)[2]
     half = jax.ShapeDtypeStruct((size // 2, 128), jnp.float32)
+    vmem = pl.BlockSpec(memory_space=pltpu.VMEM)
     return pl.pallas_call(
-        pack_kernel,
-        out_shape=(half, half),
-        in_specs=[pl.BlockSpec(memory_space=pltpu.SMEM)] + [pl.BlockSpec(memory_space=pltpu.VMEM)] * 2,
-        out_specs=[pl.BlockSpec(memory_space=pltpu.VMEM)] * 2,
+        functools.partial(pack_kernel, len(blocks)),
+        out_shape=(half, half, jax.ShapeDtypeStruct((n, blocks[0].shape[1]), jnp.float32)),
+        in_specs=[pl.BlockSpec(memory_space=pltpu.SMEM)] + [vmem] * (1 + len(blocks)),
+        out_specs=[vmem] * 3,
         scratch_shapes=[pltpu.VMEM((size, 128), jnp.float32)],
         compiler_params=pltpu.CompilerParams(vmem_limit_bytes=32 * 2**20),
         name="gram_pack",
-    )(core.reshape(1), whole, gram)
+    )(place, gram, *blocks)
 
 
 def lower_inverse(small):
@@ -132,7 +182,7 @@
     return jnp.concatenate(done, 0)
 
 
-def iterations_kernel(iters, core_ref, mine_ref, other_ref, start_ref, factor_ref, packed, gram):
+def iterations_kernel(iters, place_ref, mine_ref, other_ref, start_ref, factor_ref, packed, gram):
     def times(a, b, dims):
         return lax.dot_general(a, b, (dims, ((), ())), precision=HIGHEST, preferred_element_type=jnp.float32)
 
@@ -140,7 +190,7 @@
     places, corner, size = layout(n)
     edge = n // 128 * 128
     half = size // 2
-    core = core_ref[0]
+    core = place_ref[1]
     packed[pl.ds(pl.multiple_of(core * half, 8), half), :] = mine_ref[...]
     packed[pl.ds(pl.multiple_of((1 - core) * half, 8), half), :] = other_ref[...]
     for j, (at, rows, strip) in enumerate(places):
@@ -164,7 +214,7 @@
             factor_ref[...] = times(image, inverse, ((1,), (1,)))
 
 
-def iterations(core, mine, other, start, iters):
+def iterations(place, mine, other, start, iters):
     n = start.shape[0]
     return pl.pallas_call(
         functools.partial(iterations_kernel, iters),
@@ -174,7 +224,7 @@
         scratch_shapes=[pltpu.VMEM((layout(n)[2], 128), jnp.float32), pltpu.VMEM((n, n), jnp.float32)],
         compiler_params=pltpu.CompilerParams(vmem_limit_bytes=32 * 2**20),
         name="iterations",
-    )(core.reshape(1), mine, other, start)
+    )(place, mine, other, start)
 
 
 def sum_everywhere(mine, theirs, fibre, rest):
@@ -199,51 +249,65 @@
     return out, swap(out, "fibre", fibre, 1)
 
 
+def assemble_kernel(place_ref, *refs):
+    blocks, (mine_ref, theirs_ref) = refs[:-2], refs[-2:]
+    z, core = place_ref[0], place_ref[1]
+    own, part = mine_ref.shape[0], blocks[0].shape[1]
+    for bits, block in enumerate(blocks):
+        at = pl.multiple_of((z ^ bits) * part, 128)
+        first, last = block[:own, :], block[own:, :]
+        mine_ref[:, pl.ds(at, part)] = jnp.where(core == 0, first, last)
+        theirs_ref[:, pl.ds(at, part)] = jnp.where(core == 0, last, first)
+
+
+def assemble(place, blocks):
+    two_own, part = blocks[0].shape
+    vmem = pl.BlockSpec(memory_space=pltpu.VMEM)
+    half = jax.ShapeDtypeStruct((two_own // 2, part * len(blocks)), jnp.float32)
+    return pl.pallas_call(
+        assemble_kernel,
+        out_shape=(half, half),
+        in_specs=[pl.BlockSpec(memory_space=pltpu.SMEM)] + [vmem] * len(blocks),
+        out_specs=[vmem] * 2,
+        compiler_params=pltpu.CompilerParams(vmem_limit_bytes=32 * 2**20),
+        name="assemble",
+    )(place, *blocks)
+
+
 def shards(fibre, rest, slab, start_basis):
     rows, cols = slab.shape
     zs = fibre // 2
     f = lax.axis_index("fibre")
     z, core = f // 2, f % 2
+    place = jnp.stack([z, core])
     half = cols // 2
     part = half // zs
     chunks = [(0, part * 3 // 4), (part * 3 // 4, part // 4)]
-    order = list(range(zs - 1, -1, -1))
-    fibres = []
-    before = [None] * zs
-    for start, width in chunks:
-        whole = jnp.zeros((zs, 2 * rows, width), jnp.float32)
-        for bits in order:
-            at = (z ^ bits) * part + start
-            mine = lax.dynamic_slice(slab, (0, core * half + at), (rows, width))
-            theirs = lax.dynamic_slice(slab, (0, (1 - core) * half + at), (rows, width))
-            block = in_order(core, mine, swap(theirs, "fibre", fibre, 1), 0)
-            slab, block = lax.optimization_barrier((slab, block))
-            if bits:
-                if before[bits] is not None:
-                    block, before[bits] = lax.optimization_barrier((block, before[bits]))
-                block = before[bits] = swap(block, "fibre", fibre, 2 * bits)
-            whole = lax.dynamic_update_slice(whole, block[None], (z ^ bits, 0, 0))
-        fibres.append(whole.reshape(zs * 2 * rows, width))
     n = zs * 2 * rows
-    gram = jnp.dot(fibres[0], fibres[0].T, precision=HIGH, preferred_element_type=jnp.float32)
-    mine, other = sum_everywhere(*pack(core, fibres[1], gram), fibre, rest)
-    basis = iterations(core, mine, other, start_basis, ITERS)
-    rank = basis.shape[1]
-    own = rank // fibre
+    theirs = lax.dynamic_slice(slab, (0, (1 - core) * half), (rows, half))
+    early, late = prepare(place, slab, swap(theirs, "fibre", fibre, 1), zs, chunks)
+    arrived = [early[0]] + [swap(early[bits], "fibre", fibre, 2 * bits) for bits in range(1, zs)]
+    last = [late[0]]
+    for bits in range(1, zs):
+        gate = bits if 2 * bits < zs else zs - 1
+        block, arrived[gate] = lax.optimization_barrier((late[bits], arrived[gate]))
+        last.append(swap(block, "fibre", fibre, 2 * bits))
+    whole = jnp.zeros((zs, 2 * rows, chunks[0][1]), jnp.float32)
+    for bits in range(zs):
+        whole = lax.dynamic_update_slice(whole, arrived[bits][None], (z ^ bits, 0, 0))
+    whole = whole.reshape(n, chunks[0][1])
+    gram = jnp.dot(whole, whole.T, precision=HIGH, preferred_element_type=jnp.float32)
+    mine, theirs, end = pack(place, gram, last)
+    mine, other = sum_everywhere(mine, theirs, fibre, rest)
+    basis = iterations(place, mine, other, start_basis, ITERS)
+    own = basis.shape[1] // fibre
     rows_of = [lax.dynamic_slice(basis.T, ((z ^ bits) * 2 * own, 0), (2 * own, n)) for bits in range(zs)]
     rows_of = jnp.concatenate(rows_of, 0)
-    share = [jnp.dot(rows_of, whole, precision=HIGH, preferred_element_type=jnp.float32) for whole in fibres]
+    share = [jnp.dot(rows_of, columns, precision=HIGH, preferred_element_type=jnp.float32) for columns in (whole, end)]
     share = jnp.concatenate(share, 1)
-    arrived = jnp.zeros((zs, 2 * own, part), jnp.float32)
-    for bits in order:
-        block = share[2 * own * bits : 2 * own * (bits + 1)]
-        if bits:
-            block = swap(block, "fibre", fibre, 2 * bits)
-        arrived = lax.dynamic_update_slice(arrived, block[None], (z ^ bits, 0, 0))
-    mine = lax.dynamic_slice(arrived, (0, core * own, 0), (zs, own, part))
-    theirs = lax.dynamic_slice(arrived, (0, (1 - core) * own, 0), (zs, own, part))
-    theirs = theirs.transpose(1, 0, 2).reshape(own, half)
-    mine = mine.transpose(1, 0, 2).reshape(own, half)
+    blocks = [share[2 * own * bits : 2 * own * (bits + 1)] for bits in range(zs)]
+    blocks = blocks[:1] + [swap(blocks[bits], "fibre", fibre, 2 * bits) for bits in range(1, zs)]
+    mine, theirs = assemble(place, blocks)
     return (basis, in_order(core, mine, swap(theirs, "fibre", fibre, 1), 1))
 
 

time: 231 us -> 230 us (level)
  starting transfers between devices: 47.7 us -> 29.5 us
  waiting for transfers between devices: 132 us -> 139 us
  matrix products: 7.13 us -> 13.2 us
  local copies, waits for them, and re-layouts: 17.3 us -> 21.9 us
  other arithmetic: 5.29 us -> 1.69 us
    ppermute x29 -> x22, starting transfers between devices: 47.7 us -> 29.5 us  [swap(): return lax.ppermute(x, axis, [(i, i ^ bits) for i in range(size)])]
    ppermute x29 -> x22, waiting for transfers between devices: 132 us -> 139 us  [swap(): return lax.ppermute(x, axis, [(i, i ^ bits) for i in range(size)])]
    dynamic_slice x8 -> x1, local copies, waits for them, and re-layouts: 9.98 us -> 3.59 us  [shards(): theirs = lax.dynamic_slice(slab, (0, (1 - core) * half), (rows, half))]
    dot_general x3, matrix products: 7.13 us -> 13.2 us  [the longest x1 9.02 us: shards(): jnp.dot(whole, whole.T, precision=HIGH, preferred_element_type=jnp.float32)]
    pallas_call x0 -> x1, local copies, waits for them, and re-layouts: none -> 5.03 us  [prepare(): pl.pallas_call(functools.partial(prepare_kernel, chunks), out_shape=outs,...]
    select_n x9 -> x1, other arithmetic: 4.76 us -> 1.08 us  [in_order(): jnp.where(core == 0, jnp.concatenate([mine, other], axis), jnp.concatenat...]
    dynamic_update_slice x13 -> x3, local copies, waits for them, and re-layouts: 3.93 us -> 6.73 us  [shards(): lax.dynamic_update_slice(whole, arrived[bits][None], (z ^ bits, 0, 0))]
  transfers between devices with their start and end apart: 29 -> 22, of which waited for: 20 -> 18; matrix products, arithmetic and copies ran while one was open for 7% -> 8% of each run, Pallas kernels for 0% -> 0%
where the time goes in v4:
time: 230 us; the launch traced here: 228 us
  waiting for transfers between devices  139 us (60%)
  starting transfers between devices  29.5 us (13%)
  local copies, waits for them, and re-layouts  21.9 us (10%)
  Pallas kernels  21.9 us (10%)
  matrix products  13.2 us (6%)
    ppermute x22, waiting for transfers between devices, swap(): return lax.ppermute(x, axis, [(i, i ^ bits) for i in range(size)])  139 us
    ppermute x22, starting transfers between devices, swap(): return lax.ppermute(x, axis, [(i, i ^ bits) for i in range(size)])  29.5 us
    pallas_call x1, Pallas kernels, iterations(): pl.pallas_call(functools.partial(iterations_kernel, iters), out_shape=jax...  18.7 us
    dot_general x1, matrix products, shards(): jnp.dot(whole, whole.T, precision=HIGH, preferred_element_type=jnp.float32)  9.02 us
    dynamic_update_slice x3, local copies, waits for them, and re-layouts, shards(): lax.dynamic_update_slice(whole, arrived[bits][None], (z ^ bits, 0, 0))  6.73 us
    pallas_call x1, local copies, waits for them, and re-layouts, prepare(): pl.pallas_call(functools.partial(prepare_kernel, chunks), out_shape=outs,...  5.03 us
  transfers between devices with their start and end apart: 22, of which 18 were waited for; matrix products, arithmetic and copies ran while one was open for 8% of the time, Pallas kernels for 0%

profile of v4, /device:TPU:1, one launch (start us, length us, event | category | flops | bytes accessed | tf_op | source)
XLA Modules:
  0.0 227.9 jit_solution(17405136699171223964)
XLA Ops:
  0.6 3.6 %constant_dynamic-slice_fusion.3 = f32[84,8192]{1,0:T(8,128)} fusion(f32[84,16384]{1,0:T(8,128)} %param.2, s32[]{:T(128)S(6)} %select_n.72), kind=kLoop, calls=%fused_computation.29 | loop fusion | bytes 5505028 | tf_op jit(solution)/shard_map/dynamic_slice | solution.py:287
  4.4 5.4 %collective-permute-done = f32[84,8192]{1,0:T(8,128)S(1)} collective-permute-done((f32[84,8192]{1,0:T(8,128)}, f32[84,8192]{1,0:T(8,128)S(1)}, u32[]{:S(2)}, u32[]{:S(2)}) %collective-permute-start) | collective-permute-done | bytes 2752544 | tf_op jit(solution)/shard_map/ppermute | solution.py:16
  9.7 1.6 copy-done
  11.3 2.4 %broadcast_in_dim.31 = f32[4,168,1536]{2,1,0:T(8,128)} broadcast(f32[]{:T(128)} %constant.48.clone.1), dimensions={} | broadcast | bytes 4128772 | tf_op jit(solution)/shard_map/broadcast_in_dim | solution.py:295
  13.8 5.0 %prepare.1 = (f32[4,168,1536]{2,1,0:T(8,128)}, f32[168,512]{1,0:T(8,128)S(1)}, f32[168,1536]{1,0:T(8,128)S(1)}, f32[168,1536]{1,0:T(8,128)S(1)}, f32[168,512]{1,...) fusion(f32[4,168,1536]{2,1,0:T(8,128)} %broadcast_in_dim.31, ...), kind=kCustom, calls=%fused_computation.7 | custom fusion | bytes 14155788 | tf_op jit(solution)/shard_map/prepare/pallas_call | solution.py:55
  18.8 4.5 %collective-permute-start.3 = (f32[168,1536]{1,0:T(8,128)}, f32[168,1536]{1,0:T(8,128)}, u32[]{:S(2)}, u32[]{:S(2)}) collective-permute-start(f32[168,1536]{1,0:T(8,128)} %get-tuple-element.55), channel_id=1, source_target_pairs={{0,24},{4,28},{8,16},{12,20},{16,8},{20,12},{24,0},{28,4},{1,25},{... | collective-permute-start | bytes 3096584 | tf_op jit(solution)/shard_map/ppermute | solution.py:16
  23.7 22.9 %collective-permute-done.3 = f32[168,1536]{1,0:T(8,128)} collective-permute-done((f32[168,1536]{1,0:T(8,128)}, f32[168,1536]{1,0:T(8,128)}, u32[]{:S(2)}, u32[]{:S(2)}) %collective-permute-start.3) | collective-permute-done | bytes 1032224 | tf_op jit(solution)/shard_map/ppermute | solution.py:16
  46.6 23.6 %collective-permute-done.1 = f32[168,1536]{1,0:T(8,128)} collective-permute-done((f32[168,1536]{1,0:T(8,128)S(1)}, f32[168,1536]{1,0:T(8,128)}, u32[]{:S(2)}, u32[]{:S(2)}) %collective-permute-start.1) | collective-permute-done | bytes 1032224 | tf_op jit(solution)/shard_map/ppermute | solution.py:16
  71.0 2.7 %collective-permute-start.4 = (f32[168,512]{1,0:T(8,128)S(1)}, f32[168,512]{1,0:T(8,128)S(1)}, u32[]{:S(2)}, u32[]{:S(2)}) collective-permute-start(f32[168,512]{1,0:T(8,128)S(1)} %get-tuple-element.32), channel_id=1, source_target_pairs={{0,8},{4,12},{8,0},{12,4},{16,24},{20,28},{24,16},{28,20},{1,9},{5... | collective-permute-start | bytes 1032200 | tf_op jit(solution)/shard_map/ppermute | solution.py:16
  73.7 2.2 bitcast_dynamic-update-slice_fusion.2
  75.9 50.5 %collective-permute-done.2 = f32[168,1536]{1,0:T(8,128)} collective-permute-done((f32[168,1536]{1,0:T(8,128)S(1)}, f32[168,1536]{1,0:T(8,128)}, u32[]{:S(2)}, u32[]{:S(2)}) %collective-permute-start.2) | collective-permute-done | bytes 1032224 | tf_op jit(solution)/shard_map/ppermute | solution.py:16
  126.4 2.3 bitcast_dynamic-update-slice_fusion.1
  128.7 2.2 bitcast_dynamic-update-slice_fusion
  131.0 9.0 %fusion.12.gram_ref = f32[672,672]{1,0:T(8,128)S(1)} fusion(f32[672,1536]{1,0:T(8,128)} %bitcast.6), kind=kOutput, calls=%fused_computation.40 | convolution fusion | flops 4161798144 | bytes 5935104 | tf_op jit(solution)/shard_map/dot_general | solution.py:299
  141.1 2.6 %gram_pack.1 = (f32[1056,128]{1,0:T(8,128)S(1)}, f32[1056,128]{1,0:T(8,128)S(1)}, f32[672,512]{1,0:T(8,128)S(1)}) custom-call(s32[2]{0:T(128)S(1)} %pad_add_fusion.place_ref, f32[672,672]{1,0:T(8,128)S(1)} %fusion.12.gram_ref, f32[168,512]{1,0:T(8,128)S(1)} %get-tuple-element.57.refs_0_, f32[168,512]{1,0:T(8,128)S(1)} %collective-permute-done.4.refs_1_, ...), custom_call_target="tpu_custom_call" | custom-call | tf_op jit(solution)/shard_map/gram_pack/pallas_call | solution.py:119
  144.9 1.6 collective-permute-done.7
  146.6 2.2 collective-permute-start.10
  149.3 3.0 %collective-permute-done.10 = f32[264,128]{1,0:T(8,128)S(1)} collective-permute-done((f32[264,128]{1,0:T(8,128)S(1)}, f32[264,128]{1,0:T(8,128)S(1)}, u32[]{:S(2)}, u32[]{:S(2)}) %collective-permute-start.10) | collective-permute-done | bytes 135200 | tf_op jit(solution)/shard_map/ppermute | solution.py:16
  152.3 3.0 %collective-permute-done.8 = f32[264,128]{1,0:T(8,128)S(1)} collective-permute-done((f32[264,128]{1,0:T(8,128)S(1)}, f32[264,128]{1,0:T(8,128)S(1)}, u32[]{:S(2)}, u32[]{:S(2)}) %collective-permute-start.8) | collective-permute-done | bytes 135200 | tf_op jit(solution)/shard_map/ppermute | solution.py:16
  155.7 2.5 %collective-permute-start.12 = (f32[264,128]{1,0:T(8,128)S(1)}, f32[264,128]{1,0:T(8,128)S(1)}, u32[]{:S(2)}, u32[]{:S(2)}) collective-permute-start(f32[264,128]{1,0:T(8,128)S(1)} %add_add_fusion.1), channel_id=1, source_target_pairs={{0,16},{4,20},{8,24},{12,28},{16,0},{20,4},{24,8},{28,12},{1,17},{... | collective-permute-start | bytes 405512 | tf_op jit(solution)/shard_map/ppermute | solution.py:16
  159.2 2.6 %collective-permute-done.11 = f32[264,128]{1,0:T(8,128)S(1)} collective-permute-done((f32[264,128]{1,0:T(8,128)S(1)}, f32[264,128]{1,0:T(8,128)S(1)}, u32[]{:S(2)}, u32[]{:S(2)}) %collective-permute-start.11) | collective-permute-done | bytes 135200 | tf_op jit(solution)/shard_map/ppermute | solution.py:16
  161.8 4.9 %collective-permute-done.13 = f32[264,128]{1,0:T(8,128)S(1)} collective-permute-done((f32[264,128]{1,0:T(8,128)S(1)}, f32[264,128]{1,0:T(8,128)S(1)}, u32[]{:S(2)}, u32[]{:S(2)}) %collective-permute-start.13) | collective-permute-done | bytes 135200 | tf_op jit(solution)/shard_map/ppermute | solution.py:16
  168.1 2.1 collective-permute-start.15
  170.8 2.4 %collective-permute-done.15 = f32[264,128]{1,0:T(8,128)S(1)} collective-permute-done((f32[264,128]{1,0:T(8,128)S(1)}, f32[264,128]{1,0:T(8,128)S(1)}, u32[]{:S(2)}, u32[]{:S(2)}) %collective-permute-start.15) | collective-permute-done | bytes 135200 | tf_op jit(solution)/shard_map/ppermute | solution.py:16
  173.2 3.0 %collective-permute-done.16 = f32[264,128]{1,0:T(8,128)S(1)} collective-permute-done((f32[264,128]{1,0:T(8,128)S(1)}, f32[264,128]{1,0:T(8,128)S(1)}, u32[]{:S(2)}, u32[]{:S(2)}) %collective-permute-start.16) | collective-permute-done | bytes 135200 | tf_op jit(solution)/shard_map/ppermute | solution.py:16
  176.1 2.9 %collective-permute-start.17 = (f32[1056,128]{1,0:T(8,128)S(1)}, f32[1056,128]{1,0:T(8,128)S(1)}, u32[]{:S(2)}, u32[]{:S(2)}) collective-permute-start(f32[1056,128]{1,0:T(8,128)S(1)} %bitcast.34), channel_id=1, source_target_pairs={{0,4},{4,0},{8,12},{12,8},{16,20},{20,16},{24,28},{28,24},{1,5},{5... | collective-permute-start | bytes 1622024 | tf_op jit(solution)/shard_map/ppermute | solution.py:16
  180.6 18.7 %iterations.1 = f32[672,96]{1,0:T(8,128)S(1)} custom-call(s32[2]{0:T(128)S(1)} %pad_add_fusion.place_ref, f32[1056,128]{1,0:T(8,128)S(1)} %bitcast.35, f32[1056,128]{1,0:T(8,128)S(1)} %collective-permute-done.17.other_ref, f32[672,96]{1,0:T(8,128)S(1)} %copy.4.start_ref), custom_call_target="tpu_custom_call" | custom-call | tf_op jit(solution)/shard_map/iterations/pallas_call | solution.py:219
  200.1 3.6 %fusion.13 = f32[96,1536]{1,0:T(8,128)S(1)} fusion(f32[96,672]{0,1:T(8,128)S(1)} %pad_maximum_fusion, f32[672,1536]{1,0:T(8,128)} %bitcast.6), kind=kOutput, calls=%fused_computation.41 | convolution fusion | flops 594542592 | bytes 4976640 | tf_op jit(solution)/shard_map/dot_general | solution.py:306
  204.3 2.4 %collective-permute-start.18 = (f32[24,2048]{1,0:T(8,128)S(1)}, f32[24,2048]{1,0:T(8,128)S(1)}, u32[]{:S(2)}, u32[]{:S(2)}) collective-permute-start(f32[24,2048]{1,0:T(8,128)S(1)} %get-tuple-element.62), channel_id=1, source_target_pairs={{0,8},{4,12},{8,0},{12,4},{16,24},{20,28},{24,16},{28,20},{1,9},{5... | collective-permute-start | bytes 589832 | tf_op jit(solution)/shard_map/ppermute | solution.py:16
  208.9 6.4 %collective-permute-done.18.refs_1_ = f32[24,2048]{1,0:T(8,128)S(1)} collective-permute-done((f32[24,2048]{1,0:T(8,128)S(1)}, f32[24,2048]{1,0:T(8,128)S(1)}, u32[]{:S(2)}, u32[]{:S(2)}) %collective-permute-start.18) | collective-permute-done | bytes 196640 | tf_op jit(solution)/shard_map/ppermute | solution.py:16
  215.3 6.7 %collective-permute-done.20.refs_3_ = f32[24,2048]{1,0:T(8,128)S(1)} collective-permute-done((f32[24,2048]{1,0:T(8,128)S(1)}, f32[24,2048]{1,0:T(8,128)S(1)}, u32[]{:S(2)}, u32[]{:S(2)}) %collective-permute-start.20) | collective-permute-done | bytes 196640 | tf_op jit(solution)/shard_map/ppermute | solution.py:16
  222.7 2.6 %collective-permute-start.21 = (f32[12,8192]{1,0:T(8,128)S(1)}, f32[12,8192]{1,0:T(8,128)S(1)}, u32[]{:S(2)}, u32[]{:S(2)}) collective-permute-start(f32[12,8192]{1,0:T(8,128)S(1)} %get-tuple-element.39), channel_id=1, source_target_pairs={{0,4},{4,0},{8,12},{12,8},{16,20},{20,16},{24,28},{28,24},{1,5},{5... | collective-permute-start | bytes 1179656 | tf_op jit(solution)/shard_map/ppermute | solution.py:16
  (41 shorter events, 16.1 us)
Async XLA Ops:
  4.2 5.5 %collective-permute-start = (f32[84,8192]{1,0:T(8,128)}, f32[84,8192]{1,0:T(8,128)S(1)}, u32[]{:S(2)}, u32[]{:S(2)}) collective-permute-start(f32[84,8192]{1,0:T(8,128)} %constant_dynamic-slice_fusion.3), channel_id=1, source_target_pairs={{0,4},{4,0},{8,12},{12,8},{16,20},{20,16},{24,28},{28,24},{1,5},{5... | collective-permute-start | bytes 8257544 | tf_op jit(solution)/shard_map/ppermute | solution.py:16
  9.7 1.6 copy-start
  18.8 27.8 %collective-permute-start.3 = (f32[168,1536]{1,0:T(8,128)}, f32[168,1536]{1,0:T(8,128)}, u32[]{:S(2)}, u32[]{:S(2)}) collective-permute-start(f32[168,1536]{1,0:T(8,128)} %get-tuple-element.55), channel_id=1, source_target_pairs={{0,24},{4,28},{8,16},{12,20},{16,8},{20,12},{24,0},{28,4},{1,25},{... | collective-permute-start | bytes 3096584 | tf_op jit(solution)/shard_map/ppermute | solution.py:16
  23.3 46.9 %collective-permute-start.1 = (f32[168,1536]{1,0:T(8,128)S(1)}, f32[168,1536]{1,0:T(8,128)}, u32[]{:S(2)}, u32[]{:S(2)}) collective-permute-start(f32[168,1536]{1,0:T(8,128)S(1)} %get-tuple-element.47), channel_id=1, source_target_pairs={{0,8},{4,12},{8,0},{12,4},{16,24},{20,28},{24,16},{28,20},{1,9},{5... | collective-permute-start | bytes 3096584 | tf_op jit(solution)/shard_map/ppermute | solution.py:16
  23.3 103.1 %collective-permute-start.2 = (f32[168,1536]{1,0:T(8,128)S(1)}, f32[168,1536]{1,0:T(8,128)}, u32[]{:S(2)}, u32[]{:S(2)}) collective-permute-start(f32[168,1536]{1,0:T(8,128)S(1)} %get-tuple-element.49), channel_id=1, source_target_pairs={{0,16},{4,20},{8,24},{12,28},{16,0},{20,4},{24,8},{28,12},{1,17},{... | collective-permute-start | bytes 3096584 | tf_op jit(solution)/shard_map/ppermute | solution.py:16
  70.2 69.8 %collective-permute-start.6 = (f32[168,512]{1,0:T(8,128)S(1)}, f32[168,512]{1,0:T(8,128)S(1)}, u32[]{:S(2)}, u32[]{:S(2)}) collective-permute-start(f32[168,512]{1,0:T(8,128)S(1)} %get-tuple-element.34), channel_id=1, source_target_pairs={{0,24},{4,28},{8,16},{12,20},{16,8},{20,12},{24,0},{28,4},{1,25},{... | collective-permute-start | bytes 1032200 | tf_op jit(solution)/shard_map/ppermute | solution.py:16
  70.2 70.9 %collective-permute-start.5 = (f32[168,512]{1,0:T(8,128)S(1)}, f32[168,512]{1,0:T(8,128)S(1)}, u32[]{:S(2)}, u32[]{:S(2)}) collective-permute-start(f32[168,512]{1,0:T(8,128)S(1)} %get-tuple-element.33), channel_id=1, source_target_pairs={{0,16},{4,20},{8,24},{12,28},{16,0},{20,4},{24,8},{28,12},{1,17},{... | collective-permute-start | bytes 1032200 | tf_op jit(solution)/shard_map/ppermute | solution.py:16
  71.0 70.1 %collective-permute-start.4 = (f32[168,512]{1,0:T(8,128)S(1)}, f32[168,512]{1,0:T(8,128)S(1)}, u32[]{:S(2)}, u32[]{:S(2)}) collective-permute-start(f32[168,512]{1,0:T(8,128)S(1)} %get-tuple-element.32), channel_id=1, source_target_pairs={{0,8},{4,12},{8,0},{12,4},{16,24},{20,28},{24,16},{28,20},{1,9},{5... | collective-permute-start | bytes 1032200 | tf_op jit(solution)/shard_map/ppermute | solution.py:16
  143.6 2.8 %collective-permute-start.7 = (f32[1056,128]{1,0:T(8,128)S(1)}, f32[1056,128]{1,0:T(8,128)S(1)}, u32[]{:S(2)}, u32[]{:S(2)}) collective-permute-start(f32[1056,128]{1,0:T(8,128)S(1)} %get-tuple-element.36), channel_id=1, source_target_pairs={{0,4},{4,0},{8,12},{12,8},{16,20},{20,16},{24,28},{28,24},{1,5},{5... | collective-permute-start | bytes 1622024 | tf_op jit(solution)/shard_map/ppermute | solution.py:16
  146.6 5.8 %collective-permute-start.10 = (f32[264,128]{1,0:T(8,128)S(1)}, f32[264,128]{1,0:T(8,128)S(1)}, u32[]{:S(2)}, u32[]{:S(2)}) collective-permute-start(f32[264,128]{1,0:T(8,128)S(1)} %get-tuple-element.65), channel_id=1, source_target_pairs={{0,3},{1,2},{2,1},{3,0},{4,7},{5,6},{6,5},{7,4},{8,11},{9,10},{10,... | collective-permute-start | bytes 405512 | tf_op jit(solution)/shard_map/ppermute | solution.py:16
  148.8 6.5 %collective-permute-start.8 = (f32[264,128]{1,0:T(8,128)S(1)}, f32[264,128]{1,0:T(8,128)S(1)}, u32[]{:S(2)}, u32[]{:S(2)}) collective-permute-start(f32[264,128]{1,0:T(8,128)S(1)} %get-tuple-element.64), channel_id=1, source_target_pairs={{0,1},{1,0},{2,3},{3,2},{4,5},{5,4},{6,7},{7,6},{8,9},{9,8},{10,11... | collective-permute-start | bytes 405512 | tf_op jit(solution)/shard_map/ppermute | solution.py:16
  149.1 6.5 %collective-permute-start.9 = (f32[264,128]{1,0:T(8,128)S(1)}, f32[264,128]{1,0:T(8,128)S(1)}, u32[]{:S(2)}, u32[]{:S(2)}) collective-permute-start(f32[264,128]{1,0:T(8,128)S(1)} %get-tuple-element.66), channel_id=1, source_target_pairs={{0,2},{1,3},{2,0},{3,1},{4,6},{5,7},{6,4},{7,5},{8,10},{9,11},{10,... | collective-permute-start | bytes 405512 | tf_op jit(solution)/shard_map/ppermute | solution.py:16
  155.6 6.2 %collective-permute-start.11 = (f32[264,128]{1,0:T(8,128)S(1)}, f32[264,128]{1,0:T(8,128)S(1)}, u32[]{:S(2)}, u32[]{:S(2)}) collective-permute-start(f32[264,128]{1,0:T(8,128)S(1)} %add_add_fusion.1), channel_id=1, source_target_pairs={{0,8},{4,12},{8,0},{12,4},{16,24},{20,28},{24,16},{28,20},{1,9},{5... | collective-permute-start | bytes 405512 | tf_op jit(solution)/shard_map/ppermute | solution.py:16
  155.7 6.1 %collective-permute-start.12 = (f32[264,128]{1,0:T(8,128)S(1)}, f32[264,128]{1,0:T(8,128)S(1)}, u32[]{:S(2)}, u32[]{:S(2)}) collective-permute-start(f32[264,128]{1,0:T(8,128)S(1)} %add_add_fusion.1), channel_id=1, source_target_pairs={{0,16},{4,20},{8,24},{12,28},{16,0},{20,4},{24,8},{28,12},{1,17},{... | collective-permute-start | bytes 405512 | tf_op jit(solution)/shard_map/ppermute | solution.py:16
  158.2 8.6 %collective-permute-start.13 = (f32[264,128]{1,0:T(8,128)S(1)}, f32[264,128]{1,0:T(8,128)S(1)}, u32[]{:S(2)}, u32[]{:S(2)}) collective-permute-start(f32[264,128]{1,0:T(8,128)S(1)} %add_add_fusion.1), channel_id=1, source_target_pairs={{0,24},{4,28},{8,16},{12,20},{16,8},{20,12},{24,0},{28,4},{1,25},{... | collective-permute-start | bytes 405512 | tf_op jit(solution)/shard_map/ppermute | solution.py:16
  166.8 3.9 %collective-permute-start.14 = (f32[264,128]{1,0:T(8,128)S(1)}, f32[264,128]{1,0:T(8,128)S(1)}, u32[]{:S(2)}, u32[]{:S(2)}) collective-permute-start(f32[264,128]{1,0:T(8,128)S(1)} %get-tuple-element.59), channel_id=1, source_target_pairs={{0,1},{1,0},{2,3},{3,2},{4,5},{5,4},{6,7},{7,6},{8,9},{9,8},{10,11... | collective-permute-start | bytes 405512 | tf_op jit(solution)/shard_map/ppermute | solution.py:16
  168.1 5.1 %collective-permute-start.15 = (f32[264,128]{1,0:T(8,128)S(1)}, f32[264,128]{1,0:T(8,128)S(1)}, u32[]{:S(2)}, u32[]{:S(2)}) collective-permute-start(f32[264,128]{1,0:T(8,128)S(1)} %get-tuple-element.59), channel_id=1, source_target_pairs={{0,2},{1,3},{2,0},{3,1},{4,6},{5,7},{6,4},{7,5},{8,10},{9,11},{10,... | collective-permute-start | bytes 405512 | tf_op jit(solution)/shard_map/ppermute | solution.py:16
  170.2 5.9 %collective-permute-start.16 = (f32[264,128]{1,0:T(8,128)S(1)}, f32[264,128]{1,0:T(8,128)S(1)}, u32[]{:S(2)}, u32[]{:S(2)}) collective-permute-start(f32[264,128]{1,0:T(8,128)S(1)} %get-tuple-element.59), channel_id=1, source_target_pairs={{0,3},{1,2},{2,1},{3,0},{4,7},{5,6},{6,5},{7,4},{8,11},{9,10},{10,... | collective-permute-start | bytes 405512 | tf_op jit(solution)/shard_map/ppermute | solution.py:16
  176.1 4.4 %collective-permute-start.17 = (f32[1056,128]{1,0:T(8,128)S(1)}, f32[1056,128]{1,0:T(8,128)S(1)}, u32[]{:S(2)}, u32[]{:S(2)}) collective-permute-start(f32[1056,128]{1,0:T(8,128)S(1)} %bitcast.34), channel_id=1, source_target_pairs={{0,4},{4,0},{8,12},{12,8},{16,20},{20,16},{24,28},{28,24},{1,5},{5... | collective-permute-start | bytes 1622024 | tf_op jit(solution)/shard_map/ppermute | solution.py:16
  204.3 11.0 %collective-permute-start.18 = (f32[24,2048]{1,0:T(8,128)S(1)}, f32[24,2048]{1,0:T(8,128)S(1)}, u32[]{:S(2)}, u32[]{:S(2)}) collective-permute-start(f32[24,2048]{1,0:T(8,128)S(1)} %get-tuple-element.62), channel_id=1, source_target_pairs={{0,8},{4,12},{8,0},{12,4},{16,24},{20,28},{24,16},{28,20},{1,9},{5... | collective-permute-start | bytes 589832 | tf_op jit(solution)/shard_map/ppermute | solution.py:16
  206.7 8.6 %collective-permute-start.19 = (f32[24,2048]{1,0:T(8,128)S(1)}, f32[24,2048]{1,0:T(8,128)S(1)}, u32[]{:S(2)}, u32[]{:S(2)}) collective-permute-start(f32[24,2048]{1,0:T(8,128)S(1)} %get-tuple-element.63), channel_id=1, source_target_pairs={{0,16},{4,20},{8,24},{12,28},{16,0},{20,4},{24,8},{28,12},{1,17},{... | collective-permute-start | bytes 589832 | tf_op jit(solution)/shard_map/ppermute | solution.py:16
  207.8 14.2 %collective-permute-start.20 = (f32[24,2048]{1,0:T(8,128)S(1)}, f32[24,2048]{1,0:T(8,128)S(1)}, u32[]{:S(2)}, u32[]{:S(2)}) collective-permute-start(f32[24,2048]{1,0:T(8,128)S(1)} %get-tuple-element.60), channel_id=1, source_target_pairs={{0,24},{4,28},{8,16},{12,20},{16,8},{20,12},{24,0},{28,4},{1,25},{... | collective-permute-start | bytes 589832 | tf_op jit(solution)/shard_map/ppermute | solution.py:16
  222.7 4.1 %collective-permute-start.21 = (f32[12,8192]{1,0:T(8,128)S(1)}, f32[12,8192]{1,0:T(8,128)S(1)}, u32[]{:S(2)}, u32[]{:S(2)}) collective-permute-start(f32[12,8192]{1,0:T(8,128)S(1)} %get-tuple-element.39), channel_id=1, source_target_pairs={{0,4},{4,0},{8,12},{12,8},{16,20},{20,16},{24,28},{28,24},{1,5},{5... | collective-permute-start | bytes 1179656 | tf_op jit(solution)/shard_map/ppermute | solution.py:16

commit v5 on v4

--- a/solution.py
+++ b/solution.py
@@ -20,8 +20,9 @@
     return jnp.where(core == 0, jnp.concatenate([mine, other], axis), jnp.concatenate([other, mine], axis))
 
 
-def prepare_kernel(chunks, place_ref, slab_ref, got_ref, *refs):
-    outs, own, sems = refs[:-2], refs[-2], refs[-1]
+def prepare_kernel(pieces, place_ref, slab_ref, got_ref, *refs):
+    distances = sorted({bits for bits, _, _ in pieces}, reverse=True)
+    outs, (own, sems) = refs[:-2], refs[-2:]
     zs, rows, part = own.shape
     z, core = place_ref[0], place_ref[1]
 
@@ -29,39 +30,40 @@
         at = pl.multiple_of(core * (zs * part) + (z ^ bits) * part, 128)
         return pltpu.make_async_copy(slab_ref.at[:, pl.ds(at, part)], own.at[bits], sems.at[bits])
 
-    for bits in reversed(range(zs)):
+    for bits in distances:
         fetch(bits).start()
-    for bits in reversed(range(zs)):
+    for order, bits in enumerate(distances):
         fetch(bits).wait()
-        for c, (start, width) in enumerate(chunks):
-            out = outs[c * zs + bits]
-            at = pl.multiple_of((z ^ bits) * part + start, 128)
+        for out, (which, start, width) in zip(outs, pieces):
+            if which != bits:
+                continue
+            columns = slice(start, start + width)
+            other = slice(order * part + start, order * part + start + width)
 
             @pl.when(core == 0)
             def _():
-                out[:rows, :] = own[bits, :, start : start + width]
-                out[rows:, :] = got_ref[:, pl.ds(at, width)]
+                out[:rows, :] = own[bits, :, columns]
+                out[rows:, :] = got_ref[:, other]
 
             @pl.when(core == 1)
             def _():
-                out[:rows, :] = got_ref[:, pl.ds(at, width)]
-                out[rows:, :] = own[bits, :, start : start + width]
-
-
-def prepare(place, slab, got, zs, chunks):
-    rows, half = got.shape
+                out[:rows, :] = got_ref[:, other]
+                out[rows:, :] = own[bits, :, columns]
+
+
+def prepare(place, slab, got, zs, pieces):
+    rows, part = got.shape[0], got.shape[1] // (zs - 1)
     vmem = pl.BlockSpec(memory_space=pltpu.VMEM)
-    outs = [jax.ShapeDtypeStruct((2 * rows, width), jnp.float32) for _, width in chunks for _ in range(zs)]
-    outs = pl.pallas_call(
-        functools.partial(prepare_kernel, chunks),
-        out_shape=outs,
+    return pl.pallas_call(
+        functools.partial(prepare_kernel, pieces),
+        out_shape=[jax.ShapeDtypeStruct((2 * rows, width), jnp.float32) for _, _, width in pieces],
         in_specs=[pl.BlockSpec(memory_space=pltpu.SMEM), pl.BlockSpec(memory_space=pl.ANY), vmem],
-        out_specs=[vmem] * len(outs),
-        scratch_shapes=[pltpu.VMEM((zs, rows, half // zs), jnp.float32), pltpu.SemaphoreType.DMA((zs,))],
-        compiler_params=pltpu.CompilerParams(vmem_limit_bytes=40 * 2**20),
+        out_specs=[vmem] * len(pieces),
+        scratch_shapes=[pltpu.VMEM((zs, rows, part), jnp.float32), pltpu.SemaphoreType.DMA((zs,))],
+        compiler_params=pltpu.CompilerParams(vmem_limit_bytes=32 * 2**20),
+        cost_estimate=pl.CostEstimate(flops=0, bytes_accessed=100_000_000, transcendentals=0),
         name="prepare",
     )(place, slab, got)
-    return [outs[c * zs : (c + 1) * zs] for c in range(len(chunks))]
 
 
 def split(x):
@@ -77,54 +79,85 @@
     return places, at, at + strip
 
 
-def pack_kernel(zs, place_ref, gram_ref, *refs):
-    blocks, (mine_ref, theirs_ref, whole_ref, packed) = refs[:zs], refs[zs:]
-    n = whole_ref.shape[0]
+def add_gram(starts, width, place_ref, blocks, whole, high_ref, low_ref, packed, base_ref):
+    zs = len(blocks)
+    n = whole.shape[0]
     deep = n // zs
-    z, core = place_ref[0], place_ref[1]
-    for bits in range(zs):
-        whole_ref[pl.ds(pl.multiple_of((z ^ bits) * deep, 8), deep), :] = blocks[bits][...]
+    z = place_ref[0]
+    for bits, (block, start) in enumerate(zip(blocks, starts)):
+        if deep % 8 == 0:
+            whole[pl.ds(pl.multiple_of((z ^ bits) * deep, 8), deep), :] = block[:, start : start + width]
+            continue
+        for here in range(zs):
+
+            @pl.when(z == here)
+            def _():
+                at = (here ^ bits) * deep
+                whole[at : at + deep, :] = block[:, start : start + width]
+
     places, corner, size = layout(n)
     edge = n // 128 * 128
-    high, low = split(whole_ref[...])
-
-    def block(r0, r1, c0, c1):
+    high_ref[...], low_ref[...] = split(whole[...])
+
+    def product(r0, r1, c0, c1):
         def times(a, b):
-            return lax.dot_general(a, b, (((1,), (1,)), ((), ())), preferred_element_type=jnp.float32)
-
-        total = times(high[r0:r1], low[c0:c1]) + times(low[r0:r1], high[c0:c1]) + times(high[r0:r1], high[c0:c1])
-        return total + gram_ref[r0:r1, c0:c1]
+            return lax.dot_general(a[r0:r1, :], b[c0:c1, :], (((1,), (1,)), ((), ())), preferred_element_type=jnp.float32)
+
+        return times(high_ref, low_ref) + times(low_ref, high_ref) + times(high_ref, high_ref)
+
+    def put(at, value):
+        rows = slice(at, at + value.shape[0])
+        packed[rows, :] = value if base_ref is None else value + base_ref[rows, :]
 
     for start in range(0, edge, 256):
         stop = min(start + 256, edge)
-        upper = block(0, stop, start, stop)
+        upper = product(0, stop, start, stop)
         for j in range(start // 128, stop // 128):
             at, rows, _ = places[j]
-            packed[at : at + rows, :] = upper[:rows, 128 * j - start : 128 * j - start + 128]
+            put(at, upper[:rows, 128 * j - start : 128 * j - start + 128])
     if n > edge:
-        strip = block(edge, n, 0, n)
+        strip = product(edge, n, 0, n)
         for j, (_, _, at) in enumerate(places):
-            packed[at : at + n - edge, :] = strip[:, 128 * j : 128 * j + 128]
-        packed[corner:size, :] = jnp.pad(strip[:, edge:], ((0, 0), (0, 128 - (n - edge))))
-    half = size // 2
+            put(at, strip[:, 128 * j : 128 * j + 128])
+        put(corner, jnp.pad(strip[:, edge:], ((0, 0), (0, 128 - (n - edge)))))
+
+
+def early_kernel(starts, width, place_ref, *refs):
+    blocks, (packed, high_ref, low_ref, whole) = refs[: len(starts)], refs[len(starts) :]
+    add_gram(starts, width, place_ref, blocks, whole, high_ref, low_ref, packed, None)
+
+
+def late_kernel(starts, width, place_ref, base_ref, *refs):
+    blocks, (mine_ref, theirs_ref, high_ref, low_ref, whole, packed) = refs[: len(starts)], refs[len(starts) :]
+    add_gram(starts, width, place_ref, blocks, whole, high_ref, low_ref, packed, base_ref)
+    half = mine_ref.shape[0]
+    core = place_ref[1]
     mine_ref[...] = packed[pl.ds(pl.multiple_of(core * half, 8), half), :]
     theirs_ref[...] = packed[pl.ds(pl.multiple_of((1 - core) * half, 8), half), :]
 
 
-def pack(place, gram, blocks):
-    n = gram.shape[0]
+def gram_part(place, base, blocks, starts, width):
+    n = blocks[0].shape[0] * len(blocks)
     size = layout(n)[2]
-    half = jax.ShapeDtypeStruct((size // 2, 128), jnp.float32)
     vmem = pl.BlockSpec(memory_space=pltpu.VMEM)
-    return pl.pallas_call(
-        functools.partial(pack_kernel, len(blocks)),
-        out_shape=(half, half, jax.ShapeDtypeStruct((n, blocks[0].shape[1]), jnp.float32)),
-        in_specs=[pl.BlockSpec(memory_space=pltpu.SMEM)] + [vmem] * (1 + len(blocks)),
-        out_specs=[vmem] * 3,
-        scratch_shapes=[pltpu.VMEM((size, 128), jnp.float32)],
-        compiler_params=pltpu.CompilerParams(vmem_limit_bytes=32 * 2**20),
-        name="gram_pack",
-    )(place, gram, *blocks)
+    parts = [jax.ShapeDtypeStruct((n, width), jnp.bfloat16)] * 2
+    packed = (size, 128)
+    whole = pltpu.VMEM((n, width), jnp.float32)
+    if base is None:
+        kernel, sums, scratch, first = early_kernel, [jax.ShapeDtypeStruct(packed, jnp.float32)], [whole], []
+    else:
+        half = jax.ShapeDtypeStruct((size // 2, 128), jnp.float32)
+        kernel, sums, scratch, first = late_kernel, [half, half], [whole, pltpu.VMEM(packed, jnp.float32)], [base]
+    return pl.pallas_call(
+        functools.partial(kernel, starts, width),
+        out_shape=[*sums, *parts],
+        in_specs=[pl.BlockSpec(memory_space=pltpu.SMEM)] + [vmem] * (len(first) + len(blocks)),
+        out_specs=[vmem] * (len(sums) + 2),
+        scratch_shapes=scratch,
+        compiler_params=pltpu.CompilerParams(vmem_limit_bytes=40 * 2**20),
+        cost_estimate=pl.CostEstimate(flops=6 * n * n * width, bytes_accessed=8 * n * width, transcendentals=0),
+        name="gram_early" if base is None else "gram_late",
+    )(place, *first, *blocks)
 
 
 def lower_inverse(small):
@@ -249,6 +282,43 @@
     return out, swap(out, "fibre", fibre, 1)
 
 
+def core_kernel(place_ref, basis_ref, *refs):
+    parts, outs, share = refs[:4], refs[4:-1], refs[-1]
+    zs = len(outs)
+    two_own = share.shape[0] // zs
+    high, low = split(basis_ref[...])
+
+    def times(a, b):
+        return lax.dot_general(a, b[...], (((0,), (0,)), ((), ())), preferred_element_type=jnp.float32)
+
+    at = 0
+    for first, second in (parts[:2], parts[2:]):
+        width = first.shape[1]
+        share[:, at : at + width] = times(high, second) + times(low, first) + times(high, first)
+        at += width
+    for here in range(zs):
+
+        @pl.when(place_ref[0] == here)
+        def _():
+            for bits, out in enumerate(outs):
+                out[...] = share[two_own * (here ^ bits) : two_own * (here ^ bits) + two_own, :]
+
+
+def core_parts(place, basis, parts, zs):
+    rank = basis.shape[1]
+    part = parts[0].shape[1] + parts[2].shape[1]
+    vmem = pl.BlockSpec(memory_space=pltpu.VMEM)
+    return pl.pallas_call(
+        core_kernel,
+        out_shape=[jax.ShapeDtypeStruct((rank // zs, part), jnp.float32)] * zs,
+        in_specs=[pl.BlockSpec(memory_space=pltpu.SMEM)] + [vmem] * 5,
+        out_specs=[vmem] * zs,
+        scratch_shapes=[pltpu.VMEM((rank, part), jnp.float32)],
+        compiler_params=pltpu.CompilerParams(vmem_limit_bytes=32 * 2**20),
+        name="core_parts",
+    )(place, basis, *parts)
+
+
 def assemble_kernel(place_ref, *refs):
     blocks, (mine_ref, theirs_ref) = refs[:-2], refs[-2:]
     z, core = place_ref[0], place_ref[1]
@@ -282,31 +352,37 @@
     place = jnp.stack([z, core])
     half = cols // 2
     part = half // zs
-    chunks = [(0, part * 3 // 4), (part * 3 // 4, part // 4)]
-    n = zs * 2 * rows
-    theirs = lax.dynamic_slice(slab, (0, (1 - core) * half), (rows, half))
-    early, late = prepare(place, slab, swap(theirs, "fibre", fibre, 1), zs, chunks)
-    arrived = [early[0]] + [swap(early[bits], "fibre", fibre, 2 * bits) for bits in range(1, zs)]
-    last = [late[0]]
-    for bits in range(1, zs):
-        gate = bits if 2 * bits < zs else zs - 1
-        block, arrived[gate] = lax.optimization_barrier((late[bits], arrived[gate]))
-        last.append(swap(block, "fibre", fibre, 2 * bits))
-    whole = jnp.zeros((zs, 2 * rows, chunks[0][1]), jnp.float32)
-    for bits in range(zs):
-        whole = lax.dynamic_update_slice(whole, arrived[bits][None], (z ^ bits, 0, 0))
-    whole = whole.reshape(n, chunks[0][1])
-    gram = jnp.dot(whole, whole.T, precision=HIGH, preferred_element_type=jnp.float32)
-    mine, theirs, end = pack(place, gram, last)
+    early = part * 3 // 4
+
+    def cut(slab, whose, bits):
+        return lax.dynamic_slice(slab, (0, whose * half + (z ^ bits) * part), (rows, part))
+
+    far = zs - 1
+    got = swap(cut(slab, 1 - core, far), "fibre", fibre, 1)
+    block = in_order(core, cut(slab, core, far), got, 0)
+    slab, block = lax.optimization_barrier((slab, block))
+    arrived = {far: swap(block, "fibre", fibre, 2 * far)}
+    others = list(range(far - 1, -1, -1))
+    theirs = jnp.concatenate([cut(slab, 1 - core, bits) for bits in others], 1)
+    got = swap(theirs, "fibre", fibre, 1)
+    pieces = []
+    for bits in others:
+        pieces += [(bits, 0, early), (bits, early, part - early)] if bits > 1 else [(bits, 0, part)]
+    late = {}
+    for (bits, start, _), block in zip(pieces, prepare(place, slab, got, zs, pieces)):
+        if start:
+            block, arrived[far] = lax.optimization_barrier((block, arrived[far]))
+        into = late if start else arrived
+        into[bits] = swap(block, "fibre", fibre, 2 * bits) if bits else block
+    first = [arrived[bits] for bits in range(zs)]
+    last = [late.get(bits, arrived[bits]) for bits in range(zs)]
+    last_from = tuple(0 if bits in late else early for bits in range(zs))
+    packed, *parts = gram_part(place, None, first, (0,) * zs, early)
+    mine, theirs, *more = gram_part(place, packed, last, last_from, part - early)
     mine, other = sum_everywhere(mine, theirs, fibre, rest)
     basis = iterations(place, mine, other, start_basis, ITERS)
-    own = basis.shape[1] // fibre
-    rows_of = [lax.dynamic_slice(basis.T, ((z ^ bits) * 2 * own, 0), (2 * own, n)) for bits in range(zs)]
-    rows_of = jnp.concatenate(rows_of, 0)
-    share = [jnp.dot(rows_of, columns, precision=HIGH, preferred_element_type=jnp.float32) for columns in (whole, end)]
-    share = jnp.concatenate(share, 1)
-    blocks = [share[2 * own * bits : 2 * own * (bits + 1)] for bits in range(zs)]
-    blocks = blocks[:1] + [swap(blocks[bits], "fibre", fibre, 2 * bits) for bits in range(1, zs)]
+    blocks = core_parts(place, basis, [*parts, *more], zs)
+    blocks = [blocks[0]] + [swap(blocks[bits], "fibre", fibre, 2 * bits) for bits in range(1, zs)]
     mine, theirs = assemble(place, blocks)
     return (basis, in_order(core, mine, swap(theirs, "fibre", fibre, 1), 1))
 

time: 230 us -> 221 us (0.961)
  starting transfers between devices: 29.5 us -> 61.7 us
  waiting for transfers between devices: 139 us -> 110 us
  matrix products: 13.2 us -> 0 us
  local copies, waits for them, and re-layouts: 21.9 us -> 10.9 us
  Pallas kernels: 21.9 us -> 32.5 us
    ppermute x22 -> x21, starting transfers between devices: 29.5 us -> 61.7 us  [swap(): return lax.ppermute(x, axis, [(i, i ^ bits) for i in range(size)])]
    ppermute x22 -> x21, waiting for transfers between devices: 139 us -> 110 us  [swap(): return lax.ppermute(x, axis, [(i, i ^ bits) for i in range(size)])]
    dot_general x3 -> x0, matrix products: 13.2 us -> none  [the longest x1 9.02 us: shards(): jnp.dot(whole, whole.T, precision=HIGH, preferred_element_type=jnp.float32)]
    pallas_call x1 -> x4, Pallas kernels: 2.55 us -> 12.6 us  [the longest x2 9.43 us: gram_part(): pl.pallas_call(functools.partial(kernel, starts, width), out_shape=[*sums...]
    dynamic_update_slice x3 -> x0, local copies, waits for them, and re-layouts: 6.73 us -> none  [shards(): lax.dynamic_update_slice(whole, arrived[bits][None], (z ^ bits, 0, 0))]
    pallas_call x1 -> x0, local copies, waits for them, and re-layouts: 5.03 us -> none  [prepare(): pl.pallas_call(functools.partial(prepare_kernel, chunks), out_shape=outs,...]
    unnamed x4 -> x20, local copies, waits for them, and re-layouts: 3.58 us -> 7.45 us
    broadcast_in_dim x1 -> x0, local copies, waits for them, and re-layouts: 2.43 us -> none  [shards(): whole = jnp.zeros((zs, 2 * rows, chunks[0][1]), jnp.float32)]
  transfers between devices with their start and end apart: 22 -> 21, of which waited for: 18 -> 16; matrix products, arithmetic and copies ran while one was open for 8% -> 1% of each run, Pallas kernels for 0% -> 3%
where the time goes in v5:
time: 221 us; the launch traced here: 219 us
  waiting for transfers between devices  110 us (50%)
  starting transfers between devices  61.7 us (28%)
  Pallas kernels  32.5 us (15%)
  local copies, waits for them, and re-layouts  10.9 us (5%)
  other arithmetic  2.69 us (1%)
    ppermute x21, waiting for transfers between devices, swap(): return lax.ppermute(x, axis, [(i, i ^ bits) for i in range(size)])  110 us
    ppermute x21, starting transfers between devices, swap(): return lax.ppermute(x, axis, [(i, i ^ bits) for i in range(size)])  61.7 us
    pallas_call x1, Pallas kernels, iterations(): pl.pallas_call(functools.partial(iterations_kernel, iters), out_shape=jax...  19.2 us
    pallas_call x2, Pallas kernels, gram_part(): pl.pallas_call(functools.partial(kernel, starts, width), out_shape=[*sums...  9.43 us
    unnamed x20, local copies, waits for them, and re-layouts  7.45 us
  transfers between devices with their start and end apart: 21, of which 16 were waited for; matrix products, arithmetic and copies ran while one was open for 1% of the time, Pallas kernels for 3%

profile of v5, /device:TPU:1, one launch (start us, length us, event | category | flops | bytes accessed | tf_op | source)
XLA Modules:
  0.0 219.0 jit_solution(2251546957040641787)
XLA Ops:
  0.7 1.4 constant_dynamic-slice_fusion.7
  2.2 2.1 collective-permute-done
  4.5 1.9 constant_dynamic-slice_fusion.5
  6.9 4.7 %collective-permute-start.4 = (f32[168,2048]{1,0:T(8,128)S(1)}, f32[168,2048]{1,0:T(8,128)S(1)}, u32[]{:S(2)}, u32[]{:S(2)}) collective-permute-start(f32[168,2048]{1,0:T(8,128)S(1)} %maximum_select_fusion), channel_id=1, source_target_pairs={{0,24},{4,28},{8,16},{12,20},{16,8},{20,12},{24,0},{28,4},{1,25},{... | collective-permute-start | bytes 4128776 | tf_op jit(solution)/shard_map/ppermute | solution.py:16
  12.7 1.8 collective-permute-start.2
  14.5 2.3 %collective-permute-start.3 = (f32[168,1536]{1,0:T(8,128)S(1)}, f32[168,1536]{1,0:T(8,128)S(1)}, u32[]{:S(2)}, u32[]{:S(2)}) collective-permute-start(f32[168,1536]{1,0:T(8,128)S(1)} %get-tuple-element.26), channel_id=1, source_target_pairs={{0,16},{4,20},{8,24},{12,28},{16,0},{20,4},{24,8},{28,12},{1,17},{... | collective-permute-start | bytes 3096584 | tf_op jit(solution)/shard_map/ppermute | solution.py:16
  16.9 25.2 %collective-permute-done.4.refs_3_ = f32[168,2048]{1,0:T(8,128)S(1)} collective-permute-done((f32[168,2048]{1,0:T(8,128)S(1)}, f32[168,2048]{1,0:T(8,128)S(1)}, u32[]{:S(2)}, u32[]{:S(2)}) %collective-permute-start.4) | collective-permute-done | bytes 1376288 | tf_op jit(solution)/shard_map/ppermute | solution.py:16
  42.1 29.6 %collective-permute-start.5 = (f32[168,512]{1,0:T(8,128)S(1)}, f32[168,512]{1,0:T(8,128)S(1)}, u32[]{:S(2)}, u32[]{:S(2)}) collective-permute-start(f32[168,512]{1,0:T(8,128)S(1)} %get-tuple-element.31), channel_id=1, source_target_pairs={{0,16},{4,20},{8,24},{12,28},{16,0},{20,4},{24,8},{28,12},{1,17},{... | collective-permute-start | bytes 1032200 | tf_op jit(solution)/shard_map/ppermute | solution.py:16
  71.7 50.3 %collective-permute-done.3.refs_2_ = f32[168,1536]{1,0:T(8,128)S(1)} collective-permute-done((f32[168,1536]{1,0:T(8,128)S(1)}, f32[168,1536]{1,0:T(8,128)S(1)}, u32[]{:S(2)}, u32[]{:S(2)}) %collective-permute-start.3) | collective-permute-done | bytes 1032224 | tf_op jit(solution)/shard_map/ppermute | solution.py:16
  122.0 6.1 %gram_early.1 = (f32[2112,128]{1,0:T(8,128)S(1)}, bf16[672,1536]{1,0:T(8,128)(2,1)S(1)}, bf16[672,1536]{1,0:T(8,128)(2,1)S(1)}) custom-call(s32[2]{0:T(128)S(1)} %pad_add_fusion.place_ref, f32[168,2048]{1,0:T(8,128)S(1)} %get-tuple-element.24.refs_0_, f32[168,2048]{1,0:T(8,128)S(1)} %collective-permute-done.2.refs_1_, ...), custom_call_target="tpu_custom_call" | custom-call | flops 4161798144 | bytes 8257536 | tf_op jit(solution)/shard_map/gram_early/pallas_call | solution.py:151
  128.1 1.4 copy-done
  129.4 3.4 %gram_late.1 = (f32[1056,128]{1,0:T(8,128)S(1)}, f32[1056,128]{1,0:T(8,128)}, bf16[672,512]{1,0:T(8,128)(2,1)S(1)}, bf16[672,512]{1,0:T(8,128)(2,1)S(1)}) custom-call(s32[2]{0:T(128)S(1)} %pad_add_fusion.place_ref, f32[2112,128]{1,0:T(8,128)S(1)} %get-tuple-element.30.base_ref, f32[168,2048]{1,0:T(8,128)S(1)} %get-tuple-element.24.refs_0_, ...), custom_call_target="tpu_custom_call" | custom-call | flops 1387266048 | bytes 2752512 | tf_op jit(solution)/shard_map/gram_late/pallas_call | solution.py:151
  134.5 1.5 collective-permute-start.6
  136.0 1.8 collective-permute-done.6
  139.8 1.3 collective-permute-start.7
  141.0 1.2 collective-permute-start.8
  142.5 2.1 collective-permute-done.7
  145.5 2.9 %collective-permute-done.9 = f32[264,128]{1,0:T(8,128)S(1)} collective-permute-done((f32[264,128]{1,0:T(8,128)S(1)}, f32[264,128]{1,0:T(8,128)S(1)}, u32[]{:S(2)}, u32[]{:S(2)}) %collective-permute-start.9) | collective-permute-done | bytes 135200 | tf_op jit(solution)/shard_map/ppermute | solution.py:16
  148.5 2.4 %collective-permute-start.11 = (f32[264,128]{1,0:T(8,128)S(1)}, f32[264,128]{1,0:T(8,128)S(1)}, u32[]{:S(2)}, u32[]{:S(2)}) collective-permute-start(f32[264,128]{1,0:T(8,128)S(1)} %add_add_fusion.1), channel_id=1, source_target_pairs={{0,16},{4,20},{8,24},{12,28},{16,0},{20,4},{24,8},{28,12},{1,17},{... | collective-permute-start | bytes 405512 | tf_op jit(solution)/shard_map/ppermute | solution.py:16
  152.0 2.3 %collective-permute-done.10 = f32[264,128]{1,0:T(8,128)S(1)} collective-permute-done((f32[264,128]{1,0:T(8,128)S(1)}, f32[264,128]{1,0:T(8,128)S(1)}, u32[]{:S(2)}, u32[]{:S(2)}) %collective-permute-start.10) | collective-permute-done | bytes 135200 | tf_op jit(solution)/shard_map/ppermute | solution.py:16
  154.4 4.1 %collective-permute-done.12 = f32[264,128]{1,0:T(8,128)S(1)} collective-permute-done((f32[264,128]{1,0:T(8,128)S(1)}, f32[264,128]{1,0:T(8,128)S(1)}, u32[]{:S(2)}, u32[]{:S(2)}) %collective-permute-start.12) | collective-permute-done | bytes 135200 | tf_op jit(solution)/shard_map/ppermute | solution.py:16
  158.6 2.1 collective-permute-start.13
  160.7 1.3 collective-permute-start.15
  163.1 3.2 %collective-permute-done.14 = f32[264,128]{1,0:T(8,128)S(1)} collective-permute-done((f32[264,128]{1,0:T(8,128)S(1)}, f32[264,128]{1,0:T(8,128)S(1)}, u32[]{:S(2)}, u32[]{:S(2)}) %collective-permute-start.14) | collective-permute-done | bytes 135200 | tf_op jit(solution)/shard_map/ppermute | solution.py:16
  166.3 4.7 %collective-permute-start.16 = (f32[1056,128]{1,0:T(8,128)S(1)}, f32[1056,128]{1,0:T(8,128)}, u32[]{:S(2)}, u32[]{:S(2)}) collective-permute-start(f32[1056,128]{1,0:T(8,128)S(1)} %bitcast.13), channel_id=1, source_target_pairs={{0,4},{4,0},{8,12},{12,8},{16,20},{20,16},{24,28},{28,24},{1,5},{5... | collective-permute-start | bytes 1622024 | tf_op jit(solution)/shard_map/ppermute | solution.py:16
  172.8 19.2 %iterations.1.basis_ref = f32[672,96]{1,0:T(8,128)S(1)} custom-call(s32[2]{0:T(128)S(1)} %pad_add_fusion.place_ref, f32[1056,128]{1,0:T(8,128)S(1)} %bitcast.14, f32[1056,128]{1,0:T(8,128)} %collective-permute-done.16.other_ref, f32[672,96]{1,0:T(8,128)S(1)} %copy.4.start_ref), custom_call_target="tpu_custom_call" | custom-call | tf_op jit(solution)/shard_map/iterations/pallas_call | solution.py:252
  192.0 1.6 copy-done.1
  193.5 2.1 core_parts.1
  195.7 2.2 %collective-permute-start.17 = (f32[24,2048]{1,0:T(8,128)S(1)}, f32[24,2048]{1,0:T(8,128)S(1)}, u32[]{:S(2)}, u32[]{:S(2)}) collective-permute-start(f32[24,2048]{1,0:T(8,128)S(1)} %get-tuple-element.39), channel_id=1, source_target_pairs={{0,8},{4,12},{8,0},{12,4},{16,24},{20,28},{24,16},{28,20},{1,9},{5... | collective-permute-start | bytes 589832 | tf_op jit(solution)/shard_map/ppermute | solution.py:16
  200.0 6.4 %collective-permute-done.17.refs_1_ = f32[24,2048]{1,0:T(8,128)S(1)} collective-permute-done((f32[24,2048]{1,0:T(8,128)S(1)}, f32[24,2048]{1,0:T(8,128)S(1)}, u32[]{:S(2)}, u32[]{:S(2)}) %collective-permute-start.17) | collective-permute-done | bytes 196640 | tf_op jit(solution)/shard_map/ppermute | solution.py:16
  206.5 6.7 %collective-permute-done.19.refs_3_ = f32[24,2048]{1,0:T(8,128)S(1)} collective-permute-done((f32[24,2048]{1,0:T(8,128)S(1)}, f32[24,2048]{1,0:T(8,128)S(1)}, u32[]{:S(2)}, u32[]{:S(2)}) %collective-permute-start.19) | collective-permute-done | bytes 196640 | tf_op jit(solution)/shard_map/ppermute | solution.py:16
  213.8 2.6 %collective-permute-start.20 = (f32[12,8192]{1,0:T(8,128)S(1)}, f32[12,8192]{1,0:T(8,128)S(1)}, u32[]{:S(2)}, u32[]{:S(2)}) collective-permute-start(f32[12,8192]{1,0:T(8,128)S(1)} %get-tuple-element.43), channel_id=1, source_target_pairs={{0,4},{4,0},{8,12},{12,8},{16,20},{20,16},{24,28},{28,24},{1,5},{5... | collective-permute-start | bytes 1179656 | tf_op jit(solution)/shard_map/ppermute | solution.py:16
  (51 shorter events, 16.2 us)
Async XLA Ops:
  2.1 2.3 %collective-permute-start = (f32[84,2048]{1,0:T(8,128)S(1)}, f32[84,2048]{1,0:T(8,128)S(1)}, u32[]{:S(2)}, u32[]{:S(2)}) collective-permute-start(f32[84,2048]{1,0:T(8,128)S(1)} %get-tuple-element.52), channel_id=1, source_target_pairs={{0,4},{4,0},{8,12},{12,8},{16,20},{20,16},{24,28},{28,24},{1,5},{5... | collective-permute-start | bytes 2064392 | tf_op jit(solution)/shard_map/ppermute | solution.py:16
  4.4 7.3 %slice-start = ((s8[5767168]{0:T(1024)(128)(4,1)}), s8[4194304]{0:T(1024)(128)(4,1)S(1)}, s32[]{:S(2)}) async-start(s8[5767168]{0:T(1024)(128)(4,1)} %bitcast.11), calls=%async_computation | async-start | bytes 8388608
  4.5 7.1 %slice-start.1 = ((s8[5767168]{0:T(1024)(128)(4,1)}), s8[1572864]{0:T(1024)(128)(4,1)S(1)}, s32[]{:S(2)}) async-start(s8[5767168]{0:T(1024)(128)(4,1)} %bitcast.11), calls=%async_computation.1 | async-start | bytes 3145728
  6.7 5.0 %collective-permute-start.1 = (f32[84,6144]{1,0:T(8,128)S(1)}, f32[84,6144]{1,0:T(8,128)S(1)}, u32[]{:S(2)}, u32[]{:S(2)}) collective-permute-start(f32[84,6144]{1,0:T(8,128)S(1)} %pad_maximum_fusion), channel_id=1, source_target_pairs={{0,4},{4,0},{8,12},{12,8},{16,20},{20,16},{24,28},{28,24},{1,5},{5... | collective-permute-start | bytes 6193160 | tf_op jit(solution)/shard_map/ppermute | solution.py:16
  6.9 35.2 %collective-permute-start.4 = (f32[168,2048]{1,0:T(8,128)S(1)}, f32[168,2048]{1,0:T(8,128)S(1)}, u32[]{:S(2)}, u32[]{:S(2)}) collective-permute-start(f32[168,2048]{1,0:T(8,128)S(1)} %maximum_select_fusion), channel_id=1, source_target_pairs={{0,24},{4,28},{8,16},{12,20},{16,8},{20,12},{24,0},{28,4},{1,25},{... | collective-permute-start | bytes 4128776 | tf_op jit(solution)/shard_map/ppermute | solution.py:16
  12.7 109.3 %collective-permute-start.2 = (f32[168,2048]{1,0:T(8,128)S(1)}, f32[168,2048]{1,0:T(8,128)S(1)}, u32[]{:S(2)}, u32[]{:S(2)}) collective-permute-start(f32[168,2048]{1,0:T(8,128)S(1)} %get-tuple-element.25), channel_id=1, source_target_pairs={{0,8},{4,12},{8,0},{12,4},{16,24},{20,28},{24,16},{28,20},{1,9},{5... | collective-permute-start | bytes 4128776 | tf_op jit(solution)/shard_map/ppermute | solution.py:16
  14.5 107.5 %collective-permute-start.3 = (f32[168,1536]{1,0:T(8,128)S(1)}, f32[168,1536]{1,0:T(8,128)S(1)}, u32[]{:S(2)}, u32[]{:S(2)}) collective-permute-start(f32[168,1536]{1,0:T(8,128)S(1)} %get-tuple-element.26), channel_id=1, source_target_pairs={{0,16},{4,20},{8,24},{12,28},{16,0},{20,4},{24,8},{28,12},{1,17},{... | collective-permute-start | bytes 3096584 | tf_op jit(solution)/shard_map/ppermute | solution.py:16
  42.1 87.4 %collective-permute-start.5 = (f32[168,512]{1,0:T(8,128)S(1)}, f32[168,512]{1,0:T(8,128)S(1)}, u32[]{:S(2)}, u32[]{:S(2)}) collective-permute-start(f32[168,512]{1,0:T(8,128)S(1)} %get-tuple-element.31), channel_id=1, source_target_pairs={{0,16},{4,20},{8,24},{12,28},{16,0},{20,4},{24,8},{28,12},{1,17},{... | collective-permute-start | bytes 1032200 | tf_op jit(solution)/shard_map/ppermute | solution.py:16
  128.1 1.4 copy-start
  132.8 0.8 copy-start.2
  133.7 0.9 copy-start.4
  134.5 3.3 %collective-permute-start.6 = (f32[1056,128]{1,0:T(8,128)}, f32[1056,128]{1,0:T(8,128)S(1)}, u32[]{:S(2)}, u32[]{:S(2)}) collective-permute-start(f32[1056,128]{1,0:T(8,128)} %get-tuple-element.33), channel_id=1, source_target_pairs={{0,4},{4,0},{8,12},{12,8},{16,20},{20,16},{24,28},{28,24},{1,5},{5... | collective-permute-start | bytes 1622024 | tf_op jit(solution)/shard_map/ppermute | solution.py:16
  137.8 0.8 copy-start.6
  139.8 4.9 %collective-permute-start.7 = (f32[264,128]{1,0:T(8,128)S(1)}, f32[264,128]{1,0:T(8,128)S(1)}, u32[]{:S(2)}, u32[]{:S(2)}) collective-permute-start(f32[264,128]{1,0:T(8,128)S(1)} %get-tuple-element.53), channel_id=1, source_target_pairs={{0,1},{1,0},{2,3},{3,2},{4,5},{5,4},{6,7},{7,6},{8,9},{9,8},{10,11... | collective-permute-start | bytes 405512 | tf_op jit(solution)/shard_map/ppermute | solution.py:16
  141.0 4.5 %collective-permute-start.8 = (f32[264,128]{1,0:T(8,128)S(1)}, f32[264,128]{1,0:T(8,128)S(1)}, u32[]{:S(2)}, u32[]{:S(2)}) collective-permute-start(f32[264,128]{1,0:T(8,128)S(1)} %get-tuple-element.55), channel_id=1, source_target_pairs={{0,2},{1,3},{2,0},{3,1},{4,6},{5,7},{6,4},{7,5},{8,10},{9,11},{10,... | collective-permute-start | bytes 405512 | tf_op jit(solution)/shard_map/ppermute | solution.py:16
  142.3 6.1 %collective-permute-start.9 = (f32[264,128]{1,0:T(8,128)S(1)}, f32[264,128]{1,0:T(8,128)S(1)}, u32[]{:S(2)}, u32[]{:S(2)}) collective-permute-start(f32[264,128]{1,0:T(8,128)S(1)} %get-tuple-element.54), channel_id=1, source_target_pairs={{0,3},{1,2},{2,1},{3,0},{4,7},{5,6},{6,5},{7,4},{8,11},{9,10},{10,... | collective-permute-start | bytes 405512 | tf_op jit(solution)/shard_map/ppermute | solution.py:16
  148.4 5.9 %collective-permute-start.10 = (f32[264,128]{1,0:T(8,128)S(1)}, f32[264,128]{1,0:T(8,128)S(1)}, u32[]{:S(2)}, u32[]{:S(2)}) collective-permute-start(f32[264,128]{1,0:T(8,128)S(1)} %add_add_fusion.1), channel_id=1, source_target_pairs={{0,8},{4,12},{8,0},{12,4},{16,24},{20,28},{24,16},{28,20},{1,9},{5... | collective-permute-start | bytes 405512 | tf_op jit(solution)/shard_map/ppermute | solution.py:16
  148.5 5.9 %collective-permute-start.11 = (f32[264,128]{1,0:T(8,128)S(1)}, f32[264,128]{1,0:T(8,128)S(1)}, u32[]{:S(2)}, u32[]{:S(2)}) collective-permute-start(f32[264,128]{1,0:T(8,128)S(1)} %add_add_fusion.1), channel_id=1, source_target_pairs={{0,16},{4,20},{8,24},{12,28},{16,0},{20,4},{24,8},{28,12},{1,17},{... | collective-permute-start | bytes 405512 | tf_op jit(solution)/shard_map/ppermute | solution.py:16
  150.9 7.5 %collective-permute-start.12 = (f32[264,128]{1,0:T(8,128)S(1)}, f32[264,128]{1,0:T(8,128)S(1)}, u32[]{:S(2)}, u32[]{:S(2)}) collective-permute-start(f32[264,128]{1,0:T(8,128)S(1)} %add_add_fusion.1), channel_id=1, source_target_pairs={{0,24},{4,28},{8,16},{12,20},{16,8},{20,12},{24,0},{28,4},{1,25},{... | collective-permute-start | bytes 405512 | tf_op jit(solution)/shard_map/ppermute | solution.py:16
  158.6 4.5 %collective-permute-start.13 = (f32[264,128]{1,0:T(8,128)S(1)}, f32[264,128]{1,0:T(8,128)S(1)}, u32[]{:S(2)}, u32[]{:S(2)}) collective-permute-start(f32[264,128]{1,0:T(8,128)S(1)} %get-tuple-element.47), channel_id=1, source_target_pairs={{0,1},{1,0},{2,3},{3,2},{4,5},{5,4},{6,7},{7,6},{8,9},{9,8},{10,11... | collective-permute-start | bytes 405512 | tf_op jit(solution)/shard_map/ppermute | solution.py:16
  160.7 5.6 %collective-permute-start.14 = (f32[264,128]{1,0:T(8,128)S(1)}, f32[264,128]{1,0:T(8,128)S(1)}, u32[]{:S(2)}, u32[]{:S(2)}) collective-permute-start(f32[264,128]{1,0:T(8,128)S(1)} %get-tuple-element.47), channel_id=1, source_target_pairs={{0,2},{1,3},{2,0},{3,1},{4,6},{5,7},{6,4},{7,5},{8,10},{9,11},{10,... | collective-permute-start | bytes 405512 | tf_op jit(solution)/shard_map/ppermute | solution.py:16
  160.7 5.6 %collective-permute-start.15 = (f32[264,128]{1,0:T(8,128)S(1)}, f32[264,128]{1,0:T(8,128)S(1)}, u32[]{:S(2)}, u32[]{:S(2)}) collective-permute-start(f32[264,128]{1,0:T(8,128)S(1)} %get-tuple-element.47), channel_id=1, source_target_pairs={{0,3},{1,2},{2,1},{3,0},{4,7},{5,6},{6,5},{7,4},{8,11},{9,10},{10,... | collective-permute-start | bytes 405512 | tf_op jit(solution)/shard_map/ppermute | solution.py:16
  166.3 6.4 %collective-permute-start.16 = (f32[1056,128]{1,0:T(8,128)S(1)}, f32[1056,128]{1,0:T(8,128)}, u32[]{:S(2)}, u32[]{:S(2)}) collective-permute-start(f32[1056,128]{1,0:T(8,128)S(1)} %bitcast.13), channel_id=1, source_target_pairs={{0,4},{4,0},{8,12},{12,8},{16,20},{20,16},{24,28},{28,24},{1,5},{5... | collective-permute-start | bytes 1622024 | tf_op jit(solution)/shard_map/ppermute | solution.py:16
  172.2 19.7 %copy-start.3 = (bf16[672,512]{1,0:T(8,128)(2,1)S(1)}, bf16[672,512]{1,0:T(8,128)(2,1)}, u32[]{:S(2)}) copy-start(bf16[672,512]{1,0:T(8,128)(2,1)} %copy-done.2) | copy-start | bytes 2064388
  172.2 19.7 %copy-start.5 = (bf16[672,512]{1,0:T(8,128)(2,1)S(1)}, bf16[672,512]{1,0:T(8,128)(2,1)}, u32[]{:S(2)}) copy-start(bf16[672,512]{1,0:T(8,128)(2,1)} %copy-done.4) | copy-start | bytes 2064388
  192.0 1.6 copy-start.1
  195.7 10.8 %collective-permute-start.17 = (f32[24,2048]{1,0:T(8,128)S(1)}, f32[24,2048]{1,0:T(8,128)S(1)}, u32[]{:S(2)}, u32[]{:S(2)}) collective-permute-start(f32[24,2048]{1,0:T(8,128)S(1)} %get-tuple-element.39), channel_id=1, source_target_pairs={{0,8},{4,12},{8,0},{12,4},{16,24},{20,28},{24,16},{28,20},{1,9},{5... | collective-permute-start | bytes 589832 | tf_op jit(solution)/shard_map/ppermute | solution.py:16
  197.9 8.6 %collective-permute-start.18 = (f32[24,2048]{1,0:T(8,128)S(1)}, f32[24,2048]{1,0:T(8,128)S(1)}, u32[]{:S(2)}, u32[]{:S(2)}) collective-permute-start(f32[24,2048]{1,0:T(8,128)S(1)} %get-tuple-element.40), channel_id=1, source_target_pairs={{0,16},{4,20},{8,24},{12,28},{16,0},{20,4},{24,8},{28,12},{1,17},{... | collective-permute-start | bytes 589832 | tf_op jit(solution)/shard_map/ppermute | solution.py:16
  198.9 14.2 %collective-permute-start.19 = (f32[24,2048]{1,0:T(8,128)S(1)}, f32[24,2048]{1,0:T(8,128)S(1)}, u32[]{:S(2)}, u32[]{:S(2)}) collective-permute-start(f32[24,2048]{1,0:T(8,128)S(1)} %get-tuple-element.41), channel_id=1, source_target_pairs={{0,24},{4,28},{8,16},{12,20},{16,8},{20,12},{24,0},{28,4},{1,25},{... | collective-permute-start | bytes 589832 | tf_op jit(solution)/shard_map/ppermute | solution.py:16
  213.8 4.1 %collective-permute-start.20 = (f32[12,8192]{1,0:T(8,128)S(1)}, f32[12,8192]{1,0:T(8,128)S(1)}, u32[]{:S(2)}, u32[]{:S(2)}) collective-permute-start(f32[12,8192]{1,0:T(8,128)S(1)} %get-tuple-element.43), channel_id=1, source_target_pairs={{0,4},{4,0},{8,12},{12,8},{16,20},{20,16},{24,28},{28,24},{1,5},{5... | collective-permute-start | bytes 1179656 | tf_op jit(solution)/shard_map/ppermute | solution.py:16

commit v6 on v5

--- a/solution.py
+++ b/solution.py
@@ -20,8 +20,7 @@
     return jnp.where(core == 0, jnp.concatenate([mine, other], axis), jnp.concatenate([other, mine], axis))
 
 
-def prepare_kernel(pieces, place_ref, slab_ref, got_ref, *refs):
-    distances = sorted({bits for bits, _, _ in pieces}, reverse=True)
+def prepare_kernel(cuts, pieces, place_ref, slab_ref, got_ref, *refs):
     outs, (own, sems) = refs[:-2], refs[-2:]
     zs, rows, part = own.shape
     z, core = place_ref[0], place_ref[1]
@@ -30,15 +29,16 @@
         at = pl.multiple_of(core * (zs * part) + (z ^ bits) * part, 128)
         return pltpu.make_async_copy(slab_ref.at[:, pl.ds(at, part)], own.at[bits], sems.at[bits])
 
-    for bits in distances:
+    for bits, _, _ in cuts:
         fetch(bits).start()
-    for order, bits in enumerate(distances):
+    begin = 0
+    for bits, from_, depth in cuts:
         fetch(bits).wait()
         for out, (which, start, width) in zip(outs, pieces):
             if which != bits:
                 continue
             columns = slice(start, start + width)
-            other = slice(order * part + start, order * part + start + width)
+            other = slice(begin + start - from_, begin + start - from_ + width)
 
             @pl.when(core == 0)
             def _():
@@ -50,17 +50,19 @@
                 out[:rows, :] = got_ref[:, other]
                 out[rows:, :] = own[bits, :, columns]
 
-
-def prepare(place, slab, got, zs, pieces):
-    rows, part = got.shape[0], got.shape[1] // (zs - 1)
+        begin += depth
+
+
+def prepare(place, slab, got, part, zs, cuts, pieces):
+    rows = got.shape[0]
     vmem = pl.BlockSpec(memory_space=pltpu.VMEM)
     return pl.pallas_call(
-        functools.partial(prepare_kernel, pieces),
+        functools.partial(prepare_kernel, cuts, pieces),
         out_shape=[jax.ShapeDtypeStruct((2 * rows, width), jnp.float32) for _, _, width in pieces],
         in_specs=[pl.BlockSpec(memory_space=pltpu.SMEM), pl.BlockSpec(memory_space=pl.ANY), vmem],
         out_specs=[vmem] * len(pieces),
         scratch_shapes=[pltpu.VMEM((zs, rows, part), jnp.float32), pltpu.SemaphoreType.DMA((zs,))],
-        compiler_params=pltpu.CompilerParams(vmem_limit_bytes=32 * 2**20),
+        compiler_params=pltpu.CompilerParams(vmem_limit_bytes=24 * 2**20),
         cost_estimate=pl.CostEstimate(flops=0, bytes_accessed=100_000_000, transcendentals=0),
         name="prepare",
     )(place, slab, got)
@@ -110,16 +112,17 @@
         packed[rows, :] = value if base_ref is None else value + base_ref[rows, :]
 
     for start in range(0, edge, 256):
+        last = start + 256 >= edge
         stop = min(start + 256, edge)
-        upper = product(0, stop, start, stop)
+        upper = product(0, n if last else stop, start, n if last else stop)
         for j in range(start // 128, stop // 128):
             at, rows, _ = places[j]
             put(at, upper[:rows, 128 * j - start : 128 * j - start + 128])
     if n > edge:
-        strip = product(edge, n, 0, n)
+        strip = upper[:, edge - start :]
         for j, (_, _, at) in enumerate(places):
-            put(at, strip[:, 128 * j : 128 * j + 128])
-        put(corner, jnp.pad(strip[:, edge:], ((0, 0), (0, 128 - (n - edge)))))
+            put(at, strip[128 * j : 128 * j + 128].T)
+        put(corner, jnp.pad(strip[edge:], ((0, 0), (0, 128 - (n - edge)))))
 
 
 def early_kernel(starts, width, place_ref, *refs):
@@ -154,7 +157,7 @@
         in_specs=[pl.BlockSpec(memory_space=pltpu.SMEM)] + [vmem] * (len(first) + len(blocks)),
         out_specs=[vmem] * (len(sums) + 2),
         scratch_shapes=scratch,
-        compiler_params=pltpu.CompilerParams(vmem_limit_bytes=40 * 2**20),
+        compiler_params=pltpu.CompilerParams(vmem_limit_bytes=24 * 2**20),
         cost_estimate=pl.CostEstimate(flops=6 * n * n * width, bytes_accessed=8 * n * width, transcendentals=0),
         name="gram_early" if base is None else "gram_late",
     )(place, *first, *blocks)
@@ -215,7 +218,7 @@
     return jnp.concatenate(done, 0)
 
 
-def iterations_kernel(iters, place_ref, mine_ref, other_ref, start_ref, factor_ref, packed, gram):
+def iterations_kernel(iters, place_ref, mine_ref, other_ref, start_ref, factor_ref, packed, gram, high, low):
     def times(a, b, dims):
         return lax.dot_general(a, b, (dims, ((), ())), precision=HIGHEST, preferred_element_type=jnp.float32)
 
@@ -237,12 +240,22 @@
     if n > edge:
         gram[edge:, edge:] = packed[corner:size, : n - edge]
 
-    image = times(gram[...], start_ref[...], ((1,), (0,)))
+    high[...], low[...] = split(gram[...])
+
+    def apply_gram(x):
+        x_high, x_low = split(x)
+
+        def part(a, b):
+            return lax.dot_general(a[...], b, (((1,), (0,)), ((), ())), preferred_element_type=jnp.float32)
+
+        return part(high, x_low) + part(low, x_high) + part(high, x_high)
+
+    image = apply_gram(start_ref[...])
     for step in range(iters):
         small = times(image, image, ((0,), (0,)))
         inverse = lower_inverse(jnp.pad(small, ((0, 0), (0, 128 - small.shape[1]))))[:, : small.shape[1]]
         if step < iters - 1:
-            image = times(times(gram[...], image, ((1,), (0,))), inverse, ((1,), (1,)))
+            image = times(apply_gram(image), inverse, ((1,), (1,)))
         else:
             factor_ref[...] = times(image, inverse, ((1,), (1,)))
 
@@ -254,8 +267,8 @@
         out_shape=jax.ShapeDtypeStruct(start.shape, jnp.float32),
         in_specs=[pl.BlockSpec(memory_space=pltpu.SMEM)] + [pl.BlockSpec(memory_space=pltpu.VMEM)] * 3,
         out_specs=pl.BlockSpec(memory_space=pltpu.VMEM),
-        scratch_shapes=[pltpu.VMEM((layout(n)[2], 128), jnp.float32), pltpu.VMEM((n, n), jnp.float32)],
-        compiler_params=pltpu.CompilerParams(vmem_limit_bytes=32 * 2**20),
+        scratch_shapes=[pltpu.VMEM((layout(n)[2], 128), jnp.float32), pltpu.VMEM((n, n), jnp.float32)] + [pltpu.VMEM((n, n), jnp.bfloat16)] * 2,
+        compiler_params=pltpu.CompilerParams(vmem_limit_bytes=16 * 2**20),
         name="iterations",
     )(place, mine, other, start)
 
@@ -314,7 +327,7 @@
         in_specs=[pl.BlockSpec(memory_space=pltpu.SMEM)] + [vmem] * 5,
         out_specs=[vmem] * zs,
         scratch_shapes=[pltpu.VMEM((rank, part), jnp.float32)],
-        compiler_params=pltpu.CompilerParams(vmem_limit_bytes=32 * 2**20),
+        compiler_params=pltpu.CompilerParams(vmem_limit_bytes=16 * 2**20),
         name="core_parts",
     )(place, basis, *parts)
 
@@ -339,7 +352,7 @@
         out_shape=(half, half),
         in_specs=[pl.BlockSpec(memory_space=pltpu.SMEM)] + [vmem] * len(blocks),
         out_specs=[vmem] * 2,
-        compiler_params=pltpu.CompilerParams(vmem_limit_bytes=32 * 2**20),
+        compiler_params=pltpu.CompilerParams(vmem_limit_bytes=16 * 2**20),
         name="assemble",
     )(place, *blocks)
 
@@ -352,26 +365,26 @@
     place = jnp.stack([z, core])
     half = cols // 2
     part = half // zs
-    early = part * 3 // 4
-
-    def cut(slab, whose, bits):
-        return lax.dynamic_slice(slab, (0, whose * half + (z ^ bits) * part), (rows, part))
+    early = part * 7 // 8
+
+    def cut(slab, whose, bits, start, width):
+        return lax.dynamic_slice(slab, (0, whose * half + (z ^ bits) * part + start), (rows, width))
 
     far = zs - 1
-    got = swap(cut(slab, 1 - core, far), "fibre", fibre, 1)
-    block = in_order(core, cut(slab, core, far), got, 0)
+    got = swap(cut(slab, 1 - core, far, 0, part), "fibre", fibre, 1)
+    block = in_order(core, cut(slab, core, far, 0, part), got, 0)
     slab, block = lax.optimization_barrier((slab, block))
     arrived = {far: swap(block, "fibre", fibre, 2 * far)}
-    others = list(range(far - 1, -1, -1))
-    theirs = jnp.concatenate([cut(slab, 1 - core, bits) for bits in others], 1)
-    got = swap(theirs, "fibre", fibre, 1)
+    cuts = [(bits, 0, part) for bits in range(far - 1, -1, -1)]
+    got = swap(jnp.concatenate([cut(slab, 1 - core, *c) for c in cuts], 1), "fibre", fibre, 1)
     pieces = []
-    for bits in others:
-        pieces += [(bits, 0, early), (bits, early, part - early)] if bits > 1 else [(bits, 0, part)]
+    for bits, start, width in cuts:
+        split_here = bits > 1
+        pieces += [(bits, 0, early), (bits, early, part - early)] if split_here else [(bits, start, width)]
     late = {}
-    for (bits, start, _), block in zip(pieces, prepare(place, slab, got, zs, pieces)):
+    for (bits, start, _), block in zip(pieces, prepare(place, slab, got, part, zs, cuts, pieces)):
         if start:
-            block, arrived[far] = lax.optimization_barrier((block, arrived[far]))
+            block, arrived[bits] = lax.optimization_barrier((block, arrived[bits]))
         into = late if start else arrived
         into[bits] = swap(block, "fibre", fibre, 2 * bits) if bits else block
     first = [arrived[bits] for bits in range(zs)]

time: 221 us -> 226 us (1.023)
  waiting for transfers between devices: 110 us -> 143 us
  starting transfers between devices: 61.7 us -> 32.2 us
  local copies, waits for them, and re-layouts: 10.9 us -> 15.2 us
  Pallas kernels: 32.5 us -> 28.9 us
    ppermute x21, waiting for transfers between devices: 110 us -> 143 us  [swap(): return lax.ppermute(x, axis, [(i, i ^ bits) for i in range(size)])]
    ppermute x21, starting transfers between devices: 61.7 us -> 32.2 us  [swap(): return lax.ppermute(x, axis, [(i, i ^ bits) for i in range(size)])]
    unnamed x20 -> x24, local copies, waits for them, and re-layouts: 7.45 us -> 11.1 us
  transfers between devices with their start and end apart: 21 -> 21, of which waited for: 16 -> 14; matrix products, arithmetic and copies ran while one was open for 1% -> 1% of each run, Pallas kernels for 3% -> 3%
where the time goes in v6:
time: 226 us; the launch traced here: 225 us
  waiting for transfers between devices  143 us (63%)
  starting transfers between devices  32.2 us (14%)
  Pallas kernels  28.9 us (13%)
  local copies, waits for them, and re-layouts  15.2 us (7%)
  other arithmetic  4.51 us (2%)
    ppermute x21, waiting for transfers between devices, swap(): return lax.ppermute(x, axis, [(i, i ^ bits) for i in range(size)])  143 us
    ppermute x21, starting transfers between devices, swap(): return lax.ppermute(x, axis, [(i, i ^ bits) for i in range(size)])  32.2 us
    pallas_call x1, Pallas kernels, iterations(): pl.pallas_call(functools.partial(iterations_kernel, iters), out_shape=jax...  17.5 us
    unnamed x24, local copies, waits for them, and re-layouts  11.1 us
    pallas_call x2, Pallas kernels, gram_part(): pl.pallas_call(functools.partial(kernel, starts, width), out_shape=[*sums...  7.56 us
  transfers between devices with their start and end apart: 21, of which 14 were waited for; matrix products, arithmetic and copies ran while one was open for 1% of the time, Pallas kernels for 3%

profile of v6, /device:TPU:1, one launch (start us, length us, event | category | flops | bytes accessed | tf_op | source)
XLA Modules:
  0.0 224.6 jit_solution(4362570162782293965)
XLA Ops:
  0.7 1.4 constant_dynamic-slice_fusion.7
  2.2 2.1 collective-permute-done
  4.5 1.9 constant_dynamic-slice_fusion.5
  6.9 4.7 %collective-permute-start.4 = (f32[168,2048]{1,0:T(8,128)S(1)}, f32[168,2048]{1,0:T(8,128)S(1)}, u32[]{:S(2)}, u32[]{:S(2)}) collective-permute-start(f32[168,2048]{1,0:T(8,128)S(1)} %maximum_select_fusion), channel_id=1, source_target_pairs={{0,24},{4,28},{8,16},{12,20},{16,8},{20,12},{24,0},{28,4},{1,25},{... | collective-permute-start | bytes 4128776 | tf_op jit(solution)/shard_map/ppermute | solution.py:16
  12.7 1.8 collective-permute-start.2
  14.5 2.3 %collective-permute-start.3 = (f32[168,1792]{1,0:T(8,128)S(1)}, f32[168,1792]{1,0:T(8,128)S(1)}, u32[]{:S(2)}, u32[]{:S(2)}) collective-permute-start(f32[168,1792]{1,0:T(8,128)S(1)} %get-tuple-element.27), channel_id=1, source_target_pairs={{0,16},{4,20},{8,24},{12,28},{16,0},{20,4},{24,8},{28,12},{1,17},{... | collective-permute-start | bytes 3612680 | tf_op jit(solution)/shard_map/ppermute | solution.py:16
  16.8 105.2 %collective-permute-done.3.refs_2_ = f32[168,1792]{1,0:T(8,128)S(1)} collective-permute-done((f32[168,1792]{1,0:T(8,128)S(1)}, f32[168,1792]{1,0:T(8,128)S(1)}, u32[]{:S(2)}, u32[]{:S(2)}) %collective-permute-start.3) | collective-permute-done | bytes 1204256 | tf_op jit(solution)/shard_map/ppermute | solution.py:16
  122.0 5.2 %gram_early.1 = (f32[2112,128]{1,0:T(8,128)S(1)}, bf16[672,1792]{1,0:T(8,128)(2,1)S(1)}, bf16[672,1792]{1,0:T(8,128)(2,1)S(1)}) custom-call(s32[2]{0:T(128)S(1)} %pad_add_fusion.place_ref, f32[168,2048]{1,0:T(8,128)S(1)} %get-tuple-element.24.refs_0_, f32[168,2048]{1,0:T(8,128)S(1)} %collective-permute-done.2.refs_1_, ...), custom_call_target="tpu_custom_call" | custom-call | flops 4855431168 | bytes 9633792 | tf_op jit(solution)/shard_map/gram_early/pallas_call | solution.py:154
  127.2 1.5 copy-done
  128.7 4.0 %collective-permute-done.5.refs_2_ = f32[168,256]{1,0:T(8,128)S(1)} collective-permute-done((f32[168,256]{1,0:T(8,128)S(1)}, f32[168,256]{1,0:T(8,128)S(1)}, u32[]{:S(2)}, u32[]{:S(2)}) %collective-permute-start.5) | collective-permute-done | bytes 172064 | tf_op jit(solution)/shard_map/ppermute | solution.py:16
  132.7 2.4 %gram_late.1 = (f32[1056,128]{1,0:T(8,128)S(1)}, f32[1056,128]{1,0:T(8,128)}, bf16[672,256]{1,0:T(8,128)(2,1)S(1)}, bf16[672,256]{1,0:T(8,128)(2,1)S(1)}) custom-call(s32[2]{0:T(128)S(1)} %pad_add_fusion.place_ref, f32[2112,128]{1,0:T(8,128)S(1)} %get-tuple-element.30.base_ref, f32[168,2048]{1,0:T(8,128)S(1)} %get-tuple-element.24.refs_0_, ...), custom_call_target="tpu_custom_call" | custom-call | flops 693633024 | bytes 1376256 | tf_op jit(solution)/shard_map/gram_late/pallas_call | solution.py:154
  137.1 1.8 collective-permute-done.6
  141.5 1.2 collective-permute-start.7
  142.7 1.2 collective-permute-start.8
  144.1 2.4 %collective-permute-done.7 = f32[264,128]{1,0:T(8,128)S(1)} collective-permute-done((f32[264,128]{1,0:T(8,128)}, f32[264,128]{1,0:T(8,128)S(1)}, u32[]{:S(2)}, u32[]{:S(2)}) %collective-permute-start.7) | collective-permute-done | bytes 135200 | tf_op jit(solution)/shard_map/ppermute | solution.py:16
  147.1 3.3 %collective-permute-done.9 = f32[264,128]{1,0:T(8,128)} collective-permute-done((f32[264,128]{1,0:T(8,128)S(1)}, f32[264,128]{1,0:T(8,128)}, u32[]{:S(2)}, u32[]{:S(2)}) %collective-permute-start.9) | collective-permute-done | bytes 135200 | tf_op jit(solution)/shard_map/ppermute | solution.py:16
  151.5 1.3 collective-permute-start.11
  152.9 2.2 collective-permute-start.12
  155.1 2.5 %collective-permute-done.10 = f32[264,128]{1,0:T(8,128)S(1)} collective-permute-done((f32[264,128]{1,0:T(8,128)S(1)}, f32[264,128]{1,0:T(8,128)S(1)}, u32[]{:S(2)}, u32[]{:S(2)}) %collective-permute-start.10) | collective-permute-done | bytes 135200 | tf_op jit(solution)/shard_map/ppermute | solution.py:16
  157.5 3.3 %collective-permute-done.12 = f32[264,128]{1,0:T(8,128)S(1)} collective-permute-done((f32[264,128]{1,0:T(8,128)S(1)}, f32[264,128]{1,0:T(8,128)S(1)}, u32[]{:S(2)}, u32[]{:S(2)}) %collective-permute-start.12) | collective-permute-done | bytes 135200 | tf_op jit(solution)/shard_map/ppermute | solution.py:16
  163.2 1.3 collective-permute-start.15
  165.7 2.6 %collective-permute-done.14 = f32[264,128]{1,0:T(8,128)S(1)} collective-permute-done((f32[264,128]{1,0:T(8,128)S(1)}, f32[264,128]{1,0:T(8,128)S(1)}, u32[]{:S(2)}, u32[]{:S(2)}) %collective-permute-start.14) | collective-permute-done | bytes 135200 | tf_op jit(solution)/shard_map/ppermute | solution.py:16
  168.4 6.4 %collective-permute-start.16 = (f32[1056,128]{1,0:T(8,128)S(1)}, f32[1056,128]{1,0:T(8,128)}, u32[]{:S(2)}, u32[]{:S(2)}) collective-permute-start(f32[1056,128]{1,0:T(8,128)S(1)} %bitcast.13), channel_id=1, source_target_pairs={{0,4},{4,0},{8,12},{12,8},{16,20},{20,16},{24,28},{28,24},{1,5},{5... | collective-permute-start | bytes 1622024 | tf_op jit(solution)/shard_map/ppermute | solution.py:16
  174.8 1.9 copy.4.start_ref
  177.7 17.5 %iterations.1.basis_ref = f32[672,96]{1,0:T(8,128)S(1)} custom-call(s32[2]{0:T(128)S(1)} %pad_add_fusion.place_ref, f32[1056,128]{1,0:T(8,128)S(1)} %bitcast.14, f32[1056,128]{1,0:T(8,128)} %collective-permute-done.16.other_ref, f32[672,96]{1,0:T(8,128)S(1)} %copy-done.2), custom_call_target="tpu_custom_call" | custom-call | tf_op jit(solution)/shard_map/iterations/pallas_call | solution.py:265
  195.2 1.7 copy-done.1
  198.8 2.1 core_parts.1
  200.9 2.6 %collective-permute-start.17 = (f32[24,2048]{1,0:T(8,128)S(1)}, f32[24,2048]{1,0:T(8,128)S(1)}, u32[]{:S(2)}, u32[]{:S(2)}) collective-permute-start(f32[24,2048]{1,0:T(8,128)S(1)} %get-tuple-element.39), channel_id=1, source_target_pairs={{0,8},{4,12},{8,0},{12,4},{16,24},{20,28},{24,16},{28,20},{1,9},{5... | collective-permute-start | bytes 589832 | tf_op jit(solution)/shard_map/ppermute | solution.py:16
  203.5 2.2 collective-permute-start.19
  205.7 6.0 %collective-permute-done.17.refs_1_ = f32[24,2048]{1,0:T(8,128)S(1)} collective-permute-done((f32[24,2048]{1,0:T(8,128)S(1)}, f32[24,2048]{1,0:T(8,128)S(1)}, u32[]{:S(2)}, u32[]{:S(2)}) %collective-permute-start.17) | collective-permute-done | bytes 196640 | tf_op jit(solution)/shard_map/ppermute | solution.py:16
  211.7 7.2 %collective-permute-done.18.refs_2_ = f32[24,2048]{1,0:T(8,128)S(1)} collective-permute-done((f32[24,2048]{1,0:T(8,128)S(1)}, f32[24,2048]{1,0:T(8,128)S(1)}, u32[]{:S(2)}, u32[]{:S(2)}) %collective-permute-start.18) | collective-permute-done | bytes 196640 | tf_op jit(solution)/shard_map/ppermute | solution.py:16
  219.6 2.3 %collective-permute-start.20 = (f32[12,8192]{1,0:T(8,128)S(1)}, f32[12,8192]{1,0:T(8,128)S(1)}, u32[]{:S(2)}, u32[]{:S(2)}) collective-permute-start(f32[12,8192]{1,0:T(8,128)S(1)} %get-tuple-element.43), channel_id=1, source_target_pairs={{0,4},{4,0},{8,12},{12,8},{16,20},{20,16},{24,28},{28,24},{1,5},{5... | collective-permute-start | bytes 1179656 | tf_op jit(solution)/shard_map/ppermute | solution.py:16
  (55 shorter events, 18.2 us)
Async XLA Ops:
  2.1 2.3 %collective-permute-start = (f32[84,2048]{1,0:T(8,128)S(1)}, f32[84,2048]{1,0:T(8,128)S(1)}, u32[]{:S(2)}, u32[]{:S(2)}) collective-permute-start(f32[84,2048]{1,0:T(8,128)S(1)} %get-tuple-element.52), channel_id=1, source_target_pairs={{0,4},{4,0},{8,12},{12,8},{16,20},{20,16},{24,28},{28,24},{1,5},{5... | collective-permute-start | bytes 2064392 | tf_op jit(solution)/shard_map/ppermute | solution.py:16
  4.4 7.2 %slice-start = ((s8[5767168]{0:T(1024)(128)(4,1)}), s8[4194304]{0:T(1024)(128)(4,1)S(1)}, s32[]{:S(2)}) async-start(s8[5767168]{0:T(1024)(128)(4,1)} %bitcast.11), calls=%async_computation | async-start | bytes 8388608
  4.5 7.1 %slice-start.1 = ((s8[5767168]{0:T(1024)(128)(4,1)}), s8[1572864]{0:T(1024)(128)(4,1)S(1)}, s32[]{:S(2)}) async-start(s8[5767168]{0:T(1024)(128)(4,1)} %bitcast.11), calls=%async_computation.1 | async-start | bytes 3145728
  6.6 5.0 %collective-permute-start.1 = (f32[84,6144]{1,0:T(8,128)S(1)}, f32[84,6144]{1,0:T(8,128)S(1)}, u32[]{:S(2)}, u32[]{:S(2)}) collective-permute-start(f32[84,6144]{1,0:T(8,128)S(1)} %pad_maximum_fusion), channel_id=1, source_target_pairs={{0,4},{4,0},{8,12},{12,8},{16,20},{20,16},{24,28},{28,24},{1,5},{5... | collective-permute-start | bytes 6193160 | tf_op jit(solution)/shard_map/ppermute | solution.py:16
  6.9 115.1 %collective-permute-start.4 = (f32[168,2048]{1,0:T(8,128)S(1)}, f32[168,2048]{1,0:T(8,128)S(1)}, u32[]{:S(2)}, u32[]{:S(2)}) collective-permute-start(f32[168,2048]{1,0:T(8,128)S(1)} %maximum_select_fusion), channel_id=1, source_target_pairs={{0,24},{4,28},{8,16},{12,20},{16,8},{20,12},{24,0},{28,4},{1,25},{... | collective-permute-start | bytes 4128776 | tf_op jit(solution)/shard_map/ppermute | solution.py:16
  12.7 109.4 %collective-permute-start.2 = (f32[168,2048]{1,0:T(8,128)S(1)}, f32[168,2048]{1,0:T(8,128)S(1)}, u32[]{:S(2)}, u32[]{:S(2)}) collective-permute-start(f32[168,2048]{1,0:T(8,128)S(1)} %get-tuple-element.25), channel_id=1, source_target_pairs={{0,8},{4,12},{8,0},{12,4},{16,24},{20,28},{24,16},{28,20},{1,9},{5... | collective-permute-start | bytes 4128776 | tf_op jit(solution)/shard_map/ppermute | solution.py:16
  14.5 107.5 %collective-permute-start.3 = (f32[168,1792]{1,0:T(8,128)S(1)}, f32[168,1792]{1,0:T(8,128)S(1)}, u32[]{:S(2)}, u32[]{:S(2)}) collective-permute-start(f32[168,1792]{1,0:T(8,128)S(1)} %get-tuple-element.27), channel_id=1, source_target_pairs={{0,16},{4,20},{8,24},{12,28},{16,0},{20,4},{24,8},{28,12},{1,17},{... | collective-permute-start | bytes 3612680 | tf_op jit(solution)/shard_map/ppermute | solution.py:16
  122.0 10.7 %collective-permute-start.5 = (f32[168,256]{1,0:T(8,128)S(1)}, f32[168,256]{1,0:T(8,128)S(1)}, u32[]{:S(2)}, u32[]{:S(2)}) collective-permute-start(f32[168,256]{1,0:T(8,128)S(1)} %get-tuple-element.31), channel_id=1, source_target_pairs={{0,16},{4,20},{8,24},{12,28},{16,0},{20,4},{24,8},{28,12},{1,17},{... | collective-permute-start | bytes 516104 | tf_op jit(solution)/shard_map/ppermute | solution.py:16
  127.2 1.5 copy-start
  135.1 0.7 copy-start.3
  135.9 0.7 copy-start.5
  136.6 2.3 %collective-permute-start.6 = (f32[1056,128]{1,0:T(8,128)}, f32[1056,128]{1,0:T(8,128)S(1)}, u32[]{:S(2)}, u32[]{:S(2)}) collective-permute-start(f32[1056,128]{1,0:T(8,128)} %get-tuple-element.33), channel_id=1, source_target_pairs={{0,4},{4,0},{8,12},{12,8},{16,20},{20,16},{24,28},{28,24},{1,5},{5... | collective-permute-start | bytes 1622024 | tf_op jit(solution)/shard_map/ppermute | solution.py:16
  138.8 0.8 copy-start.7
  141.5 5.0 %collective-permute-start.7 = (f32[264,128]{1,0:T(8,128)}, f32[264,128]{1,0:T(8,128)S(1)}, u32[]{:S(2)}, u32[]{:S(2)}) collective-permute-start(f32[264,128]{1,0:T(8,128)} %get-tuple-element.53), channel_id=1, source_target_pairs={{0,1},{1,0},{2,3},{3,2},{4,5},{5,4},{6,7},{7,6},{8,9},{9,8},{10,11... | collective-permute-start | bytes 405512 | tf_op jit(solution)/shard_map/ppermute | solution.py:16
  142.7 4.5 %collective-permute-start.8 = (f32[264,128]{1,0:T(8,128)S(1)}, f32[264,128]{1,0:T(8,128)S(1)}, u32[]{:S(2)}, u32[]{:S(2)}) collective-permute-start(f32[264,128]{1,0:T(8,128)S(1)} %get-tuple-element.55), channel_id=1, source_target_pairs={{0,2},{1,3},{2,0},{3,1},{4,6},{5,7},{6,4},{7,5},{8,10},{9,11},{10,... | collective-permute-start | bytes 405512 | tf_op jit(solution)/shard_map/ppermute | solution.py:16
  143.9 6.6 %collective-permute-start.9 = (f32[264,128]{1,0:T(8,128)S(1)}, f32[264,128]{1,0:T(8,128)}, u32[]{:S(2)}, u32[]{:S(2)}) collective-permute-start(f32[264,128]{1,0:T(8,128)S(1)} %get-tuple-element.54), channel_id=1, source_target_pairs={{0,3},{1,2},{2,1},{3,0},{4,7},{5,6},{6,5},{7,4},{8,11},{9,10},{10,... | collective-permute-start | bytes 405512 | tf_op jit(solution)/shard_map/ppermute | solution.py:16
  151.4 6.1 %copy-start.8 = (f32[264,128]{1,0:T(8,128)}, f32[264,128]{1,0:T(8,128)S(1)}, u32[]{:S(2)}) copy-start(f32[264,128]{1,0:T(8,128)S(1)} %add_add_fusion.1) | copy-start | bytes 405508
  151.4 6.1 %collective-permute-start.10 = (f32[264,128]{1,0:T(8,128)S(1)}, f32[264,128]{1,0:T(8,128)S(1)}, u32[]{:S(2)}, u32[]{:S(2)}) collective-permute-start(f32[264,128]{1,0:T(8,128)S(1)} %add_add_fusion.1), channel_id=1, source_target_pairs={{0,8},{4,12},{8,0},{12,4},{16,24},{20,28},{24,16},{28,20},{1,9},{5... | collective-permute-start | bytes 405512 | tf_op jit(solution)/shard_map/ppermute | solution.py:16
  151.5 6.0 %collective-permute-start.11 = (f32[264,128]{1,0:T(8,128)S(1)}, f32[264,128]{1,0:T(8,128)S(1)}, u32[]{:S(2)}, u32[]{:S(2)}) collective-permute-start(f32[264,128]{1,0:T(8,128)S(1)} %add_add_fusion.1), channel_id=1, source_target_pairs={{0,16},{4,20},{8,24},{12,28},{16,0},{20,4},{24,8},{28,12},{1,17},{... | collective-permute-start | bytes 405512 | tf_op jit(solution)/shard_map/ppermute | solution.py:16
  152.9 7.9 %collective-permute-start.12 = (f32[264,128]{1,0:T(8,128)S(1)}, f32[264,128]{1,0:T(8,128)S(1)}, u32[]{:S(2)}, u32[]{:S(2)}) collective-permute-start(f32[264,128]{1,0:T(8,128)S(1)} %add_add_fusion.1), channel_id=1, source_target_pairs={{0,24},{4,28},{8,16},{12,20},{16,8},{20,12},{24,0},{28,4},{1,25},{... | collective-permute-start | bytes 405512 | tf_op jit(solution)/shard_map/ppermute | solution.py:16
  161.8 3.9 %collective-permute-start.13 = (f32[264,128]{1,0:T(8,128)S(1)}, f32[264,128]{1,0:T(8,128)S(1)}, u32[]{:S(2)}, u32[]{:S(2)}) collective-permute-start(f32[264,128]{1,0:T(8,128)S(1)} %get-tuple-element.47), channel_id=1, source_target_pairs={{0,1},{1,0},{2,3},{3,2},{4,5},{5,4},{6,7},{7,6},{8,9},{9,8},{10,11... | collective-permute-start | bytes 405512 | tf_op jit(solution)/shard_map/ppermute | solution.py:16
  163.0 5.3 %collective-permute-start.14 = (f32[264,128]{1,0:T(8,128)S(1)}, f32[264,128]{1,0:T(8,128)S(1)}, u32[]{:S(2)}, u32[]{:S(2)}) collective-permute-start(f32[264,128]{1,0:T(8,128)S(1)} %get-tuple-element.47), channel_id=1, source_target_pairs={{0,2},{1,3},{2,0},{3,1},{4,6},{5,7},{6,4},{7,5},{8,10},{9,11},{10,... | collective-permute-start | bytes 405512 | tf_op jit(solution)/shard_map/ppermute | solution.py:16
  163.2 5.1 %collective-permute-start.15 = (f32[264,128]{1,0:T(8,128)S(1)}, f32[264,128]{1,0:T(8,128)S(1)}, u32[]{:S(2)}, u32[]{:S(2)}) collective-permute-start(f32[264,128]{1,0:T(8,128)S(1)} %get-tuple-element.47), channel_id=1, source_target_pairs={{0,3},{1,2},{2,1},{3,0},{4,7},{5,6},{6,5},{7,4},{8,11},{9,10},{10,... | collective-permute-start | bytes 405512 | tf_op jit(solution)/shard_map/ppermute | solution.py:16
  168.4 8.3 %collective-permute-start.16 = (f32[1056,128]{1,0:T(8,128)S(1)}, f32[1056,128]{1,0:T(8,128)}, u32[]{:S(2)}, u32[]{:S(2)}) collective-permute-start(f32[1056,128]{1,0:T(8,128)S(1)} %bitcast.13), channel_id=1, source_target_pairs={{0,4},{4,0},{8,12},{12,8},{16,20},{20,16},{24,28},{28,24},{1,5},{5... | collective-permute-start | bytes 1622024 | tf_op jit(solution)/shard_map/ppermute | solution.py:16
  176.7 1.0 copy-start.2
  195.2 1.7 copy-start.1
  196.9 1.0 copy-start.4
  197.8 1.0 copy-start.6
  200.9 10.8 %collective-permute-start.17 = (f32[24,2048]{1,0:T(8,128)S(1)}, f32[24,2048]{1,0:T(8,128)S(1)}, u32[]{:S(2)}, u32[]{:S(2)}) collective-permute-start(f32[24,2048]{1,0:T(8,128)S(1)} %get-tuple-element.39), channel_id=1, source_target_pairs={{0,8},{4,12},{8,0},{12,4},{16,24},{20,28},{24,16},{28,20},{1,9},{5... | collective-permute-start | bytes 589832 | tf_op jit(solution)/shard_map/ppermute | solution.py:16
  203.5 15.4 %collective-permute-start.18 = (f32[24,2048]{1,0:T(8,128)S(1)}, f32[24,2048]{1,0:T(8,128)S(1)}, u32[]{:S(2)}, u32[]{:S(2)}) collective-permute-start(f32[24,2048]{1,0:T(8,128)S(1)} %get-tuple-element.40), channel_id=1, source_target_pairs={{0,16},{4,20},{8,24},{12,28},{16,0},{20,4},{24,8},{28,12},{1,17},{... | collective-permute-start | bytes 589832 | tf_op jit(solution)/shard_map/ppermute | solution.py:16
  203.5 15.4 %collective-permute-start.19 = (f32[24,2048]{1,0:T(8,128)S(1)}, f32[24,2048]{1,0:T(8,128)S(1)}, u32[]{:S(2)}, u32[]{:S(2)}) collective-permute-start(f32[24,2048]{1,0:T(8,128)S(1)} %get-tuple-element.41), channel_id=1, source_target_pairs={{0,24},{4,28},{8,16},{12,20},{16,8},{20,12},{24,0},{28,4},{1,25},{... | collective-permute-start | bytes 589832 | tf_op jit(solution)/shard_map/ppermute | solution.py:16
  219.6 3.9 %collective-permute-start.20 = (f32[12,8192]{1,0:T(8,128)S(1)}, f32[12,8192]{1,0:T(8,128)S(1)}, u32[]{:S(2)}, u32[]{:S(2)}) collective-permute-start(f32[12,8192]{1,0:T(8,128)S(1)} %get-tuple-element.43), channel_id=1, source_target_pairs={{0,4},{4,0},{8,12},{12,8},{16,20},{20,16},{24,28},{28,24},{1,5},{5... | collective-permute-start | bytes 1179656 | tf_op jit(solution)/shard_map/ppermute | solution.py:16

commit v7 on v6

--- a/solution.py
+++ b/solution.py
@@ -218,7 +218,7 @@
     return jnp.concatenate(done, 0)
 
 
-def iterations_kernel(iters, place_ref, mine_ref, other_ref, start_ref, factor_ref, packed, gram, high, low):
+def iterations_kernel(iters, place_ref, mine_ref, other_ref, start_ref, factor_ref, copy_ref, packed, gram, high, low):
     def times(a, b, dims):
         return lax.dot_general(a, b, (dims, ((), ())), precision=HIGHEST, preferred_element_type=jnp.float32)
 
@@ -242,55 +242,73 @@
 
     high[...], low[...] = split(gram[...])
 
-    def apply_gram(x):
+    def apply_gram(x, over=0):
         x_high, x_low = split(x)
 
         def part(a, b):
-            return lax.dot_general(a[...], b, (((1,), (0,)), ((), ())), preferred_element_type=jnp.float32)
+            return lax.dot_general(a[...], b, (((1,), (over,)), ((), ())), preferred_element_type=jnp.float32)
 
         return part(high, x_low) + part(low, x_high) + part(high, x_high)
 
-    image = apply_gram(start_ref[...])
+    image = apply_gram(start_ref[...], 1)
     for step in range(iters):
         small = times(image, image, ((0,), (0,)))
         inverse = lower_inverse(jnp.pad(small, ((0, 0), (0, 128 - small.shape[1]))))[:, : small.shape[1]]
         if step < iters - 1:
             image = times(apply_gram(image), inverse, ((1,), (1,)))
         else:
-            factor_ref[...] = times(image, inverse, ((1,), (1,)))
+            factor_ref[...] = times(inverse, image, ((1,), (1,)))
+            copy_ref[...] = factor_ref[...]
 
 
 def iterations(place, mine, other, start, iters):
-    n = start.shape[0]
+    n = start.shape[1]
     return pl.pallas_call(
         functools.partial(iterations_kernel, iters),
-        out_shape=jax.ShapeDtypeStruct(start.shape, jnp.float32),
+        out_shape=[jax.ShapeDtypeStruct(start.shape, jnp.float32)] * 2,
         in_specs=[pl.BlockSpec(memory_space=pltpu.SMEM)] + [pl.BlockSpec(memory_space=pltpu.VMEM)] * 3,
-        out_specs=pl.BlockSpec(memory_space=pltpu.VMEM),
+        out_specs=[pl.BlockSpec(memory_space=pltpu.VMEM)] * 2,
         scratch_shapes=[pltpu.VMEM((layout(n)[2], 128), jnp.float32), pltpu.VMEM((n, n), jnp.float32)] + [pltpu.VMEM((n, n), jnp.bfloat16)] * 2,
         compiler_params=pltpu.CompilerParams(vmem_limit_bytes=16 * 2**20),
         name="iterations",
     )(place, mine, other, start)
 
 
-def sum_everywhere(mine, theirs, fibre, rest):
+def farthest_first(size):
+    return [size - 1, *range(1, size - 1)]
+
+
+def mirrored(bits, rest):
+    side = int(rest**0.5)
+    return bits % side * side + bits // side if side * side == rest else bits
+
+
+def swap_rest(x, fibre, rest, bits):
+    other = mirrored(bits, rest)
+    pairs = [(f * rest + r, f * rest + (r ^ (other if f % 2 else bits))) for f in range(fibre) for r in range(rest)]
+    return lax.ppermute(x, ("fibre", "rest"), pairs)
+
+
+def sum_everywhere(core, mine, theirs, fibre, rest):
     r = lax.axis_index("rest")
     half, width = mine.shape
     piece = -(-half // (8 * rest)) * 8
     mine = mine + swap(theirs, "fibre", fibre, 1)
     mine = jnp.pad(mine, ((0, piece * rest - half), (0, 0)))
+    peers = {bits: r ^ jnp.where(core == 0, bits, mirrored(bits, rest)) for bits in farthest_first(rest)}
     total = lax.dynamic_slice(mine, (r * piece, 0), (piece, width))
-    for bits in range(1, rest):
-        part = lax.dynamic_slice(mine, ((r ^ bits) * piece, 0), (piece, width))
-        total = total + swap(part, "rest", rest, bits)
-    terms = [total] + [swap(total, "fibre", fibre, 2 * bits) for bits in range(1, fibre // 2)]
+    for bits, peer in peers.items():
+        part = lax.dynamic_slice(mine, (peer * piece, 0), (piece, width))
+        total = total + swap_rest(part, fibre, rest, bits)
+    terms = {bits: swap(total, "fibre", fibre, 2 * bits) for bits in farthest_first(fibre // 2)}
+    terms = [terms.get(bits, total) for bits in range(fibre // 2)]
     while len(terms) > 1:
-        terms = [terms[i] + terms[i + 1] for i in range(0, len(terms), 2)]
+        last = len(terms) - 1
+        terms = [terms[i] + terms[last - i] for i in range(1, len(terms) // 2)] + [terms[last] + terms[0]]
     total = terms[0]
-    out = jnp.zeros((rest, piece, width), jnp.float32)
-    for bits in range(rest):
-        got = swap(total, "rest", rest, bits) if bits else total
-        out = lax.dynamic_update_slice(out, got[None], (r ^ bits, 0, 0))
+    out = lax.dynamic_update_slice(jnp.zeros((rest, piece, width), jnp.float32), total[None], (r, 0, 0))
+    for bits, peer in peers.items():
+        out = lax.dynamic_update_slice(out, swap_rest(total, fibre, rest, bits)[None], (peer, 0, 0))
     out = out.reshape(rest * piece, width)[:half]
     return out, swap(out, "fibre", fibre, 1)
 
@@ -302,7 +320,7 @@
     high, low = split(basis_ref[...])
 
     def times(a, b):
-        return lax.dot_general(a, b[...], (((0,), (0,)), ((), ())), preferred_element_type=jnp.float32)
+        return lax.dot_general(a, b[...], (((1,), (0,)), ((), ())), preferred_element_type=jnp.float32)
 
     at = 0
     for first, second in (parts[:2], parts[2:]):
@@ -318,7 +336,7 @@
 
 
 def core_parts(place, basis, parts, zs):
-    rank = basis.shape[1]
+    rank = basis.shape[0]
     part = parts[0].shape[1] + parts[2].shape[1]
     vmem = pl.BlockSpec(memory_space=pltpu.VMEM)
     return pl.pallas_call(
@@ -332,23 +350,24 @@
     )(place, basis, *parts)
 
 
-def assemble_kernel(place_ref, *refs):
+def assemble_kernel(distances, place_ref, *refs):
     blocks, (mine_ref, theirs_ref) = refs[:-2], refs[-2:]
     z, core = place_ref[0], place_ref[1]
     own, part = mine_ref.shape[0], blocks[0].shape[1]
-    for bits, block in enumerate(blocks):
+    for bits, block in zip(distances, blocks):
         at = pl.multiple_of((z ^ bits) * part, 128)
         first, last = block[:own, :], block[own:, :]
         mine_ref[:, pl.ds(at, part)] = jnp.where(core == 0, first, last)
         theirs_ref[:, pl.ds(at, part)] = jnp.where(core == 0, last, first)
 
 
-def assemble(place, blocks):
+def assemble(place, moved):
+    blocks = list(moved.values())
     two_own, part = blocks[0].shape
     vmem = pl.BlockSpec(memory_space=pltpu.VMEM)
     half = jax.ShapeDtypeStruct((two_own // 2, part * len(blocks)), jnp.float32)
     return pl.pallas_call(
-        assemble_kernel,
+        functools.partial(assemble_kernel, tuple(moved)),
         out_shape=(half, half),
         in_specs=[pl.BlockSpec(memory_space=pltpu.SMEM)] + [vmem] * len(blocks),
         out_specs=[vmem] * 2,
@@ -365,18 +384,20 @@
     place = jnp.stack([z, core])
     half = cols // 2
     part = half // zs
-    early = part * 7 // 8
+    early = part * 3 // 4
 
     def cut(slab, whose, bits, start, width):
         return lax.dynamic_slice(slab, (0, whose * half + (z ^ bits) * part + start), (rows, width))
 
     far = zs - 1
-    got = swap(cut(slab, 1 - core, far, 0, part), "fibre", fibre, 1)
-    block = in_order(core, cut(slab, core, far, 0, part), got, 0)
-    slab, block = lax.optimization_barrier((slab, block))
+    theirs, mine = cut(slab, 1 - core, far, 0, part), cut(slab, core, far, 0, part)
+    slab, theirs, mine = lax.optimization_barrier((slab, theirs, mine))
+    cuts = [(bits, 0, part) for bits in range(far - 1, -1, -1)]
+    others = jnp.concatenate([cut(slab, 1 - core, *c) for c in cuts], 1)
+    block = in_order(core, mine, swap(theirs, "fibre", fibre, 1), 0)
+    others, block = lax.optimization_barrier((others, block))
     arrived = {far: swap(block, "fibre", fibre, 2 * far)}
-    cuts = [(bits, 0, part) for bits in range(far - 1, -1, -1)]
-    got = swap(jnp.concatenate([cut(slab, 1 - core, *c) for c in cuts], 1), "fibre", fibre, 1)
+    got = swap(others, "fibre", fibre, 1)
     pieces = []
     for bits, start, width in cuts:
         split_here = bits > 1
@@ -384,7 +405,7 @@
     late = {}
     for (bits, start, _), block in zip(pieces, prepare(place, slab, got, part, zs, cuts, pieces)):
         if start:
-            block, arrived[bits] = lax.optimization_barrier((block, arrived[bits]))
+            block, arrived[far] = lax.optimization_barrier((block, arrived[far]))
         into = late if start else arrived
         into[bits] = swap(block, "fibre", fibre, 2 * bits) if bits else block
     first = [arrived[bits] for bits in range(zs)]
@@ -392,12 +413,13 @@
     last_from = tuple(0 if bits in late else early for bits in range(zs))
     packed, *parts = gram_part(place, None, first, (0,) * zs, early)
     mine, theirs, *more = gram_part(place, packed, last, last_from, part - early)
-    mine, other = sum_everywhere(mine, theirs, fibre, rest)
-    basis = iterations(place, mine, other, start_basis, ITERS)
+    mine, other = sum_everywhere(core, mine, theirs, fibre, rest)
+    factor, basis = iterations(place, mine, other, start_basis.T, ITERS)
     blocks = core_parts(place, basis, [*parts, *more], zs)
-    blocks = [blocks[0]] + [swap(blocks[bits], "fibre", fibre, 2 * bits) for bits in range(1, zs)]
-    mine, theirs = assemble(place, blocks)
-    return (basis, in_order(core, mine, swap(theirs, "fibre", fibre, 1), 1))
+    moved = {bits: swap(blocks[bits], "fibre", fibre, 2 * bits) for bits in farthest_first(zs)}
+    moved[0] = blocks[0]
+    mine, theirs = assemble(place, moved)
+    return (factor.T, in_order(core, mine, swap(theirs, "fibre", fibre, 1), 1))
 
 
 def solution(mesh):

time: 226 us -> 221 us (0.978)
  waiting for transfers between devices: 143 us -> 119 us
  starting transfers between devices: 32.2 us -> 55.2 us
  local copies, waits for them, and re-layouts: 15.2 us -> 8.79 us
  other arithmetic: 4.51 us -> 7.51 us
    ppermute x21 -> x15, waiting for transfers between devices: 143 us -> 106 us  [swap(): return lax.ppermute(x, axis, [(i, i ^ bits) for i in range(size)])]
    ppermute x21 -> x15, starting transfers between devices: 32.2 us -> 49.8 us  [swap(): return lax.ppermute(x, axis, [(i, i ^ bits) for i in range(size)])]
    ppermute x0 -> x6, waiting for transfers between devices: none -> 12.7 us  [swap_rest(): return lax.ppermute(x, ('fibre', 'rest'), pairs)]
    unnamed x24 -> x14, local copies, waits for them, and re-layouts: 11.1 us -> 4.27 us
    ppermute x0 -> x6, starting transfers between devices: none -> 5.36 us  [swap_rest(): return lax.ppermute(x, ('fibre', 'rest'), pairs)]
  transfers between devices with their start and end apart: 21 -> 21, of which waited for: 14 -> 17; matrix products, arithmetic and copies ran while one was open for 1% -> 1% of each run, Pallas kernels for 3% -> 3%
where the time goes in v7:
time: 221 us
  waiting for transfers between devices  119 us (54%)
  starting transfers between devices  55.2 us (25%)
  Pallas kernels  29.2 us (13%)
  local copies, waits for them, and re-layouts  8.79 us (4%)
  other arithmetic  7.51 us (3%)
    ppermute x15, waiting for transfers between devices, swap(): return lax.ppermute(x, axis, [(i, i ^ bits) for i in range(size)])  106 us
    ppermute x15, starting transfers between devices, swap(): return lax.ppermute(x, axis, [(i, i ^ bits) for i in range(size)])  49.8 us
    pallas_call x1, Pallas kernels, iterations(): pl.pallas_call(functools.partial(iterations_kernel, iters), out_shape=[ja...  17.9 us
    ppermute x6, waiting for transfers between devices, swap_rest(): return lax.ppermute(x, ('fibre', 'rest'), pairs)  12.7 us
    pallas_call x2, Pallas kernels, gram_part(): pl.pallas_call(functools.partial(kernel, starts, width), out_shape=[*sums...  7.47 us
    ppermute x6, starting transfers between devices, swap_rest(): return lax.ppermute(x, ('fibre', 'rest'), pairs)  5.36 us
  transfers between devices with their start and end apart: 21, of which 17 were waited for; matrix products, arithmetic and copies ran while one was open for 1% of the time, Pallas kernels for 3%

profile of v7, /device:TPU:1, one launch (start us, length us, event | category | flops | bytes accessed | tf_op | source)
XLA Modules:
  0.0 220.5 jit_solution(17801353422903788897)
XLA Ops:
  0.7 1.5 constant_dynamic-slice_fusion.6
  2.4 1.8 constant_dynamic-slice_fusion.5
  4.6 1.5 maximum_select_fusion
  6.5 4.6 %collective-permute-start.4 = (f32[168,2048]{1,0:T(8,128)S(1)}, f32[168,2048]{1,0:T(8,128)S(1)}, u32[]{:S(2)}, u32[]{:S(2)}) collective-permute-start(f32[168,2048]{1,0:T(8,128)S(1)} %maximum_select_fusion), channel_id=1, source_target_pairs={{0,24},{4,28},{8,16},{12,20},{16,8},{20,12},{24,0},{28,4},{1,25},{... | collective-permute-start | bytes 4128776 | tf_op jit(solution)/shard_map/ppermute | solution.py:16
  12.2 1.9 collective-permute-start.2
  14.1 2.3 %collective-permute-start.3 = (f32[168,1536]{1,0:T(8,128)S(1)}, f32[168,1536]{1,0:T(8,128)S(1)}, u32[]{:S(2)}, u32[]{:S(2)}) collective-permute-start(f32[168,1536]{1,0:T(8,128)S(1)} %get-tuple-element.34), channel_id=1, source_target_pairs={{0,16},{4,20},{8,24},{12,28},{16,0},{20,4},{24,8},{28,12},{1,17},{... | collective-permute-start | bytes 3096584 | tf_op jit(solution)/shard_map/ppermute | solution.py:16
  16.4 25.2 %collective-permute-done.4.refs_3_ = f32[168,2048]{1,0:T(8,128)S(1)} collective-permute-done((f32[168,2048]{1,0:T(8,128)S(1)}, f32[168,2048]{1,0:T(8,128)S(1)}, u32[]{:S(2)}, u32[]{:S(2)}) %collective-permute-start.4) | collective-permute-done | bytes 1376288 | tf_op jit(solution)/shard_map/ppermute | solution.py:16
  41.6 29.5 %collective-permute-start.5 = (f32[168,512]{1,0:T(8,128)S(1)}, f32[168,512]{1,0:T(8,128)S(1)}, u32[]{:S(2)}, u32[]{:S(2)}) collective-permute-start(f32[168,512]{1,0:T(8,128)S(1)} %get-tuple-element.39), channel_id=1, source_target_pairs={{0,16},{4,20},{8,24},{12,28},{16,0},{20,4},{24,8},{28,12},{1,17},{... | collective-permute-start | bytes 1032200 | tf_op jit(solution)/shard_map/ppermute | solution.py:16
  71.1 50.3 %collective-permute-done.3.refs_2_ = f32[168,1536]{1,0:T(8,128)S(1)} collective-permute-done((f32[168,1536]{1,0:T(8,128)S(1)}, f32[168,1536]{1,0:T(8,128)S(1)}, u32[]{:S(2)}, u32[]{:S(2)}) %collective-permute-start.3) | collective-permute-done | bytes 1032224 | tf_op jit(solution)/shard_map/ppermute | solution.py:16
  121.4 4.5 %gram_early.1 = (f32[2112,128]{1,0:T(8,128)S(1)}, bf16[672,1536]{1,0:T(8,128)(2,1)S(1)}, bf16[672,1536]{1,0:T(8,128)(2,1)S(1)}) custom-call(s32[2]{0:T(128)S(1)} %pad_add_fusion.place_ref, f32[168,2048]{1,0:T(8,128)S(1)} %get-tuple-element.32.refs_0_, f32[168,2048]{1,0:T(8,128)S(1)} %collective-permute-done.2.refs_1_, ...), custom_call_target="tpu_custom_call" | custom-call | flops 4161798144 | bytes 8257536 | tf_op jit(solution)/shard_map/gram_early/pallas_call | solution.py:154
  128.8 3.0 %gram_late.1 = (f32[1056,128]{1,0:T(8,128)S(1)}, f32[1056,128]{1,0:T(8,128)}, bf16[672,512]{1,0:T(8,128)(2,1)S(1)}, bf16[672,512]{1,0:T(8,128)(2,1)S(1)}) custom-call(s32[2]{0:T(128)S(1)} %pad_add_fusion.place_ref, f32[2112,128]{1,0:T(8,128)S(1)} %get-tuple-element.38.base_ref, f32[168,2048]{1,0:T(8,128)S(1)} %get-tuple-element.32.refs_0_, ...), custom_call_target="tpu_custom_call" | custom-call | flops 1387266048 | bytes 2752512 | tf_op jit(solution)/shard_map/gram_late/pallas_call | solution.py:154
  133.6 1.9 collective-permute-done.6
  135.5 1.9 add.91
  138.5 2.2 %collective-permute-start.7 = (f32[264,128]{1,0:T(8,128)S(1)}, f32[264,128]{1,0:T(8,128)S(1)}, u32[]{:S(2)}, u32[]{:S(2)}) collective-permute-start(f32[264,128]{1,0:T(8,128)S(1)} %get-tuple-element.61), channel_id=1, source_target_pairs={{0,3},{1,2},{2,1},{3,0},{4,7},{5,6},{6,5},{7,4},{8,11},{9,10},{10,... | collective-permute-start | bytes 405512 | tf_op jit(solution)/shard_map/ppermute | solution.py:289
  141.2 3.0 %collective-permute-done.7 = f32[264,128]{1,0:T(8,128)S(1)} collective-permute-done((f32[264,128]{1,0:T(8,128)S(1)}, f32[264,128]{1,0:T(8,128)S(1)}, u32[]{:S(2)}, u32[]{:S(2)}) %collective-permute-start.7) | collective-permute-done | bytes 135200 | tf_op jit(solution)/shard_map/ppermute | solution.py:289
  144.3 3.6 %collective-permute-done.8 = f32[264,128]{1,0:T(8,128)S(1)} collective-permute-done((f32[264,128]{1,0:T(8,128)S(1)}, f32[264,128]{1,0:T(8,128)S(1)}, u32[]{:S(2)}, u32[]{:S(2)}) %collective-permute-start.8) | collective-permute-done | bytes 135200 | tf_op jit(solution)/shard_map/ppermute | solution.py:289
  148.9 2.3 %collective-permute-start.10 = (f32[264,128]{1,0:T(8,128)S(1)}, f32[264,128]{1,0:T(8,128)}, u32[]{:S(2)}, u32[]{:S(2)}) collective-permute-start(f32[264,128]{1,0:T(8,128)S(1)} %add_add_fusion.1), channel_id=1, source_target_pairs={{0,24},{4,28},{8,16},{12,20},{16,8},{20,12},{24,0},{28,4},{1,25},{... | collective-permute-start | bytes 405512 | tf_op jit(solution)/shard_map/ppermute | solution.py:16
  152.5 3.0 %collective-permute-done.10 = f32[264,128]{1,0:T(8,128)} collective-permute-done((f32[264,128]{1,0:T(8,128)S(1)}, f32[264,128]{1,0:T(8,128)}, u32[]{:S(2)}, u32[]{:S(2)}) %collective-permute-start.10) | collective-permute-done | bytes 135200 | tf_op jit(solution)/shard_map/ppermute | solution.py:16
  155.5 6.7 %collective-permute-done.11 = f32[264,128]{1,0:T(8,128)} collective-permute-done((f32[264,128]{1,0:T(8,128)S(1)}, f32[264,128]{1,0:T(8,128)}, u32[]{:S(2)}, u32[]{:S(2)}) %collective-permute-start.11) | collective-permute-done | bytes 135200 | tf_op jit(solution)/shard_map/ppermute | solution.py:16
  162.3 1.7 bitcast_dynamic-update-slice_fusion.3
  164.2 1.8 collective-permute-start.14
  166.6 3.1 %collective-permute-done.13 = f32[264,128]{1,0:T(8,128)S(1)} collective-permute-done((f32[264,128]{1,0:T(8,128)}, f32[264,128]{1,0:T(8,128)S(1)}, u32[]{:S(2)}, u32[]{:S(2)}) %collective-permute-start.13) | collective-permute-done | bytes 135200 | tf_op jit(solution)/shard_map/ppermute | solution.py:289
  169.7 2.4 %collective-permute-done.14 = f32[264,128]{1,0:T(8,128)S(1)} collective-permute-done((f32[264,128]{1,0:T(8,128)}, f32[264,128]{1,0:T(8,128)S(1)}, u32[]{:S(2)}, u32[]{:S(2)}) %collective-permute-start.14) | collective-permute-done | bytes 135200 | tf_op jit(solution)/shard_map/ppermute | solution.py:289
  172.8 1.6 collective-permute-start.16
  174.3 1.6 collective-permute-done.16.other_ref
  176.8 17.9 %iterations.1 = (f32[96,672]{1,0:T(8,128)}, f32[96,672]{1,0:T(8,128)S(1)}) custom-call(s32[2]{0:T(128)S(1)} %pad_add_fusion.place_ref, f32[1056,128]{1,0:T(8,128)S(1)} %bitcast.16, f32[1056,128]{1,0:T(8,128)S(1)} %collective-permute-done.16.other_ref, f32[96,672]{1,0:T(8,128)S(1)} %bitcast.17), custom_call_target="tpu_custom_call" | custom-call | tf_op jit(solution)/shard_map/iterations/pallas_call | solution.py:266
  195.9 2.1 core_parts.1
  198.8 2.8 %collective-permute-start.19 = (f32[24,2048]{1,0:T(8,128)S(1)}, f32[24,2048]{1,0:T(8,128)S(1)}, u32[]{:S(2)}, u32[]{:S(2)}) collective-permute-start(f32[24,2048]{1,0:T(8,128)S(1)} %get-tuple-element.50), channel_id=1, source_target_pairs={{0,16},{4,20},{8,24},{12,28},{16,0},{20,4},{24,8},{28,12},{1,17},{... | collective-permute-start | bytes 589832 | tf_op jit(solution)/shard_map/ppermute | solution.py:16
  201.6 4.4 %collective-permute-done.17.refs_0_ = f32[24,2048]{1,0:T(8,128)S(1)} collective-permute-done((f32[24,2048]{1,0:T(8,128)S(1)}, f32[24,2048]{1,0:T(8,128)S(1)}, u32[]{:S(2)}, u32[]{:S(2)}) %collective-permute-start.17) | collective-permute-done | bytes 196640 | tf_op jit(solution)/shard_map/ppermute | solution.py:16
  206.0 4.9 %collective-permute-done.18.refs_1_ = f32[24,2048]{1,0:T(8,128)S(1)} collective-permute-done((f32[24,2048]{1,0:T(8,128)S(1)}, f32[24,2048]{1,0:T(8,128)S(1)}, u32[]{:S(2)}, u32[]{:S(2)}) %collective-permute-start.18) | collective-permute-done | bytes 196640 | tf_op jit(solution)/shard_map/ppermute | solution.py:16
  210.8 5.1 %collective-permute-done.19.refs_2_ = f32[24,2048]{1,0:T(8,128)S(1)} collective-permute-done((f32[24,2048]{1,0:T(8,128)S(1)}, f32[24,2048]{1,0:T(8,128)S(1)}, u32[]{:S(2)}, u32[]{:S(2)}) %collective-permute-start.19) | collective-permute-done | bytes 196640 | tf_op jit(solution)/shard_map/ppermute | solution.py:16
  217.9 1.5 collective-permute-done.20
  (45 shorter events, 18.1 us)
Async XLA Ops:
  0.7 10.5 %slice-start = ((s8[5767168]{0:T(1024)(128)(4,1)}), s8[1572864]{0:T(1024)(128)(4,1)S(1)}, s32[]{:S(2)}) async-start(s8[5767168]{0:T(1024)(128)(4,1)} %bitcast.13), calls=%async_computation | async-start | bytes 3145728
  2.2 2.4 %collective-permute-start = (f32[84,2048]{1,0:T(8,128)S(1)}, f32[84,2048]{1,0:T(8,128)}, u32[]{:S(2)}, u32[]{:S(2)}) collective-permute-start(f32[84,2048]{1,0:T(8,128)S(1)} %get-tuple-element.30), channel_id=1, source_target_pairs={{0,4},{4,0},{8,12},{12,8},{16,20},{20,16},{24,28},{28,24},{1,5},{5... | collective-permute-start | bytes 2064392 | tf_op jit(solution)/shard_map/ppermute | solution.py:16
  2.4 8.8 %slice-start.1 = ((s8[5767168]{0:T(1024)(128)(4,1)}), s8[4194304]{0:T(1024)(128)(4,1)S(1)}, s32[]{:S(2)}) async-start(s8[5767168]{0:T(1024)(128)(4,1)} %bitcast.13), calls=%async_computation.1 | async-start | bytes 8388608
  6.2 5.0 %collective-permute-start.1 = (f32[84,6144]{1,0:T(8,128)S(1)}, f32[84,6144]{1,0:T(8,128)S(1)}, u32[]{:S(2)}, u32[]{:S(2)}) collective-permute-start(f32[84,6144]{1,0:T(8,128)S(1)} %pad_maximum_fusion), channel_id=1, source_target_pairs={{0,4},{4,0},{8,12},{12,8},{16,20},{20,16},{24,28},{28,24},{1,5},{5... | collective-permute-start | bytes 6193160 | tf_op jit(solution)/shard_map/ppermute | solution.py:16
  6.5 35.1 %collective-permute-start.4 = (f32[168,2048]{1,0:T(8,128)S(1)}, f32[168,2048]{1,0:T(8,128)S(1)}, u32[]{:S(2)}, u32[]{:S(2)}) collective-permute-start(f32[168,2048]{1,0:T(8,128)S(1)} %maximum_select_fusion), channel_id=1, source_target_pairs={{0,24},{4,28},{8,16},{12,20},{16,8},{20,12},{24,0},{28,4},{1,25},{... | collective-permute-start | bytes 4128776 | tf_op jit(solution)/shard_map/ppermute | solution.py:16
  12.2 109.2 %collective-permute-start.2 = (f32[168,2048]{1,0:T(8,128)S(1)}, f32[168,2048]{1,0:T(8,128)S(1)}, u32[]{:S(2)}, u32[]{:S(2)}) collective-permute-start(f32[168,2048]{1,0:T(8,128)S(1)} %get-tuple-element.33), channel_id=1, source_target_pairs={{0,8},{4,12},{8,0},{12,4},{16,24},{20,28},{24,16},{28,20},{1,9},{5... | collective-permute-start | bytes 4128776 | tf_op jit(solution)/shard_map/ppermute | solution.py:16
  14.1 107.3 %collective-permute-start.3 = (f32[168,1536]{1,0:T(8,128)S(1)}, f32[168,1536]{1,0:T(8,128)S(1)}, u32[]{:S(2)}, u32[]{:S(2)}) collective-permute-start(f32[168,1536]{1,0:T(8,128)S(1)} %get-tuple-element.34), channel_id=1, source_target_pairs={{0,16},{4,20},{8,24},{12,28},{16,0},{20,4},{24,8},{28,12},{1,17},{... | collective-permute-start | bytes 3096584 | tf_op jit(solution)/shard_map/ppermute | solution.py:16
  41.6 87.2 %collective-permute-start.5 = (f32[168,512]{1,0:T(8,128)S(1)}, f32[168,512]{1,0:T(8,128)S(1)}, u32[]{:S(2)}, u32[]{:S(2)}) collective-permute-start(f32[168,512]{1,0:T(8,128)S(1)} %get-tuple-element.39), channel_id=1, source_target_pairs={{0,16},{4,20},{8,24},{12,28},{16,0},{20,4},{24,8},{28,12},{1,17},{... | collective-permute-start | bytes 1032200 | tf_op jit(solution)/shard_map/ppermute | solution.py:16
  125.9 1.4 copy-start
  131.8 0.8 copy-start.2
  132.6 2.9 %collective-permute-start.6 = (f32[1056,128]{1,0:T(8,128)}, f32[1056,128]{1,0:T(8,128)}, u32[]{:S(2)}, u32[]{:S(2)}) collective-permute-start(f32[1056,128]{1,0:T(8,128)} %get-tuple-element.41), channel_id=1, source_target_pairs={{0,4},{4,0},{8,12},{12,8},{16,20},{20,16},{24,28},{28,24},{1,5},{5... | collective-permute-start | bytes 1622024 | tf_op jit(solution)/shard_map/ppermute | solution.py:16
  138.5 5.8 %collective-permute-start.7 = (f32[264,128]{1,0:T(8,128)S(1)}, f32[264,128]{1,0:T(8,128)S(1)}, u32[]{:S(2)}, u32[]{:S(2)}) collective-permute-start(f32[264,128]{1,0:T(8,128)S(1)} %get-tuple-element.61), channel_id=1, source_target_pairs={{0,3},{1,2},{2,1},{3,0},{4,7},{5,6},{6,5},{7,4},{8,11},{9,10},{10,... | collective-permute-start | bytes 405512 | tf_op jit(solution)/shard_map/ppermute | solution.py:289
  140.7 7.1 %collective-permute-start.8 = (f32[264,128]{1,0:T(8,128)S(1)}, f32[264,128]{1,0:T(8,128)S(1)}, u32[]{:S(2)}, u32[]{:S(2)}) collective-permute-start(f32[264,128]{1,0:T(8,128)S(1)} %get-tuple-element.63), channel_id=1, source_target_pairs={{0,1},{1,0},{2,3},{3,2},{4,6},{5,7},{6,4},{7,5},{8,9},{9,8},{10,11... | collective-permute-start | bytes 405512 | tf_op jit(solution)/shard_map/ppermute | solution.py:289
  141.0 6.9 %collective-permute-start.9 = (f32[264,128]{1,0:T(8,128)S(1)}, f32[264,128]{1,0:T(8,128)}, u32[]{:S(2)}, u32[]{:S(2)}) collective-permute-start(f32[264,128]{1,0:T(8,128)S(1)} %get-tuple-element.62), channel_id=1, source_target_pairs={{0,2},{1,3},{2,0},{3,1},{4,5},{5,4},{6,7},{7,6},{8,10},{9,11},{10,... | collective-permute-start | bytes 405512 | tf_op jit(solution)/shard_map/ppermute | solution.py:289
  148.9 6.6 %collective-permute-start.10 = (f32[264,128]{1,0:T(8,128)S(1)}, f32[264,128]{1,0:T(8,128)}, u32[]{:S(2)}, u32[]{:S(2)}) collective-permute-start(f32[264,128]{1,0:T(8,128)S(1)} %add_add_fusion.1), channel_id=1, source_target_pairs={{0,24},{4,28},{8,16},{12,20},{16,8},{20,12},{24,0},{28,4},{1,25},{... | collective-permute-start | bytes 405512 | tf_op jit(solution)/shard_map/ppermute | solution.py:16
  151.1 11.1 %collective-permute-start.11 = (f32[264,128]{1,0:T(8,128)S(1)}, f32[264,128]{1,0:T(8,128)}, u32[]{:S(2)}, u32[]{:S(2)}) collective-permute-start(f32[264,128]{1,0:T(8,128)S(1)} %add_add_fusion.1), channel_id=1, source_target_pairs={{0,8},{4,12},{8,0},{12,4},{16,24},{20,28},{24,16},{28,20},{1,9},{5... | collective-permute-start | bytes 405512 | tf_op jit(solution)/shard_map/ppermute | solution.py:16
  151.2 11.1 %collective-permute-start.12 = (f32[264,128]{1,0:T(8,128)S(1)}, f32[264,128]{1,0:T(8,128)}, u32[]{:S(2)}, u32[]{:S(2)}) collective-permute-start(f32[264,128]{1,0:T(8,128)S(1)} %add_add_fusion.1), channel_id=1, source_target_pairs={{0,16},{4,20},{8,24},{12,28},{16,0},{20,4},{24,8},{28,12},{1,17},{... | collective-permute-start | bytes 405512 | tf_op jit(solution)/shard_map/ppermute | solution.py:16
  164.0 5.7 %collective-permute-start.13 = (f32[264,128]{1,0:T(8,128)}, f32[264,128]{1,0:T(8,128)S(1)}, u32[]{:S(2)}, u32[]{:S(2)}) collective-permute-start(f32[264,128]{1,0:T(8,128)} %get-tuple-element.55), channel_id=1, source_target_pairs={{0,3},{1,2},{2,1},{3,0},{4,7},{5,6},{6,5},{7,4},{8,11},{9,10},{10,... | collective-permute-start | bytes 405512 | tf_op jit(solution)/shard_map/ppermute | solution.py:289
  164.2 30.6 %copy-start.1 = (bf16[672,1536]{1,0:T(8,128)(2,1)S(1)}, bf16[672,1536]{1,0:T(8,128)(2,1)}, u32[]{:S(2)}) copy-start(bf16[672,1536]{1,0:T(8,128)(2,1)} %copy-done) | copy-start | bytes 6193156
  164.2 7.9 %collective-permute-start.14 = (f32[264,128]{1,0:T(8,128)}, f32[264,128]{1,0:T(8,128)S(1)}, u32[]{:S(2)}, u32[]{:S(2)}) collective-permute-start(f32[264,128]{1,0:T(8,128)} %get-tuple-element.55), channel_id=1, source_target_pairs={{0,1},{1,0},{2,3},{3,2},{4,6},{5,7},{6,4},{7,5},{8,9},{9,8},{10,11... | collective-permute-start | bytes 405512 | tf_op jit(solution)/shard_map/ppermute | solution.py:289
  166.0 6.8 %collective-permute-start.15 = (f32[264,128]{1,0:T(8,128)}, f32[264,128]{1,0:T(8,128)S(1)}, u32[]{:S(2)}, u32[]{:S(2)}) collective-permute-start(f32[264,128]{1,0:T(8,128)} %get-tuple-element.55), channel_id=1, source_target_pairs={{0,2},{1,3},{2,0},{3,1},{4,5},{5,4},{6,7},{7,6},{8,10},{9,11},{10,... | collective-permute-start | bytes 405512 | tf_op jit(solution)/shard_map/ppermute | solution.py:289
  172.8 3.1 %collective-permute-start.16 = (f32[1056,128]{1,0:T(8,128)S(1)}, f32[1056,128]{1,0:T(8,128)S(1)}, u32[]{:S(2)}, u32[]{:S(2)}) collective-permute-start(f32[1056,128]{1,0:T(8,128)S(1)} %bitcast.15), channel_id=1, source_target_pairs={{0,4},{4,0},{8,12},{12,8},{16,20},{20,16},{24,28},{28,24},{1,5},{5... | collective-permute-start | bytes 1622024 | tf_op jit(solution)/shard_map/ppermute | solution.py:16
  175.9 1.0 copy-start.4
  194.8 1.1 copy-start.3
  198.0 8.0 %collective-permute-start.17 = (f32[24,2048]{1,0:T(8,128)S(1)}, f32[24,2048]{1,0:T(8,128)S(1)}, u32[]{:S(2)}, u32[]{:S(2)}) collective-permute-start(f32[24,2048]{1,0:T(8,128)S(1)} %get-tuple-element.48), channel_id=1, source_target_pairs={{0,24},{4,28},{8,16},{12,20},{16,8},{20,12},{24,0},{28,4},{1,25},{... | collective-permute-start | bytes 589832 | tf_op jit(solution)/shard_map/ppermute | solution.py:16
  198.7 12.2 %collective-permute-start.18 = (f32[24,2048]{1,0:T(8,128)S(1)}, f32[24,2048]{1,0:T(8,128)S(1)}, u32[]{:S(2)}, u32[]{:S(2)}) collective-permute-start(f32[24,2048]{1,0:T(8,128)S(1)} %get-tuple-element.49), channel_id=1, source_target_pairs={{0,8},{4,12},{8,0},{12,4},{16,24},{20,28},{24,16},{28,20},{1,9},{5... | collective-permute-start | bytes 589832 | tf_op jit(solution)/shard_map/ppermute | solution.py:16
  198.8 17.2 %collective-permute-start.19 = (f32[24,2048]{1,0:T(8,128)S(1)}, f32[24,2048]{1,0:T(8,128)S(1)}, u32[]{:S(2)}, u32[]{:S(2)}) collective-permute-start(f32[24,2048]{1,0:T(8,128)S(1)} %get-tuple-element.50), channel_id=1, source_target_pairs={{0,16},{4,20},{8,24},{12,28},{16,0},{20,4},{24,8},{28,12},{1,17},{... | collective-permute-start | bytes 589832 | tf_op jit(solution)/shard_map/ppermute | solution.py:16
  216.7 2.8 %collective-permute-start.20 = (f32[12,8192]{1,0:T(8,128)S(1)}, f32[12,8192]{1,0:T(8,128)S(1)}, u32[]{:S(2)}, u32[]{:S(2)}) collective-permute-start(f32[12,8192]{1,0:T(8,128)S(1)} %get-tuple-element.53), channel_id=1, source_target_pairs={{0,4},{4,0},{8,12},{12,8},{16,20},{20,16},{24,28},{28,24},{1,5},{5... | collective-permute-start | bytes 1179656 | tf_op jit(solution)/shard_map/ppermute | solution.py:16

commit v8 on v7

--- a/solution.py
+++ b/solution.py
@@ -59,7 +59,7 @@
     return pl.pallas_call(
         functools.partial(prepare_kernel, cuts, pieces),
         out_shape=[jax.ShapeDtypeStruct((2 * rows, width), jnp.float32) for _, _, width in pieces],
-        in_specs=[pl.BlockSpec(memory_space=pltpu.SMEM), pl.BlockSpec(memory_space=pl.ANY), vmem],
+        in_specs=[pl.BlockSpec(memory_space=pltpu.SMEM), pl.BlockSpec(memory_space=pltpu.HBM), vmem],
         out_specs=[vmem] * len(pieces),
         scratch_shapes=[pltpu.VMEM((zs, rows, part), jnp.float32), pltpu.SemaphoreType.DMA((zs,))],
         compiler_params=pltpu.CompilerParams(vmem_limit_bytes=24 * 2**20),
@@ -81,7 +81,8 @@
     return places, at, at + strip
 
 
-def add_gram(starts, width, place_ref, blocks, whole, high_ref, low_ref, packed, base_ref):
+def add_gram(starts, width, place_ref, blocks, whole, parts, packed, base_ref):
+    high_out, low_out, high_ref, low_ref, sems = parts
     zs = len(blocks)
     n = whole.shape[0]
     deep = n // zs
@@ -100,6 +101,12 @@
     places, corner, size = layout(n)
     edge = n // 128 * 128
     high_ref[...], low_ref[...] = split(whole[...])
+    saves = [
+        pltpu.make_async_copy(high_ref, high_out, sems.at[0]),
+        pltpu.make_async_copy(low_ref, low_out, sems.at[1]),
+    ]
+    for save in saves:
+        save.start()
 
     def product(r0, r1, c0, c1):
         def times(a, b):
@@ -123,16 +130,18 @@
         for j, (_, _, at) in enumerate(places):
             put(at, strip[128 * j : 128 * j + 128].T)
         put(corner, jnp.pad(strip[edge:], ((0, 0), (0, 128 - (n - edge)))))
+    for save in saves:
+        save.wait()
 
 
 def early_kernel(starts, width, place_ref, *refs):
-    blocks, (packed, high_ref, low_ref, whole) = refs[: len(starts)], refs[len(starts) :]
-    add_gram(starts, width, place_ref, blocks, whole, high_ref, low_ref, packed, None)
+    blocks, (packed, *parts, whole) = refs[: len(starts)], refs[len(starts) :]
+    add_gram(starts, width, place_ref, blocks, whole, parts, packed, None)
 
 
 def late_kernel(starts, width, place_ref, base_ref, *refs):
-    blocks, (mine_ref, theirs_ref, high_ref, low_ref, whole, packed) = refs[: len(starts)], refs[len(starts) :]
-    add_gram(starts, width, place_ref, blocks, whole, high_ref, low_ref, packed, base_ref)
+    blocks, (mine_ref, theirs_ref, *parts, whole, packed) = refs[: len(starts)], refs[len(starts) :]
+    add_gram(starts, width, place_ref, blocks, whole, parts, packed, base_ref)
     half = mine_ref.shape[0]
     core = place_ref[1]
     mine_ref[...] = packed[pl.ds(pl.multiple_of(core * half, 8), half), :]
@@ -144,18 +153,19 @@
     size = layout(n)[2]
     vmem = pl.BlockSpec(memory_space=pltpu.VMEM)
     parts = [jax.ShapeDtypeStruct((n, width), jnp.bfloat16)] * 2
-    packed = (size, 128)
-    whole = pltpu.VMEM((n, width), jnp.float32)
+    scratch = [pltpu.VMEM((n, width), jnp.bfloat16)] * 2
+    scratch += [pltpu.SemaphoreType.DMA((2,)), pltpu.VMEM((n, width), jnp.float32)]
     if base is None:
-        kernel, sums, scratch, first = early_kernel, [jax.ShapeDtypeStruct(packed, jnp.float32)], [whole], []
+        kernel, sums, first = early_kernel, [jax.ShapeDtypeStruct((size, 128), jnp.float32)], []
     else:
         half = jax.ShapeDtypeStruct((size // 2, 128), jnp.float32)
-        kernel, sums, scratch, first = late_kernel, [half, half], [whole, pltpu.VMEM(packed, jnp.float32)], [base]
+        kernel, sums, first = late_kernel, [half, half], [base]
+        scratch.append(pltpu.VMEM((size, 128), jnp.float32))
     return pl.pallas_call(
         functools.partial(kernel, starts, width),
         out_shape=[*sums, *parts],
         in_specs=[pl.BlockSpec(memory_space=pltpu.SMEM)] + [vmem] * (len(first) + len(blocks)),
-        out_specs=[vmem] * (len(sums) + 2),
+        out_specs=[vmem] * len(sums) + [pl.BlockSpec(memory_space=pltpu.HBM)] * 2,
         scratch_shapes=scratch,
         compiler_params=pltpu.CompilerParams(vmem_limit_bytes=24 * 2**20),
         cost_estimate=pl.CostEstimate(flops=6 * n * n * width, bytes_accessed=8 * n * width, transcendentals=0),
@@ -175,32 +185,20 @@
     for p in range(n // 8):
         at = 8 * p
         d = {(a, b): jnp.broadcast_to(left[p][a : a + 1, at + b : at + b + 1], full) for a in range(8) for b in range(a + 1)}
-        low, inv_diag = {}, []
+        lrow = [jnp.broadcast_to(left[p][k : k + 1, :], full) for k in range(8)]
+        rrow = [jnp.broadcast_to(right[p][k : k + 1, :], full) for k in range(8)]
+        low, scale, y, v = {}, [], [], []
         for b in range(8):
-            r = lax.rsqrt(d[b, b])
-            inv_diag.append(r)
+            scale.append(lax.rsqrt(d[b, b]))
+            y.append(lrow[b] * scale[b])
+            v.append(rrow[b] * scale[b])
             for a in range(b + 1, 8):
-                low[a, b] = d[a, b] * r
+                low[a, b] = d[a, b] * scale[b]
             for a in range(b + 1, 8):
                 for c in range(b + 1, a + 1):
                     d[a, c] = d[a, c] - low[a, b] * low[c, b]
-        inv = {}
-        for b in range(8):
-            inv[b, b] = inv_diag[b]
-            for a in range(b + 1, 8):
-                s = low[a, b] * inv[b, b]
-                for k in range(b + 1, a):
-                    s = s + low[a, k] * inv[k, b]
-                inv[a, b] = -s * inv_diag[a]
-        lrow = [jnp.broadcast_to(left[p][k : k + 1, :], full) for k in range(8)]
-        rrow = [jnp.broadcast_to(right[p][k : k + 1, :], full) for k in range(8)]
-        y, v = [], []
-        for m in range(8):
-            ym, vm = inv[m, 0] * lrow[0], inv[m, 0] * rrow[0]
-            for k in range(1, m + 1):
-                ym, vm = ym + inv[m, k] * lrow[k], vm + inv[m, k] * rrow[k]
-            y.append(ym)
-            v.append(vm)
+                lrow[a] = lrow[a] - low[a, b] * y[b]
+                rrow[a] = rrow[a] - low[a, b] * v[b]
         out = v[0]
         for m in range(1, 8):
             out = jnp.where(row == m, v[m], out)
@@ -209,16 +207,28 @@
             c = [jnp.broadcast_to(left[i][:, at + k : at + k + 1], full) for k in range(8)]
             li, ri = left[i], right[i]
             for m in range(8):
-                f = inv[m, 0] * c[0]
-                for k in range(1, m + 1):
-                    f = f + inv[m, k] * c[k]
+                f = c[m] * scale[m]
                 li = li - f * y[m]
                 ri = ri - f * v[m]
+                for k in range(m + 1, 8):
+                    c[k] = c[k] - low[k, m] * f
             left[i], right[i] = li, ri
     return jnp.concatenate(done, 0)
 
 
-def iterations_kernel(iters, place_ref, mine_ref, other_ref, start_ref, factor_ref, copy_ref, packed, gram, high, low):
+def iterations_kernel(iters, zs, place_ref, mine_ref, other_ref, start_ref, *refs):
+    kept, (factor_ref, *outs) = refs[:4], refs[4 : 5 + zs]
+    packed, gram, high, low, columns_high, columns_low, share, sems = refs[5 + zs :]
+    early = kept[0].shape[1]
+    fetches = [
+        pltpu.make_async_copy(kept[0], columns_high.at[:, :early], sems.at[0]),
+        pltpu.make_async_copy(kept[1], columns_low.at[:, :early], sems.at[1]),
+        pltpu.make_async_copy(kept[2], columns_high.at[:, early:], sems.at[2]),
+        pltpu.make_async_copy(kept[3], columns_low.at[:, early:], sems.at[3]),
+    ]
+    for fetch in fetches:
+        fetch.start()
+
     def times(a, b, dims):
         return lax.dot_general(a, b, (dims, ((), ())), precision=HIGHEST, preferred_element_type=jnp.float32)
 
@@ -257,21 +267,43 @@
         if step < iters - 1:
             image = times(apply_gram(image), inverse, ((1,), (1,)))
         else:
-            factor_ref[...] = times(inverse, image, ((1,), (1,)))
-            copy_ref[...] = factor_ref[...]
-
-
-def iterations(place, mine, other, start, iters):
-    n = start.shape[1]
+            basis = times(inverse, image, ((1,), (1,)))
+
+    factor_ref[...] = basis
+    basis_high, basis_low = split(basis)
+    for fetch in fetches:
+        fetch.wait()
+
+    def on_columns(a, b):
+        return lax.dot_general(a, b[...], (((1,), (0,)), ((), ())), preferred_element_type=jnp.float32)
+
+    share[...] = on_columns(basis_high, columns_low) + on_columns(basis_low, columns_high) + on_columns(basis_high, columns_high)
+    two_own = share.shape[0] // zs
+    for here in range(zs):
+
+        @pl.when(place_ref[0] == here)
+        def _():
+            for bits, out in enumerate(outs):
+                out[...] = share[two_own * (here ^ bits) : two_own * (here ^ bits) + two_own, :]
+
+
+def iterations(place, mine, other, start, parts, iters, zs):
+    rank, n = start.shape
+    part = parts[0].shape[1] + parts[2].shape[1]
+    vmem, hbm = pl.BlockSpec(memory_space=pltpu.VMEM), pl.BlockSpec(memory_space=pltpu.HBM)
     return pl.pallas_call(
-        functools.partial(iterations_kernel, iters),
-        out_shape=[jax.ShapeDtypeStruct(start.shape, jnp.float32)] * 2,
-        in_specs=[pl.BlockSpec(memory_space=pltpu.SMEM)] + [pl.BlockSpec(memory_space=pltpu.VMEM)] * 3,
-        out_specs=[pl.BlockSpec(memory_space=pltpu.VMEM)] * 2,
-        scratch_shapes=[pltpu.VMEM((layout(n)[2], 128), jnp.float32), pltpu.VMEM((n, n), jnp.float32)] + [pltpu.VMEM((n, n), jnp.bfloat16)] * 2,
-        compiler_params=pltpu.CompilerParams(vmem_limit_bytes=16 * 2**20),
+        functools.partial(iterations_kernel, iters, zs),
+        out_shape=[jax.ShapeDtypeStruct(start.shape, jnp.float32)]
+        + [jax.ShapeDtypeStruct((rank // zs, part), jnp.float32)] * zs,
+        in_specs=[pl.BlockSpec(memory_space=pltpu.SMEM)] + [vmem] * 3 + [hbm] * 4,
+        out_specs=[vmem] * (1 + zs),
+        scratch_shapes=[pltpu.VMEM((layout(n)[2], 128), jnp.float32), pltpu.VMEM((n, n), jnp.float32)]
+        + [pltpu.VMEM((n, n), jnp.bfloat16)] * 2
+        + [pltpu.VMEM((n, part), jnp.bfloat16)] * 2
+        + [pltpu.VMEM((rank, part), jnp.float32), pltpu.SemaphoreType.DMA((4,))],
+        compiler_params=pltpu.CompilerParams(vmem_limit_bytes=24 * 2**20),
         name="iterations",
-    )(place, mine, other, start)
+    )(place, mine, other, start, *parts)
 
 
 def farthest_first(size):
@@ -311,43 +343,6 @@
         out = lax.dynamic_update_slice(out, swap_rest(total, fibre, rest, bits)[None], (peer, 0, 0))
     out = out.reshape(rest * piece, width)[:half]
     return out, swap(out, "fibre", fibre, 1)
-
-
-def core_kernel(place_ref, basis_ref, *refs):
-    parts, outs, share = refs[:4], refs[4:-1], refs[-1]
-    zs = len(outs)
-    two_own = share.shape[0] // zs
-    high, low = split(basis_ref[...])
-
-    def times(a, b):
-        return lax.dot_general(a, b[...], (((1,), (0,)), ((), ())), preferred_element_type=jnp.float32)
-
-    at = 0
-    for first, second in (parts[:2], parts[2:]):
-        width = first.shape[1]
-        share[:, at : at + width] = times(high, second) + times(low, first) + times(high, first)
-        at += width
-    for here in range(zs):
-
-        @pl.when(place_ref[0] == here)
-        def _():
-            for bits, out in enumerate(outs):
-                out[...] = share[two_own * (here ^ bits) : two_own * (here ^ bits) + two_own, :]
-
-
-def core_parts(place, basis, parts, zs):
-    rank = basis.shape[0]
-    part = parts[0].shape[1] + parts[2].shape[1]
-    vmem = pl.BlockSpec(memory_space=pltpu.VMEM)
-    return pl.pallas_call(
-        core_kernel,
-        out_shape=[jax.ShapeDtypeStruct((rank // zs, part), jnp.float32)] * zs,
-        in_specs=[pl.BlockSpec(memory_space=pltpu.SMEM)] + [vmem] * 5,
-        out_specs=[vmem] * zs,
-        scratch_shapes=[pltpu.VMEM((rank, part), jnp.float32)],
-        compiler_params=pltpu.CompilerParams(vmem_limit_bytes=16 * 2**20),
-        name="core_parts",
-    )(place, basis, *parts)
 
 
 def assemble_kernel(distances, place_ref, *refs):
@@ -414,8 +409,7 @@
     packed, *parts = gram_part(place, None, first, (0,) * zs, early)
     mine, theirs, *more = gram_part(place, packed, last, last_from, part - early)
     mine, other = sum_everywhere(core, mine, theirs, fibre, rest)
-    factor, basis = iterations(place, mine, other, start_basis.T, ITERS)
-    blocks = core_parts(place, basis, [*parts, *more], zs)
+    factor, *blocks = iterations(place, mine, other, start_basis.T, [*parts, *more], ITERS, zs)
     moved = {bits: swap(blocks[bits], "fibre", fibre, 2 * bits) for bits in farthest_first(zs)}
     moved[0] = blocks[0]
     mine, theirs = assemble(place, moved)

time: 221 us -> 222 us (level)
    pallas_call x2, Pallas kernels: 7.47 us -> 10.1 us  [gram_part(): pl.pallas_call(functools.partial(kernel, starts, width), out_shape=[*sums...]
    unnamed x14 -> x18, local copies, waits for them, and re-layouts: 4.27 us -> 6.65 us
    pallas_call x2 -> x1, Pallas kernels: 20 us -> 18.3 us  [iterations(): pl.pallas_call(functools.partial(iterations_kernel, iters, zs), out_shape...]
  transfers between devices with their start and end apart: 21 -> 21, of which waited for: 17 -> 16; matrix products, arithmetic and copies ran while one was open for 1% -> 1% of each run, Pallas kernels for 3% -> 3%
where the time goes in v8:
time: 222 us; the launch traced here: 221 us
  waiting for transfers between devices  118 us (53%)
  starting transfers between devices  55.8 us (25%)
  Pallas kernels  30.2 us (14%)
  local copies, waits for them, and re-layouts  10.1 us (5%)
  other arithmetic  6.84 us (3%)
    ppermute x15, waiting for transfers between devices, swap(): return lax.ppermute(x, axis, [(i, i ^ bits) for i in range(size)])  105 us
    ppermute x15, starting transfers between devices, swap(): return lax.ppermute(x, axis, [(i, i ^ bits) for i in range(size)])  50.5 us
    pallas_call x1, Pallas kernels, iterations(): pl.pallas_call(functools.partial(iterations_kernel, iters, zs), out_shape...  18.3 us
    ppermute x6, waiting for transfers between devices, swap_rest(): return lax.ppermute(x, ('fibre', 'rest'), pairs)  12.7 us
    pallas_call x2, Pallas kernels, gram_part(): pl.pallas_call(functools.partial(kernel, starts, width), out_shape=[*sums...  10.1 us
    unnamed x18, local copies, waits for them, and re-layouts  6.65 us
    ppermute x6, starting transfers between devices, swap_rest(): return lax.ppermute(x, ('fibre', 'rest'), pairs)  5.36 us
  transfers between devices with their start and end apart: 21, of which 16 were waited for; matrix products, arithmetic and copies ran while one was open for 1% of the time, Pallas kernels for 3%

profile of v8, /device:TPU:1, one launch (start us, length us, event | category | flops | bytes accessed | tf_op | source)
XLA Modules:
  0.0 221.4 jit_solution(12351180432179797628)
XLA Ops:
  0.7 1.5 constant_dynamic-slice_fusion.6
  2.4 1.8 constant_dynamic-slice_fusion.5
  4.6 1.6 maximum_select_fusion
  6.6 4.6 %collective-permute-start.4 = (f32[168,2048]{1,0:T(8,128)S(1)}, f32[168,2048]{1,0:T(8,128)S(1)}, u32[]{:S(2)}, u32[]{:S(2)}) collective-permute-start(f32[168,2048]{1,0:T(8,128)S(1)} %maximum_select_fusion), channel_id=1, source_target_pairs={{0,24},{4,28},{8,16},{12,20},{16,8},{20,12},{24,0},{28,4},{1,25},{... | collective-permute-start | bytes 4128776 | tf_op jit(solution)/shard_map/ppermute | solution.py:16
  12.3 1.9 collective-permute-start.2
  14.2 2.3 %collective-permute-start.3 = (f32[168,1536]{1,0:T(8,128)S(1)}, f32[168,1536]{1,0:T(8,128)S(1)}, u32[]{:S(2)}, u32[]{:S(2)}) collective-permute-start(f32[168,1536]{1,0:T(8,128)S(1)} %get-tuple-element.33), channel_id=1, source_target_pairs={{0,16},{4,20},{8,24},{12,28},{16,0},{20,4},{24,8},{28,12},{1,17},{... | collective-permute-start | bytes 3096584 | tf_op jit(solution)/shard_map/ppermute | solution.py:16
  16.5 25.2 %collective-permute-done.4.refs_3_ = f32[168,2048]{1,0:T(8,128)S(1)} collective-permute-done((f32[168,2048]{1,0:T(8,128)S(1)}, f32[168,2048]{1,0:T(8,128)S(1)}, u32[]{:S(2)}, u32[]{:S(2)}) %collective-permute-start.4) | collective-permute-done | bytes 1376288 | tf_op jit(solution)/shard_map/ppermute | solution.py:16
  41.7 29.5 %collective-permute-start.5 = (f32[168,512]{1,0:T(8,128)S(1)}, f32[168,512]{1,0:T(8,128)S(1)}, u32[]{:S(2)}, u32[]{:S(2)}) collective-permute-start(f32[168,512]{1,0:T(8,128)S(1)} %get-tuple-element.38), channel_id=1, source_target_pairs={{0,16},{4,20},{8,24},{12,28},{16,0},{20,4},{24,8},{28,12},{1,17},{... | collective-permute-start | bytes 1032200 | tf_op jit(solution)/shard_map/ppermute | solution.py:16
  71.2 50.3 %collective-permute-done.3.refs_2_ = f32[168,1536]{1,0:T(8,128)S(1)} collective-permute-done((f32[168,1536]{1,0:T(8,128)S(1)}, f32[168,1536]{1,0:T(8,128)S(1)}, u32[]{:S(2)}, u32[]{:S(2)}) %collective-permute-start.3) | collective-permute-done | bytes 1032224 | tf_op jit(solution)/shard_map/ppermute | solution.py:16
  121.5 6.3 %gram_early.1 = (f32[2112,128]{1,0:T(8,128)S(1)}, bf16[672,1536]{1,0:T(8,128)(2,1)S(1)}, bf16[672,1536]{1,0:T(8,128)(2,1)S(1)}) custom-call(s32[2]{0:T(128)S(1)} %pad_add_fusion.place_ref, f32[168,2048]{1,0:T(8,128)S(1)} %get-tuple-element.31.refs_0_, f32[168,2048]{1,0:T(8,128)S(1)} %collective-permute-done.2.refs_1_, ...), custom_call_target="tpu_custom_call" | custom-call | flops 4161798144 | bytes 8257536 | tf_op jit(solution)/shard_map/gram_early/pallas_call | solution.py:164
  129.2 3.8 %gram_late.1 = (f32[1056,128]{1,0:T(8,128)S(1)}, f32[1056,128]{1,0:T(8,128)}, bf16[672,512]{1,0:T(8,128)(2,1)S(1)}, bf16[672,512]{1,0:T(8,128)(2,1)S(1)}) custom-call(s32[2]{0:T(128)S(1)} %pad_add_fusion.place_ref, f32[2112,128]{1,0:T(8,128)S(1)} %get-tuple-element.37.base_ref, f32[168,2048]{1,0:T(8,128)S(1)} %get-tuple-element.31.refs_0_, ...), custom_call_target="tpu_custom_call" | custom-call | flops 1387266048 | bytes 2752512 | tf_op jit(solution)/shard_map/gram_late/pallas_call | solution.py:164
  133.9 1.6 collective-permute-start.6
  135.5 1.9 collective-permute-done.6
  139.4 2.2 %collective-permute-start.7 = (f32[264,128]{1,0:T(8,128)S(1)}, f32[264,128]{1,0:T(8,128)S(1)}, u32[]{:S(2)}, u32[]{:S(2)}) collective-permute-start(f32[264,128]{1,0:T(8,128)S(1)} %get-tuple-element.59), channel_id=1, source_target_pairs={{0,3},{1,2},{2,1},{3,0},{4,7},{5,6},{6,5},{7,4},{8,11},{9,10},{10,... | collective-permute-start | bytes 405512 | tf_op jit(solution)/shard_map/ppermute | solution.py:321
  142.1 3.0 %collective-permute-done.7 = f32[264,128]{1,0:T(8,128)S(1)} collective-permute-done((f32[264,128]{1,0:T(8,128)S(1)}, f32[264,128]{1,0:T(8,128)S(1)}, u32[]{:S(2)}, u32[]{:S(2)}) %collective-permute-start.7) | collective-permute-done | bytes 135200 | tf_op jit(solution)/shard_map/ppermute | solution.py:321
  145.2 3.6 %collective-permute-done.8 = f32[264,128]{1,0:T(8,128)S(1)} collective-permute-done((f32[264,128]{1,0:T(8,128)S(1)}, f32[264,128]{1,0:T(8,128)S(1)}, u32[]{:S(2)}, u32[]{:S(2)}) %collective-permute-start.8) | collective-permute-done | bytes 135200 | tf_op jit(solution)/shard_map/ppermute | solution.py:321
  149.8 2.3 %collective-permute-start.10 = (f32[264,128]{1,0:T(8,128)S(1)}, f32[264,128]{1,0:T(8,128)S(1)}, u32[]{:S(2)}, u32[]{:S(2)}) collective-permute-start(f32[264,128]{1,0:T(8,128)S(1)} %add_add_fusion.1), channel_id=1, source_target_pairs={{0,24},{4,28},{8,16},{12,20},{16,8},{20,12},{24,0},{28,4},{1,25},{... | collective-permute-start | bytes 405512 | tf_op jit(solution)/shard_map/ppermute | solution.py:16
  153.4 2.9 %collective-permute-done.10 = f32[264,128]{1,0:T(8,128)S(1)} collective-permute-done((f32[264,128]{1,0:T(8,128)S(1)}, f32[264,128]{1,0:T(8,128)S(1)}, u32[]{:S(2)}, u32[]{:S(2)}) %collective-permute-start.10) | collective-permute-done | bytes 135200 | tf_op jit(solution)/shard_map/ppermute | solution.py:16
  156.3 6.8 %collective-permute-done.11 = f32[264,128]{1,0:T(8,128)} collective-permute-done((f32[264,128]{1,0:T(8,128)S(1)}, f32[264,128]{1,0:T(8,128)}, u32[]{:S(2)}, u32[]{:S(2)}) %collective-permute-start.11) | collective-permute-done | bytes 135200 | tf_op jit(solution)/shard_map/ppermute | solution.py:16
  163.2 1.7 bitcast_dynamic-update-slice_fusion.3
  165.1 1.8 collective-permute-start.14
  167.6 3.1 %collective-permute-done.13 = f32[264,128]{1,0:T(8,128)S(1)} collective-permute-done((f32[264,128]{1,0:T(8,128)}, f32[264,128]{1,0:T(8,128)S(1)}, u32[]{:S(2)}, u32[]{:S(2)}) %collective-permute-start.13) | collective-permute-done | bytes 135200 | tf_op jit(solution)/shard_map/ppermute | solution.py:321
  170.6 2.4 %collective-permute-done.14 = f32[264,128]{1,0:T(8,128)S(1)} collective-permute-done((f32[264,128]{1,0:T(8,128)}, f32[264,128]{1,0:T(8,128)S(1)}, u32[]{:S(2)}, u32[]{:S(2)}) %collective-permute-start.14) | collective-permute-done | bytes 135200 | tf_op jit(solution)/shard_map/ppermute | solution.py:321
  173.7 1.6 collective-permute-start.16
  175.2 1.6 collective-permute-done.16.other_ref
  176.8 1.6 copy-done.1
  180.4 18.3 %iterations.1 = (f32[96,672]{1,0:T(8,128)}, f32[24,2048]{1,0:T(8,128)S(1)}, f32[24,2048]{1,0:T(8,128)S(1)}, f32[24,2048]{1,0:T(8,128)S(1)}, f32[24,2048]{1,0:T(8,128)S(1)}) custom-call(s32[2]{0:T(128)S(1)} %pad_add_fusion.place_ref, f32[1056,128]{1,0:T(8,128)S(1)} %bitcast.16, f32[1056,128]{1,0:T(8,128)S(1)} %collective-permute-done.16.other_ref, ...), custom_call_target="tpu_custom_call" | custom-call | tf_op jit(solution)/shard_map/iterations/pallas_call | solution.py:294
  199.6 2.8 %collective-permute-start.19 = (f32[24,2048]{1,0:T(8,128)S(1)}, f32[24,2048]{1,0:T(8,128)S(1)}, u32[]{:S(2)}, u32[]{:S(2)}) collective-permute-start(f32[24,2048]{1,0:T(8,128)S(1)} %get-tuple-element.48), channel_id=1, source_target_pairs={{0,16},{4,20},{8,24},{12,28},{16,0},{20,4},{24,8},{28,12},{1,17},{... | collective-permute-start | bytes 589832 | tf_op jit(solution)/shard_map/ppermute | solution.py:16
  202.3 4.4 %collective-permute-done.17.refs_0_ = f32[24,2048]{1,0:T(8,128)S(1)} collective-permute-done((f32[24,2048]{1,0:T(8,128)S(1)}, f32[24,2048]{1,0:T(8,128)S(1)}, u32[]{:S(2)}, u32[]{:S(2)}) %collective-permute-start.17) | collective-permute-done | bytes 196640 | tf_op jit(solution)/shard_map/ppermute | solution.py:16
  206.8 4.9 %collective-permute-done.18.refs_1_ = f32[24,2048]{1,0:T(8,128)S(1)} collective-permute-done((f32[24,2048]{1,0:T(8,128)S(1)}, f32[24,2048]{1,0:T(8,128)S(1)}, u32[]{:S(2)}, u32[]{:S(2)}) %collective-permute-start.18) | collective-permute-done | bytes 196640 | tf_op jit(solution)/shard_map/ppermute | solution.py:16
  211.7 5.1 %collective-permute-done.19.refs_2_ = f32[24,2048]{1,0:T(8,128)S(1)} collective-permute-done((f32[24,2048]{1,0:T(8,128)S(1)}, f32[24,2048]{1,0:T(8,128)S(1)}, u32[]{:S(2)}, u32[]{:S(2)}) %collective-permute-start.19) | collective-permute-done | bytes 196640 | tf_op jit(solution)/shard_map/ppermute | solution.py:16
  218.7 1.5 collective-permute-done.20
  (48 shorter events, 16.4 us)
Async XLA Ops:
  0.7 10.6 %slice-start = ((s8[5767168]{0:T(1024)(128)(4,1)}), s8[1572864]{0:T(1024)(128)(4,1)S(1)}, s32[]{:S(2)}) async-start(s8[5767168]{0:T(1024)(128)(4,1)} %bitcast.13), calls=%async_computation | async-start | bytes 3145728
  2.2 2.4 %collective-permute-start = (f32[84,2048]{1,0:T(8,128)S(1)}, f32[84,2048]{1,0:T(8,128)}, u32[]{:S(2)}, u32[]{:S(2)}) collective-permute-start(f32[84,2048]{1,0:T(8,128)S(1)} %get-tuple-element.29), channel_id=1, source_target_pairs={{0,4},{4,0},{8,12},{12,8},{16,20},{20,16},{24,28},{28,24},{1,5},{5... | collective-permute-start | bytes 2064392 | tf_op jit(solution)/shard_map/ppermute | solution.py:16
  2.4 8.9 %slice-start.1 = ((s8[5767168]{0:T(1024)(128)(4,1)}), s8[4194304]{0:T(1024)(128)(4,1)S(1)}, s32[]{:S(2)}) async-start(s8[5767168]{0:T(1024)(128)(4,1)} %bitcast.13), calls=%async_computation.1 | async-start | bytes 8388608
  6.3 5.0 %collective-permute-start.1 = (f32[84,6144]{1,0:T(8,128)S(1)}, f32[84,6144]{1,0:T(8,128)S(1)}, u32[]{:S(2)}, u32[]{:S(2)}) collective-permute-start(f32[84,6144]{1,0:T(8,128)S(1)} %pad_maximum_fusion), channel_id=1, source_target_pairs={{0,4},{4,0},{8,12},{12,8},{16,20},{20,16},{24,28},{28,24},{1,5},{5... | collective-permute-start | bytes 6193160 | tf_op jit(solution)/shard_map/ppermute | solution.py:16
  6.6 35.1 %collective-permute-start.4 = (f32[168,2048]{1,0:T(8,128)S(1)}, f32[168,2048]{1,0:T(8,128)S(1)}, u32[]{:S(2)}, u32[]{:S(2)}) collective-permute-start(f32[168,2048]{1,0:T(8,128)S(1)} %maximum_select_fusion), channel_id=1, source_target_pairs={{0,24},{4,28},{8,16},{12,20},{16,8},{20,12},{24,0},{28,4},{1,25},{... | collective-permute-start | bytes 4128776 | tf_op jit(solution)/shard_map/ppermute | solution.py:16
  12.3 109.2 %collective-permute-start.2 = (f32[168,2048]{1,0:T(8,128)S(1)}, f32[168,2048]{1,0:T(8,128)S(1)}, u32[]{:S(2)}, u32[]{:S(2)}) collective-permute-start(f32[168,2048]{1,0:T(8,128)S(1)} %get-tuple-element.32), channel_id=1, source_target_pairs={{0,8},{4,12},{8,0},{12,4},{16,24},{20,28},{24,16},{28,20},{1,9},{5... | collective-permute-start | bytes 4128776 | tf_op jit(solution)/shard_map/ppermute | solution.py:16
  14.2 107.3 %collective-permute-start.3 = (f32[168,1536]{1,0:T(8,128)S(1)}, f32[168,1536]{1,0:T(8,128)S(1)}, u32[]{:S(2)}, u32[]{:S(2)}) collective-permute-start(f32[168,1536]{1,0:T(8,128)S(1)} %get-tuple-element.33), channel_id=1, source_target_pairs={{0,16},{4,20},{8,24},{12,28},{16,0},{20,4},{24,8},{28,12},{1,17},{... | collective-permute-start | bytes 3096584 | tf_op jit(solution)/shard_map/ppermute | solution.py:16
  41.7 87.6 %collective-permute-start.5 = (f32[168,512]{1,0:T(8,128)S(1)}, f32[168,512]{1,0:T(8,128)S(1)}, u32[]{:S(2)}, u32[]{:S(2)}) collective-permute-start(f32[168,512]{1,0:T(8,128)S(1)} %get-tuple-element.38), channel_id=1, source_target_pairs={{0,16},{4,20},{8,24},{12,28},{16,0},{20,4},{24,8},{28,12},{1,17},{... | collective-permute-start | bytes 1032200 | tf_op jit(solution)/shard_map/ppermute | solution.py:16
  127.9 1.4 copy-start
  133.1 0.8 copy-start.2
  133.9 3.5 %collective-permute-start.6 = (f32[1056,128]{1,0:T(8,128)}, f32[1056,128]{1,0:T(8,128)}, u32[]{:S(2)}, u32[]{:S(2)}) collective-permute-start(f32[1056,128]{1,0:T(8,128)} %get-tuple-element.40), channel_id=1, source_target_pairs={{0,4},{4,0},{8,12},{12,8},{16,20},{20,16},{24,28},{28,24},{1,5},{5... | collective-permute-start | bytes 1622024 | tf_op jit(solution)/shard_map/ppermute | solution.py:16
  138.6 0.8 copy-start.5
  139.4 5.8 %collective-permute-start.7 = (f32[264,128]{1,0:T(8,128)S(1)}, f32[264,128]{1,0:T(8,128)S(1)}, u32[]{:S(2)}, u32[]{:S(2)}) collective-permute-start(f32[264,128]{1,0:T(8,128)S(1)} %get-tuple-element.59), channel_id=1, source_target_pairs={{0,3},{1,2},{2,1},{3,0},{4,7},{5,6},{6,5},{7,4},{8,11},{9,10},{10,... | collective-permute-start | bytes 405512 | tf_op jit(solution)/shard_map/ppermute | solution.py:321
  141.6 7.1 %collective-permute-start.8 = (f32[264,128]{1,0:T(8,128)S(1)}, f32[264,128]{1,0:T(8,128)S(1)}, u32[]{:S(2)}, u32[]{:S(2)}) collective-permute-start(f32[264,128]{1,0:T(8,128)S(1)} %get-tuple-element.61), channel_id=1, source_target_pairs={{0,1},{1,0},{2,3},{3,2},{4,6},{5,7},{6,4},{7,5},{8,9},{9,8},{10,11... | collective-permute-start | bytes 405512 | tf_op jit(solution)/shard_map/ppermute | solution.py:321
  141.9 6.9 %collective-permute-start.9 = (f32[264,128]{1,0:T(8,128)S(1)}, f32[264,128]{1,0:T(8,128)}, u32[]{:S(2)}, u32[]{:S(2)}) collective-permute-start(f32[264,128]{1,0:T(8,128)S(1)} %get-tuple-element.60), channel_id=1, source_target_pairs={{0,2},{1,3},{2,0},{3,1},{4,5},{5,4},{6,7},{7,6},{8,10},{9,11},{10,... | collective-permute-start | bytes 405512 | tf_op jit(solution)/shard_map/ppermute | solution.py:321
  149.8 6.5 %collective-permute-start.10 = (f32[264,128]{1,0:T(8,128)S(1)}, f32[264,128]{1,0:T(8,128)S(1)}, u32[]{:S(2)}, u32[]{:S(2)}) collective-permute-start(f32[264,128]{1,0:T(8,128)S(1)} %add_add_fusion.1), channel_id=1, source_target_pairs={{0,24},{4,28},{8,16},{12,20},{16,8},{20,12},{24,0},{28,4},{1,25},{... | collective-permute-start | bytes 405512 | tf_op jit(solution)/shard_map/ppermute | solution.py:16
  152.1 11.1 %collective-permute-start.11 = (f32[264,128]{1,0:T(8,128)S(1)}, f32[264,128]{1,0:T(8,128)}, u32[]{:S(2)}, u32[]{:S(2)}) collective-permute-start(f32[264,128]{1,0:T(8,128)S(1)} %add_add_fusion.1), channel_id=1, source_target_pairs={{0,8},{4,12},{8,0},{12,4},{16,24},{20,28},{24,16},{28,20},{1,9},{5... | collective-permute-start | bytes 405512 | tf_op jit(solution)/shard_map/ppermute | solution.py:16
  152.1 11.1 %collective-permute-start.12 = (f32[264,128]{1,0:T(8,128)S(1)}, f32[264,128]{1,0:T(8,128)}, u32[]{:S(2)}, u32[]{:S(2)}) collective-permute-start(f32[264,128]{1,0:T(8,128)S(1)} %add_add_fusion.1), channel_id=1, source_target_pairs={{0,16},{4,20},{8,24},{12,28},{16,0},{20,4},{24,8},{28,12},{1,17},{... | collective-permute-start | bytes 405512 | tf_op jit(solution)/shard_map/ppermute | solution.py:16
  156.3 6.8 %copy-start.6 = (f32[264,128]{1,0:T(8,128)}, f32[264,128]{1,0:T(8,128)S(1)}, u32[]{:S(2)}) copy-start(f32[264,128]{1,0:T(8,128)S(1)} %collective-permute-done.10) | copy-start | bytes 405508
  164.9 5.7 %collective-permute-start.13 = (f32[264,128]{1,0:T(8,128)}, f32[264,128]{1,0:T(8,128)S(1)}, u32[]{:S(2)}, u32[]{:S(2)}) collective-permute-start(f32[264,128]{1,0:T(8,128)} %get-tuple-element.53), channel_id=1, source_target_pairs={{0,3},{1,2},{2,1},{3,0},{4,7},{5,6},{6,5},{7,4},{8,11},{9,10},{10,... | collective-permute-start | bytes 405512 | tf_op jit(solution)/shard_map/ppermute | solution.py:321
  165.1 7.9 %collective-permute-start.14 = (f32[264,128]{1,0:T(8,128)}, f32[264,128]{1,0:T(8,128)S(1)}, u32[]{:S(2)}, u32[]{:S(2)}) collective-permute-start(f32[264,128]{1,0:T(8,128)} %get-tuple-element.53), channel_id=1, source_target_pairs={{0,1},{1,0},{2,3},{3,2},{4,6},{5,7},{6,4},{7,5},{8,9},{9,8},{10,11... | collective-permute-start | bytes 405512 | tf_op jit(solution)/shard_map/ppermute | solution.py:321
  166.9 6.8 %collective-permute-start.15 = (f32[264,128]{1,0:T(8,128)}, f32[264,128]{1,0:T(8,128)S(1)}, u32[]{:S(2)}, u32[]{:S(2)}) collective-permute-start(f32[264,128]{1,0:T(8,128)} %get-tuple-element.53), channel_id=1, source_target_pairs={{0,2},{1,3},{2,0},{3,1},{4,5},{5,4},{6,7},{7,6},{8,10},{9,11},{10,... | collective-permute-start | bytes 405512 | tf_op jit(solution)/shard_map/ppermute | solution.py:321
  173.7 3.1 %collective-permute-start.16 = (f32[1056,128]{1,0:T(8,128)S(1)}, f32[1056,128]{1,0:T(8,128)S(1)}, u32[]{:S(2)}, u32[]{:S(2)}) collective-permute-start(f32[1056,128]{1,0:T(8,128)S(1)} %bitcast.15), channel_id=1, source_target_pairs={{0,4},{4,0},{8,12},{12,8},{16,20},{20,16},{24,28},{28,24},{1,5},{5... | collective-permute-start | bytes 1622024 | tf_op jit(solution)/shard_map/ppermute | solution.py:16
  176.8 1.6 copy-start.1
  178.4 1.1 copy-start.3
  179.5 1.0 copy-start.4
  198.7 8.0 %collective-permute-start.17 = (f32[24,2048]{1,0:T(8,128)S(1)}, f32[24,2048]{1,0:T(8,128)S(1)}, u32[]{:S(2)}, u32[]{:S(2)}) collective-permute-start(f32[24,2048]{1,0:T(8,128)S(1)} %get-tuple-element.46), channel_id=1, source_target_pairs={{0,24},{4,28},{8,16},{12,20},{16,8},{20,12},{24,0},{28,4},{1,25},{... | collective-permute-start | bytes 589832 | tf_op jit(solution)/shard_map/ppermute | solution.py:16
  199.5 12.2 %collective-permute-start.18 = (f32[24,2048]{1,0:T(8,128)S(1)}, f32[24,2048]{1,0:T(8,128)S(1)}, u32[]{:S(2)}, u32[]{:S(2)}) collective-permute-start(f32[24,2048]{1,0:T(8,128)S(1)} %get-tuple-element.47), channel_id=1, source_target_pairs={{0,8},{4,12},{8,0},{12,4},{16,24},{20,28},{24,16},{28,20},{1,9},{5... | collective-permute-start | bytes 589832 | tf_op jit(solution)/shard_map/ppermute | solution.py:16
  199.6 17.2 %collective-permute-start.19 = (f32[24,2048]{1,0:T(8,128)S(1)}, f32[24,2048]{1,0:T(8,128)S(1)}, u32[]{:S(2)}, u32[]{:S(2)}) collective-permute-start(f32[24,2048]{1,0:T(8,128)S(1)} %get-tuple-element.48), channel_id=1, source_target_pairs={{0,16},{4,20},{8,24},{12,28},{16,0},{20,4},{24,8},{28,12},{1,17},{... | collective-permute-start | bytes 589832 | tf_op jit(solution)/shard_map/ppermute | solution.py:16
  217.5 2.8 %collective-permute-start.20 = (f32[12,8192]{1,0:T(8,128)S(1)}, f32[12,8192]{1,0:T(8,128)S(1)}, u32[]{:S(2)}, u32[]{:S(2)}) collective-permute-start(f32[12,8192]{1,0:T(8,128)S(1)} %get-tuple-element.51), channel_id=1, source_target_pairs={{0,4},{4,0},{8,12},{12,8},{16,20},{20,16},{24,28},{28,24},{1,5},{5... | collective-permute-start | bytes 1179656 | tf_op jit(solution)/shard_map/ppermute | solution.py:16

commit v9 on v8

--- a/solution.py
+++ b/solution.py
@@ -81,22 +81,31 @@
     return places, at, at + strip
 
 
-def add_gram(starts, width, place_ref, blocks, whole, parts, packed, base_ref):
-    high_out, low_out, high_ref, low_ref, sems = parts
+def add_gram(starts, place_ref, blocks, whole, parts, packed, base):
+    high_out, low_out, high_ref, low_ref, sems, *staged = parts
     zs = len(blocks)
-    n = whole.shape[0]
+    n, width = whole.shape
     deep = n // zs
     z = place_ref[0]
-    for bits, (block, start) in enumerate(zip(blocks, starts)):
-        if deep % 8 == 0:
-            whole[pl.ds(pl.multiple_of((z ^ bits) * deep, 8), deep), :] = block[:, start : start + width]
-            continue
-        for here in range(zs):
-
-            @pl.when(z == here)
-            def _():
-                at = (here ^ bits) * deep
-                whole[at : at + deep, :] = block[:, start : start + width]
+
+    def fetch(bits):
+        source = blocks[bits].at[:, pl.ds(starts[bits], width)]
+        target = staged[0].at[bits] if staged else whole.at[pl.ds(pl.multiple_of((z ^ bits) * deep, 8), deep)]
+        return pltpu.make_async_copy(source, target, sems.at[2 + bits])
+
+    fetches = [fetch(bits) for bits in range(zs)]
+    if base is not None:
+        fetches.append(pltpu.make_async_copy(base[0], base[1], sems.at[2 + zs]))
+    for copy in fetches:
+        copy.start()
+    for copy in fetches:
+        copy.wait()
+    for here in range(zs if staged else 0):
+
+        @pl.when(z == here)
+        def _():
+            for bits in range(zs):
+                whole[(here ^ bits) * deep : (here ^ bits) * deep + deep, :] = staged[0][bits]
 
     places, corner, size = layout(n)
     edge = n // 128 * 128
@@ -116,7 +125,7 @@
 
     def put(at, value):
         rows = slice(at, at + value.shape[0])
-        packed[rows, :] = value if base_ref is None else value + base_ref[rows, :]
+        packed[rows, :] = value if base is None else value + base[1][rows, :]
 
     for start in range(0, edge, 256):
         last = start + 256 >= edge
@@ -134,14 +143,15 @@
         save.wait()
 
 
-def early_kernel(starts, width, place_ref, *refs):
-    blocks, (packed, *parts, whole) = refs[: len(starts)], refs[len(starts) :]
-    add_gram(starts, width, place_ref, blocks, whole, parts, packed, None)
-
-
-def late_kernel(starts, width, place_ref, base_ref, *refs):
-    blocks, (mine_ref, theirs_ref, *parts, whole, packed) = refs[: len(starts)], refs[len(starts) :]
-    add_gram(starts, width, place_ref, blocks, whole, parts, packed, base_ref)
+def early_kernel(starts, place_ref, *refs):
+    blocks, (packed, high_out, low_out, whole, *parts) = refs[: len(starts)], refs[len(starts) :]
+    add_gram(starts, place_ref, blocks, whole, [high_out, low_out, *parts], packed, None)
+
+
+def late_kernel(starts, place_ref, base_ref, *refs):
+    blocks, (mine_ref, theirs_ref, high_out, low_out) = refs[: len(starts)], refs[len(starts) : len(starts) + 4]
+    packed, base, whole, *parts = refs[len(starts) + 4 :]
+    add_gram(starts, place_ref, blocks, whole, [high_out, low_out, *parts], packed, (base_ref, base))
     half = mine_ref.shape[0]
     core = place_ref[1]
     mine_ref[...] = packed[pl.ds(pl.multiple_of(core * half, 8), half), :]
@@ -149,25 +159,27 @@
 
 
 def gram_part(place, base, blocks, starts, width):
-    n = blocks[0].shape[0] * len(blocks)
+    zs, deep = len(blocks), blocks[0].shape[0]
+    n = zs * deep
     size = layout(n)[2]
-    vmem = pl.BlockSpec(memory_space=pltpu.VMEM)
+    vmem, hbm = pl.BlockSpec(memory_space=pltpu.VMEM), pl.BlockSpec(memory_space=pltpu.HBM)
     parts = [jax.ShapeDtypeStruct((n, width), jnp.bfloat16)] * 2
-    scratch = [pltpu.VMEM((n, width), jnp.bfloat16)] * 2
-    scratch += [pltpu.SemaphoreType.DMA((2,)), pltpu.VMEM((n, width), jnp.float32)]
+    scratch = [pltpu.VMEM((n, width), jnp.float32)] + [pltpu.VMEM((n, width), jnp.bfloat16)] * 2
+    scratch += [pltpu.SemaphoreType.DMA((3 + zs,))]
+    scratch += [pltpu.VMEM((zs, deep, width), jnp.float32)] if deep % 8 else []
     if base is None:
         kernel, sums, first = early_kernel, [jax.ShapeDtypeStruct((size, 128), jnp.float32)], []
     else:
         half = jax.ShapeDtypeStruct((size // 2, 128), jnp.float32)
         kernel, sums, first = late_kernel, [half, half], [base]
-        scratch.append(pltpu.VMEM((size, 128), jnp.float32))
+        scratch = [pltpu.VMEM((size, 128), jnp.float32)] * 2 + scratch
     return pl.pallas_call(
-        functools.partial(kernel, starts, width),
+        functools.partial(kernel, starts),
         out_shape=[*sums, *parts],
-        in_specs=[pl.BlockSpec(memory_space=pltpu.SMEM)] + [vmem] * (len(first) + len(blocks)),
-        out_specs=[vmem] * len(sums) + [pl.BlockSpec(memory_space=pltpu.HBM)] * 2,
+        in_specs=[pl.BlockSpec(memory_space=pltpu.SMEM)] + [hbm] * (len(first) + len(blocks)),
+        out_specs=[vmem] * len(sums) + [hbm] * 2,
         scratch_shapes=scratch,
-        compiler_params=pltpu.CompilerParams(vmem_limit_bytes=24 * 2**20),
+        compiler_params=pltpu.CompilerParams(vmem_limit_bytes=48 * 2**20),
         cost_estimate=pl.CostEstimate(flops=6 * n * n * width, bytes_accessed=8 * n * width, transcendentals=0),
         name="gram_early" if base is None else "gram_late",
     )(place, *first, *blocks)
@@ -301,7 +313,7 @@
         + [pltpu.VMEM((n, n), jnp.bfloat16)] * 2
         + [pltpu.VMEM((n, part), jnp.bfloat16)] * 2
         + [pltpu.VMEM((rank, part), jnp.float32), pltpu.SemaphoreType.DMA((4,))],
-        compiler_params=pltpu.CompilerParams(vmem_limit_bytes=24 * 2**20),
+        compiler_params=pltpu.CompilerParams(vmem_limit_bytes=50 * 2**20),
         name="iterations",
     )(place, mine, other, start, *parts)
 

time: 222 us -> 211 us (0.950)
  local copies, waits for them, and re-layouts: 10.1 us -> 3.52 us
  other arithmetic: 6.84 us -> 3.11 us
    unnamed x18 -> x10, local copies, waits for them, and re-layouts: 6.65 us -> 0.02 us
  transfers between devices with their start and end apart: 21 -> 21, of which waited for: 16 -> 17; matrix products, arithmetic and copies ran while one was open for 1% -> 1% of each run, Pallas kernels for 3% -> 4%
where the time goes in v9:
time: 211 us; the launch traced here: 210 us
  waiting for transfers between devices  118 us (56%)
  starting transfers between devices  55.3 us (26%)
  Pallas kernels  29.9 us (14%)
  local copies, waits for them, and re-layouts  3.52 us (2%)
  other arithmetic  3.11 us (1%)
    ppermute x15, waiting for transfers between devices, swap(): return lax.ppermute(x, axis, [(i, i ^ bits) for i in range(size)])  105 us
    ppermute x15, starting transfers between devices, swap(): return lax.ppermute(x, axis, [(i, i ^ bits) for i in range(size)])  49.9 us
    pallas_call x1, Pallas kernels, iterations(): pl.pallas_call(functools.partial(iterations_kernel, iters, zs), out_shape...  17.7 us
    ppermute x6, waiting for transfers between devices, swap_rest(): return lax.ppermute(x, ('fibre', 'rest'), pairs)  12.4 us
    pallas_call x2, Pallas kernels, gram_part(): pl.pallas_call(functools.partial(kernel, starts), out_shape=[*sums, *part...  10.4 us
    ppermute x6, starting transfers between devices, swap_rest(): return lax.ppermute(x, ('fibre', 'rest'), pairs)  5.43 us
  transfers between devices with their start and end apart: 21, of which 17 were waited for; matrix products, arithmetic and copies ran while one was open for 1% of the time, Pallas kernels for 4%

profile of v9, /device:TPU:1, one launch (start us, length us, event | category | flops | bytes accessed | tf_op | source)
XLA Modules:
  0.0 210.3 jit_solution(5267950048522046804)
XLA Ops:
  0.7 1.5 constant_dynamic-slice_fusion.6
  2.4 1.8 constant_dynamic-slice_fusion.5
  4.6 1.6 maximum_select_fusion
  6.5 4.6 %collective-permute-start.4 = (f32[168,2048]{1,0:T(8,128)S(1)}, f32[168,2048]{1,0:T(8,128)S(1)}, u32[]{:S(2)}, u32[]{:S(2)}) collective-permute-start(f32[168,2048]{1,0:T(8,128)S(1)} %maximum_select_fusion), channel_id=1, source_target_pairs={{0,24},{4,28},{8,16},{12,20},{16,8},{20,12},{24,0},{28,4},{1,25},{... | collective-permute-start | bytes 4128776 | tf_op jit(solution)/shard_map/ppermute | solution.py:16
  12.3 1.9 collective-permute-start.2
  14.2 2.3 %collective-permute-start.3 = (f32[168,1536]{1,0:T(8,128)S(1)}, f32[168,1536]{1,0:T(8,128)S(1)}, u32[]{:S(2)}, u32[]{:S(2)}) collective-permute-start(f32[168,1536]{1,0:T(8,128)S(1)} %get-tuple-element.33), channel_id=1, source_target_pairs={{0,16},{4,20},{8,24},{12,28},{16,0},{20,4},{24,8},{28,12},{1,17},{... | collective-permute-start | bytes 3096584 | tf_op jit(solution)/shard_map/ppermute | solution.py:16
  16.5 25.2 %collective-permute-done.4.refs_3_ = f32[168,2048]{1,0:T(8,128)S(1)} collective-permute-done((f32[168,2048]{1,0:T(8,128)S(1)}, f32[168,2048]{1,0:T(8,128)S(1)}, u32[]{:S(2)}, u32[]{:S(2)}) %collective-permute-start.4) | collective-permute-done | bytes 1376288 | tf_op jit(solution)/shard_map/ppermute | solution.py:16
  41.7 29.5 %collective-permute-start.5 = (f32[168,512]{1,0:T(8,128)S(1)}, f32[168,512]{1,0:T(8,128)S(1)}, u32[]{:S(2)}, u32[]{:S(2)}) collective-permute-start(f32[168,512]{1,0:T(8,128)S(1)} %get-tuple-element.38), channel_id=1, source_target_pairs={{0,16},{4,20},{8,24},{12,28},{16,0},{20,4},{24,8},{28,12},{1,17},{... | collective-permute-start | bytes 1032200 | tf_op jit(solution)/shard_map/ppermute | solution.py:16
  71.2 50.3 %collective-permute-done.3.refs_2_ = f32[168,1536]{1,0:T(8,128)S(1)} collective-permute-done((f32[168,1536]{1,0:T(8,128)S(1)}, f32[168,1536]{1,0:T(8,128)S(1)}, u32[]{:S(2)}, u32[]{:S(2)}) %collective-permute-start.3) | collective-permute-done | bytes 1032224 | tf_op jit(solution)/shard_map/ppermute | solution.py:16
  121.5 6.5 %gram_early.1 = (f32[2112,128]{1,0:T(8,128)S(1)}, bf16[672,1536]{1,0:T(8,128)(2,1)}, bf16[672,1536]{1,0:T(8,128)(2,1)}) custom-call(s32[2]{0:T(128)S(1)} %pad_add_fusion.place_ref, f32[168,2048]{1,0:T(8,128)S(1)} %get-tuple-element.31.refs_0_, f32[168,2048]{1,0:T(8,128)S(1)} %collective-permute-done.2.refs_1_, ...), custom_call_target="tpu_custom_call" | custom-call | flops 4161798144 | bytes 8257536 | tf_op jit(solution)/shard_map/gram_early/pallas_call | solution.py:176
  128.9 3.9 %gram_late.1 = (f32[1056,128]{1,0:T(8,128)S(1)}, f32[1056,128]{1,0:T(8,128)S(1)}, bf16[672,512]{1,0:T(8,128)(2,1)S(1)}, bf16[672,512]{1,0:T(8,128)(2,1)S(1)}) custom-call(s32[2]{0:T(128)S(1)} %pad_add_fusion.place_ref, f32[2112,128]{1,0:T(8,128)S(1)} %get-tuple-element.37.base_ref, f32[168,2048]{1,0:T(8,128)S(1)} %get-tuple-element.31.refs_0_, ...), custom_call_target="tpu_custom_call" | custom-call | flops 1387266048 | bytes 2752512 | tf_op jit(solution)/shard_map/gram_late/pallas_call | solution.py:176
  132.8 1.1 collective-permute-start.6
  133.9 1.6 collective-permute-done.6
  135.6 2.2 %collective-permute-start.7 = (f32[264,128]{1,0:T(8,128)S(1)}, f32[264,128]{1,0:T(8,128)S(1)}, u32[]{:S(2)}, u32[]{:S(2)}) collective-permute-start(f32[264,128]{1,0:T(8,128)S(1)} %get-tuple-element.59), channel_id=1, source_target_pairs={{0,3},{1,2},{2,1},{3,0},{4,7},{5,6},{6,5},{7,4},{8,11},{9,10},{10,... | collective-permute-start | bytes 405512 | tf_op jit(solution)/shard_map/ppermute | solution.py:333
  138.3 3.0 %collective-permute-done.7 = f32[264,128]{1,0:T(8,128)S(1)} collective-permute-done((f32[264,128]{1,0:T(8,128)S(1)}, f32[264,128]{1,0:T(8,128)S(1)}, u32[]{:S(2)}, u32[]{:S(2)}) %collective-permute-start.7) | collective-permute-done | bytes 135200 | tf_op jit(solution)/shard_map/ppermute | solution.py:333
  141.4 3.5 %collective-permute-done.8 = f32[264,128]{1,0:T(8,128)S(1)} collective-permute-done((f32[264,128]{1,0:T(8,128)S(1)}, f32[264,128]{1,0:T(8,128)S(1)}, u32[]{:S(2)}, u32[]{:S(2)}) %collective-permute-start.8) | collective-permute-done | bytes 135200 | tf_op jit(solution)/shard_map/ppermute | solution.py:333
  144.9 2.3 %collective-permute-start.10 = (f32[264,128]{1,0:T(8,128)S(1)}, f32[264,128]{1,0:T(8,128)S(1)}, u32[]{:S(2)}, u32[]{:S(2)}) collective-permute-start(f32[264,128]{1,0:T(8,128)S(1)} %add_add_fusion.1), channel_id=1, source_target_pairs={{0,24},{4,28},{8,16},{12,20},{16,8},{20,12},{24,0},{28,4},{1,25},{... | collective-permute-start | bytes 405512 | tf_op jit(solution)/shard_map/ppermute | solution.py:16
  147.2 1.4 collective-permute-start.12
  148.5 2.8 %collective-permute-done.10 = f32[264,128]{1,0:T(8,128)S(1)} collective-permute-done((f32[264,128]{1,0:T(8,128)S(1)}, f32[264,128]{1,0:T(8,128)S(1)}, u32[]{:S(2)}, u32[]{:S(2)}) %collective-permute-start.10) | collective-permute-done | bytes 135200 | tf_op jit(solution)/shard_map/ppermute | solution.py:16
  151.3 6.8 %collective-permute-done.11 = f32[264,128]{1,0:T(8,128)S(1)} collective-permute-done((f32[264,128]{1,0:T(8,128)S(1)}, f32[264,128]{1,0:T(8,128)S(1)}, u32[]{:S(2)}, u32[]{:S(2)}) %collective-permute-start.11) | collective-permute-done | bytes 135200 | tf_op jit(solution)/shard_map/ppermute | solution.py:16
  158.5 1.7 collective-permute-start.14
  160.9 2.8 %collective-permute-done.13 = f32[264,128]{1,0:T(8,128)S(1)} collective-permute-done((f32[264,128]{1,0:T(8,128)S(1)}, f32[264,128]{1,0:T(8,128)S(1)}, u32[]{:S(2)}, u32[]{:S(2)}) %collective-permute-start.13) | collective-permute-done | bytes 135200 | tf_op jit(solution)/shard_map/ppermute | solution.py:333
  163.8 2.2 %collective-permute-done.14 = f32[264,128]{1,0:T(8,128)S(1)} collective-permute-done((f32[264,128]{1,0:T(8,128)S(1)}, f32[264,128]{1,0:T(8,128)S(1)}, u32[]{:S(2)}, u32[]{:S(2)}) %collective-permute-start.14) | collective-permute-done | bytes 135200 | tf_op jit(solution)/shard_map/ppermute | solution.py:333
  166.9 1.5 collective-permute-start.16
  168.4 1.6 collective-permute-done.16.other_ref
  170.0 17.7 %iterations.1 = (f32[96,672]{1,0:T(8,128)}, f32[24,2048]{1,0:T(8,128)S(1)}, f32[24,2048]{1,0:T(8,128)S(1)}, f32[24,2048]{1,0:T(8,128)S(1)}, f32[24,2048]{1,0:T(8,128)S(1)}) custom-call(s32[2]{0:T(128)S(1)} %pad_add_fusion.place_ref, f32[1056,128]{1,0:T(8,128)S(1)} %bitcast.16, f32[1056,128]{1,0:T(8,128)S(1)} %collective-permute-done.16.other_ref, ...), custom_call_target="tpu_custom_call" | custom-call | tf_op jit(solution)/shard_map/iterations/pallas_call | solution.py:306
  188.5 2.8 %collective-permute-start.19 = (f32[24,2048]{1,0:T(8,128)S(1)}, f32[24,2048]{1,0:T(8,128)S(1)}, u32[]{:S(2)}, u32[]{:S(2)}) collective-permute-start(f32[24,2048]{1,0:T(8,128)S(1)} %get-tuple-element.48), channel_id=1, source_target_pairs={{0,16},{4,20},{8,24},{12,28},{16,0},{20,4},{24,8},{28,12},{1,17},{... | collective-permute-start | bytes 589832 | tf_op jit(solution)/shard_map/ppermute | solution.py:16
  191.3 4.4 %collective-permute-done.17.refs_0_ = f32[24,2048]{1,0:T(8,128)S(1)} collective-permute-done((f32[24,2048]{1,0:T(8,128)S(1)}, f32[24,2048]{1,0:T(8,128)S(1)}, u32[]{:S(2)}, u32[]{:S(2)}) %collective-permute-start.17) | collective-permute-done | bytes 196640 | tf_op jit(solution)/shard_map/ppermute | solution.py:16
  195.7 4.9 %collective-permute-done.18.refs_1_ = f32[24,2048]{1,0:T(8,128)S(1)} collective-permute-done((f32[24,2048]{1,0:T(8,128)S(1)}, f32[24,2048]{1,0:T(8,128)S(1)}, u32[]{:S(2)}, u32[]{:S(2)}) %collective-permute-start.18) | collective-permute-done | bytes 196640 | tf_op jit(solution)/shard_map/ppermute | solution.py:16
  200.6 5.1 %collective-permute-done.19.refs_2_ = f32[24,2048]{1,0:T(8,128)S(1)} collective-permute-done((f32[24,2048]{1,0:T(8,128)S(1)}, f32[24,2048]{1,0:T(8,128)S(1)}, u32[]{:S(2)}, u32[]{:S(2)}) %collective-permute-start.19) | collective-permute-done | bytes 196640 | tf_op jit(solution)/shard_map/ppermute | solution.py:16
  206.4 1.3 collective-permute-start.20
  207.7 1.5 collective-permute-done.20
  (40 shorter events, 8.0 us)
Async XLA Ops:
  0.7 10.6 %slice-start = ((s8[5767168]{0:T(1024)(128)(4,1)}), s8[1572864]{0:T(1024)(128)(4,1)S(1)}, s32[]{:S(2)}) async-start(s8[5767168]{0:T(1024)(128)(4,1)} %bitcast.13), calls=%async_computation | async-start | bytes 3145728
  2.2 2.4 %collective-permute-start = (f32[84,2048]{1,0:T(8,128)S(1)}, f32[84,2048]{1,0:T(8,128)}, u32[]{:S(2)}, u32[]{:S(2)}) collective-permute-start(f32[84,2048]{1,0:T(8,128)S(1)} %get-tuple-element.29), channel_id=1, source_target_pairs={{0,4},{4,0},{8,12},{12,8},{16,20},{20,16},{24,28},{28,24},{1,5},{5... | collective-permute-start | bytes 2064392 | tf_op jit(solution)/shard_map/ppermute | solution.py:16
  2.4 8.9 %slice-start.1 = ((s8[5767168]{0:T(1024)(128)(4,1)}), s8[4194304]{0:T(1024)(128)(4,1)S(1)}, s32[]{:S(2)}) async-start(s8[5767168]{0:T(1024)(128)(4,1)} %bitcast.13), calls=%async_computation.1 | async-start | bytes 8388608
  6.3 5.0 %collective-permute-start.1 = (f32[84,6144]{1,0:T(8,128)S(1)}, f32[84,6144]{1,0:T(8,128)S(1)}, u32[]{:S(2)}, u32[]{:S(2)}) collective-permute-start(f32[84,6144]{1,0:T(8,128)S(1)} %pad_maximum_fusion), channel_id=1, source_target_pairs={{0,4},{4,0},{8,12},{12,8},{16,20},{20,16},{24,28},{28,24},{1,5},{5... | collective-permute-start | bytes 6193160 | tf_op jit(solution)/shard_map/ppermute | solution.py:16
  6.5 35.1 %collective-permute-start.4 = (f32[168,2048]{1,0:T(8,128)S(1)}, f32[168,2048]{1,0:T(8,128)S(1)}, u32[]{:S(2)}, u32[]{:S(2)}) collective-permute-start(f32[168,2048]{1,0:T(8,128)S(1)} %maximum_select_fusion), channel_id=1, source_target_pairs={{0,24},{4,28},{8,16},{12,20},{16,8},{20,12},{24,0},{28,4},{1,25},{... | collective-permute-start | bytes 4128776 | tf_op jit(solution)/shard_map/ppermute | solution.py:16
  12.3 109.2 %collective-permute-start.2 = (f32[168,2048]{1,0:T(8,128)S(1)}, f32[168,2048]{1,0:T(8,128)S(1)}, u32[]{:S(2)}, u32[]{:S(2)}) collective-permute-start(f32[168,2048]{1,0:T(8,128)S(1)} %get-tuple-element.32), channel_id=1, source_target_pairs={{0,8},{4,12},{8,0},{12,4},{16,24},{20,28},{24,16},{28,20},{1,9},{5... | collective-permute-start | bytes 4128776 | tf_op jit(solution)/shard_map/ppermute | solution.py:16
  14.2 107.3 %collective-permute-start.3 = (f32[168,1536]{1,0:T(8,128)S(1)}, f32[168,1536]{1,0:T(8,128)S(1)}, u32[]{:S(2)}, u32[]{:S(2)}) collective-permute-start(f32[168,1536]{1,0:T(8,128)S(1)} %get-tuple-element.33), channel_id=1, source_target_pairs={{0,16},{4,20},{8,24},{12,28},{16,0},{20,4},{24,8},{28,12},{1,17},{... | collective-permute-start | bytes 3096584 | tf_op jit(solution)/shard_map/ppermute | solution.py:16
  41.7 79.9 %copy-start.2 = (f32[168,2048]{1,0:T(8,128)}, f32[168,2048]{1,0:T(8,128)S(1)}, u32[]{:S(2)}) copy-start(f32[168,2048]{1,0:T(8,128)S(1)} %collective-permute-done.4.refs_3_) | copy-start | bytes 4128772
  41.7 87.2 %collective-permute-start.5 = (f32[168,512]{1,0:T(8,128)S(1)}, f32[168,512]{1,0:T(8,128)S(1)}, u32[]{:S(2)}, u32[]{:S(2)}) collective-permute-start(f32[168,512]{1,0:T(8,128)S(1)} %get-tuple-element.38), channel_id=1, source_target_pairs={{0,16},{4,20},{8,24},{12,28},{16,0},{20,4},{24,8},{28,12},{1,17},{... | collective-permute-start | bytes 1032200 | tf_op jit(solution)/shard_map/ppermute | solution.py:16
  121.5 6.5 %copy-start = (f32[168,2048]{1,0:T(8,128)}, f32[168,2048]{1,0:T(8,128)S(1)}, u32[]{:S(2)}) copy-start(f32[168,2048]{1,0:T(8,128)S(1)} %collective-permute-done.2.refs_1_) | copy-start | bytes 4128772
  132.8 2.6 %collective-permute-start.6 = (f32[1056,128]{1,0:T(8,128)S(1)}, f32[1056,128]{1,0:T(8,128)S(1)}, u32[]{:S(2)}, u32[]{:S(2)}) collective-permute-start(f32[1056,128]{1,0:T(8,128)S(1)} %get-tuple-element.40), channel_id=1, source_target_pairs={{0,4},{4,0},{8,12},{12,8},{16,20},{20,16},{24,28},{28,24},{1,5},{5... | collective-permute-start | bytes 1622024 | tf_op jit(solution)/shard_map/ppermute | solution.py:16
  135.6 5.8 %collective-permute-start.7 = (f32[264,128]{1,0:T(8,128)S(1)}, f32[264,128]{1,0:T(8,128)S(1)}, u32[]{:S(2)}, u32[]{:S(2)}) collective-permute-start(f32[264,128]{1,0:T(8,128)S(1)} %get-tuple-element.59), channel_id=1, source_target_pairs={{0,3},{1,2},{2,1},{3,0},{4,7},{5,6},{6,5},{7,4},{8,11},{9,10},{10,... | collective-permute-start | bytes 405512 | tf_op jit(solution)/shard_map/ppermute | solution.py:333
  137.8 7.0 %collective-permute-start.8 = (f32[264,128]{1,0:T(8,128)S(1)}, f32[264,128]{1,0:T(8,128)S(1)}, u32[]{:S(2)}, u32[]{:S(2)}) collective-permute-start(f32[264,128]{1,0:T(8,128)S(1)} %get-tuple-element.61), channel_id=1, source_target_pairs={{0,1},{1,0},{2,3},{3,2},{4,6},{5,7},{6,4},{7,5},{8,9},{9,8},{10,11... | collective-permute-start | bytes 405512 | tf_op jit(solution)/shard_map/ppermute | solution.py:333
  138.1 6.8 %collective-permute-start.9 = (f32[264,128]{1,0:T(8,128)S(1)}, f32[264,128]{1,0:T(8,128)S(1)}, u32[]{:S(2)}, u32[]{:S(2)}) collective-permute-start(f32[264,128]{1,0:T(8,128)S(1)} %get-tuple-element.60), channel_id=1, source_target_pairs={{0,2},{1,3},{2,0},{3,1},{4,5},{5,4},{6,7},{7,6},{8,10},{9,11},{10,... | collective-permute-start | bytes 405512 | tf_op jit(solution)/shard_map/ppermute | solution.py:333
  138.3 31.7 %copy-start.1 = (f32[672,96]{0,1:T(8,128)S(1)}, f32[672,96]{0,1:T(8,128)}, u32[]{:S(2)}) copy-start(f32[672,96]{0,1:T(8,128)} %param.3) | copy-start | bytes 774148
  144.9 6.4 %collective-permute-start.10 = (f32[264,128]{1,0:T(8,128)S(1)}, f32[264,128]{1,0:T(8,128)S(1)}, u32[]{:S(2)}, u32[]{:S(2)}) collective-permute-start(f32[264,128]{1,0:T(8,128)S(1)} %add_add_fusion.1), channel_id=1, source_target_pairs={{0,24},{4,28},{8,16},{12,20},{16,8},{20,12},{24,0},{28,4},{1,25},{... | collective-permute-start | bytes 405512 | tf_op jit(solution)/shard_map/ppermute | solution.py:16
  147.2 11.0 %collective-permute-start.11 = (f32[264,128]{1,0:T(8,128)S(1)}, f32[264,128]{1,0:T(8,128)S(1)}, u32[]{:S(2)}, u32[]{:S(2)}) collective-permute-start(f32[264,128]{1,0:T(8,128)S(1)} %add_add_fusion.1), channel_id=1, source_target_pairs={{0,8},{4,12},{8,0},{12,4},{16,24},{20,28},{24,16},{28,20},{1,9},{5... | collective-permute-start | bytes 405512 | tf_op jit(solution)/shard_map/ppermute | solution.py:16
  147.2 11.0 %collective-permute-start.12 = (f32[264,128]{1,0:T(8,128)S(1)}, f32[264,128]{1,0:T(8,128)S(1)}, u32[]{:S(2)}, u32[]{:S(2)}) collective-permute-start(f32[264,128]{1,0:T(8,128)S(1)} %add_add_fusion.1), channel_id=1, source_target_pairs={{0,16},{4,20},{8,24},{12,28},{16,0},{20,4},{24,8},{28,12},{1,17},{... | collective-permute-start | bytes 405512 | tf_op jit(solution)/shard_map/ppermute | solution.py:16
  158.2 5.6 %collective-permute-start.13 = (f32[264,128]{1,0:T(8,128)S(1)}, f32[264,128]{1,0:T(8,128)S(1)}, u32[]{:S(2)}, u32[]{:S(2)}) collective-permute-start(f32[264,128]{1,0:T(8,128)S(1)} %get-tuple-element.53), channel_id=1, source_target_pairs={{0,3},{1,2},{2,1},{3,0},{4,7},{5,6},{6,5},{7,4},{8,11},{9,10},{10,... | collective-permute-start | bytes 405512 | tf_op jit(solution)/shard_map/ppermute | solution.py:333
  158.5 7.5 %collective-permute-start.14 = (f32[264,128]{1,0:T(8,128)S(1)}, f32[264,128]{1,0:T(8,128)S(1)}, u32[]{:S(2)}, u32[]{:S(2)}) collective-permute-start(f32[264,128]{1,0:T(8,128)S(1)} %get-tuple-element.53), channel_id=1, source_target_pairs={{0,1},{1,0},{2,3},{3,2},{4,6},{5,7},{6,4},{7,5},{8,9},{9,8},{10,11... | collective-permute-start | bytes 405512 | tf_op jit(solution)/shard_map/ppermute | solution.py:333
  160.2 6.6 %collective-permute-start.15 = (f32[264,128]{1,0:T(8,128)S(1)}, f32[264,128]{1,0:T(8,128)S(1)}, u32[]{:S(2)}, u32[]{:S(2)}) collective-permute-start(f32[264,128]{1,0:T(8,128)S(1)} %get-tuple-element.53), channel_id=1, source_target_pairs={{0,2},{1,3},{2,0},{3,1},{4,5},{5,4},{6,7},{7,6},{8,10},{9,11},{10,... | collective-permute-start | bytes 405512 | tf_op jit(solution)/shard_map/ppermute | solution.py:333
  166.9 3.1 %collective-permute-start.16 = (f32[1056,128]{1,0:T(8,128)S(1)}, f32[1056,128]{1,0:T(8,128)S(1)}, u32[]{:S(2)}, u32[]{:S(2)}) collective-permute-start(f32[1056,128]{1,0:T(8,128)S(1)} %bitcast.15), channel_id=1, source_target_pairs={{0,4},{4,0},{8,12},{12,8},{16,20},{20,16},{24,28},{28,24},{1,5},{5... | collective-permute-start | bytes 1622024 | tf_op jit(solution)/shard_map/ppermute | solution.py:16
  187.7 8.0 %collective-permute-start.17 = (f32[24,2048]{1,0:T(8,128)S(1)}, f32[24,2048]{1,0:T(8,128)S(1)}, u32[]{:S(2)}, u32[]{:S(2)}) collective-permute-start(f32[24,2048]{1,0:T(8,128)S(1)} %get-tuple-element.46), channel_id=1, source_target_pairs={{0,24},{4,28},{8,16},{12,20},{16,8},{20,12},{24,0},{28,4},{1,25},{... | collective-permute-start | bytes 589832 | tf_op jit(solution)/shard_map/ppermute | solution.py:16
  188.4 12.2 %collective-permute-start.18 = (f32[24,2048]{1,0:T(8,128)S(1)}, f32[24,2048]{1,0:T(8,128)S(1)}, u32[]{:S(2)}, u32[]{:S(2)}) collective-permute-start(f32[24,2048]{1,0:T(8,128)S(1)} %get-tuple-element.47), channel_id=1, source_target_pairs={{0,8},{4,12},{8,0},{12,4},{16,24},{20,28},{24,16},{28,20},{1,9},{5... | collective-permute-start | bytes 589832 | tf_op jit(solution)/shard_map/ppermute | solution.py:16
  188.5 17.2 %collective-permute-start.19 = (f32[24,2048]{1,0:T(8,128)S(1)}, f32[24,2048]{1,0:T(8,128)S(1)}, u32[]{:S(2)}, u32[]{:S(2)}) collective-permute-start(f32[24,2048]{1,0:T(8,128)S(1)} %get-tuple-element.48), channel_id=1, source_target_pairs={{0,16},{4,20},{8,24},{12,28},{16,0},{20,4},{24,8},{28,12},{1,17},{... | collective-permute-start | bytes 589832 | tf_op jit(solution)/shard_map/ppermute | solution.py:16
  206.4 2.8 %collective-permute-start.20 = (f32[12,8192]{1,0:T(8,128)S(1)}, f32[12,8192]{1,0:T(8,128)S(1)}, u32[]{:S(2)}, u32[]{:S(2)}) collective-permute-start(f32[12,8192]{1,0:T(8,128)S(1)} %get-tuple-element.51), channel_id=1, source_target_pairs={{0,4},{4,0},{8,12},{12,8},{16,20},{20,16},{24,28},{28,24},{1,5},{5... | collective-permute-start | bytes 1179656 | tf_op jit(solution)/shard_map/ppermute | solution.py:16

commit v10 on v9

--- a/solution.py
+++ b/solution.py
@@ -62,7 +62,7 @@
         in_specs=[pl.BlockSpec(memory_space=pltpu.SMEM), pl.BlockSpec(memory_space=pltpu.HBM), vmem],
         out_specs=[vmem] * len(pieces),
         scratch_shapes=[pltpu.VMEM((zs, rows, part), jnp.float32), pltpu.SemaphoreType.DMA((zs,))],
-        compiler_params=pltpu.CompilerParams(vmem_limit_bytes=24 * 2**20),
+        compiler_params=pltpu.CompilerParams(vmem_limit_bytes=50 * 2**20),
         cost_estimate=pl.CostEstimate(flops=0, bytes_accessed=100_000_000, transcendentals=0),
         name="prepare",
     )(place, slab, got)
@@ -74,11 +74,22 @@
 
 
 def layout(n):
-    places, at, strip = [], 0, n % 128
-    for j in range(n // 128):
-        places.append((at, 128 * (j + 1), at + 128 * (j + 1)))
-        at += 128 * (j + 1) + strip
-    return places, at, at + strip
+    blocks, strip = n // 128, n % 128
+    above, strips, at = [], [], 0
+    for j in range(blocks):
+        above.append(at)
+        strips.append(at + 128 * j)
+        at += 128 * j + strip
+    folded = [at + 128 * k for k in range((blocks + 1) // 2)]
+    diagonals = at + 128 * len(folded)
+    corner = diagonals + 8
+    if blocks % 2 and strip <= 64:
+        return above, strips, folded, diagonals, folded[-1] + 128 - strip, -(-corner // 64) * 64
+    return above, strips, folded, diagonals, corner, -(-(corner + strip) // 64) * 64
+
+
+def square(op):
+    return op(lax.broadcasted_iota(jnp.int32, (128, 128), 0), lax.broadcasted_iota(jnp.int32, (128, 128), 1))
 
 
 def add_gram(starts, place_ref, blocks, whole, parts, packed, base):
@@ -94,10 +105,11 @@
         return pltpu.make_async_copy(source, target, sems.at[2 + bits])
 
     fetches = [fetch(bits) for bits in range(zs)]
-    if base is not None:
-        fetches.append(pltpu.make_async_copy(base[0], base[1], sems.at[2 + zs]))
     for copy in fetches:
         copy.start()
+    if base is not None:
+        base_copy = pltpu.make_async_copy(base[0], base[1], sems.at[2 + zs])
+        base_copy.start()
     for copy in fetches:
         copy.wait()
     for here in range(zs if staged else 0):
@@ -107,7 +119,7 @@
             for bits in range(zs):
                 whole[(here ^ bits) * deep : (here ^ bits) * deep + deep, :] = staged[0][bits]
 
-    places, corner, size = layout(n)
+    above, strips, folded, diagonals, corner, size = layout(n)
     edge = n // 128 * 128
     high_ref[...], low_ref[...] = split(whole[...])
     saves = [
@@ -127,18 +139,42 @@
         rows = slice(at, at + value.shape[0])
         packed[rows, :] = value if base is None else value + base[1][rows, :]
 
+    if base is not None:
+        base_copy.wait()
+    squares = []
     for start in range(0, edge, 256):
         last = start + 256 >= edge
         stop = min(start + 256, edge)
         upper = product(0, n if last else stop, start, n if last else stop)
         for j in range(start // 128, stop // 128):
-            at, rows, _ = places[j]
-            put(at, upper[:rows, 128 * j - start : 128 * j - start + 128])
+            columns = slice(128 * j - start, 128 * j - start + 128)
+            if j:
+                put(above[j], upper[: 128 * j, columns])
+            squares.append(upper[128 * j : 128 * j + 128, columns])
+    rest = jnp.zeros((0, 128), jnp.float32)
     if n > edge:
         strip = upper[:, edge - start :]
-        for j, (_, _, at) in enumerate(places):
+        for j, at in enumerate(strips):
             put(at, strip[128 * j : 128 * j + 128].T)
-        put(corner, jnp.pad(strip[edge:], ((0, 0), (0, 128 - (n - edge)))))
+        rest = jnp.pad(strip[edge:], ((0, 0), (0, 128 - (n - edge))))
+    diagonal_rows = jnp.zeros((8, 128), jnp.float32)
+    row = lax.broadcasted_iota(jnp.int32, (8, 128), 0)
+    for k, at in enumerate(folded):
+        value = squares[2 * k]
+        if 2 * k + 1 < len(squares):
+            other = squares[2 * k + 1]
+            value = jnp.where(square(jnp.less_equal), value, other)
+            diagonal = jnp.sum(jnp.where(square(jnp.equal), other, 0.0), axis=0, keepdims=True)
+            diagonal_rows = jnp.where(row == k, diagonal, diagonal_rows)
+        elif corner < diagonals:
+            value = jnp.where(square(jnp.less_equal), value, jnp.pad(rest, ((128 - (n - edge), 0), (0, 0))))
+        put(at, value)
+    put(diagonals, diagonal_rows)
+    if n > edge and corner > diagonals:
+        put(corner, rest)
+    filled = diagonals + 8 if corner < diagonals else corner + n - edge
+    if filled < size:
+        packed[filled:size, :] = jnp.zeros((size - filled, 128), jnp.float32)
     for save in saves:
         save.wait()
 
@@ -161,7 +197,7 @@
 def gram_part(place, base, blocks, starts, width):
     zs, deep = len(blocks), blocks[0].shape[0]
     n = zs * deep
-    size = layout(n)[2]
+    size = layout(n)[-1]
     vmem, hbm = pl.BlockSpec(memory_space=pltpu.VMEM), pl.BlockSpec(memory_space=pltpu.HBM)
     parts = [jax.ShapeDtypeStruct((n, width), jnp.bfloat16)] * 2
     scratch = [pltpu.VMEM((n, width), jnp.float32)] + [pltpu.VMEM((n, width), jnp.bfloat16)] * 2
@@ -245,22 +281,30 @@
         return lax.dot_general(a, b, (dims, ((), ())), precision=HIGHEST, preferred_element_type=jnp.float32)
 
     n = gram.shape[0]
-    places, corner, size = layout(n)
+    above, strips, folded, diagonals, corner, size = layout(n)
     edge = n // 128 * 128
     half = size // 2
     core = place_ref[1]
     packed[pl.ds(pl.multiple_of(core * half, 8), half), :] = mine_ref[...]
     packed[pl.ds(pl.multiple_of((1 - core) * half, 8), half), :] = other_ref[...]
-    for j, (at, rows, strip) in enumerate(places):
+    for j, (at, strip) in enumerate(zip(above, strips)):
         cols = slice(128 * j, 128 * j + 128)
-        gram[:rows, cols] = packed[at : at + rows, :]
+        if j:
+            gram[: 128 * j, cols] = packed[at : at + 128 * j, :]
         for i in range(j):
             gram[cols, 128 * i : 128 * i + 128] = packed[at + 128 * i : at + 128 * i + 128, :].T
+        fold = packed[folded[j // 2] : folded[j // 2] + 128, :]
+        if j % 2 == 0:
+            gram[cols, cols] = jnp.where(square(jnp.less_equal), fold, fold.T)
+        else:
+            diagonal = packed[diagonals : diagonals + 8, :][j // 2 : j // 2 + 1, :]
+            fold = jnp.where(square(jnp.greater), fold, fold.T)
+            gram[cols, cols] = jnp.where(square(jnp.equal), diagonal, fold)
         if n > edge:
             gram[edge:, cols] = packed[strip : strip + n - edge, :]
             gram[cols, edge:] = packed[strip : strip + n - edge, :].T
     if n > edge:
-        gram[edge:, edge:] = packed[corner:size, : n - edge]
+        gram[edge:, edge:] = packed[corner : corner + n - edge, : n - edge]
 
     high[...], low[...] = split(gram[...])
 
@@ -309,7 +353,7 @@
         + [jax.ShapeDtypeStruct((rank // zs, part), jnp.float32)] * zs,
         in_specs=[pl.BlockSpec(memory_space=pltpu.SMEM)] + [vmem] * 3 + [hbm] * 4,
         out_specs=[vmem] * (1 + zs),
-        scratch_shapes=[pltpu.VMEM((layout(n)[2], 128), jnp.float32), pltpu.VMEM((n, n), jnp.float32)]
+        scratch_shapes=[pltpu.VMEM((layout(n)[-1], 128), jnp.float32), pltpu.VMEM((n, n), jnp.float32)]
         + [pltpu.VMEM((n, n), jnp.bfloat16)] * 2
         + [pltpu.VMEM((n, part), jnp.bfloat16)] * 2
         + [pltpu.VMEM((rank, part), jnp.float32), pltpu.SemaphoreType.DMA((4,))],

time: 211 us -> 207 us (0.981)
  waiting for transfers between devices: 118 us -> 110 us
  local copies, waits for them, and re-layouts: 3.52 us -> 6.45 us
    ppermute x15, waiting for transfers between devices: 105 us -> 98.5 us  [swap(): return lax.ppermute(x, axis, [(i, i ^ bits) for i in range(size)])]
    pallas_call x1, Pallas kernels: 1.05 us -> 4.38 us  [prepare(): pl.pallas_call(functools.partial(prepare_kernel, cuts, pieces), out_shape...]
    unnamed x10, local copies, waits for them, and re-layouts: 0.02 us -> 3.24 us
  transfers between devices with their start and end apart: 21 -> 21, of which waited for: 17 -> 17; matrix products, arithmetic and copies ran while one was open for 1% -> 1% of each run, Pallas kernels for 4% -> 5%
where the time goes in v10:
time: 207 us; the launch traced here: 206 us
  waiting for transfers between devices  110 us (53%)
  starting transfers between devices  55.8 us (27%)
  Pallas kernels  32 us (15%)
  local copies, waits for them, and re-layouts  6.45 us (3%)
    ppermute x15, waiting for transfers between devices, swap(): return lax.ppermute(x, axis, [(i, i ^ bits) for i in range(size)])  98.5 us
    ppermute x15, starting transfers between devices, swap(): return lax.ppermute(x, axis, [(i, i ^ bits) for i in range(size)])  50.2 us
    pallas_call x1, Pallas kernels, iterations(): pl.pallas_call(functools.partial(iterations_kernel, iters, zs), out_shape...  17.7 us
    ppermute x6, waiting for transfers between devices, swap_rest(): return lax.ppermute(x, ('fibre', 'rest'), pairs)  11 us
    pallas_call x2, Pallas kernels, gram_part(): pl.pallas_call(functools.partial(kernel, starts), out_shape=[*sums, *part...  9.28 us
    ppermute x6, starting transfers between devices, swap_rest(): return lax.ppermute(x, ('fibre', 'rest'), pairs)  5.58 us
    pallas_call x1, Pallas kernels, prepare(): pl.pallas_call(functools.partial(prepare_kernel, cuts, pieces), out_shape...  4.38 us
  transfers between devices with their start and end apart: 21, of which 17 were waited for; matrix products, arithmetic and copies ran while one was open for 1% of the time, Pallas kernels for 5%

profile of v10, /device:TPU:1, one launch (start us, length us, event | category | flops | bytes accessed | tf_op | source)
XLA Modules:
  0.0 206.2 jit_solution(10135593068751502788)
XLA Ops:
  0.7 1.4 constant_dynamic-slice_fusion.6
  2.2 1.7 constant_dynamic-slice_fusion.5
  4.8 4.6 %collective-permute-start.4 = (f32[168,2048]{1,0:T(8,128)S(1)}, f32[168,2048]{1,0:T(8,128)S(1)}, u32[]{:S(2)}, u32[]{:S(2)}) collective-permute-start(f32[168,2048]{1,0:T(8,128)S(1)} %maximum_select_fusion), channel_id=1, source_target_pairs={{0,24},{4,28},{8,16},{12,20},{16,8},{20,12},{24,0},{28,4},{1,25},{... | collective-permute-start | bytes 4128776 | tf_op jit(solution)/shard_map/ppermute | solution.py:16
  9.5 1.4 copy-done.4
  10.9 4.4 %prepare.1 = (f32[168,1536]{1,0:T(8,128)S(1)}, f32[168,512]{1,0:T(8,128)S(1)}, f32[168,2048]{1,0:T(8,128)S(1)}, f32[168,2048]{1,0:T(8,128)}) custom-call(s32[2]{0:T(128)S(1)} %pad_add_fusion.place_ref, f32[84,16384]{1,0:T(8,128)} %slab_ref, f32[84,6144]{1,0:T(8,128)} %copy-done.4), custom_call_target="tpu_custom_call" | custom-call | bytes 100000000 | tf_op jit(solution)/shard_map/prepare/pallas_call | solution.py:59
  15.3 1.9 collective-permute-start.2
  17.2 2.3 %collective-permute-start.3 = (f32[168,1536]{1,0:T(8,128)S(1)}, f32[168,1536]{1,0:T(8,128)S(1)}, u32[]{:S(2)}, u32[]{:S(2)}) collective-permute-start(f32[168,1536]{1,0:T(8,128)S(1)} %get-tuple-element.33), channel_id=1, source_target_pairs={{0,16},{4,20},{8,24},{12,28},{16,0},{20,4},{24,8},{28,12},{1,17},{... | collective-permute-start | bytes 3096584 | tf_op jit(solution)/shard_map/ppermute | solution.py:16
  19.5 20.5 %collective-permute-done.4.refs_3_ = f32[168,2048]{1,0:T(8,128)S(1)} collective-permute-done((f32[168,2048]{1,0:T(8,128)S(1)}, f32[168,2048]{1,0:T(8,128)S(1)}, u32[]{:S(2)}, u32[]{:S(2)}) %collective-permute-start.4) | collective-permute-done | bytes 1376288 | tf_op jit(solution)/shard_map/ppermute | solution.py:16
  40.0 29.5 %collective-permute-start.5 = (f32[168,512]{1,0:T(8,128)S(1)}, f32[168,512]{1,0:T(8,128)S(1)}, u32[]{:S(2)}, u32[]{:S(2)}) collective-permute-start(f32[168,512]{1,0:T(8,128)S(1)} %get-tuple-element.38), channel_id=1, source_target_pairs={{0,16},{4,20},{8,24},{12,28},{16,0},{20,4},{24,8},{28,12},{1,17},{... | collective-permute-start | bytes 1032200 | tf_op jit(solution)/shard_map/ppermute | solution.py:16
  69.5 50.3 %collective-permute-done.3.refs_2_ = f32[168,1536]{1,0:T(8,128)S(1)} collective-permute-done((f32[168,1536]{1,0:T(8,128)S(1)}, f32[168,1536]{1,0:T(8,128)S(1)}, u32[]{:S(2)}, u32[]{:S(2)}) %collective-permute-start.3) | collective-permute-done | bytes 1032224 | tf_op jit(solution)/shard_map/ppermute | solution.py:16
  119.8 1.8 copy-done.1
  121.7 5.4 %gram_early.1 = (f32[1856,128]{1,0:T(8,128)S(1)}, bf16[672,1536]{1,0:T(8,128)(2,1)}, bf16[672,1536]{1,0:T(8,128)(2,1)}) custom-call(s32[2]{0:T(128)S(1)} %pad_add_fusion.place_ref, f32[168,2048]{1,0:T(8,128)S(1)} %copy-done.1, f32[168,2048]{1,0:T(8,128)S(1)} %collective-permute-done.2.refs_1_, f32[168,1536]{1,0:T(8,128)S(1)} %collective-permute-done.3.refs_2_, ...), custom_call_target="tpu_custom_call" | custom-call | flops 4161798144 | bytes 8257536 | tf_op jit(solution)/shard_map/gram_early/pallas_call | solution.py:212
  127.2 3.9 %gram_late.1 = (f32[928,128]{1,0:T(8,128)S(1)}, f32[928,128]{1,0:T(8,128)S(1)}, bf16[672,512]{1,0:T(8,128)(2,1)S(1)}, bf16[672,512]{1,0:T(8,128)(2,1)S(1)}) custom-call(s32[2]{0:T(128)S(1)} %pad_add_fusion.place_ref, f32[1856,128]{1,0:T(8,128)S(1)} %get-tuple-element.37.base_ref, f32[168,2048]{1,0:T(8,128)S(1)} %copy-done.1, f32[168,2048]{1,0:T(8,128)} %copy-done.2, ...), custom_call_target="tpu_custom_call" | custom-call | flops 1387266048 | bytes 2752512 | tf_op jit(solution)/shard_map/gram_late/pallas_call | solution.py:212
  131.1 1.5 collective-permute-start.6
  132.7 1.5 collective-permute-done.6
  134.2 2.2 %collective-permute-start.7 = (f32[232,128]{1,0:T(8,128)S(1)}, f32[232,128]{1,0:T(8,128)S(1)}, u32[]{:S(2)}, u32[]{:S(2)}) collective-permute-start(f32[232,128]{1,0:T(8,128)S(1)} %get-tuple-element.59), channel_id=1, source_target_pairs={{0,3},{1,2},{2,1},{3,0},{4,7},{5,6},{6,5},{7,4},{8,11},{9,10},{10,... | collective-permute-start | bytes 356360 | tf_op jit(solution)/shard_map/ppermute | solution.py:377
  136.9 2.7 %collective-permute-done.7 = f32[232,128]{1,0:T(8,128)S(1)} collective-permute-done((f32[232,128]{1,0:T(8,128)S(1)}, f32[232,128]{1,0:T(8,128)S(1)}, u32[]{:S(2)}, u32[]{:S(2)}) %collective-permute-start.7) | collective-permute-done | bytes 118816 | tf_op jit(solution)/shard_map/ppermute | solution.py:377
  139.6 2.9 %collective-permute-done.8 = f32[232,128]{1,0:T(8,128)S(1)} collective-permute-done((f32[232,128]{1,0:T(8,128)S(1)}, f32[232,128]{1,0:T(8,128)S(1)}, u32[]{:S(2)}, u32[]{:S(2)}) %collective-permute-start.8) | collective-permute-done | bytes 118816 | tf_op jit(solution)/shard_map/ppermute | solution.py:377
  142.6 2.3 %collective-permute-start.10 = (f32[232,128]{1,0:T(8,128)S(1)}, f32[232,128]{1,0:T(8,128)S(1)}, u32[]{:S(2)}, u32[]{:S(2)}) collective-permute-start(f32[232,128]{1,0:T(8,128)S(1)} %add_add_fusion.1), channel_id=1, source_target_pairs={{0,24},{4,28},{8,16},{12,20},{16,8},{20,12},{24,0},{28,4},{1,25},{... | collective-permute-start | bytes 356360 | tf_op jit(solution)/shard_map/ppermute | solution.py:16
  144.9 1.3 collective-permute-start.12
  146.2 2.0 collective-permute-done.10
  148.2 6.4 %collective-permute-done.11 = f32[232,128]{1,0:T(8,128)S(1)} collective-permute-done((f32[232,128]{1,0:T(8,128)S(1)}, f32[232,128]{1,0:T(8,128)S(1)}, u32[]{:S(2)}, u32[]{:S(2)}) %collective-permute-start.11) | collective-permute-done | bytes 118816 | tf_op jit(solution)/shard_map/ppermute | solution.py:16
  157.6 2.4 %collective-permute-done.13 = f32[232,128]{1,0:T(8,128)S(1)} collective-permute-done((f32[232,128]{1,0:T(8,128)S(1)}, f32[232,128]{1,0:T(8,128)S(1)}, u32[]{:S(2)}, u32[]{:S(2)}) %collective-permute-start.13) | collective-permute-done | bytes 118816 | tf_op jit(solution)/shard_map/ppermute | solution.py:377
  160.0 2.4 %collective-permute-done.14 = f32[232,128]{1,0:T(8,128)S(1)} collective-permute-done((f32[232,128]{1,0:T(8,128)S(1)}, f32[232,128]{1,0:T(8,128)S(1)}, u32[]{:S(2)}, u32[]{:S(2)}) %collective-permute-start.14) | collective-permute-done | bytes 118816 | tf_op jit(solution)/shard_map/ppermute | solution.py:377
  163.1 1.4 collective-permute-start.16
  164.5 1.5 collective-permute-done.16.other_ref
  166.0 17.7 %iterations.1 = (f32[96,672]{1,0:T(8,128)}, f32[24,2048]{1,0:T(8,128)S(1)}, f32[24,2048]{1,0:T(8,128)S(1)}, f32[24,2048]{1,0:T(8,128)S(1)}, f32[24,2048]{1,0:T(8,128)S(1)}) custom-call(s32[2]{0:T(128)S(1)} %pad_add_fusion.place_ref, f32[928,128]{1,0:T(8,128)S(1)} %bitcast.14, f32[928,128]{1,0:T(8,128)S(1)} %collective-permute-done.16.other_ref, ...), custom_call_target="tpu_custom_call" | custom-call | tf_op jit(solution)/shard_map/iterations/pallas_call | solution.py:350
  184.5 2.8 %collective-permute-start.19 = (f32[24,2048]{1,0:T(8,128)S(1)}, f32[24,2048]{1,0:T(8,128)S(1)}, u32[]{:S(2)}, u32[]{:S(2)}) collective-permute-start(f32[24,2048]{1,0:T(8,128)S(1)} %get-tuple-element.48), channel_id=1, source_target_pairs={{0,16},{4,20},{8,24},{12,28},{16,0},{20,4},{24,8},{28,12},{1,17},{... | collective-permute-start | bytes 589832 | tf_op jit(solution)/shard_map/ppermute | solution.py:16
  187.3 4.4 %collective-permute-done.17.refs_0_ = f32[24,2048]{1,0:T(8,128)S(1)} collective-permute-done((f32[24,2048]{1,0:T(8,128)S(1)}, f32[24,2048]{1,0:T(8,128)S(1)}, u32[]{:S(2)}, u32[]{:S(2)}) %collective-permute-start.17) | collective-permute-done | bytes 196640 | tf_op jit(solution)/shard_map/ppermute | solution.py:16
  191.7 4.9 %collective-permute-done.18.refs_1_ = f32[24,2048]{1,0:T(8,128)S(1)} collective-permute-done((f32[24,2048]{1,0:T(8,128)S(1)}, f32[24,2048]{1,0:T(8,128)S(1)}, u32[]{:S(2)}, u32[]{:S(2)}) %collective-permute-start.18) | collective-permute-done | bytes 196640 | tf_op jit(solution)/shard_map/ppermute | solution.py:16
  196.6 5.0 %collective-permute-done.19.refs_2_ = f32[24,2048]{1,0:T(8,128)S(1)} collective-permute-done((f32[24,2048]{1,0:T(8,128)S(1)}, f32[24,2048]{1,0:T(8,128)S(1)}, u32[]{:S(2)}, u32[]{:S(2)}) %collective-permute-start.19) | collective-permute-done | bytes 196640 | tf_op jit(solution)/shard_map/ppermute | solution.py:16
  203.6 1.5 collective-permute-done.20
  (39 shorter events, 9.3 us)
Async XLA Ops:
  2.1 2.3 %collective-permute-start = (f32[84,2048]{1,0:T(8,128)S(1)}, f32[84,2048]{1,0:T(8,128)S(1)}, u32[]{:S(2)}, u32[]{:S(2)}) collective-permute-start(f32[84,2048]{1,0:T(8,128)S(1)} %get-tuple-element.29), channel_id=1, source_target_pairs={{0,4},{4,0},{8,12},{12,8},{16,20},{20,16},{24,28},{28,24},{1,5},{5... | collective-permute-start | bytes 2064392 | tf_op jit(solution)/shard_map/ppermute | solution.py:16
  4.5 5.0 %collective-permute-start.1 = (f32[84,6144]{1,0:T(8,128)S(1)}, f32[84,6144]{1,0:T(8,128)S(1)}, u32[]{:S(2)}, u32[]{:S(2)}) collective-permute-start(f32[84,6144]{1,0:T(8,128)S(1)} %pad_maximum_fusion), channel_id=1, source_target_pairs={{0,4},{4,0},{8,12},{12,8},{16,20},{20,16},{24,28},{28,24},{1,5},{5... | collective-permute-start | bytes 6193160 | tf_op jit(solution)/shard_map/ppermute | solution.py:16
  4.8 35.2 %collective-permute-start.4 = (f32[168,2048]{1,0:T(8,128)S(1)}, f32[168,2048]{1,0:T(8,128)S(1)}, u32[]{:S(2)}, u32[]{:S(2)}) collective-permute-start(f32[168,2048]{1,0:T(8,128)S(1)} %maximum_select_fusion), channel_id=1, source_target_pairs={{0,24},{4,28},{8,16},{12,20},{16,8},{20,12},{24,0},{28,4},{1,25},{... | collective-permute-start | bytes 4128776 | tf_op jit(solution)/shard_map/ppermute | solution.py:16
  9.5 1.4 copy-start.4
  15.3 104.5 %collective-permute-start.2 = (f32[168,2048]{1,0:T(8,128)S(1)}, f32[168,2048]{1,0:T(8,128)S(1)}, u32[]{:S(2)}, u32[]{:S(2)}) collective-permute-start(f32[168,2048]{1,0:T(8,128)S(1)} %get-tuple-element.32), channel_id=1, source_target_pairs={{0,8},{4,12},{8,0},{12,4},{16,24},{20,28},{24,16},{28,20},{1,9},{5... | collective-permute-start | bytes 4128776 | tf_op jit(solution)/shard_map/ppermute | solution.py:16
  17.2 102.6 %collective-permute-start.3 = (f32[168,1536]{1,0:T(8,128)S(1)}, f32[168,1536]{1,0:T(8,128)S(1)}, u32[]{:S(2)}, u32[]{:S(2)}) collective-permute-start(f32[168,1536]{1,0:T(8,128)S(1)} %get-tuple-element.33), channel_id=1, source_target_pairs={{0,16},{4,20},{8,24},{12,28},{16,0},{20,4},{24,8},{28,12},{1,17},{... | collective-permute-start | bytes 3096584 | tf_op jit(solution)/shard_map/ppermute | solution.py:16
  40.0 87.1 %copy-start = (f32[168,2048]{1,0:T(8,128)}, f32[168,2048]{1,0:T(8,128)S(1)}, u32[]{:S(2)}) copy-start(f32[168,2048]{1,0:T(8,128)S(1)} %collective-permute-done.4.refs_3_) | copy-start | bytes 4128772
  40.0 87.2 %collective-permute-start.5 = (f32[168,512]{1,0:T(8,128)S(1)}, f32[168,512]{1,0:T(8,128)S(1)}, u32[]{:S(2)}, u32[]{:S(2)}) collective-permute-start(f32[168,512]{1,0:T(8,128)S(1)} %get-tuple-element.38), channel_id=1, source_target_pairs={{0,16},{4,20},{8,24},{12,28},{16,0},{20,4},{24,8},{28,12},{1,17},{... | collective-permute-start | bytes 1032200 | tf_op jit(solution)/shard_map/ppermute | solution.py:16
  119.8 7.2 %copy-start.2 = (f32[168,2048]{1,0:T(8,128)}, f32[168,2048]{1,0:T(8,128)S(1)}, u32[]{:S(2)}) copy-start(f32[168,2048]{1,0:T(8,128)S(1)} %collective-permute-done.2.refs_1_) | copy-start | bytes 4128772
  119.8 1.8 copy-start.1
  131.1 3.0 %collective-permute-start.6 = (f32[928,128]{1,0:T(8,128)S(1)}, f32[928,128]{1,0:T(8,128)S(1)}, u32[]{:S(2)}, u32[]{:S(2)}) collective-permute-start(f32[928,128]{1,0:T(8,128)S(1)} %get-tuple-element.40), channel_id=1, source_target_pairs={{0,4},{4,0},{8,12},{12,8},{16,20},{20,16},{24,28},{28,24},{1,5},{5... | collective-permute-start | bytes 1425416 | tf_op jit(solution)/shard_map/ppermute | solution.py:16
  134.1 31.8 %copy-start.3 = (f32[672,96]{0,1:T(8,128)S(1)}, f32[672,96]{0,1:T(8,128)}, u32[]{:S(2)}) copy-start(f32[672,96]{0,1:T(8,128)} %param.3) | copy-start | bytes 774148
  134.2 5.4 %collective-permute-start.7 = (f32[232,128]{1,0:T(8,128)S(1)}, f32[232,128]{1,0:T(8,128)S(1)}, u32[]{:S(2)}, u32[]{:S(2)}) collective-permute-start(f32[232,128]{1,0:T(8,128)S(1)} %get-tuple-element.59), channel_id=1, source_target_pairs={{0,3},{1,2},{2,1},{3,0},{4,7},{5,6},{6,5},{7,4},{8,11},{9,10},{10,... | collective-permute-start | bytes 356360 | tf_op jit(solution)/shard_map/ppermute | solution.py:377
  136.5 6.1 %collective-permute-start.8 = (f32[232,128]{1,0:T(8,128)S(1)}, f32[232,128]{1,0:T(8,128)S(1)}, u32[]{:S(2)}, u32[]{:S(2)}) collective-permute-start(f32[232,128]{1,0:T(8,128)S(1)} %get-tuple-element.61), channel_id=1, source_target_pairs={{0,1},{1,0},{2,3},{3,2},{4,6},{5,7},{6,4},{7,5},{8,9},{9,8},{10,11... | collective-permute-start | bytes 356360 | tf_op jit(solution)/shard_map/ppermute | solution.py:377
  136.7 5.9 %collective-permute-start.9 = (f32[232,128]{1,0:T(8,128)S(1)}, f32[232,128]{1,0:T(8,128)S(1)}, u32[]{:S(2)}, u32[]{:S(2)}) collective-permute-start(f32[232,128]{1,0:T(8,128)S(1)} %get-tuple-element.60), channel_id=1, source_target_pairs={{0,2},{1,3},{2,0},{3,1},{4,5},{5,4},{6,7},{7,6},{8,10},{9,11},{10,... | collective-permute-start | bytes 356360 | tf_op jit(solution)/shard_map/ppermute | solution.py:377
  142.6 5.6 %collective-permute-start.10 = (f32[232,128]{1,0:T(8,128)S(1)}, f32[232,128]{1,0:T(8,128)S(1)}, u32[]{:S(2)}, u32[]{:S(2)}) collective-permute-start(f32[232,128]{1,0:T(8,128)S(1)} %add_add_fusion.1), channel_id=1, source_target_pairs={{0,24},{4,28},{8,16},{12,20},{16,8},{20,12},{24,0},{28,4},{1,25},{... | collective-permute-start | bytes 356360 | tf_op jit(solution)/shard_map/ppermute | solution.py:16
  144.9 9.8 %collective-permute-start.11 = (f32[232,128]{1,0:T(8,128)S(1)}, f32[232,128]{1,0:T(8,128)S(1)}, u32[]{:S(2)}, u32[]{:S(2)}) collective-permute-start(f32[232,128]{1,0:T(8,128)S(1)} %add_add_fusion.1), channel_id=1, source_target_pairs={{0,8},{4,12},{8,0},{12,4},{16,24},{20,28},{24,16},{28,20},{1,9},{5... | collective-permute-start | bytes 356360 | tf_op jit(solution)/shard_map/ppermute | solution.py:16
  144.9 9.8 %collective-permute-start.12 = (f32[232,128]{1,0:T(8,128)S(1)}, f32[232,128]{1,0:T(8,128)S(1)}, u32[]{:S(2)}, u32[]{:S(2)}) collective-permute-start(f32[232,128]{1,0:T(8,128)S(1)} %add_add_fusion.1), channel_id=1, source_target_pairs={{0,16},{4,20},{8,24},{12,28},{16,0},{20,4},{24,8},{28,12},{1,17},{... | collective-permute-start | bytes 356360 | tf_op jit(solution)/shard_map/ppermute | solution.py:16
  154.7 5.3 %collective-permute-start.13 = (f32[232,128]{1,0:T(8,128)S(1)}, f32[232,128]{1,0:T(8,128)S(1)}, u32[]{:S(2)}, u32[]{:S(2)}) collective-permute-start(f32[232,128]{1,0:T(8,128)S(1)} %get-tuple-element.53), channel_id=1, source_target_pairs={{0,3},{1,2},{2,1},{3,0},{4,7},{5,6},{6,5},{7,4},{8,11},{9,10},{10,... | collective-permute-start | bytes 356360 | tf_op jit(solution)/shard_map/ppermute | solution.py:377
  155.7 6.8 %collective-permute-start.14 = (f32[232,128]{1,0:T(8,128)S(1)}, f32[232,128]{1,0:T(8,128)S(1)}, u32[]{:S(2)}, u32[]{:S(2)}) collective-permute-start(f32[232,128]{1,0:T(8,128)S(1)} %get-tuple-element.53), channel_id=1, source_target_pairs={{0,1},{1,0},{2,3},{3,2},{4,6},{5,7},{6,4},{7,5},{8,9},{9,8},{10,11... | collective-permute-start | bytes 356360 | tf_op jit(solution)/shard_map/ppermute | solution.py:377
  157.0 6.1 %collective-permute-start.15 = (f32[232,128]{1,0:T(8,128)S(1)}, f32[232,128]{1,0:T(8,128)S(1)}, u32[]{:S(2)}, u32[]{:S(2)}) collective-permute-start(f32[232,128]{1,0:T(8,128)S(1)} %get-tuple-element.53), channel_id=1, source_target_pairs={{0,2},{1,3},{2,0},{3,1},{4,5},{5,4},{6,7},{7,6},{8,10},{9,11},{10,... | collective-permute-start | bytes 356360 | tf_op jit(solution)/shard_map/ppermute | solution.py:377
  163.1 2.9 %collective-permute-start.16 = (f32[928,128]{1,0:T(8,128)S(1)}, f32[928,128]{1,0:T(8,128)S(1)}, u32[]{:S(2)}, u32[]{:S(2)}) collective-permute-start(f32[928,128]{1,0:T(8,128)S(1)} %bitcast.13), channel_id=1, source_target_pairs={{0,4},{4,0},{8,12},{12,8},{16,20},{20,16},{24,28},{28,24},{1,5},{5... | collective-permute-start | bytes 1425416 | tf_op jit(solution)/shard_map/ppermute | solution.py:16
  183.7 8.0 %collective-permute-start.17 = (f32[24,2048]{1,0:T(8,128)S(1)}, f32[24,2048]{1,0:T(8,128)S(1)}, u32[]{:S(2)}, u32[]{:S(2)}) collective-permute-start(f32[24,2048]{1,0:T(8,128)S(1)} %get-tuple-element.46), channel_id=1, source_target_pairs={{0,24},{4,28},{8,16},{12,20},{16,8},{20,12},{24,0},{28,4},{1,25},{... | collective-permute-start | bytes 589832 | tf_op jit(solution)/shard_map/ppermute | solution.py:16
  184.4 12.3 %collective-permute-start.18 = (f32[24,2048]{1,0:T(8,128)S(1)}, f32[24,2048]{1,0:T(8,128)S(1)}, u32[]{:S(2)}, u32[]{:S(2)}) collective-permute-start(f32[24,2048]{1,0:T(8,128)S(1)} %get-tuple-element.47), channel_id=1, source_target_pairs={{0,8},{4,12},{8,0},{12,4},{16,24},{20,28},{24,16},{28,20},{1,9},{5... | collective-permute-start | bytes 589832 | tf_op jit(solution)/shard_map/ppermute | solution.py:16
  184.5 17.1 %collective-permute-start.19 = (f32[24,2048]{1,0:T(8,128)S(1)}, f32[24,2048]{1,0:T(8,128)S(1)}, u32[]{:S(2)}, u32[]{:S(2)}) collective-permute-start(f32[24,2048]{1,0:T(8,128)S(1)} %get-tuple-element.48), channel_id=1, source_target_pairs={{0,16},{4,20},{8,24},{12,28},{16,0},{20,4},{24,8},{28,12},{1,17},{... | collective-permute-start | bytes 589832 | tf_op jit(solution)/shard_map/ppermute | solution.py:16
  202.3 2.8 %collective-permute-start.20 = (f32[12,8192]{1,0:T(8,128)S(1)}, f32[12,8192]{1,0:T(8,128)S(1)}, u32[]{:S(2)}, u32[]{:S(2)}) collective-permute-start(f32[12,8192]{1,0:T(8,128)S(1)} %get-tuple-element.51), channel_id=1, source_target_pairs={{0,4},{4,0},{8,12},{12,8},{16,20},{20,16},{24,28},{28,24},{1,5},{5... | collective-permute-start | bytes 1179656 | tf_op jit(solution)/shard_map/ppermute | solution.py:16

commit v11 on v10

--- a/solution.py
+++ b/solution.py
@@ -8,8 +8,6 @@
 from jax.sharding import PartitionSpec as P
 
 ITERS = 3
-HIGH = lax.Precision.HIGH
-HIGHEST = lax.Precision.HIGHEST
 
 
 def swap(x, axis, size, bits):
@@ -71,6 +69,25 @@
 def split(x):
     high = x.astype(jnp.bfloat16)
     return high, (x - high.astype(jnp.float32)).astype(jnp.bfloat16)
+
+
+def split3(x):
+    high = x.astype(jnp.bfloat16)
+    rest = x - high.astype(jnp.float32)
+    middle = rest.astype(jnp.bfloat16)
+    return high, middle, (rest - middle.astype(jnp.float32)).astype(jnp.bfloat16)
+
+
+def contract(a, b, over_a, over_b):
+    return lax.dot_general(a, b, (((over_a,), (over_b,)), ((), ())), preferred_element_type=jnp.float32)
+
+
+def side_by_side(*parts):
+    return jnp.concatenate(parts, 1)
+
+
+def quarters(x):
+    return (x[:128, :128] + x[128:, 128:]) + (x[:128, 128:] + x[128:, :128])
 
 
 def layout(n):
@@ -277,9 +294,6 @@
     for fetch in fetches:
         fetch.start()
 
-    def times(a, b, dims):
-        return lax.dot_general(a, b, (dims, ((), ())), precision=HIGHEST, preferred_element_type=jnp.float32)
-
     n = gram.shape[0]
     above, strips, folded, diagonals, corner, size = layout(n)
     edge = n // 128 * 128
@@ -308,32 +322,37 @@
 
     high[...], low[...] = split(gram[...])
 
-    def apply_gram(x, over=0):
-        x_high, x_low = split(x)
-
-        def part(a, b):
-            return lax.dot_general(a[...], b, (((1,), (over,)), ((), ())), preferred_element_type=jnp.float32)
-
-        return part(high, x_low) + part(low, x_high) + part(high, x_high)
-
-    image = apply_gram(start_ref[...], 1)
+    rank = start_ref.shape[0]
+    x_high, x_low = split(jnp.pad(start_ref[...], ((0, 128 - rank), (0, 0))))
+    both = contract(high[...], jnp.concatenate([x_high, x_low], 0), 1, 1)
+    image = both[:, :128] + both[:, 128:] + contract(low[...], x_high, 1, 1)
     for step in range(iters):
-        small = times(image, image, ((0,), (0,)))
-        inverse = lower_inverse(jnp.pad(small, ((0, 0), (0, 128 - small.shape[1]))))[:, : small.shape[1]]
+        parts = split3(image)
+        first = side_by_side(parts[0], parts[1])
+        cross = contract(parts[0], parts[2], 0, 0)
+        small = quarters(contract(first, first, 0, 0)) + (cross + cross.T)
+        inverse = jnp.pad(lower_inverse(small[:rank]), ((0, 128 - rank), (0, 0)))
+        inv = split3(inverse)
         if step < iters - 1:
-            image = times(apply_gram(image), inverse, ((1,), (1,)))
+            both = contract(high[...], first, 1, 0)
+            image = both[:, :128] + both[:, 128:] + contract(low[...], parts[0], 1, 0)
+            parts = split3(image)
+            twice = [side_by_side(inv[0], inv[0]), side_by_side(inv[1], inv[1])]
+            both = contract(side_by_side(parts[0], parts[1]), jnp.concatenate(twice, 0), 1, 1)
+            last = contract(side_by_side(parts[0], parts[2]), side_by_side(inv[2], inv[0]), 1, 1)
+            image = both[:, :128] + both[:, 128:] + last
         else:
-            basis = times(inverse, image, ((1,), (1,)))
-
+            basis = contract(side_by_side(inv[0], inv[2]), side_by_side(parts[2], parts[0]), 1, 1)
+            basis += contract(side_by_side(inv[0], inv[1]), side_by_side(parts[1], parts[1]), 1, 1)
+            basis += contract(side_by_side(inv[0], inv[1]), side_by_side(parts[0], parts[0]), 1, 1)
+
+    basis = basis[:rank]
     factor_ref[...] = basis
     basis_high, basis_low = split(basis)
     for fetch in fetches:
         fetch.wait()
-
-    def on_columns(a, b):
-        return lax.dot_general(a, b[...], (((1,), (0,)), ((), ())), preferred_element_type=jnp.float32)
-
-    share[...] = on_columns(basis_high, columns_low) + on_columns(basis_low, columns_high) + on_columns(basis_high, columns_high)
+    both = contract(jnp.concatenate([basis_high, basis_low], 0), columns_high[...], 1, 0)
+    share[...] = both[:rank] + both[rank:] + contract(basis_high, columns_low[...], 1, 0)
     two_own = share.shape[0] // zs
     for here in range(zs):
 

time: 207 us -> 205 us (level)
  Pallas kernels: 32 us -> 29.7 us
    pallas_call x1, Pallas kernels: 17.7 us -> 15.4 us  [iterations(): pl.pallas_call(functools.partial(iterations_kernel, iters, zs), out_shape...]
where the time goes in v11:
time: 205 us; the launch traced here: 204 us
  waiting for transfers between devices  110 us (54%)
  starting transfers between devices  55.8 us (27%)
  Pallas kernels  29.7 us (14%)
  local copies, waits for them, and re-layouts  6.45 us (3%)
    ppermute x15, waiting for transfers between devices, swap(): return lax.ppermute(x, axis, [(i, i ^ bits) for i in range(size)])  98.6 us
    ppermute x15, starting transfers between devices, swap(): return lax.ppermute(x, axis, [(i, i ^ bits) for i in range(size)])  50.2 us
    pallas_call x1, Pallas kernels, iterations(): pl.pallas_call(functools.partial(iterations_kernel, iters, zs), out_shape...  15.4 us
    ppermute x6, waiting for transfers between devices, swap_rest(): return lax.ppermute(x, ('fibre', 'rest'), pairs)  11 us
    pallas_call x2, Pallas kernels, gram_part(): pl.pallas_call(functools.partial(kernel, starts), out_shape=[*sums, *part...  9.28 us
    ppermute x6, starting transfers between devices, swap_rest(): return lax.ppermute(x, ('fibre', 'rest'), pairs)  5.58 us
    pallas_call x1, Pallas kernels, prepare(): pl.pallas_call(functools.partial(prepare_kernel, cuts, pieces), out_shape...  4.38 us
  transfers between devices with their start and end apart: 21, of which 17 were waited for; matrix products, arithmetic and copies ran while one was open for 1% of the time, Pallas kernels for 5%

profile of v11, /device:TPU:1, one launch (start us, length us, event | category | flops | bytes accessed | tf_op | source)
XLA Modules:
  0.0 203.9 jit_solution(2504660699802661565)
XLA Ops:
  0.7 1.4 constant_dynamic-slice_fusion.6
  2.2 1.7 constant_dynamic-slice_fusion.5
  4.8 4.6 %collective-permute-start.4 = (f32[168,2048]{1,0:T(8,128)S(1)}, f32[168,2048]{1,0:T(8,128)S(1)}, u32[]{:S(2)}, u32[]{:S(2)}) collective-permute-start(f32[168,2048]{1,0:T(8,128)S(1)} %maximum_select_fusion), channel_id=1, source_target_pairs={{0,24},{4,28},{8,16},{12,20},{16,8},{20,12},{24,0},{28,4},{1,25},{... | collective-permute-start | bytes 4128776 | tf_op jit(solution)/shard_map/ppermute | solution.py:14
  9.5 1.4 copy-done.4
  10.9 4.4 %prepare.1 = (f32[168,1536]{1,0:T(8,128)S(1)}, f32[168,512]{1,0:T(8,128)S(1)}, f32[168,2048]{1,0:T(8,128)S(1)}, f32[168,2048]{1,0:T(8,128)}) custom-call(s32[2]{0:T(128)S(1)} %pad_add_fusion.place_ref, f32[84,16384]{1,0:T(8,128)} %slab_ref, f32[84,6144]{1,0:T(8,128)} %copy-done.4), custom_call_target="tpu_custom_call" | custom-call | bytes 100000000 | tf_op jit(solution)/shard_map/prepare/pallas_call | solution.py:57
  15.3 1.9 collective-permute-start.2
  17.2 2.3 %collective-permute-start.3 = (f32[168,1536]{1,0:T(8,128)S(1)}, f32[168,1536]{1,0:T(8,128)S(1)}, u32[]{:S(2)}, u32[]{:S(2)}) collective-permute-start(f32[168,1536]{1,0:T(8,128)S(1)} %get-tuple-element.33), channel_id=1, source_target_pairs={{0,16},{4,20},{8,24},{12,28},{16,0},{20,4},{24,8},{28,12},{1,17},{... | collective-permute-start | bytes 3096584 | tf_op jit(solution)/shard_map/ppermute | solution.py:14
  19.5 20.5 %collective-permute-done.4.refs_3_ = f32[168,2048]{1,0:T(8,128)S(1)} collective-permute-done((f32[168,2048]{1,0:T(8,128)S(1)}, f32[168,2048]{1,0:T(8,128)S(1)}, u32[]{:S(2)}, u32[]{:S(2)}) %collective-permute-start.4) | collective-permute-done | bytes 1376288 | tf_op jit(solution)/shard_map/ppermute | solution.py:14
  40.0 29.5 %collective-permute-start.5 = (f32[168,512]{1,0:T(8,128)S(1)}, f32[168,512]{1,0:T(8,128)S(1)}, u32[]{:S(2)}, u32[]{:S(2)}) collective-permute-start(f32[168,512]{1,0:T(8,128)S(1)} %get-tuple-element.38), channel_id=1, source_target_pairs={{0,16},{4,20},{8,24},{12,28},{16,0},{20,4},{24,8},{28,12},{1,17},{... | collective-permute-start | bytes 1032200 | tf_op jit(solution)/shard_map/ppermute | solution.py:14
  69.5 50.3 %collective-permute-done.3.refs_2_ = f32[168,1536]{1,0:T(8,128)S(1)} collective-permute-done((f32[168,1536]{1,0:T(8,128)S(1)}, f32[168,1536]{1,0:T(8,128)S(1)}, u32[]{:S(2)}, u32[]{:S(2)}) %collective-permute-start.3) | collective-permute-done | bytes 1032224 | tf_op jit(solution)/shard_map/ppermute | solution.py:14
  119.8 1.8 copy-done.1
  121.7 5.4 %gram_early.1 = (f32[1856,128]{1,0:T(8,128)S(1)}, bf16[672,1536]{1,0:T(8,128)(2,1)}, bf16[672,1536]{1,0:T(8,128)(2,1)}) custom-call(s32[2]{0:T(128)S(1)} %pad_add_fusion.place_ref, f32[168,2048]{1,0:T(8,128)S(1)} %copy-done.1, f32[168,2048]{1,0:T(8,128)S(1)} %collective-permute-done.2.refs_1_, f32[168,1536]{1,0:T(8,128)S(1)} %collective-permute-done.3.refs_2_, ...), custom_call_target="tpu_custom_call" | custom-call | flops 4161798144 | bytes 8257536 | tf_op jit(solution)/shard_map/gram_early/pallas_call | solution.py:229
  127.2 3.9 %gram_late.1 = (f32[928,128]{1,0:T(8,128)S(1)}, f32[928,128]{1,0:T(8,128)S(1)}, bf16[672,512]{1,0:T(8,128)(2,1)S(1)}, bf16[672,512]{1,0:T(8,128)(2,1)S(1)}) custom-call(s32[2]{0:T(128)S(1)} %pad_add_fusion.place_ref, f32[1856,128]{1,0:T(8,128)S(1)} %get-tuple-element.37.base_ref, f32[168,2048]{1,0:T(8,128)S(1)} %copy-done.1, f32[168,2048]{1,0:T(8,128)} %copy-done.2, ...), custom_call_target="tpu_custom_call" | custom-call | flops 1387266048 | bytes 2752512 | tf_op jit(solution)/shard_map/gram_late/pallas_call | solution.py:229
  131.1 1.5 collective-permute-start.6
  132.7 1.5 collective-permute-done.6
  134.2 2.2 %collective-permute-start.7 = (f32[232,128]{1,0:T(8,128)S(1)}, f32[232,128]{1,0:T(8,128)S(1)}, u32[]{:S(2)}, u32[]{:S(2)}) collective-permute-start(f32[232,128]{1,0:T(8,128)S(1)} %get-tuple-element.59), channel_id=1, source_target_pairs={{0,3},{1,2},{2,1},{3,0},{4,7},{5,6},{6,5},{7,4},{8,11},{9,10},{10,... | collective-permute-start | bytes 356360 | tf_op jit(solution)/shard_map/ppermute | solution.py:396
  136.9 2.7 %collective-permute-done.7 = f32[232,128]{1,0:T(8,128)S(1)} collective-permute-done((f32[232,128]{1,0:T(8,128)S(1)}, f32[232,128]{1,0:T(8,128)S(1)}, u32[]{:S(2)}, u32[]{:S(2)}) %collective-permute-start.7) | collective-permute-done | bytes 118816 | tf_op jit(solution)/shard_map/ppermute | solution.py:396
  139.6 2.9 %collective-permute-done.8 = f32[232,128]{1,0:T(8,128)S(1)} collective-permute-done((f32[232,128]{1,0:T(8,128)S(1)}, f32[232,128]{1,0:T(8,128)S(1)}, u32[]{:S(2)}, u32[]{:S(2)}) %collective-permute-start.8) | collective-permute-done | bytes 118816 | tf_op jit(solution)/shard_map/ppermute | solution.py:396
  142.6 2.3 %collective-permute-start.10 = (f32[232,128]{1,0:T(8,128)S(1)}, f32[232,128]{1,0:T(8,128)S(1)}, u32[]{:S(2)}, u32[]{:S(2)}) collective-permute-start(f32[232,128]{1,0:T(8,128)S(1)} %add_add_fusion.1), channel_id=1, source_target_pairs={{0,24},{4,28},{8,16},{12,20},{16,8},{20,12},{24,0},{28,4},{1,25},{... | collective-permute-start | bytes 356360 | tf_op jit(solution)/shard_map/ppermute | solution.py:14
  144.9 1.3 collective-permute-start.12
  146.2 2.0 collective-permute-done.10
  148.2 6.4 %collective-permute-done.11 = f32[232,128]{1,0:T(8,128)S(1)} collective-permute-done((f32[232,128]{1,0:T(8,128)S(1)}, f32[232,128]{1,0:T(8,128)S(1)}, u32[]{:S(2)}, u32[]{:S(2)}) %collective-permute-start.11) | collective-permute-done | bytes 118816 | tf_op jit(solution)/shard_map/ppermute | solution.py:14
  157.6 2.4 %collective-permute-done.13 = f32[232,128]{1,0:T(8,128)S(1)} collective-permute-done((f32[232,128]{1,0:T(8,128)S(1)}, f32[232,128]{1,0:T(8,128)S(1)}, u32[]{:S(2)}, u32[]{:S(2)}) %collective-permute-start.13) | collective-permute-done | bytes 118816 | tf_op jit(solution)/shard_map/ppermute | solution.py:396
  160.0 2.4 %collective-permute-done.14 = f32[232,128]{1,0:T(8,128)S(1)} collective-permute-done((f32[232,128]{1,0:T(8,128)S(1)}, f32[232,128]{1,0:T(8,128)S(1)}, u32[]{:S(2)}, u32[]{:S(2)}) %collective-permute-start.14) | collective-permute-done | bytes 118816 | tf_op jit(solution)/shard_map/ppermute | solution.py:396
  163.1 1.4 collective-permute-start.16
  164.5 1.5 collective-permute-done.16.other_ref
  166.0 15.4 %iterations.1 = (f32[96,672]{1,0:T(8,128)}, f32[24,2048]{1,0:T(8,128)S(1)}, f32[24,2048]{1,0:T(8,128)S(1)}, f32[24,2048]{1,0:T(8,128)S(1)}, f32[24,2048]{1,0:T(8,128)S(1)}) custom-call(s32[2]{0:T(128)S(1)} %pad_add_fusion.place_ref, f32[928,128]{1,0:T(8,128)S(1)} %bitcast.14, f32[928,128]{1,0:T(8,128)S(1)} %collective-permute-done.16.other_ref, ...), custom_call_target="tpu_custom_call" | custom-call | tf_op jit(solution)/shard_map/iterations/pallas_call | solution.py:369
  182.2 2.8 %collective-permute-start.19 = (f32[24,2048]{1,0:T(8,128)S(1)}, f32[24,2048]{1,0:T(8,128)S(1)}, u32[]{:S(2)}, u32[]{:S(2)}) collective-permute-start(f32[24,2048]{1,0:T(8,128)S(1)} %get-tuple-element.48), channel_id=1, source_target_pairs={{0,16},{4,20},{8,24},{12,28},{16,0},{20,4},{24,8},{28,12},{1,17},{... | collective-permute-start | bytes 589832 | tf_op jit(solution)/shard_map/ppermute | solution.py:14
  185.0 4.4 %collective-permute-done.17.refs_0_ = f32[24,2048]{1,0:T(8,128)S(1)} collective-permute-done((f32[24,2048]{1,0:T(8,128)S(1)}, f32[24,2048]{1,0:T(8,128)S(1)}, u32[]{:S(2)}, u32[]{:S(2)}) %collective-permute-start.17) | collective-permute-done | bytes 196640 | tf_op jit(solution)/shard_map/ppermute | solution.py:14
  189.4 4.9 %collective-permute-done.18.refs_1_ = f32[24,2048]{1,0:T(8,128)S(1)} collective-permute-done((f32[24,2048]{1,0:T(8,128)S(1)}, f32[24,2048]{1,0:T(8,128)S(1)}, u32[]{:S(2)}, u32[]{:S(2)}) %collective-permute-start.18) | collective-permute-done | bytes 196640 | tf_op jit(solution)/shard_map/ppermute | solution.py:14
  194.3 5.1 %collective-permute-done.19.refs_2_ = f32[24,2048]{1,0:T(8,128)S(1)} collective-permute-done((f32[24,2048]{1,0:T(8,128)S(1)}, f32[24,2048]{1,0:T(8,128)S(1)}, u32[]{:S(2)}, u32[]{:S(2)}) %collective-permute-start.19) | collective-permute-done | bytes 196640 | tf_op jit(solution)/shard_map/ppermute | solution.py:14
  201.3 1.5 collective-permute-done.20
  (39 shorter events, 9.3 us)
Async XLA Ops:
  2.1 2.3 %collective-permute-start = (f32[84,2048]{1,0:T(8,128)S(1)}, f32[84,2048]{1,0:T(8,128)S(1)}, u32[]{:S(2)}, u32[]{:S(2)}) collective-permute-start(f32[84,2048]{1,0:T(8,128)S(1)} %get-tuple-element.29), channel_id=1, source_target_pairs={{0,4},{4,0},{8,12},{12,8},{16,20},{20,16},{24,28},{28,24},{1,5},{5... | collective-permute-start | bytes 2064392 | tf_op jit(solution)/shard_map/ppermute | solution.py:14
  4.5 5.0 %collective-permute-start.1 = (f32[84,6144]{1,0:T(8,128)S(1)}, f32[84,6144]{1,0:T(8,128)S(1)}, u32[]{:S(2)}, u32[]{:S(2)}) collective-permute-start(f32[84,6144]{1,0:T(8,128)S(1)} %pad_maximum_fusion), channel_id=1, source_target_pairs={{0,4},{4,0},{8,12},{12,8},{16,20},{20,16},{24,28},{28,24},{1,5},{5... | collective-permute-start | bytes 6193160 | tf_op jit(solution)/shard_map/ppermute | solution.py:14
  4.8 35.2 %collective-permute-start.4 = (f32[168,2048]{1,0:T(8,128)S(1)}, f32[168,2048]{1,0:T(8,128)S(1)}, u32[]{:S(2)}, u32[]{:S(2)}) collective-permute-start(f32[168,2048]{1,0:T(8,128)S(1)} %maximum_select_fusion), channel_id=1, source_target_pairs={{0,24},{4,28},{8,16},{12,20},{16,8},{20,12},{24,0},{28,4},{1,25},{... | collective-permute-start | bytes 4128776 | tf_op jit(solution)/shard_map/ppermute | solution.py:14
  9.5 1.4 copy-start.4
  15.3 104.5 %collective-permute-start.2 = (f32[168,2048]{1,0:T(8,128)S(1)}, f32[168,2048]{1,0:T(8,128)S(1)}, u32[]{:S(2)}, u32[]{:S(2)}) collective-permute-start(f32[168,2048]{1,0:T(8,128)S(1)} %get-tuple-element.32), channel_id=1, source_target_pairs={{0,8},{4,12},{8,0},{12,4},{16,24},{20,28},{24,16},{28,20},{1,9},{5... | collective-permute-start | bytes 4128776 | tf_op jit(solution)/shard_map/ppermute | solution.py:14
  17.2 102.6 %collective-permute-start.3 = (f32[168,1536]{1,0:T(8,128)S(1)}, f32[168,1536]{1,0:T(8,128)S(1)}, u32[]{:S(2)}, u32[]{:S(2)}) collective-permute-start(f32[168,1536]{1,0:T(8,128)S(1)} %get-tuple-element.33), channel_id=1, source_target_pairs={{0,16},{4,20},{8,24},{12,28},{16,0},{20,4},{24,8},{28,12},{1,17},{... | collective-permute-start | bytes 3096584 | tf_op jit(solution)/shard_map/ppermute | solution.py:14
  40.0 87.1 %copy-start = (f32[168,2048]{1,0:T(8,128)}, f32[168,2048]{1,0:T(8,128)S(1)}, u32[]{:S(2)}) copy-start(f32[168,2048]{1,0:T(8,128)S(1)} %collective-permute-done.4.refs_3_) | copy-start | bytes 4128772
  40.0 87.2 %collective-permute-start.5 = (f32[168,512]{1,0:T(8,128)S(1)}, f32[168,512]{1,0:T(8,128)S(1)}, u32[]{:S(2)}, u32[]{:S(2)}) collective-permute-start(f32[168,512]{1,0:T(8,128)S(1)} %get-tuple-element.38), channel_id=1, source_target_pairs={{0,16},{4,20},{8,24},{12,28},{16,0},{20,4},{24,8},{28,12},{1,17},{... | collective-permute-start | bytes 1032200 | tf_op jit(solution)/shard_map/ppermute | solution.py:14
  119.8 7.2 %copy-start.2 = (f32[168,2048]{1,0:T(8,128)}, f32[168,2048]{1,0:T(8,128)S(1)}, u32[]{:S(2)}) copy-start(f32[168,2048]{1,0:T(8,128)S(1)} %collective-permute-done.2.refs_1_) | copy-start | bytes 4128772
  119.8 1.8 copy-start.1
  131.1 3.0 %collective-permute-start.6 = (f32[928,128]{1,0:T(8,128)S(1)}, f32[928,128]{1,0:T(8,128)S(1)}, u32[]{:S(2)}, u32[]{:S(2)}) collective-permute-start(f32[928,128]{1,0:T(8,128)S(1)} %get-tuple-element.40), channel_id=1, source_target_pairs={{0,4},{4,0},{8,12},{12,8},{16,20},{20,16},{24,28},{28,24},{1,5},{5... | collective-permute-start | bytes 1425416 | tf_op jit(solution)/shard_map/ppermute | solution.py:14
  134.1 31.8 %copy-start.3 = (f32[672,96]{0,1:T(8,128)S(1)}, f32[672,96]{0,1:T(8,128)}, u32[]{:S(2)}) copy-start(f32[672,96]{0,1:T(8,128)} %param.3) | copy-start | bytes 774148
  134.2 5.4 %collective-permute-start.7 = (f32[232,128]{1,0:T(8,128)S(1)}, f32[232,128]{1,0:T(8,128)S(1)}, u32[]{:S(2)}, u32[]{:S(2)}) collective-permute-start(f32[232,128]{1,0:T(8,128)S(1)} %get-tuple-element.59), channel_id=1, source_target_pairs={{0,3},{1,2},{2,1},{3,0},{4,7},{5,6},{6,5},{7,4},{8,11},{9,10},{10,... | collective-permute-start | bytes 356360 | tf_op jit(solution)/shard_map/ppermute | solution.py:396
  136.5 6.1 %collective-permute-start.8 = (f32[232,128]{1,0:T(8,128)S(1)}, f32[232,128]{1,0:T(8,128)S(1)}, u32[]{:S(2)}, u32[]{:S(2)}) collective-permute-start(f32[232,128]{1,0:T(8,128)S(1)} %get-tuple-element.61), channel_id=1, source_target_pairs={{0,1},{1,0},{2,3},{3,2},{4,6},{5,7},{6,4},{7,5},{8,9},{9,8},{10,11... | collective-permute-start | bytes 356360 | tf_op jit(solution)/shard_map/ppermute | solution.py:396
  136.7 5.9 %collective-permute-start.9 = (f32[232,128]{1,0:T(8,128)S(1)}, f32[232,128]{1,0:T(8,128)S(1)}, u32[]{:S(2)}, u32[]{:S(2)}) collective-permute-start(f32[232,128]{1,0:T(8,128)S(1)} %get-tuple-element.60), channel_id=1, source_target_pairs={{0,2},{1,3},{2,0},{3,1},{4,5},{5,4},{6,7},{7,6},{8,10},{9,11},{10,... | collective-permute-start | bytes 356360 | tf_op jit(solution)/shard_map/ppermute | solution.py:396
  142.6 5.6 %collective-permute-start.10 = (f32[232,128]{1,0:T(8,128)S(1)}, f32[232,128]{1,0:T(8,128)S(1)}, u32[]{:S(2)}, u32[]{:S(2)}) collective-permute-start(f32[232,128]{1,0:T(8,128)S(1)} %add_add_fusion.1), channel_id=1, source_target_pairs={{0,24},{4,28},{8,16},{12,20},{16,8},{20,12},{24,0},{28,4},{1,25},{... | collective-permute-start | bytes 356360 | tf_op jit(solution)/shard_map/ppermute | solution.py:14
  144.9 9.8 %collective-permute-start.11 = (f32[232,128]{1,0:T(8,128)S(1)}, f32[232,128]{1,0:T(8,128)S(1)}, u32[]{:S(2)}, u32[]{:S(2)}) collective-permute-start(f32[232,128]{1,0:T(8,128)S(1)} %add_add_fusion.1), channel_id=1, source_target_pairs={{0,8},{4,12},{8,0},{12,4},{16,24},{20,28},{24,16},{28,20},{1,9},{5... | collective-permute-start | bytes 356360 | tf_op jit(solution)/shard_map/ppermute | solution.py:14
  144.9 9.8 %collective-permute-start.12 = (f32[232,128]{1,0:T(8,128)S(1)}, f32[232,128]{1,0:T(8,128)S(1)}, u32[]{:S(2)}, u32[]{:S(2)}) collective-permute-start(f32[232,128]{1,0:T(8,128)S(1)} %add_add_fusion.1), channel_id=1, source_target_pairs={{0,16},{4,20},{8,24},{12,28},{16,0},{20,4},{24,8},{28,12},{1,17},{... | collective-permute-start | bytes 356360 | tf_op jit(solution)/shard_map/ppermute | solution.py:14
  154.7 5.3 %collective-permute-start.13 = (f32[232,128]{1,0:T(8,128)S(1)}, f32[232,128]{1,0:T(8,128)S(1)}, u32[]{:S(2)}, u32[]{:S(2)}) collective-permute-start(f32[232,128]{1,0:T(8,128)S(1)} %get-tuple-element.53), channel_id=1, source_target_pairs={{0,3},{1,2},{2,1},{3,0},{4,7},{5,6},{6,5},{7,4},{8,11},{9,10},{10,... | collective-permute-start | bytes 356360 | tf_op jit(solution)/shard_map/ppermute | solution.py:396
  155.7 6.8 %collective-permute-start.14 = (f32[232,128]{1,0:T(8,128)S(1)}, f32[232,128]{1,0:T(8,128)S(1)}, u32[]{:S(2)}, u32[]{:S(2)}) collective-permute-start(f32[232,128]{1,0:T(8,128)S(1)} %get-tuple-element.53), channel_id=1, source_target_pairs={{0,1},{1,0},{2,3},{3,2},{4,6},{5,7},{6,4},{7,5},{8,9},{9,8},{10,11... | collective-permute-start | bytes 356360 | tf_op jit(solution)/shard_map/ppermute | solution.py:396
  157.0 6.1 %collective-permute-start.15 = (f32[232,128]{1,0:T(8,128)S(1)}, f32[232,128]{1,0:T(8,128)S(1)}, u32[]{:S(2)}, u32[]{:S(2)}) collective-permute-start(f32[232,128]{1,0:T(8,128)S(1)} %get-tuple-element.53), channel_id=1, source_target_pairs={{0,2},{1,3},{2,0},{3,1},{4,5},{5,4},{6,7},{7,6},{8,10},{9,11},{10,... | collective-permute-start | bytes 356360 | tf_op jit(solution)/shard_map/ppermute | solution.py:396
  163.1 2.9 %collective-permute-start.16 = (f32[928,128]{1,0:T(8,128)S(1)}, f32[928,128]{1,0:T(8,128)S(1)}, u32[]{:S(2)}, u32[]{:S(2)}) collective-permute-start(f32[928,128]{1,0:T(8,128)S(1)} %bitcast.13), channel_id=1, source_target_pairs={{0,4},{4,0},{8,12},{12,8},{16,20},{20,16},{24,28},{28,24},{1,5},{5... | collective-permute-start | bytes 1425416 | tf_op jit(solution)/shard_map/ppermute | solution.py:14
  181.3 8.0 %collective-permute-start.17 = (f32[24,2048]{1,0:T(8,128)S(1)}, f32[24,2048]{1,0:T(8,128)S(1)}, u32[]{:S(2)}, u32[]{:S(2)}) collective-permute-start(f32[24,2048]{1,0:T(8,128)S(1)} %get-tuple-element.46), channel_id=1, source_target_pairs={{0,24},{4,28},{8,16},{12,20},{16,8},{20,12},{24,0},{28,4},{1,25},{... | collective-permute-start | bytes 589832 | tf_op jit(solution)/shard_map/ppermute | solution.py:14
  182.1 12.2 %collective-permute-start.18 = (f32[24,2048]{1,0:T(8,128)S(1)}, f32[24,2048]{1,0:T(8,128)S(1)}, u32[]{:S(2)}, u32[]{:S(2)}) collective-permute-start(f32[24,2048]{1,0:T(8,128)S(1)} %get-tuple-element.47), channel_id=1, source_target_pairs={{0,8},{4,12},{8,0},{12,4},{16,24},{20,28},{24,16},{28,20},{1,9},{5... | collective-permute-start | bytes 589832 | tf_op jit(solution)/shard_map/ppermute | solution.py:14
  182.2 17.2 %collective-permute-start.19 = (f32[24,2048]{1,0:T(8,128)S(1)}, f32[24,2048]{1,0:T(8,128)S(1)}, u32[]{:S(2)}, u32[]{:S(2)}) collective-permute-start(f32[24,2048]{1,0:T(8,128)S(1)} %get-tuple-element.48), channel_id=1, source_target_pairs={{0,16},{4,20},{8,24},{12,28},{16,0},{20,4},{24,8},{28,12},{1,17},{... | collective-permute-start | bytes 589832 | tf_op jit(solution)/shard_map/ppermute | solution.py:14
  200.1 2.8 %collective-permute-start.20 = (f32[12,8192]{1,0:T(8,128)S(1)}, f32[12,8192]{1,0:T(8,128)S(1)}, u32[]{:S(2)}, u32[]{:S(2)}) collective-permute-start(f32[12,8192]{1,0:T(8,128)S(1)} %get-tuple-element.51), channel_id=1, source_target_pairs={{0,4},{4,0},{8,12},{12,8},{16,20},{20,16},{24,28},{28,24},{1,5},{5... | collective-permute-start | bytes 1179656 | tf_op jit(solution)/shard_map/ppermute | solution.py:14

commit v12 on v11

--- a/solution.py
+++ b/solution.py
@@ -282,8 +282,8 @@
 
 
 def iterations_kernel(iters, zs, place_ref, mine_ref, other_ref, start_ref, *refs):
-    kept, (factor_ref, *outs) = refs[:4], refs[4 : 5 + zs]
-    packed, gram, high, low, columns_high, columns_low, share, sems = refs[5 + zs :]
+    kept, (factor_ref, *outs) = refs[:4], refs[4 : 5 + 2 * zs]
+    packed, gram, high, low, columns_high, columns_low, share, sems = refs[5 + 2 * zs :]
     early = kept[0].shape[1]
     fetches = [
         pltpu.make_async_copy(kept[0], columns_high.at[:, :early], sems.at[0]),
@@ -353,13 +353,15 @@
         fetch.wait()
     both = contract(jnp.concatenate([basis_high, basis_low], 0), columns_high[...], 1, 0)
     share[...] = both[:rank] + both[rank:] + contract(basis_high, columns_low[...], 1, 0)
-    two_own = share.shape[0] // zs
-    for here in range(zs):
-
-        @pl.when(place_ref[0] == here)
+    own, wide = outs[0].shape[0] // 2, outs[0].shape[1]
+    for here in range(2 * zs):
+
+        @pl.when(2 * place_ref[0] + place_ref[1] == here)
         def _():
             for bits, out in enumerate(outs):
-                out[...] = share[two_own * (here ^ bits) : two_own * (here ^ bits) + two_own, :]
+                rows = slice(own * (here ^ bits), own * (here ^ bits) + own)
+                out[:own, :] = share[rows, :wide]
+                out[own:, :] = share[rows, wide:]
 
 
 def iterations(place, mine, other, start, parts, iters, zs):
@@ -369,9 +371,9 @@
     return pl.pallas_call(
         functools.partial(iterations_kernel, iters, zs),
         out_shape=[jax.ShapeDtypeStruct(start.shape, jnp.float32)]
-        + [jax.ShapeDtypeStruct((rank // zs, part), jnp.float32)] * zs,
+        + [jax.ShapeDtypeStruct((rank // zs, part // 2), jnp.float32)] * (2 * zs),
         in_specs=[pl.BlockSpec(memory_space=pltpu.SMEM)] + [vmem] * 3 + [hbm] * 4,
-        out_specs=[vmem] * (1 + zs),
+        out_specs=[vmem] * (1 + 2 * zs),
         scratch_shapes=[pltpu.VMEM((layout(n)[-1], 128), jnp.float32), pltpu.VMEM((n, n), jnp.float32)]
         + [pltpu.VMEM((n, n), jnp.bfloat16)] * 2
         + [pltpu.VMEM((n, part), jnp.bfloat16)] * 2
@@ -421,27 +423,26 @@
 
 
 def assemble_kernel(distances, place_ref, *refs):
-    blocks, (mine_ref, theirs_ref) = refs[:-2], refs[-2:]
-    z, core = place_ref[0], place_ref[1]
-    own, part = mine_ref.shape[0], blocks[0].shape[1]
+    blocks, out_ref = refs[:-1], refs[-1]
+    f = 2 * place_ref[0] + place_ref[1]
+    own, wide = out_ref.shape[0], blocks[0].shape[1]
+    half = out_ref.shape[1] // 2
     for bits, block in zip(distances, blocks):
-        at = pl.multiple_of((z ^ bits) * part, 128)
-        first, last = block[:own, :], block[own:, :]
-        mine_ref[:, pl.ds(at, part)] = jnp.where(core == 0, first, last)
-        theirs_ref[:, pl.ds(at, part)] = jnp.where(core == 0, last, first)
-
-
-def assemble(place, moved):
+        source = f ^ bits
+        at = pl.multiple_of((source % 2) * half + (source // 2) * (2 * wide), 128)
+        out_ref[:, pl.ds(at, wide)] = block[:own, :]
+        out_ref[:, pl.ds(at + wide, wide)] = block[own:, :]
+
+
+def assemble(place, moved, cols):
     blocks = list(moved.values())
-    two_own, part = blocks[0].shape
     vmem = pl.BlockSpec(memory_space=pltpu.VMEM)
-    half = jax.ShapeDtypeStruct((two_own // 2, part * len(blocks)), jnp.float32)
     return pl.pallas_call(
         functools.partial(assemble_kernel, tuple(moved)),
-        out_shape=(half, half),
+        out_shape=jax.ShapeDtypeStruct((blocks[0].shape[0] // 2, cols), jnp.float32),
         in_specs=[pl.BlockSpec(memory_space=pltpu.SMEM)] + [vmem] * len(blocks),
-        out_specs=[vmem] * 2,
-        compiler_params=pltpu.CompilerParams(vmem_limit_bytes=16 * 2**20),
+        out_specs=vmem,
+        compiler_params=pltpu.CompilerParams(vmem_limit_bytes=24 * 2**20),
         name="assemble",
     )(place, *blocks)
 
@@ -485,10 +486,11 @@
     mine, theirs, *more = gram_part(place, packed, last, last_from, part - early)
     mine, other = sum_everywhere(core, mine, theirs, fibre, rest)
     factor, *blocks = iterations(place, mine, other, start_basis.T, [*parts, *more], ITERS, zs)
-    moved = {bits: swap(blocks[bits], "fibre", fibre, 2 * bits) for bits in farthest_first(zs)}
+    order = [2 * bits + d for bits in farthest_first(zs) for d in range(2)]
+    order.insert(2, 1)
+    moved = {bits: swap(blocks[bits], "fibre", fibre, bits) for bits in order}
     moved[0] = blocks[0]
-    mine, theirs = assemble(place, moved)
-    return (factor.T, in_order(core, mine, swap(theirs, "fibre", fibre, 1), 1))
+    return (factor.T, assemble(place, moved, cols))
 
 
 def solution(mesh):

time: 205 us -> 203 us (level)
  waiting for transfers between devices: 110 us -> 105 us
  starting transfers between devices: 55.8 us -> 59.4 us
    ppermute x15 -> x18, waiting for transfers between devices: 98.6 us -> 93.7 us  [swap(): return lax.ppermute(x, axis, [(i, i ^ bits) for i in range(size)])]
    ppermute x15 -> x18, starting transfers between devices: 50.2 us -> 53.8 us  [swap(): return lax.ppermute(x, axis, [(i, i ^ bits) for i in range(size)])]
  transfers between devices with their start and end apart: 21 -> 24, of which waited for: 17 -> 17; matrix products, arithmetic and copies ran while one was open for 1% -> 1% of each run, Pallas kernels for 5% -> 5%
where the time goes in v12:
time: 203 us
  waiting for transfers between devices  105 us (52%)
  starting transfers between devices  59.4 us (29%)
  Pallas kernels  30.8 us (15%)
  local copies, waits for them, and re-layouts  6.45 us (3%)
    ppermute x18, waiting for transfers between devices, swap(): return lax.ppermute(x, axis, [(i, i ^ bits) for i in range(size)])  93.7 us
    ppermute x18, starting transfers between devices, swap(): return lax.ppermute(x, axis, [(i, i ^ bits) for i in range(size)])  53.8 us
    pallas_call x1, Pallas kernels, iterations(): pl.pallas_call(functools.partial(iterations_kernel, iters, zs), out_shape...  15.5 us
    ppermute x6, waiting for transfers between devices, swap_rest(): return lax.ppermute(x, ('fibre', 'rest'), pairs)  11 us
    pallas_call x2, Pallas kernels, gram_part(): pl.pallas_call(functools.partial(kernel, starts), out_shape=[*sums, *part...  9.29 us
    ppermute x6, starting transfers between devices, swap_rest(): return lax.ppermute(x, ('fibre', 'rest'), pairs)  5.58 us
    pallas_call x1, Pallas kernels, prepare(): pl.pallas_call(functools.partial(prepare_kernel, cuts, pieces), out_shape...  4.37 us
  transfers between devices with their start and end apart: 24, of which 17 were waited for; matrix products, arithmetic and copies ran while one was open for 1% of the time, Pallas kernels for 5%

profile of v12, /device:TPU:1, one launch (start us, length us, event | category | flops | bytes accessed | tf_op | source)
XLA Modules:
  0.0 202.6 jit_solution(12119250624889624916)
XLA Ops:
  0.7 1.4 constant_dynamic-slice_fusion.6
  2.2 1.7 constant_dynamic-slice_fusion.5
  4.8 4.6 %collective-permute-start.4 = (f32[168,2048]{1,0:T(8,128)S(1)}, f32[168,2048]{1,0:T(8,128)S(1)}, u32[]{:S(2)}, u32[]{:S(2)}) collective-permute-start(f32[168,2048]{1,0:T(8,128)S(1)} %maximum_select_fusion), channel_id=1, source_target_pairs={{0,24},{4,28},{8,16},{12,20},{16,8},{20,12},{24,0},{28,4},{1,25},{... | collective-permute-start | bytes 4128776 | tf_op jit(solution)/shard_map/ppermute | solution.py:14
  10.9 4.4 %prepare.1 = (f32[168,1536]{1,0:T(8,128)S(1)}, f32[168,512]{1,0:T(8,128)S(1)}, f32[168,2048]{1,0:T(8,128)S(1)}, f32[168,2048]{1,0:T(8,128)}) custom-call(s32[2]{0:T(128)S(1)} %pad_add_fusion.place_ref, f32[84,16384]{1,0:T(8,128)} %slab_ref, f32[84,6144]{1,0:T(8,128)} %copy-done.4), custom_call_target="tpu_custom_call" | custom-call | bytes 100000000 | tf_op jit(solution)/shard_map/prepare/pallas_call | solution.py:57
  15.3 1.9 collective-permute-start.2
  17.2 2.3 %collective-permute-start.3 = (f32[168,1536]{1,0:T(8,128)S(1)}, f32[168,1536]{1,0:T(8,128)S(1)}, u32[]{:S(2)}, u32[]{:S(2)}) collective-permute-start(f32[168,1536]{1,0:T(8,128)S(1)} %get-tuple-element.35), channel_id=1, source_target_pairs={{0,16},{4,20},{8,24},{12,28},{16,0},{20,4},{24,8},{28,12},{1,17},{... | collective-permute-start | bytes 3096584 | tf_op jit(solution)/shard_map/ppermute | solution.py:14
  19.5 20.5 %collective-permute-done.4.refs_3_ = f32[168,2048]{1,0:T(8,128)S(1)} collective-permute-done((f32[168,2048]{1,0:T(8,128)S(1)}, f32[168,2048]{1,0:T(8,128)S(1)}, u32[]{:S(2)}, u32[]{:S(2)}) %collective-permute-start.4) | collective-permute-done | bytes 1376288 | tf_op jit(solution)/shard_map/ppermute | solution.py:14
  40.0 29.5 %collective-permute-start.5 = (f32[168,512]{1,0:T(8,128)S(1)}, f32[168,512]{1,0:T(8,128)S(1)}, u32[]{:S(2)}, u32[]{:S(2)}) collective-permute-start(f32[168,512]{1,0:T(8,128)S(1)} %get-tuple-element.40), channel_id=1, source_target_pairs={{0,16},{4,20},{8,24},{12,28},{16,0},{20,4},{24,8},{28,12},{1,17},{... | collective-permute-start | bytes 1032200 | tf_op jit(solution)/shard_map/ppermute | solution.py:14
  69.5 50.3 %collective-permute-done.3.refs_2_ = f32[168,1536]{1,0:T(8,128)S(1)} collective-permute-done((f32[168,1536]{1,0:T(8,128)S(1)}, f32[168,1536]{1,0:T(8,128)S(1)}, u32[]{:S(2)}, u32[]{:S(2)}) %collective-permute-start.3) | collective-permute-done | bytes 1032224 | tf_op jit(solution)/shard_map/ppermute | solution.py:14
  119.8 1.8 copy-done.1
  121.7 5.4 %gram_early.1 = (f32[1856,128]{1,0:T(8,128)S(1)}, bf16[672,1536]{1,0:T(8,128)(2,1)}, bf16[672,1536]{1,0:T(8,128)(2,1)}) custom-call(s32[2]{0:T(128)S(1)} %pad_add_fusion.place_ref, f32[168,2048]{1,0:T(8,128)S(1)} %copy-done.1, f32[168,2048]{1,0:T(8,128)S(1)} %collective-permute-done.2.refs_1_, f32[168,1536]{1,0:T(8,128)S(1)} %collective-permute-done.3.refs_2_, ...), custom_call_target="tpu_custom_call" | custom-call | flops 4161798144 | bytes 8257536 | tf_op jit(solution)/shard_map/gram_early/pallas_call | solution.py:229
  127.2 3.9 %gram_late.1 = (f32[928,128]{1,0:T(8,128)S(1)}, f32[928,128]{1,0:T(8,128)S(1)}, bf16[672,512]{1,0:T(8,128)(2,1)S(1)}, bf16[672,512]{1,0:T(8,128)(2,1)S(1)}) custom-call(s32[2]{0:T(128)S(1)} %pad_add_fusion.place_ref, f32[1856,128]{1,0:T(8,128)S(1)} %get-tuple-element.39.base_ref, f32[168,2048]{1,0:T(8,128)S(1)} %copy-done.1, f32[168,2048]{1,0:T(8,128)} %copy-done.2, ...), custom_call_target="tpu_custom_call" | custom-call | flops 1387266048 | bytes 2752512 | tf_op jit(solution)/shard_map/gram_late/pallas_call | solution.py:229
  131.1 1.5 collective-permute-start.6
  132.7 1.5 collective-permute-done.6
  134.2 2.2 %collective-permute-start.7 = (f32[232,128]{1,0:T(8,128)S(1)}, f32[232,128]{1,0:T(8,128)S(1)}, u32[]{:S(2)}, u32[]{:S(2)}) collective-permute-start(f32[232,128]{1,0:T(8,128)S(1)} %get-tuple-element.63), channel_id=1, source_target_pairs={{0,3},{1,2},{2,1},{3,0},{4,7},{5,6},{6,5},{7,4},{8,11},{9,10},{10,... | collective-permute-start | bytes 356360 | tf_op jit(solution)/shard_map/ppermute | solution.py:398
  136.9 2.7 %collective-permute-done.7 = f32[232,128]{1,0:T(8,128)S(1)} collective-permute-done((f32[232,128]{1,0:T(8,128)S(1)}, f32[232,128]{1,0:T(8,128)S(1)}, u32[]{:S(2)}, u32[]{:S(2)}) %collective-permute-start.7) | collective-permute-done | bytes 118816 | tf_op jit(solution)/shard_map/ppermute | solution.py:398
  139.6 2.9 %collective-permute-done.8 = f32[232,128]{1,0:T(8,128)S(1)} collective-permute-done((f32[232,128]{1,0:T(8,128)S(1)}, f32[232,128]{1,0:T(8,128)S(1)}, u32[]{:S(2)}, u32[]{:S(2)}) %collective-permute-start.8) | collective-permute-done | bytes 118816 | tf_op jit(solution)/shard_map/ppermute | solution.py:398
  142.6 2.3 %collective-permute-start.10 = (f32[232,128]{1,0:T(8,128)S(1)}, f32[232,128]{1,0:T(8,128)S(1)}, u32[]{:S(2)}, u32[]{:S(2)}) collective-permute-start(f32[232,128]{1,0:T(8,128)S(1)} %add_add_fusion.1), channel_id=1, source_target_pairs={{0,24},{4,28},{8,16},{12,20},{16,8},{20,12},{24,0},{28,4},{1,25},{... | collective-permute-start | bytes 356360 | tf_op jit(solution)/shard_map/ppermute | solution.py:14
  146.2 2.0 %collective-permute-done.10 = f32[232,128]{1,0:T(8,128)S(1)} collective-permute-done((f32[232,128]{1,0:T(8,128)S(1)}, f32[232,128]{1,0:T(8,128)S(1)}, u32[]{:S(2)}, u32[]{:S(2)}) %collective-permute-start.10) | collective-permute-done | bytes 118816 | tf_op jit(solution)/shard_map/ppermute | solution.py:14
  148.2 6.4 %collective-permute-done.11 = f32[232,128]{1,0:T(8,128)S(1)} collective-permute-done((f32[232,128]{1,0:T(8,128)S(1)}, f32[232,128]{1,0:T(8,128)S(1)}, u32[]{:S(2)}, u32[]{:S(2)}) %collective-permute-start.11) | collective-permute-done | bytes 118816 | tf_op jit(solution)/shard_map/ppermute | solution.py:14
  157.6 2.4 %collective-permute-done.13 = f32[232,128]{1,0:T(8,128)S(1)} collective-permute-done((f32[232,128]{1,0:T(8,128)S(1)}, f32[232,128]{1,0:T(8,128)S(1)}, u32[]{:S(2)}, u32[]{:S(2)}) %collective-permute-start.13) | collective-permute-done | bytes 118816 | tf_op jit(solution)/shard_map/ppermute | solution.py:398
  160.0 2.4 %collective-permute-done.14 = f32[232,128]{1,0:T(8,128)S(1)} collective-permute-done((f32[232,128]{1,0:T(8,128)S(1)}, f32[232,128]{1,0:T(8,128)S(1)}, u32[]{:S(2)}, u32[]{:S(2)}) %collective-permute-start.14) | collective-permute-done | bytes 118816 | tf_op jit(solution)/shard_map/ppermute | solution.py:398
  163.1 1.4 collective-permute-start.16
  164.5 1.5 collective-permute-done.16.other_ref
  166.0 15.5 %iterations.1 = (f32[96,672]{1,0:T(8,128)}, f32[24,1024]{1,0:T(8,128)S(1)}, f32[24,1024]{1,0:T(8,128)S(1)}, f32[24,1024]{1,0:T(8,128)S(1)}, f32[24,1024]{1,0:T(8...) custom-call(s32[2]{0:T(128)S(1)} %pad_add_fusion.place_ref, ...), custom_call_target="tpu_custom_call" | custom-call | tf_op jit(solution)/shard_map/iterations/pallas_call | solution.py:371
  182.2 3.2 %collective-permute-start.18 = (f32[24,1024]{1,0:T(8,128)S(1)}, f32[24,1024]{1,0:T(8,128)S(1)}, u32[]{:S(2)}, u32[]{:S(2)}) collective-permute-start(f32[24,1024]{1,0:T(8,128)S(1)} %get-tuple-element.49), channel_id=1, source_target_pairs={{0,28},{4,24},{8,20},{12,16},{16,12},{20,8},{24,4},{28,0},{1,29},{... | collective-permute-start | bytes 294920 | tf_op jit(solution)/shard_map/ppermute | solution.py:14
  185.3 2.1 %collective-permute-start.21 = (f32[24,1024]{1,0:T(8,128)S(1)}, f32[24,1024]{1,0:T(8,128)S(1)}, u32[]{:S(2)}, u32[]{:S(2)}) collective-permute-start(f32[24,1024]{1,0:T(8,128)S(1)} %get-tuple-element.52), channel_id=1, source_target_pairs={{0,12},{4,8},{8,4},{12,0},{16,28},{20,24},{24,20},{28,16},{1,13},{... | collective-permute-start | bytes 294920 | tf_op jit(solution)/shard_map/ppermute | solution.py:14
  188.1 2.7 %collective-permute-done.18.refs_1_ = f32[24,1024]{1,0:T(8,128)S(1)} collective-permute-done((f32[24,1024]{1,0:T(8,128)S(1)}, f32[24,1024]{1,0:T(8,128)S(1)}, u32[]{:S(2)}, u32[]{:S(2)}) %collective-permute-start.18) | collective-permute-done | bytes 98336 | tf_op jit(solution)/shard_map/ppermute | solution.py:14
  190.8 1.8 collective-permute-start.23
  193.4 3.2 %collective-permute-done.21.refs_4_ = f32[24,1024]{1,0:T(8,128)S(1)} collective-permute-done((f32[24,1024]{1,0:T(8,128)S(1)}, f32[24,1024]{1,0:T(8,128)S(1)}, u32[]{:S(2)}, u32[]{:S(2)}) %collective-permute-start.21) | collective-permute-done | bytes 98336 | tf_op jit(solution)/shard_map/ppermute | solution.py:14
  196.6 4.4 %collective-permute-done.23.refs_6_ = f32[24,1024]{1,0:T(8,128)S(1)} collective-permute-done((f32[24,1024]{1,0:T(8,128)S(1)}, f32[24,1024]{1,0:T(8,128)S(1)}, u32[]{:S(2)}, u32[]{:S(2)}) %collective-permute-start.23) | collective-permute-done | bytes 98336 | tf_op jit(solution)/shard_map/ppermute | solution.py:14
  201.0 1.6 assemble.1
  (44 shorter events, 10.3 us)
Async XLA Ops:
  2.1 2.3 %collective-permute-start = (f32[84,2048]{1,0:T(8,128)S(1)}, f32[84,2048]{1,0:T(8,128)S(1)}, u32[]{:S(2)}, u32[]{:S(2)}) collective-permute-start(f32[84,2048]{1,0:T(8,128)S(1)} %get-tuple-element.31), channel_id=1, source_target_pairs={{0,4},{4,0},{8,12},{12,8},{16,20},{20,16},{24,28},{28,24},{1,5},{5... | collective-permute-start | bytes 2064392 | tf_op jit(solution)/shard_map/ppermute | solution.py:14
  4.5 5.0 %collective-permute-start.1 = (f32[84,6144]{1,0:T(8,128)S(1)}, f32[84,6144]{1,0:T(8,128)S(1)}, u32[]{:S(2)}, u32[]{:S(2)}) collective-permute-start(f32[84,6144]{1,0:T(8,128)S(1)} %pad_maximum_fusion), channel_id=1, source_target_pairs={{0,4},{4,0},{8,12},{12,8},{16,20},{20,16},{24,28},{28,24},{1,5},{5... | collective-permute-start | bytes 6193160 | tf_op jit(solution)/shard_map/ppermute | solution.py:14
  4.8 35.2 %collective-permute-start.4 = (f32[168,2048]{1,0:T(8,128)S(1)}, f32[168,2048]{1,0:T(8,128)S(1)}, u32[]{:S(2)}, u32[]{:S(2)}) collective-permute-start(f32[168,2048]{1,0:T(8,128)S(1)} %maximum_select_fusion), channel_id=1, source_target_pairs={{0,24},{4,28},{8,16},{12,20},{16,8},{20,12},{24,0},{28,4},{1,25},{... | collective-permute-start | bytes 4128776 | tf_op jit(solution)/shard_map/ppermute | solution.py:14
  9.5 1.4 copy-start.4
  15.3 104.6 %collective-permute-start.2 = (f32[168,2048]{1,0:T(8,128)S(1)}, f32[168,2048]{1,0:T(8,128)S(1)}, u32[]{:S(2)}, u32[]{:S(2)}) collective-permute-start(f32[168,2048]{1,0:T(8,128)S(1)} %get-tuple-element.34), channel_id=1, source_target_pairs={{0,8},{4,12},{8,0},{12,4},{16,24},{20,28},{24,16},{28,20},{1,9},{5... | collective-permute-start | bytes 4128776 | tf_op jit(solution)/shard_map/ppermute | solution.py:14
  17.2 102.7 %collective-permute-start.3 = (f32[168,1536]{1,0:T(8,128)S(1)}, f32[168,1536]{1,0:T(8,128)S(1)}, u32[]{:S(2)}, u32[]{:S(2)}) collective-permute-start(f32[168,1536]{1,0:T(8,128)S(1)} %get-tuple-element.35), channel_id=1, source_target_pairs={{0,16},{4,20},{8,24},{12,28},{16,0},{20,4},{24,8},{28,12},{1,17},{... | collective-permute-start | bytes 3096584 | tf_op jit(solution)/shard_map/ppermute | solution.py:14
  40.0 87.1 %copy-start = (f32[168,2048]{1,0:T(8,128)}, f32[168,2048]{1,0:T(8,128)S(1)}, u32[]{:S(2)}) copy-start(f32[168,2048]{1,0:T(8,128)S(1)} %collective-permute-done.4.refs_3_) | copy-start | bytes 4128772
  40.0 87.2 %collective-permute-start.5 = (f32[168,512]{1,0:T(8,128)S(1)}, f32[168,512]{1,0:T(8,128)S(1)}, u32[]{:S(2)}, u32[]{:S(2)}) collective-permute-start(f32[168,512]{1,0:T(8,128)S(1)} %get-tuple-element.40), channel_id=1, source_target_pairs={{0,16},{4,20},{8,24},{12,28},{16,0},{20,4},{24,8},{28,12},{1,17},{... | collective-permute-start | bytes 1032200 | tf_op jit(solution)/shard_map/ppermute | solution.py:14
  119.8 7.2 %copy-start.2 = (f32[168,2048]{1,0:T(8,128)}, f32[168,2048]{1,0:T(8,128)S(1)}, u32[]{:S(2)}) copy-start(f32[168,2048]{1,0:T(8,128)S(1)} %collective-permute-done.2.refs_1_) | copy-start | bytes 4128772
  119.8 1.8 copy-start.1
  131.1 3.0 %collective-permute-start.6 = (f32[928,128]{1,0:T(8,128)S(1)}, f32[928,128]{1,0:T(8,128)S(1)}, u32[]{:S(2)}, u32[]{:S(2)}) collective-permute-start(f32[928,128]{1,0:T(8,128)S(1)} %get-tuple-element.42), channel_id=1, source_target_pairs={{0,4},{4,0},{8,12},{12,8},{16,20},{20,16},{24,28},{28,24},{1,5},{5... | collective-permute-start | bytes 1425416 | tf_op jit(solution)/shard_map/ppermute | solution.py:14
  134.1 31.8 %copy-start.3 = (f32[672,96]{0,1:T(8,128)S(1)}, f32[672,96]{0,1:T(8,128)}, u32[]{:S(2)}) copy-start(f32[672,96]{0,1:T(8,128)} %param.3) | copy-start | bytes 774148
  134.2 5.4 %collective-permute-start.7 = (f32[232,128]{1,0:T(8,128)S(1)}, f32[232,128]{1,0:T(8,128)S(1)}, u32[]{:S(2)}, u32[]{:S(2)}) collective-permute-start(f32[232,128]{1,0:T(8,128)S(1)} %get-tuple-element.63), channel_id=1, source_target_pairs={{0,3},{1,2},{2,1},{3,0},{4,7},{5,6},{6,5},{7,4},{8,11},{9,10},{10,... | collective-permute-start | bytes 356360 | tf_op jit(solution)/shard_map/ppermute | solution.py:398
  136.5 6.1 %collective-permute-start.8 = (f32[232,128]{1,0:T(8,128)S(1)}, f32[232,128]{1,0:T(8,128)S(1)}, u32[]{:S(2)}, u32[]{:S(2)}) collective-permute-start(f32[232,128]{1,0:T(8,128)S(1)} %get-tuple-element.65), channel_id=1, source_target_pairs={{0,1},{1,0},{2,3},{3,2},{4,6},{5,7},{6,4},{7,5},{8,9},{9,8},{10,11... | collective-permute-start | bytes 356360 | tf_op jit(solution)/shard_map/ppermute | solution.py:398
  136.7 5.9 %collective-permute-start.9 = (f32[232,128]{1,0:T(8,128)S(1)}, f32[232,128]{1,0:T(8,128)S(1)}, u32[]{:S(2)}, u32[]{:S(2)}) collective-permute-start(f32[232,128]{1,0:T(8,128)S(1)} %get-tuple-element.64), channel_id=1, source_target_pairs={{0,2},{1,3},{2,0},{3,1},{4,5},{5,4},{6,7},{7,6},{8,10},{9,11},{10,... | collective-permute-start | bytes 356360 | tf_op jit(solution)/shard_map/ppermute | solution.py:398
  142.6 5.6 %collective-permute-start.10 = (f32[232,128]{1,0:T(8,128)S(1)}, f32[232,128]{1,0:T(8,128)S(1)}, u32[]{:S(2)}, u32[]{:S(2)}) collective-permute-start(f32[232,128]{1,0:T(8,128)S(1)} %add_add_fusion.1), channel_id=1, source_target_pairs={{0,24},{4,28},{8,16},{12,20},{16,8},{20,12},{24,0},{28,4},{1,25},{... | collective-permute-start | bytes 356360 | tf_op jit(solution)/shard_map/ppermute | solution.py:14
  144.9 9.8 %collective-permute-start.11 = (f32[232,128]{1,0:T(8,128)S(1)}, f32[232,128]{1,0:T(8,128)S(1)}, u32[]{:S(2)}, u32[]{:S(2)}) collective-permute-start(f32[232,128]{1,0:T(8,128)S(1)} %add_add_fusion.1), channel_id=1, source_target_pairs={{0,8},{4,12},{8,0},{12,4},{16,24},{20,28},{24,16},{28,20},{1,9},{5... | collective-permute-start | bytes 356360 | tf_op jit(solution)/shard_map/ppermute | solution.py:14
  144.9 9.8 %collective-permute-start.12 = (f32[232,128]{1,0:T(8,128)S(1)}, f32[232,128]{1,0:T(8,128)S(1)}, u32[]{:S(2)}, u32[]{:S(2)}) collective-permute-start(f32[232,128]{1,0:T(8,128)S(1)} %add_add_fusion.1), channel_id=1, source_target_pairs={{0,16},{4,20},{8,24},{12,28},{16,0},{20,4},{24,8},{28,12},{1,17},{... | collective-permute-start | bytes 356360 | tf_op jit(solution)/shard_map/ppermute | solution.py:14
  154.7 5.3 %collective-permute-start.13 = (f32[232,128]{1,0:T(8,128)S(1)}, f32[232,128]{1,0:T(8,128)S(1)}, u32[]{:S(2)}, u32[]{:S(2)}) collective-permute-start(f32[232,128]{1,0:T(8,128)S(1)} %get-tuple-element.57), channel_id=1, source_target_pairs={{0,3},{1,2},{2,1},{3,0},{4,7},{5,6},{6,5},{7,4},{8,11},{9,10},{10,... | collective-permute-start | bytes 356360 | tf_op jit(solution)/shard_map/ppermute | solution.py:398
  155.7 6.8 %collective-permute-start.14 = (f32[232,128]{1,0:T(8,128)S(1)}, f32[232,128]{1,0:T(8,128)S(1)}, u32[]{:S(2)}, u32[]{:S(2)}) collective-permute-start(f32[232,128]{1,0:T(8,128)S(1)} %get-tuple-element.57), channel_id=1, source_target_pairs={{0,1},{1,0},{2,3},{3,2},{4,6},{5,7},{6,4},{7,5},{8,9},{9,8},{10,11... | collective-permute-start | bytes 356360 | tf_op jit(solution)/shard_map/ppermute | solution.py:398
  157.0 6.1 %collective-permute-start.15 = (f32[232,128]{1,0:T(8,128)S(1)}, f32[232,128]{1,0:T(8,128)S(1)}, u32[]{:S(2)}, u32[]{:S(2)}) collective-permute-start(f32[232,128]{1,0:T(8,128)S(1)} %get-tuple-element.57), channel_id=1, source_target_pairs={{0,2},{1,3},{2,0},{3,1},{4,5},{5,4},{6,7},{7,6},{8,10},{9,11},{10,... | collective-permute-start | bytes 356360 | tf_op jit(solution)/shard_map/ppermute | solution.py:398
  163.1 2.9 %collective-permute-start.16 = (f32[928,128]{1,0:T(8,128)S(1)}, f32[928,128]{1,0:T(8,128)S(1)}, u32[]{:S(2)}, u32[]{:S(2)}) collective-permute-start(f32[928,128]{1,0:T(8,128)S(1)} %bitcast.13), channel_id=1, source_target_pairs={{0,4},{4,0},{8,12},{12,8},{16,20},{20,16},{24,28},{28,24},{1,5},{5... | collective-permute-start | bytes 1425416 | tf_op jit(solution)/shard_map/ppermute | solution.py:14
  181.5 6.0 %collective-permute-start.17 = (f32[24,1024]{1,0:T(8,128)S(1)}, f32[24,1024]{1,0:T(8,128)S(1)}, u32[]{:S(2)}, u32[]{:S(2)}) collective-permute-start(f32[24,1024]{1,0:T(8,128)S(1)} %get-tuple-element.48), channel_id=1, source_target_pairs={{0,24},{4,28},{8,16},{12,20},{16,8},{20,12},{24,0},{28,4},{1,25},{... | collective-permute-start | bytes 294920 | tf_op jit(solution)/shard_map/ppermute | solution.py:14
  182.2 8.6 %collective-permute-start.18 = (f32[24,1024]{1,0:T(8,128)S(1)}, f32[24,1024]{1,0:T(8,128)S(1)}, u32[]{:S(2)}, u32[]{:S(2)}) collective-permute-start(f32[24,1024]{1,0:T(8,128)S(1)} %get-tuple-element.49), channel_id=1, source_target_pairs={{0,28},{4,24},{8,20},{12,16},{16,12},{20,8},{24,4},{28,0},{1,29},{... | collective-permute-start | bytes 294920 | tf_op jit(solution)/shard_map/ppermute | solution.py:14
  185.3 7.3 %collective-permute-start.19 = (f32[24,1024]{1,0:T(8,128)S(1)}, f32[24,1024]{1,0:T(8,128)S(1)}, u32[]{:S(2)}, u32[]{:S(2)}) collective-permute-start(f32[24,1024]{1,0:T(8,128)S(1)} %get-tuple-element.50), channel_id=1, source_target_pairs={{0,4},{4,0},{8,12},{12,8},{16,20},{20,16},{24,28},{28,24},{1,5},{5... | collective-permute-start | bytes 294920 | tf_op jit(solution)/shard_map/ppermute | solution.py:14
  185.3 8.1 %collective-permute-start.20 = (f32[24,1024]{1,0:T(8,128)S(1)}, f32[24,1024]{1,0:T(8,128)S(1)}, u32[]{:S(2)}, u32[]{:S(2)}) collective-permute-start(f32[24,1024]{1,0:T(8,128)S(1)} %get-tuple-element.51), channel_id=1, source_target_pairs={{0,8},{4,12},{8,0},{12,4},{16,24},{20,28},{24,16},{28,20},{1,9},{5... | collective-permute-start | bytes 294920 | tf_op jit(solution)/shard_map/ppermute | solution.py:14
  185.3 11.3 %collective-permute-start.21 = (f32[24,1024]{1,0:T(8,128)S(1)}, f32[24,1024]{1,0:T(8,128)S(1)}, u32[]{:S(2)}, u32[]{:S(2)}) collective-permute-start(f32[24,1024]{1,0:T(8,128)S(1)} %get-tuple-element.52), channel_id=1, source_target_pairs={{0,12},{4,8},{8,4},{12,0},{16,28},{20,24},{24,20},{28,16},{1,13},{... | collective-permute-start | bytes 294920 | tf_op jit(solution)/shard_map/ppermute | solution.py:14
  187.5 9.1 %collective-permute-start.22 = (f32[24,1024]{1,0:T(8,128)S(1)}, f32[24,1024]{1,0:T(8,128)S(1)}, u32[]{:S(2)}, u32[]{:S(2)}) collective-permute-start(f32[24,1024]{1,0:T(8,128)S(1)} %get-tuple-element.53), channel_id=1, source_target_pairs={{0,16},{4,20},{8,24},{12,28},{16,0},{20,4},{24,8},{28,12},{1,17},{... | collective-permute-start | bytes 294920 | tf_op jit(solution)/shard_map/ppermute | solution.py:14
  190.8 10.2 %collective-permute-start.23 = (f32[24,1024]{1,0:T(8,128)S(1)}, f32[24,1024]{1,0:T(8,128)S(1)}, u32[]{:S(2)}, u32[]{:S(2)}) collective-permute-start(f32[24,1024]{1,0:T(8,128)S(1)} %get-tuple-element.54), channel_id=1, source_target_pairs={{0,20},{4,16},{8,28},{12,24},{16,4},{20,0},{24,12},{28,8},{1,21},{... | collective-permute-start | bytes 294920 | tf_op jit(solution)/shard_map/ppermute | solution.py:14

commit v13 on v12

--- a/solution.py
+++ b/solution.py
@@ -405,19 +405,22 @@
     mine = mine + swap(theirs, "fibre", fibre, 1)
     mine = jnp.pad(mine, ((0, piece * rest - half), (0, 0)))
     peers = {bits: r ^ jnp.where(core == 0, bits, mirrored(bits, rest)) for bits in farthest_first(rest)}
-    total = lax.dynamic_slice(mine, (r * piece, 0), (piece, width))
-    for bits, peer in peers.items():
-        part = lax.dynamic_slice(mine, (peer * piece, 0), (piece, width))
-        total = total + swap_rest(part, fibre, rest, bits)
-    terms = {bits: swap(total, "fibre", fibre, 2 * bits) for bits in farthest_first(fibre // 2)}
-    terms = [terms.get(bits, total) for bits in range(fibre // 2)]
-    while len(terms) > 1:
-        last = len(terms) - 1
-        terms = [terms[i] + terms[last - i] for i in range(1, len(terms) // 2)] + [terms[last] + terms[0]]
-    total = terms[0]
-    out = lax.dynamic_update_slice(jnp.zeros((rest, piece, width), jnp.float32), total[None], (r, 0, 0))
-    for bits, peer in peers.items():
-        out = lax.dynamic_update_slice(out, swap_rest(total, fibre, rest, bits)[None], (peer, 0, 0))
+    out = jnp.zeros((rest, piece, width), jnp.float32)
+    cut = -(-piece // 16) * 8
+    for start, rows in ((0, cut), (cut, piece - cut)):
+        total = lax.dynamic_slice(mine, (r * piece + start, 0), (rows, width))
+        for bits, peer in peers.items():
+            part = lax.dynamic_slice(mine, (peer * piece + start, 0), (rows, width))
+            total = total + swap_rest(part, fibre, rest, bits)
+        terms = {bits: swap(total, "fibre", fibre, 2 * bits) for bits in farthest_first(fibre // 2)}
+        terms = [terms.get(bits, total) for bits in range(fibre // 2)]
+        while len(terms) > 1:
+            last = len(terms) - 1
+            terms = [terms[i] + terms[last - i] for i in range(1, len(terms) // 2)] + [terms[last] + terms[0]]
+        total = terms[0]
+        out = lax.dynamic_update_slice(out, total[None], (r, start, 0))
+        for bits, peer in peers.items():
+            out = lax.dynamic_update_slice(out, swap_rest(total, fibre, rest, bits)[None], (peer, start, 0))
     out = out.reshape(rest * piece, width)[:half]
     return out, swap(out, "fibre", fibre, 1)
 

time: 203 us -> 209 us (1.030)
  starting transfers between devices: 59.4 us -> 77 us
  waiting for transfers between devices: 105 us -> 92.9 us
    ppermute x18 -> x21, starting transfers between devices: 53.8 us -> 64 us  [swap(): return lax.ppermute(x, axis, [(i, i ^ bits) for i in range(size)])]
    ppermute x18 -> x21, waiting for transfers between devices: 93.7 us -> 85 us  [swap(): return lax.ppermute(x, axis, [(i, i ^ bits) for i in range(size)])]
    ppermute x6 -> x12, starting transfers between devices: 5.58 us -> 13 us  [swap_rest(): return lax.ppermute(x, ('fibre', 'rest'), pairs)]
    ppermute x6 -> x12, waiting for transfers between devices: 11 us -> 7.83 us  [swap_rest(): return lax.ppermute(x, ('fibre', 'rest'), pairs)]
  transfers between devices with their start and end apart: 24 -> 33, of which waited for: 17 -> 17; matrix products, arithmetic and copies ran while one was open for 1% -> 1% of each run, Pallas kernels for 5% -> 5%
where the time goes in v13:
time: 209 us; the launch traced here: 208 us
  waiting for transfers between devices  92.9 us (44%)
  starting transfers between devices  77 us (37%)
  Pallas kernels  30.7 us (15%)
  local copies, waits for them, and re-layouts  6.43 us (3%)
    ppermute x21, waiting for transfers between devices, swap(): return lax.ppermute(x, axis, [(i, i ^ bits) for i in range(size)])  85 us
    ppermute x21, starting transfers between devices, swap(): return lax.ppermute(x, axis, [(i, i ^ bits) for i in range(size)])  64 us
    pallas_call x1, Pallas kernels, iterations(): pl.pallas_call(functools.partial(iterations_kernel, iters, zs), out_shape...  15.4 us
    ppermute x12, starting transfers between devices, swap_rest(): return lax.ppermute(x, ('fibre', 'rest'), pairs)  13 us
    pallas_call x2, Pallas kernels, gram_part(): pl.pallas_call(functools.partial(kernel, starts), out_shape=[*sums, *part...  9.3 us
    ppermute x12, waiting for transfers between devices, swap_rest(): return lax.ppermute(x, ('fibre', 'rest'), pairs)  7.83 us
    pallas_call x1, Pallas kernels, prepare(): pl.pallas_call(functools.partial(prepare_kernel, cuts, pieces), out_shape...  4.38 us
  transfers between devices with their start and end apart: 33, of which 17 were waited for; matrix products, arithmetic and copies ran while one was open for 1% of the time, Pallas kernels for 5%

profile of v13, /device:TPU:1, one launch (start us, length us, event | category | flops | bytes accessed | tf_op | source)
XLA Modules:
  0.0 208.4 jit_solution(3166663929163440750)
XLA Ops:
  2.2 1.7 constant_dynamic-slice_fusion.8
  4.8 4.6 %collective-permute-start.4 = (f32[168,2048]{1,0:T(8,128)S(1)}, f32[168,2048]{1,0:T(8,128)S(1)}, u32[]{:S(2)}, u32[]{:S(2)}) collective-permute-start(f32[168,2048]{1,0:T(8,128)S(1)} %maximum_select_fusion), channel_id=1, source_target_pairs={{0,24},{4,28},{8,16},{12,20},{16,8},{20,12},{24,0},{28,4},{1,25},{... | collective-permute-start | bytes 4128776 | tf_op jit(solution)/shard_map/ppermute | solution.py:14
  10.9 4.4 %prepare.1 = (f32[168,1536]{1,0:T(8,128)S(1)}, f32[168,512]{1,0:T(8,128)S(1)}, f32[168,2048]{1,0:T(8,128)S(1)}, f32[168,2048]{1,0:T(8,128)}) custom-call(s32[2]{0:T(128)S(1)} %pad_add_fusion.place_ref, f32[84,16384]{1,0:T(8,128)} %slab_ref, f32[84,6144]{1,0:T(8,128)} %copy-done.4), custom_call_target="tpu_custom_call" | custom-call | bytes 100000000 | tf_op jit(solution)/shard_map/prepare/pallas_call | solution.py:57
  15.3 1.9 collective-permute-start.2
  17.2 2.3 %collective-permute-start.3 = (f32[168,1536]{1,0:T(8,128)S(1)}, f32[168,1536]{1,0:T(8,128)S(1)}, u32[]{:S(2)}, u32[]{:S(2)}) collective-permute-start(f32[168,1536]{1,0:T(8,128)S(1)} %get-tuple-element.35), channel_id=1, source_target_pairs={{0,16},{4,20},{8,24},{12,28},{16,0},{20,4},{24,8},{28,12},{1,17},{... | collective-permute-start | bytes 3096584 | tf_op jit(solution)/shard_map/ppermute | solution.py:14
  19.5 20.5 %collective-permute-done.4.refs_3_ = f32[168,2048]{1,0:T(8,128)S(1)} collective-permute-done((f32[168,2048]{1,0:T(8,128)S(1)}, f32[168,2048]{1,0:T(8,128)S(1)}, u32[]{:S(2)}, u32[]{:S(2)}) %collective-permute-start.4) | collective-permute-done | bytes 1376288 | tf_op jit(solution)/shard_map/ppermute | solution.py:14
  40.0 29.5 %collective-permute-start.5 = (f32[168,512]{1,0:T(8,128)S(1)}, f32[168,512]{1,0:T(8,128)S(1)}, u32[]{:S(2)}, u32[]{:S(2)}) collective-permute-start(f32[168,512]{1,0:T(8,128)S(1)} %get-tuple-element.40), channel_id=1, source_target_pairs={{0,16},{4,20},{8,24},{12,28},{16,0},{20,4},{24,8},{28,12},{1,17},{... | collective-permute-start | bytes 1032200 | tf_op jit(solution)/shard_map/ppermute | solution.py:14
  69.5 50.3 %collective-permute-done.3.refs_2_ = f32[168,1536]{1,0:T(8,128)S(1)} collective-permute-done((f32[168,1536]{1,0:T(8,128)S(1)}, f32[168,1536]{1,0:T(8,128)S(1)}, u32[]{:S(2)}, u32[]{:S(2)}) %collective-permute-start.3) | collective-permute-done | bytes 1032224 | tf_op jit(solution)/shard_map/ppermute | solution.py:14
  119.8 1.8 copy-done.1
  121.7 5.4 %gram_early.1 = (f32[1856,128]{1,0:T(8,128)S(1)}, bf16[672,1536]{1,0:T(8,128)(2,1)}, bf16[672,1536]{1,0:T(8,128)(2,1)}) custom-call(s32[2]{0:T(128)S(1)} %pad_add_fusion.place_ref, f32[168,2048]{1,0:T(8,128)S(1)} %copy-done.1, f32[168,2048]{1,0:T(8,128)S(1)} %collective-permute-done.2.refs_1_, f32[168,1536]{1,0:T(8,128)S(1)} %collective-permute-done.3.refs_2_, ...), custom_call_target="tpu_custom_call" | custom-call | flops 4161798144 | bytes 8257536 | tf_op jit(solution)/shard_map/gram_early/pallas_call | solution.py:229
  127.2 3.9 %gram_late.1 = (f32[928,128]{1,0:T(8,128)S(1)}, f32[928,128]{1,0:T(8,128)S(1)}, bf16[672,512]{1,0:T(8,128)(2,1)S(1)}, bf16[672,512]{1,0:T(8,128)(2,1)S(1)}) custom-call(s32[2]{0:T(128)S(1)} %pad_add_fusion.place_ref, f32[1856,128]{1,0:T(8,128)S(1)} %get-tuple-element.39.base_ref, f32[168,2048]{1,0:T(8,128)S(1)} %copy-done.1, f32[168,2048]{1,0:T(8,128)} %copy-done.2, ...), custom_call_target="tpu_custom_call" | custom-call | flops 1387266048 | bytes 2752512 | tf_op jit(solution)/shard_map/gram_late/pallas_call | solution.py:229
  131.1 1.5 collective-permute-start.6
  132.7 1.5 collective-permute-done.6
  134.2 2.2 %collective-permute-start.7 = (f32[120,128]{1,0:T(8,128)S(1)}, f32[120,128]{1,0:T(8,128)S(1)}, u32[]{:S(2)}, u32[]{:S(2)}) collective-permute-start(f32[120,128]{1,0:T(8,128)S(1)} %get-tuple-element.68), channel_id=1, source_target_pairs={{0,3},{1,2},{2,1},{3,0},{4,7},{5,6},{6,5},{7,4},{8,11},{9,10},{10,... | collective-permute-start | bytes 184328 | tf_op jit(solution)/shard_map/ppermute | solution.py:398
  138.3 1.5 collective-permute-done.8
  139.8 2.3 %collective-permute-start.10 = (f32[120,128]{1,0:T(8,128)S(1)}, f32[120,128]{1,0:T(8,128)S(1)}, u32[]{:S(2)}, u32[]{:S(2)}) collective-permute-start(f32[120,128]{1,0:T(8,128)S(1)} %add_add_fusion.1), channel_id=1, source_target_pairs={{0,24},{4,28},{8,16},{12,20},{16,8},{20,12},{24,0},{28,4},{1,25},{... | collective-permute-start | bytes 184328 | tf_op jit(solution)/shard_map/ppermute | solution.py:14
  143.5 2.1 %collective-permute-start.16 = (f32[112,128]{1,0:T(8,128)S(1)}, f32[112,128]{1,0:T(8,128)S(1)}, u32[]{:S(2)}, u32[]{:S(2)}) collective-permute-start(f32[112,128]{1,0:T(8,128)S(1)} %get-tuple-element.65), channel_id=1, source_target_pairs={{0,3},{1,2},{2,1},{3,0},{4,7},{5,6},{6,5},{7,4},{8,11},{9,10},{10,... | collective-permute-start | bytes 172040 | tf_op jit(solution)/shard_map/ppermute | solution.py:398
  146.8 2.3 %collective-permute-start.13 = (f32[120,128]{1,0:T(8,128)S(1)}, f32[120,128]{1,0:T(8,128)S(1)}, u32[]{:S(2)}, u32[]{:S(2)}) collective-permute-start(f32[120,128]{1,0:T(8,128)S(1)} %get-tuple-element.59), channel_id=1, source_target_pairs={{0,3},{1,2},{2,1},{3,0},{4,7},{5,6},{6,5},{7,4},{8,11},{9,10},{10,... | collective-permute-start | bytes 184328 | tf_op jit(solution)/shard_map/ppermute | solution.py:398
  149.2 2.0 collective-permute-start.19
  151.1 1.6 collective-permute-start.21
  157.1 1.8 collective-permute-start.22
  162.5 7.6 %collective-permute-start.25 = (f32[928,128]{1,0:T(8,128)S(1)}, f32[928,128]{1,0:T(8,128)S(1)}, u32[]{:S(2)}, u32[]{:S(2)}) collective-permute-start(f32[928,128]{1,0:T(8,128)S(1)} %bitcast.21), channel_id=1, source_target_pairs={{0,4},{4,0},{8,12},{12,8},{16,20},{20,16},{24,28},{28,24},{1,5},{5... | collective-permute-start | bytes 1425416 | tf_op jit(solution)/shard_map/ppermute | solution.py:14
  170.1 1.5 collective-permute-done.25.other_ref
  171.6 15.4 %iterations.1 = (f32[96,672]{1,0:T(8,128)}, f32[24,1024]{1,0:T(8,128)S(1)}, f32[24,1024]{1,0:T(8,128)S(1)}, f32[24,1024]{1,0:T(8,128)S(1)}, f32[24,1024]{1,0:T(8...) custom-call(s32[2]{0:T(128)S(1)} %pad_add_fusion.place_ref, ...), custom_call_target="tpu_custom_call" | custom-call | tf_op jit(solution)/shard_map/iterations/pallas_call | solution.py:371
  187.1 2.3 %collective-permute-start.26 = (f32[24,1024]{1,0:T(8,128)S(1)}, f32[24,1024]{1,0:T(8,128)S(1)}, u32[]{:S(2)}, u32[]{:S(2)}) collective-permute-start(f32[24,1024]{1,0:T(8,128)S(1)} %get-tuple-element.48), channel_id=1, source_target_pairs={{0,24},{4,28},{8,16},{12,20},{16,8},{20,12},{24,0},{28,4},{1,25},{... | collective-permute-start | bytes 294920 | tf_op jit(solution)/shard_map/ppermute | solution.py:14
  189.3 1.6 collective-permute-start.27
  190.9 2.1 %collective-permute-start.30 = (f32[24,1024]{1,0:T(8,128)S(1)}, f32[24,1024]{1,0:T(8,128)S(1)}, u32[]{:S(2)}, u32[]{:S(2)}) collective-permute-start(f32[24,1024]{1,0:T(8,128)S(1)} %get-tuple-element.52), channel_id=1, source_target_pairs={{0,12},{4,8},{8,4},{12,0},{16,28},{20,24},{24,20},{28,16},{1,13},{... | collective-permute-start | bytes 294920 | tf_op jit(solution)/shard_map/ppermute | solution.py:14
  193.8 2.6 %collective-permute-done.27.refs_1_ = f32[24,1024]{1,0:T(8,128)S(1)} collective-permute-done((f32[24,1024]{1,0:T(8,128)S(1)}, f32[24,1024]{1,0:T(8,128)S(1)}, u32[]{:S(2)}, u32[]{:S(2)}) %collective-permute-start.27) | collective-permute-done | bytes 98336 | tf_op jit(solution)/shard_map/ppermute | solution.py:14
  196.5 2.1 %collective-permute-start.32 = (f32[24,1024]{1,0:T(8,128)S(1)}, f32[24,1024]{1,0:T(8,128)S(1)}, u32[]{:S(2)}, u32[]{:S(2)}) collective-permute-start(f32[24,1024]{1,0:T(8,128)S(1)} %get-tuple-element.54), channel_id=1, source_target_pairs={{0,20},{4,16},{8,28},{12,24},{16,4},{20,0},{24,12},{28,8},{1,21},{... | collective-permute-start | bytes 294920 | tf_op jit(solution)/shard_map/ppermute | solution.py:14
  198.6 3.5 %collective-permute-done.30.refs_4_ = f32[24,1024]{1,0:T(8,128)S(1)} collective-permute-done((f32[24,1024]{1,0:T(8,128)S(1)}, f32[24,1024]{1,0:T(8,128)S(1)}, u32[]{:S(2)}, u32[]{:S(2)}) %collective-permute-start.30) | collective-permute-done | bytes 98336 | tf_op jit(solution)/shard_map/ppermute | solution.py:14
  202.1 4.7 %collective-permute-done.32.refs_6_ = f32[24,1024]{1,0:T(8,128)S(1)} collective-permute-done((f32[24,1024]{1,0:T(8,128)S(1)}, f32[24,1024]{1,0:T(8,128)S(1)}, u32[]{:S(2)}, u32[]{:S(2)}) %collective-permute-start.32) | collective-permute-done | bytes 98336 | tf_op jit(solution)/shard_map/ppermute | solution.py:14
  206.8 1.6 assemble.1
  (68 shorter events, 17.3 us)
Async XLA Ops:
  4.5 5.0 %collective-permute-start.1 = (f32[84,6144]{1,0:T(8,128)S(1)}, f32[84,6144]{1,0:T(8,128)S(1)}, u32[]{:S(2)}, u32[]{:S(2)}) collective-permute-start(f32[84,6144]{1,0:T(8,128)S(1)} %pad_maximum_fusion), channel_id=1, source_target_pairs={{0,4},{4,0},{8,12},{12,8},{16,20},{20,16},{24,28},{28,24},{1,5},{5... | collective-permute-start | bytes 6193160 | tf_op jit(solution)/shard_map/ppermute | solution.py:14
  4.8 35.2 %collective-permute-start.4 = (f32[168,2048]{1,0:T(8,128)S(1)}, f32[168,2048]{1,0:T(8,128)S(1)}, u32[]{:S(2)}, u32[]{:S(2)}) collective-permute-start(f32[168,2048]{1,0:T(8,128)S(1)} %maximum_select_fusion), channel_id=1, source_target_pairs={{0,24},{4,28},{8,16},{12,20},{16,8},{20,12},{24,0},{28,4},{1,25},{... | collective-permute-start | bytes 4128776 | tf_op jit(solution)/shard_map/ppermute | solution.py:14
  15.3 104.6 %collective-permute-start.2 = (f32[168,2048]{1,0:T(8,128)S(1)}, f32[168,2048]{1,0:T(8,128)S(1)}, u32[]{:S(2)}, u32[]{:S(2)}) collective-permute-start(f32[168,2048]{1,0:T(8,128)S(1)} %get-tuple-element.34), channel_id=1, source_target_pairs={{0,8},{4,12},{8,0},{12,4},{16,24},{20,28},{24,16},{28,20},{1,9},{5... | collective-permute-start | bytes 4128776 | tf_op jit(solution)/shard_map/ppermute | solution.py:14
  17.2 102.7 %collective-permute-start.3 = (f32[168,1536]{1,0:T(8,128)S(1)}, f32[168,1536]{1,0:T(8,128)S(1)}, u32[]{:S(2)}, u32[]{:S(2)}) collective-permute-start(f32[168,1536]{1,0:T(8,128)S(1)} %get-tuple-element.35), channel_id=1, source_target_pairs={{0,16},{4,20},{8,24},{12,28},{16,0},{20,4},{24,8},{28,12},{1,17},{... | collective-permute-start | bytes 3096584 | tf_op jit(solution)/shard_map/ppermute | solution.py:14
  40.0 87.2 %collective-permute-start.5 = (f32[168,512]{1,0:T(8,128)S(1)}, f32[168,512]{1,0:T(8,128)S(1)}, u32[]{:S(2)}, u32[]{:S(2)}) collective-permute-start(f32[168,512]{1,0:T(8,128)S(1)} %get-tuple-element.40), channel_id=1, source_target_pairs={{0,16},{4,20},{8,24},{12,28},{16,0},{20,4},{24,8},{28,12},{1,17},{... | collective-permute-start | bytes 1032200 | tf_op jit(solution)/shard_map/ppermute | solution.py:14
  131.1 3.0 %collective-permute-start.6 = (f32[928,128]{1,0:T(8,128)S(1)}, f32[928,128]{1,0:T(8,128)S(1)}, u32[]{:S(2)}, u32[]{:S(2)}) collective-permute-start(f32[928,128]{1,0:T(8,128)S(1)} %get-tuple-element.42), channel_id=1, source_target_pairs={{0,4},{4,0},{8,12},{12,8},{16,20},{20,16},{24,28},{28,24},{1,5},{5... | collective-permute-start | bytes 1425416 | tf_op jit(solution)/shard_map/ppermute | solution.py:14
  134.2 4.0 %collective-permute-start.7 = (f32[120,128]{1,0:T(8,128)S(1)}, f32[120,128]{1,0:T(8,128)S(1)}, u32[]{:S(2)}, u32[]{:S(2)}) collective-permute-start(f32[120,128]{1,0:T(8,128)S(1)} %get-tuple-element.68), channel_id=1, source_target_pairs={{0,3},{1,2},{2,1},{3,0},{4,7},{5,6},{6,5},{7,4},{8,11},{9,10},{10,... | collective-permute-start | bytes 184328 | tf_op jit(solution)/shard_map/ppermute | solution.py:398
  136.5 3.3 %collective-permute-start.8 = (f32[120,128]{1,0:T(8,128)S(1)}, f32[120,128]{1,0:T(8,128)S(1)}, u32[]{:S(2)}, u32[]{:S(2)}) collective-permute-start(f32[120,128]{1,0:T(8,128)S(1)} %get-tuple-element.70), channel_id=1, source_target_pairs={{0,1},{1,0},{2,3},{3,2},{4,6},{5,7},{6,4},{7,5},{8,9},{9,8},{10,11... | collective-permute-start | bytes 184328 | tf_op jit(solution)/shard_map/ppermute | solution.py:398
  136.7 3.1 %collective-permute-start.9 = (f32[120,128]{1,0:T(8,128)S(1)}, f32[120,128]{1,0:T(8,128)S(1)}, u32[]{:S(2)}, u32[]{:S(2)}) collective-permute-start(f32[120,128]{1,0:T(8,128)S(1)} %get-tuple-element.69), channel_id=1, source_target_pairs={{0,2},{1,3},{2,0},{3,1},{4,5},{5,4},{6,7},{7,6},{8,10},{9,11},{10,... | collective-permute-start | bytes 184328 | tf_op jit(solution)/shard_map/ppermute | solution.py:398
  139.8 5.9 %collective-permute-start.10 = (f32[120,128]{1,0:T(8,128)S(1)}, f32[120,128]{1,0:T(8,128)S(1)}, u32[]{:S(2)}, u32[]{:S(2)}) collective-permute-start(f32[120,128]{1,0:T(8,128)S(1)} %add_add_fusion.1), channel_id=1, source_target_pairs={{0,24},{4,28},{8,16},{12,20},{16,8},{20,12},{24,0},{28,4},{1,25},{... | collective-permute-start | bytes 184328 | tf_op jit(solution)/shard_map/ppermute | solution.py:14
  142.1 4.6 %collective-permute-start.11 = (f32[120,128]{1,0:T(8,128)S(1)}, f32[120,128]{1,0:T(8,128)S(1)}, u32[]{:S(2)}, u32[]{:S(2)}) collective-permute-start(f32[120,128]{1,0:T(8,128)S(1)} %add_add_fusion.1), channel_id=1, source_target_pairs={{0,8},{4,12},{8,0},{12,4},{16,24},{20,28},{24,16},{28,20},{1,9},{5... | collective-permute-start | bytes 184328 | tf_op jit(solution)/shard_map/ppermute | solution.py:14
  142.1 4.6 %collective-permute-start.12 = (f32[120,128]{1,0:T(8,128)S(1)}, f32[120,128]{1,0:T(8,128)S(1)}, u32[]{:S(2)}, u32[]{:S(2)}) collective-permute-start(f32[120,128]{1,0:T(8,128)S(1)} %add_add_fusion.1), channel_id=1, source_target_pairs={{0,16},{4,20},{8,24},{12,28},{16,0},{20,4},{24,8},{28,12},{1,17},{... | collective-permute-start | bytes 184328 | tf_op jit(solution)/shard_map/ppermute | solution.py:14
  143.5 5.6 %collective-permute-start.16 = (f32[112,128]{1,0:T(8,128)S(1)}, f32[112,128]{1,0:T(8,128)S(1)}, u32[]{:S(2)}, u32[]{:S(2)}) collective-permute-start(f32[112,128]{1,0:T(8,128)S(1)} %get-tuple-element.65), channel_id=1, source_target_pairs={{0,3},{1,2},{2,1},{3,0},{4,7},{5,6},{6,5},{7,4},{8,11},{9,10},{10,... | collective-permute-start | bytes 172040 | tf_op jit(solution)/shard_map/ppermute | solution.py:398
  145.6 3.5 %collective-permute-start.17 = (f32[112,128]{1,0:T(8,128)S(1)}, f32[112,128]{1,0:T(8,128)S(1)}, u32[]{:S(2)}, u32[]{:S(2)}) collective-permute-start(f32[112,128]{1,0:T(8,128)S(1)} %get-tuple-element.67), channel_id=1, source_target_pairs={{0,1},{1,0},{2,3},{3,2},{4,6},{5,7},{6,4},{7,5},{8,9},{9,8},{10,11... | collective-permute-start | bytes 172040 | tf_op jit(solution)/shard_map/ppermute | solution.py:398
  145.7 3.4 %collective-permute-start.18 = (f32[112,128]{1,0:T(8,128)S(1)}, f32[112,128]{1,0:T(8,128)S(1)}, u32[]{:S(2)}, u32[]{:S(2)}) collective-permute-start(f32[112,128]{1,0:T(8,128)S(1)} %get-tuple-element.66), channel_id=1, source_target_pairs={{0,2},{1,3},{2,0},{3,1},{4,5},{5,4},{6,7},{7,6},{8,10},{9,11},{10,... | collective-permute-start | bytes 172040 | tf_op jit(solution)/shard_map/ppermute | solution.py:398
  146.8 7.2 %collective-permute-start.13 = (f32[120,128]{1,0:T(8,128)S(1)}, f32[120,128]{1,0:T(8,128)S(1)}, u32[]{:S(2)}, u32[]{:S(2)}) collective-permute-start(f32[120,128]{1,0:T(8,128)S(1)} %get-tuple-element.59), channel_id=1, source_target_pairs={{0,3},{1,2},{2,1},{3,0},{4,7},{5,6},{6,5},{7,4},{8,11},{9,10},{10,... | collective-permute-start | bytes 184328 | tf_op jit(solution)/shard_map/ppermute | solution.py:398
  149.2 7.9 %collective-permute-start.19 = (f32[112,128]{1,0:T(8,128)S(1)}, f32[112,128]{1,0:T(8,128)S(1)}, u32[]{:S(2)}, u32[]{:S(2)}) collective-permute-start(f32[112,128]{1,0:T(8,128)S(1)} %add_add_fusion.3), channel_id=1, source_target_pairs={{0,24},{4,28},{8,16},{12,20},{16,8},{20,12},{24,0},{28,4},{1,25},{... | collective-permute-start | bytes 172040 | tf_op jit(solution)/shard_map/ppermute | solution.py:14
  151.1 5.9 %collective-permute-start.20 = (f32[112,128]{1,0:T(8,128)S(1)}, f32[112,128]{1,0:T(8,128)S(1)}, u32[]{:S(2)}, u32[]{:S(2)}) collective-permute-start(f32[112,128]{1,0:T(8,128)S(1)} %add_add_fusion.3), channel_id=1, source_target_pairs={{0,8},{4,12},{8,0},{12,4},{16,24},{20,28},{24,16},{28,20},{1,9},{5... | collective-permute-start | bytes 172040 | tf_op jit(solution)/shard_map/ppermute | solution.py:14
  151.1 5.9 %collective-permute-start.21 = (f32[112,128]{1,0:T(8,128)S(1)}, f32[112,128]{1,0:T(8,128)S(1)}, u32[]{:S(2)}, u32[]{:S(2)}) collective-permute-start(f32[112,128]{1,0:T(8,128)S(1)} %add_add_fusion.3), channel_id=1, source_target_pairs={{0,16},{4,20},{8,24},{12,28},{16,0},{20,4},{24,8},{28,12},{1,17},{... | collective-permute-start | bytes 172040 | tf_op jit(solution)/shard_map/ppermute | solution.py:14
  152.8 3.1 %collective-permute-start.14 = (f32[120,128]{1,0:T(8,128)S(1)}, f32[120,128]{1,0:T(8,128)S(1)}, u32[]{:S(2)}, u32[]{:S(2)}) collective-permute-start(f32[120,128]{1,0:T(8,128)S(1)} %get-tuple-element.59), channel_id=1, source_target_pairs={{0,1},{1,0},{2,3},{3,2},{4,6},{5,7},{6,4},{7,5},{8,9},{9,8},{10,11... | collective-permute-start | bytes 184328 | tf_op jit(solution)/shard_map/ppermute | solution.py:398
  154.0 3.1 %collective-permute-start.15 = (f32[120,128]{1,0:T(8,128)S(1)}, f32[120,128]{1,0:T(8,128)S(1)}, u32[]{:S(2)}, u32[]{:S(2)}) collective-permute-start(f32[120,128]{1,0:T(8,128)S(1)} %get-tuple-element.59), channel_id=1, source_target_pairs={{0,2},{1,3},{2,0},{3,1},{4,5},{5,4},{6,7},{7,6},{8,10},{9,11},{10,... | collective-permute-start | bytes 184328 | tf_op jit(solution)/shard_map/ppermute | solution.py:398
  157.1 4.0 %collective-permute-start.22 = (f32[112,128]{1,0:T(8,128)S(1)}, f32[112,128]{1,0:T(8,128)S(1)}, u32[]{:S(2)}, u32[]{:S(2)}) collective-permute-start(f32[112,128]{1,0:T(8,128)S(1)} %get-tuple-element.57), channel_id=1, source_target_pairs={{0,3},{1,2},{2,1},{3,0},{4,7},{5,6},{6,5},{7,4},{8,11},{9,10},{10,... | collective-permute-start | bytes 172040 | tf_op jit(solution)/shard_map/ppermute | solution.py:398
  158.9 3.6 %collective-permute-start.23 = (f32[112,128]{1,0:T(8,128)S(1)}, f32[112,128]{1,0:T(8,128)S(1)}, u32[]{:S(2)}, u32[]{:S(2)}) collective-permute-start(f32[112,128]{1,0:T(8,128)S(1)} %get-tuple-element.57), channel_id=1, source_target_pairs={{0,1},{1,0},{2,3},{3,2},{4,6},{5,7},{6,4},{7,5},{8,9},{9,8},{10,11... | collective-permute-start | bytes 172040 | tf_op jit(solution)/shard_map/ppermute | solution.py:398
  159.2 3.3 %collective-permute-start.24 = (f32[112,128]{1,0:T(8,128)S(1)}, f32[112,128]{1,0:T(8,128)S(1)}, u32[]{:S(2)}, u32[]{:S(2)}) collective-permute-start(f32[112,128]{1,0:T(8,128)S(1)} %get-tuple-element.57), channel_id=1, source_target_pairs={{0,2},{1,3},{2,0},{3,1},{4,5},{5,4},{6,7},{7,6},{8,10},{9,11},{10,... | collective-permute-start | bytes 172040 | tf_op jit(solution)/shard_map/ppermute | solution.py:398
  162.5 9.1 %collective-permute-start.25 = (f32[928,128]{1,0:T(8,128)S(1)}, f32[928,128]{1,0:T(8,128)S(1)}, u32[]{:S(2)}, u32[]{:S(2)}) collective-permute-start(f32[928,128]{1,0:T(8,128)S(1)} %bitcast.21), channel_id=1, source_target_pairs={{0,4},{4,0},{8,12},{12,8},{16,20},{20,16},{24,28},{28,24},{1,5},{5... | collective-permute-start | bytes 1425416 | tf_op jit(solution)/shard_map/ppermute | solution.py:14
  187.1 6.0 %collective-permute-start.26 = (f32[24,1024]{1,0:T(8,128)S(1)}, f32[24,1024]{1,0:T(8,128)S(1)}, u32[]{:S(2)}, u32[]{:S(2)}) collective-permute-start(f32[24,1024]{1,0:T(8,128)S(1)} %get-tuple-element.48), channel_id=1, source_target_pairs={{0,24},{4,28},{8,16},{12,20},{16,8},{20,12},{24,0},{28,4},{1,25},{... | collective-permute-start | bytes 294920 | tf_op jit(solution)/shard_map/ppermute | solution.py:14
  189.3 7.2 %collective-permute-start.27 = (f32[24,1024]{1,0:T(8,128)S(1)}, f32[24,1024]{1,0:T(8,128)S(1)}, u32[]{:S(2)}, u32[]{:S(2)}) collective-permute-start(f32[24,1024]{1,0:T(8,128)S(1)} %get-tuple-element.49), channel_id=1, source_target_pairs={{0,28},{4,24},{8,20},{12,16},{16,12},{20,8},{24,4},{28,0},{1,29},{... | collective-permute-start | bytes 294920 | tf_op jit(solution)/shard_map/ppermute | solution.py:14
  190.9 7.7 %collective-permute-start.28 = (f32[24,1024]{1,0:T(8,128)S(1)}, f32[24,1024]{1,0:T(8,128)S(1)}, u32[]{:S(2)}, u32[]{:S(2)}) collective-permute-start(f32[24,1024]{1,0:T(8,128)S(1)} %get-tuple-element.50), channel_id=1, source_target_pairs={{0,4},{4,0},{8,12},{12,8},{16,20},{20,16},{24,28},{28,24},{1,5},{5... | collective-permute-start | bytes 294920 | tf_op jit(solution)/shard_map/ppermute | solution.py:14
  190.9 7.7 %collective-permute-start.29 = (f32[24,1024]{1,0:T(8,128)S(1)}, f32[24,1024]{1,0:T(8,128)S(1)}, u32[]{:S(2)}, u32[]{:S(2)}) collective-permute-start(f32[24,1024]{1,0:T(8,128)S(1)} %get-tuple-element.51), channel_id=1, source_target_pairs={{0,8},{4,12},{8,0},{12,4},{16,24},{20,28},{24,16},{28,20},{1,9},{5... | collective-permute-start | bytes 294920 | tf_op jit(solution)/shard_map/ppermute | solution.py:14
  190.9 11.2 %collective-permute-start.30 = (f32[24,1024]{1,0:T(8,128)S(1)}, f32[24,1024]{1,0:T(8,128)S(1)}, u32[]{:S(2)}, u32[]{:S(2)}) collective-permute-start(f32[24,1024]{1,0:T(8,128)S(1)} %get-tuple-element.52), channel_id=1, source_target_pairs={{0,12},{4,8},{8,4},{12,0},{16,28},{20,24},{24,20},{28,16},{1,13},{... | collective-permute-start | bytes 294920 | tf_op jit(solution)/shard_map/ppermute | solution.py:14
  193.1 9.0 %collective-permute-start.31 = (f32[24,1024]{1,0:T(8,128)S(1)}, f32[24,1024]{1,0:T(8,128)S(1)}, u32[]{:S(2)}, u32[]{:S(2)}) collective-permute-start(f32[24,1024]{1,0:T(8,128)S(1)} %get-tuple-element.53), channel_id=1, source_target_pairs={{0,16},{4,20},{8,24},{12,28},{16,0},{20,4},{24,8},{28,12},{1,17},{... | collective-permute-start | bytes 294920 | tf_op jit(solution)/shard_map/ppermute | solution.py:14
  196.5 10.4 %collective-permute-start.32 = (f32[24,1024]{1,0:T(8,128)S(1)}, f32[24,1024]{1,0:T(8,128)S(1)}, u32[]{:S(2)}, u32[]{:S(2)}) collective-permute-start(f32[24,1024]{1,0:T(8,128)S(1)} %get-tuple-element.54), channel_id=1, source_target_pairs={{0,20},{4,16},{8,28},{12,24},{16,4},{20,0},{24,12},{28,8},{1,21},{... | collective-permute-start | bytes 294920 | tf_op jit(solution)/shard_map/ppermute | solution.py:14
  (6 other events, 137.2 us)

commit v14 on v12

--- a/solution.py
+++ b/solution.py
@@ -487,7 +487,7 @@
     mine, other = sum_everywhere(core, mine, theirs, fibre, rest)
     factor, *blocks = iterations(place, mine, other, start_basis.T, [*parts, *more], ITERS, zs)
     order = [2 * bits + d for bits in farthest_first(zs) for d in range(2)]
-    order.insert(2, 1)
+    order.append(1)
     moved = {bits: swap(blocks[bits], "fibre", fibre, bits) for bits in order}
     moved[0] = blocks[0]
     return (factor.T, assemble(place, moved, cols))

time: 203 us -> 202 us (level)
  waiting for transfers between devices: 105 us -> 102 us
    ppermute x18, waiting for transfers between devices: 93.7 us -> 91.1 us  [swap(): return lax.ppermute(x, axis, [(i, i ^ bits) for i in range(size)])]
where the time goes in v14:
time: 202 us
  waiting for transfers between devices  102 us (50%)
  starting transfers between devices  61 us (30%)
  Pallas kernels  30.8 us (15%)
  local copies, waits for them, and re-layouts  6.45 us (3%)
    ppermute x18, waiting for transfers between devices, swap(): return lax.ppermute(x, axis, [(i, i ^ bits) for i in range(size)])  91.1 us
    ppermute x18, starting transfers between devices, swap(): return lax.ppermute(x, axis, [(i, i ^ bits) for i in range(size)])  55.4 us
    pallas_call x1, Pallas kernels, iterations(): pl.pallas_call(functools.partial(iterations_kernel, iters, zs), out_shape...  15.5 us
    ppermute x6, waiting for transfers between devices, swap_rest(): return lax.ppermute(x, ('fibre', 'rest'), pairs)  11 us
    pallas_call x2, Pallas kernels, gram_part(): pl.pallas_call(functools.partial(kernel, starts), out_shape=[*sums, *part...  9.29 us
    ppermute x6, starting transfers between devices, swap_rest(): return lax.ppermute(x, ('fibre', 'rest'), pairs)  5.58 us
    pallas_call x1, Pallas kernels, prepare(): pl.pallas_call(functools.partial(prepare_kernel, cuts, pieces), out_shape...  4.37 us
  transfers between devices with their start and end apart: 24, of which 17 were waited for; matrix products, arithmetic and copies ran while one was open for 1% of the time, Pallas kernels for 5%

profile of v14, /device:TPU:1, one launch (start us, length us, event | category | flops | bytes accessed | tf_op | source)
XLA Modules:
  0.0 201.6 jit_solution(16704345001708112622)
XLA Ops:
  0.7 1.4 constant_dynamic-slice_fusion.6
  2.2 1.7 constant_dynamic-slice_fusion.5
  4.8 4.6 %collective-permute-start.4 = (f32[168,2048]{1,0:T(8,128)S(1)}, f32[168,2048]{1,0:T(8,128)S(1)}, u32[]{:S(2)}, u32[]{:S(2)}) collective-permute-start(f32[168,2048]{1,0:T(8,128)S(1)} %maximum_select_fusion), channel_id=1, source_target_pairs={{0,24},{4,28},{8,16},{12,20},{16,8},{20,12},{24,0},{28,4},{1,25},{... | collective-permute-start | bytes 4128776 | tf_op jit(solution)/shard_map/ppermute | solution.py:14
  10.9 4.4 %prepare.1 = (f32[168,1536]{1,0:T(8,128)S(1)}, f32[168,512]{1,0:T(8,128)S(1)}, f32[168,2048]{1,0:T(8,128)S(1)}, f32[168,2048]{1,0:T(8,128)}) custom-call(s32[2]{0:T(128)S(1)} %pad_add_fusion.place_ref, f32[84,16384]{1,0:T(8,128)} %slab_ref, f32[84,6144]{1,0:T(8,128)} %copy-done.4), custom_call_target="tpu_custom_call" | custom-call | bytes 100000000 | tf_op jit(solution)/shard_map/prepare/pallas_call | solution.py:57
  15.3 1.9 collective-permute-start.2
  17.2 2.3 %collective-permute-start.3 = (f32[168,1536]{1,0:T(8,128)S(1)}, f32[168,1536]{1,0:T(8,128)S(1)}, u32[]{:S(2)}, u32[]{:S(2)}) collective-permute-start(f32[168,1536]{1,0:T(8,128)S(1)} %get-tuple-element.35), channel_id=1, source_target_pairs={{0,16},{4,20},{8,24},{12,28},{16,0},{20,4},{24,8},{28,12},{1,17},{... | collective-permute-start | bytes 3096584 | tf_op jit(solution)/shard_map/ppermute | solution.py:14
  19.5 20.5 %collective-permute-done.4.refs_3_ = f32[168,2048]{1,0:T(8,128)S(1)} collective-permute-done((f32[168,2048]{1,0:T(8,128)S(1)}, f32[168,2048]{1,0:T(8,128)S(1)}, u32[]{:S(2)}, u32[]{:S(2)}) %collective-permute-start.4) | collective-permute-done | bytes 1376288 | tf_op jit(solution)/shard_map/ppermute | solution.py:14
  40.0 29.5 %collective-permute-start.5 = (f32[168,512]{1,0:T(8,128)S(1)}, f32[168,512]{1,0:T(8,128)S(1)}, u32[]{:S(2)}, u32[]{:S(2)}) collective-permute-start(f32[168,512]{1,0:T(8,128)S(1)} %get-tuple-element.40), channel_id=1, source_target_pairs={{0,16},{4,20},{8,24},{12,28},{16,0},{20,4},{24,8},{28,12},{1,17},{... | collective-permute-start | bytes 1032200 | tf_op jit(solution)/shard_map/ppermute | solution.py:14
  69.5 50.3 %collective-permute-done.3.refs_2_ = f32[168,1536]{1,0:T(8,128)S(1)} collective-permute-done((f32[168,1536]{1,0:T(8,128)S(1)}, f32[168,1536]{1,0:T(8,128)S(1)}, u32[]{:S(2)}, u32[]{:S(2)}) %collective-permute-start.3) | collective-permute-done | bytes 1032224 | tf_op jit(solution)/shard_map/ppermute | solution.py:14
  119.8 1.8 copy-done.1
  121.7 5.4 %gram_early.1 = (f32[1856,128]{1,0:T(8,128)S(1)}, bf16[672,1536]{1,0:T(8,128)(2,1)}, bf16[672,1536]{1,0:T(8,128)(2,1)}) custom-call(s32[2]{0:T(128)S(1)} %pad_add_fusion.place_ref, f32[168,2048]{1,0:T(8,128)S(1)} %copy-done.1, f32[168,2048]{1,0:T(8,128)S(1)} %collective-permute-done.2.refs_1_, f32[168,1536]{1,0:T(8,128)S(1)} %collective-permute-done.3.refs_2_, ...), custom_call_target="tpu_custom_call" | custom-call | flops 4161798144 | bytes 8257536 | tf_op jit(solution)/shard_map/gram_early/pallas_call | solution.py:229
  127.2 3.9 %gram_late.1 = (f32[928,128]{1,0:T(8,128)S(1)}, f32[928,128]{1,0:T(8,128)S(1)}, bf16[672,512]{1,0:T(8,128)(2,1)S(1)}, bf16[672,512]{1,0:T(8,128)(2,1)S(1)}) custom-call(s32[2]{0:T(128)S(1)} %pad_add_fusion.place_ref, f32[1856,128]{1,0:T(8,128)S(1)} %get-tuple-element.39.base_ref, f32[168,2048]{1,0:T(8,128)S(1)} %copy-done.1, f32[168,2048]{1,0:T(8,128)} %copy-done.2, ...), custom_call_target="tpu_custom_call" | custom-call | flops 1387266048 | bytes 2752512 | tf_op jit(solution)/shard_map/gram_late/pallas_call | solution.py:229
  131.1 1.5 collective-permute-start.6
  132.7 1.5 collective-permute-done.6
  134.2 2.2 %collective-permute-start.7 = (f32[232,128]{1,0:T(8,128)S(1)}, f32[232,128]{1,0:T(8,128)S(1)}, u32[]{:S(2)}, u32[]{:S(2)}) collective-permute-start(f32[232,128]{1,0:T(8,128)S(1)} %get-tuple-element.63), channel_id=1, source_target_pairs={{0,3},{1,2},{2,1},{3,0},{4,7},{5,6},{6,5},{7,4},{8,11},{9,10},{10,... | collective-permute-start | bytes 356360 | tf_op jit(solution)/shard_map/ppermute | solution.py:398
  136.9 2.7 %collective-permute-done.7 = f32[232,128]{1,0:T(8,128)S(1)} collective-permute-done((f32[232,128]{1,0:T(8,128)S(1)}, f32[232,128]{1,0:T(8,128)S(1)}, u32[]{:S(2)}, u32[]{:S(2)}) %collective-permute-start.7) | collective-permute-done | bytes 118816 | tf_op jit(solution)/shard_map/ppermute | solution.py:398
  139.6 2.9 %collective-permute-done.8 = f32[232,128]{1,0:T(8,128)S(1)} collective-permute-done((f32[232,128]{1,0:T(8,128)S(1)}, f32[232,128]{1,0:T(8,128)S(1)}, u32[]{:S(2)}, u32[]{:S(2)}) %collective-permute-start.8) | collective-permute-done | bytes 118816 | tf_op jit(solution)/shard_map/ppermute | solution.py:398
  142.6 2.3 %collective-permute-start.10 = (f32[232,128]{1,0:T(8,128)S(1)}, f32[232,128]{1,0:T(8,128)S(1)}, u32[]{:S(2)}, u32[]{:S(2)}) collective-permute-start(f32[232,128]{1,0:T(8,128)S(1)} %add_add_fusion.1), channel_id=1, source_target_pairs={{0,24},{4,28},{8,16},{12,20},{16,8},{20,12},{24,0},{28,4},{1,25},{... | collective-permute-start | bytes 356360 | tf_op jit(solution)/shard_map/ppermute | solution.py:14
  146.2 2.0 %collective-permute-done.10 = f32[232,128]{1,0:T(8,128)S(1)} collective-permute-done((f32[232,128]{1,0:T(8,128)S(1)}, f32[232,128]{1,0:T(8,128)S(1)}, u32[]{:S(2)}, u32[]{:S(2)}) %collective-permute-start.10) | collective-permute-done | bytes 118816 | tf_op jit(solution)/shard_map/ppermute | solution.py:14
  148.2 6.4 %collective-permute-done.11 = f32[232,128]{1,0:T(8,128)S(1)} collective-permute-done((f32[232,128]{1,0:T(8,128)S(1)}, f32[232,128]{1,0:T(8,128)S(1)}, u32[]{:S(2)}, u32[]{:S(2)}) %collective-permute-start.11) | collective-permute-done | bytes 118816 | tf_op jit(solution)/shard_map/ppermute | solution.py:14
  157.6 2.4 %collective-permute-done.13 = f32[232,128]{1,0:T(8,128)S(1)} collective-permute-done((f32[232,128]{1,0:T(8,128)S(1)}, f32[232,128]{1,0:T(8,128)S(1)}, u32[]{:S(2)}, u32[]{:S(2)}) %collective-permute-start.13) | collective-permute-done | bytes 118816 | tf_op jit(solution)/shard_map/ppermute | solution.py:398
  160.0 2.4 %collective-permute-done.14 = f32[232,128]{1,0:T(8,128)S(1)} collective-permute-done((f32[232,128]{1,0:T(8,128)S(1)}, f32[232,128]{1,0:T(8,128)S(1)}, u32[]{:S(2)}, u32[]{:S(2)}) %collective-permute-start.14) | collective-permute-done | bytes 118816 | tf_op jit(solution)/shard_map/ppermute | solution.py:398
  163.1 1.4 collective-permute-start.16
  164.5 1.5 collective-permute-done.16.other_ref
  166.0 15.5 %iterations.1 = (f32[96,672]{1,0:T(8,128)}, f32[24,1024]{1,0:T(8,128)S(1)}, f32[24,1024]{1,0:T(8,128)S(1)}, f32[24,1024]{1,0:T(8,128)S(1)}, f32[24,1024]{1,0:T(8...) custom-call(s32[2]{0:T(128)S(1)} %pad_add_fusion.place_ref, ...), custom_call_target="tpu_custom_call" | custom-call | tf_op jit(solution)/shard_map/iterations/pallas_call | solution.py:371
  182.2 3.2 %collective-permute-start.18 = (f32[24,1024]{1,0:T(8,128)S(1)}, f32[24,1024]{1,0:T(8,128)S(1)}, u32[]{:S(2)}, u32[]{:S(2)}) collective-permute-start(f32[24,1024]{1,0:T(8,128)S(1)} %get-tuple-element.49), channel_id=1, source_target_pairs={{0,28},{4,24},{8,20},{12,16},{16,12},{20,8},{24,4},{28,0},{1,29},{... | collective-permute-start | bytes 294920 | tf_op jit(solution)/shard_map/ppermute | solution.py:14
  185.3 1.5 collective-permute-start.20
  187.4 4.7 %collective-permute-start.22 = (f32[24,1024]{1,0:T(8,128)S(1)}, f32[24,1024]{1,0:T(8,128)S(1)}, u32[]{:S(2)}, u32[]{:S(2)}) collective-permute-start(f32[24,1024]{1,0:T(8,128)S(1)} %get-tuple-element.53), channel_id=1, source_target_pairs={{0,20},{4,16},{8,28},{12,24},{16,4},{20,0},{24,12},{28,8},{1,21},{... | collective-permute-start | bytes 294920 | tf_op jit(solution)/shard_map/ppermute | solution.py:14
  192.1 2.8 %collective-permute-done.19.refs_2_ = f32[24,1024]{1,0:T(8,128)S(1)} collective-permute-done((f32[24,1024]{1,0:T(8,128)S(1)}, f32[24,1024]{1,0:T(8,128)S(1)}, u32[]{:S(2)}, u32[]{:S(2)}) %collective-permute-start.19) | collective-permute-done | bytes 98336 | tf_op jit(solution)/shard_map/ppermute | solution.py:14
  194.8 2.5 %collective-permute-done.20.refs_3_ = f32[24,1024]{1,0:T(8,128)S(1)} collective-permute-done((f32[24,1024]{1,0:T(8,128)S(1)}, f32[24,1024]{1,0:T(8,128)S(1)}, u32[]{:S(2)}, u32[]{:S(2)}) %collective-permute-start.20) | collective-permute-done | bytes 98336 | tf_op jit(solution)/shard_map/ppermute | solution.py:14
  197.3 2.7 %collective-permute-done.22.refs_5_ = f32[24,1024]{1,0:T(8,128)S(1)} collective-permute-done((f32[24,1024]{1,0:T(8,128)S(1)}, f32[24,1024]{1,0:T(8,128)S(1)}, u32[]{:S(2)}, u32[]{:S(2)}) %collective-permute-start.22) | collective-permute-done | bytes 98336 | tf_op jit(solution)/shard_map/ppermute | solution.py:14
  200.0 1.6 assemble.1
  (44 shorter events, 9.4 us)
Async XLA Ops:
  2.1 2.3 %collective-permute-start = (f32[84,2048]{1,0:T(8,128)S(1)}, f32[84,2048]{1,0:T(8,128)S(1)}, u32[]{:S(2)}, u32[]{:S(2)}) collective-permute-start(f32[84,2048]{1,0:T(8,128)S(1)} %get-tuple-element.31), channel_id=1, source_target_pairs={{0,4},{4,0},{8,12},{12,8},{16,20},{20,16},{24,28},{28,24},{1,5},{5... | collective-permute-start | bytes 2064392 | tf_op jit(solution)/shard_map/ppermute | solution.py:14
  4.5 5.0 %collective-permute-start.1 = (f32[84,6144]{1,0:T(8,128)S(1)}, f32[84,6144]{1,0:T(8,128)S(1)}, u32[]{:S(2)}, u32[]{:S(2)}) collective-permute-start(f32[84,6144]{1,0:T(8,128)S(1)} %pad_maximum_fusion), channel_id=1, source_target_pairs={{0,4},{4,0},{8,12},{12,8},{16,20},{20,16},{24,28},{28,24},{1,5},{5... | collective-permute-start | bytes 6193160 | tf_op jit(solution)/shard_map/ppermute | solution.py:14
  4.8 35.2 %collective-permute-start.4 = (f32[168,2048]{1,0:T(8,128)S(1)}, f32[168,2048]{1,0:T(8,128)S(1)}, u32[]{:S(2)}, u32[]{:S(2)}) collective-permute-start(f32[168,2048]{1,0:T(8,128)S(1)} %maximum_select_fusion), channel_id=1, source_target_pairs={{0,24},{4,28},{8,16},{12,20},{16,8},{20,12},{24,0},{28,4},{1,25},{... | collective-permute-start | bytes 4128776 | tf_op jit(solution)/shard_map/ppermute | solution.py:14
  9.5 1.4 copy-start.4
  15.3 104.6 %collective-permute-start.2 = (f32[168,2048]{1,0:T(8,128)S(1)}, f32[168,2048]{1,0:T(8,128)S(1)}, u32[]{:S(2)}, u32[]{:S(2)}) collective-permute-start(f32[168,2048]{1,0:T(8,128)S(1)} %get-tuple-element.34), channel_id=1, source_target_pairs={{0,8},{4,12},{8,0},{12,4},{16,24},{20,28},{24,16},{28,20},{1,9},{5... | collective-permute-start | bytes 4128776 | tf_op jit(solution)/shard_map/ppermute | solution.py:14
  17.2 102.7 %collective-permute-start.3 = (f32[168,1536]{1,0:T(8,128)S(1)}, f32[168,1536]{1,0:T(8,128)S(1)}, u32[]{:S(2)}, u32[]{:S(2)}) collective-permute-start(f32[168,1536]{1,0:T(8,128)S(1)} %get-tuple-element.35), channel_id=1, source_target_pairs={{0,16},{4,20},{8,24},{12,28},{16,0},{20,4},{24,8},{28,12},{1,17},{... | collective-permute-start | bytes 3096584 | tf_op jit(solution)/shard_map/ppermute | solution.py:14
  40.0 87.1 %copy-start = (f32[168,2048]{1,0:T(8,128)}, f32[168,2048]{1,0:T(8,128)S(1)}, u32[]{:S(2)}) copy-start(f32[168,2048]{1,0:T(8,128)S(1)} %collective-permute-done.4.refs_3_) | copy-start | bytes 4128772
  40.0 87.2 %collective-permute-start.5 = (f32[168,512]{1,0:T(8,128)S(1)}, f32[168,512]{1,0:T(8,128)S(1)}, u32[]{:S(2)}, u32[]{:S(2)}) collective-permute-start(f32[168,512]{1,0:T(8,128)S(1)} %get-tuple-element.40), channel_id=1, source_target_pairs={{0,16},{4,20},{8,24},{12,28},{16,0},{20,4},{24,8},{28,12},{1,17},{... | collective-permute-start | bytes 1032200 | tf_op jit(solution)/shard_map/ppermute | solution.py:14
  119.8 7.2 %copy-start.2 = (f32[168,2048]{1,0:T(8,128)}, f32[168,2048]{1,0:T(8,128)S(1)}, u32[]{:S(2)}) copy-start(f32[168,2048]{1,0:T(8,128)S(1)} %collective-permute-done.2.refs_1_) | copy-start | bytes 4128772
  119.8 1.8 copy-start.1
  131.1 3.0 %collective-permute-start.6 = (f32[928,128]{1,0:T(8,128)S(1)}, f32[928,128]{1,0:T(8,128)S(1)}, u32[]{:S(2)}, u32[]{:S(2)}) collective-permute-start(f32[928,128]{1,0:T(8,128)S(1)} %get-tuple-element.42), channel_id=1, source_target_pairs={{0,4},{4,0},{8,12},{12,8},{16,20},{20,16},{24,28},{28,24},{1,5},{5... | collective-permute-start | bytes 1425416 | tf_op jit(solution)/shard_map/ppermute | solution.py:14
  134.1 31.8 %copy-start.3 = (f32[672,96]{0,1:T(8,128)S(1)}, f32[672,96]{0,1:T(8,128)}, u32[]{:S(2)}) copy-start(f32[672,96]{0,1:T(8,128)} %param.3) | copy-start | bytes 774148
  134.2 5.4 %collective-permute-start.7 = (f32[232,128]{1,0:T(8,128)S(1)}, f32[232,128]{1,0:T(8,128)S(1)}, u32[]{:S(2)}, u32[]{:S(2)}) collective-permute-start(f32[232,128]{1,0:T(8,128)S(1)} %get-tuple-element.63), channel_id=1, source_target_pairs={{0,3},{1,2},{2,1},{3,0},{4,7},{5,6},{6,5},{7,4},{8,11},{9,10},{10,... | collective-permute-start | bytes 356360 | tf_op jit(solution)/shard_map/ppermute | solution.py:398
  136.5 6.1 %collective-permute-start.8 = (f32[232,128]{1,0:T(8,128)S(1)}, f32[232,128]{1,0:T(8,128)S(1)}, u32[]{:S(2)}, u32[]{:S(2)}) collective-permute-start(f32[232,128]{1,0:T(8,128)S(1)} %get-tuple-element.65), channel_id=1, source_target_pairs={{0,1},{1,0},{2,3},{3,2},{4,6},{5,7},{6,4},{7,5},{8,9},{9,8},{10,11... | collective-permute-start | bytes 356360 | tf_op jit(solution)/shard_map/ppermute | solution.py:398
  136.7 5.9 %collective-permute-start.9 = (f32[232,128]{1,0:T(8,128)S(1)}, f32[232,128]{1,0:T(8,128)S(1)}, u32[]{:S(2)}, u32[]{:S(2)}) collective-permute-start(f32[232,128]{1,0:T(8,128)S(1)} %get-tuple-element.64), channel_id=1, source_target_pairs={{0,2},{1,3},{2,0},{3,1},{4,5},{5,4},{6,7},{7,6},{8,10},{9,11},{10,... | collective-permute-start | bytes 356360 | tf_op jit(solution)/shard_map/ppermute | solution.py:398
  142.6 5.6 %collective-permute-start.10 = (f32[232,128]{1,0:T(8,128)S(1)}, f32[232,128]{1,0:T(8,128)S(1)}, u32[]{:S(2)}, u32[]{:S(2)}) collective-permute-start(f32[232,128]{1,0:T(8,128)S(1)} %add_add_fusion.1), channel_id=1, source_target_pairs={{0,24},{4,28},{8,16},{12,20},{16,8},{20,12},{24,0},{28,4},{1,25},{... | collective-permute-start | bytes 356360 | tf_op jit(solution)/shard_map/ppermute | solution.py:14
  144.9 9.8 %collective-permute-start.11 = (f32[232,128]{1,0:T(8,128)S(1)}, f32[232,128]{1,0:T(8,128)S(1)}, u32[]{:S(2)}, u32[]{:S(2)}) collective-permute-start(f32[232,128]{1,0:T(8,128)S(1)} %add_add_fusion.1), channel_id=1, source_target_pairs={{0,8},{4,12},{8,0},{12,4},{16,24},{20,28},{24,16},{28,20},{1,9},{5... | collective-permute-start | bytes 356360 | tf_op jit(solution)/shard_map/ppermute | solution.py:14
  144.9 9.8 %collective-permute-start.12 = (f32[232,128]{1,0:T(8,128)S(1)}, f32[232,128]{1,0:T(8,128)S(1)}, u32[]{:S(2)}, u32[]{:S(2)}) collective-permute-start(f32[232,128]{1,0:T(8,128)S(1)} %add_add_fusion.1), channel_id=1, source_target_pairs={{0,16},{4,20},{8,24},{12,28},{16,0},{20,4},{24,8},{28,12},{1,17},{... | collective-permute-start | bytes 356360 | tf_op jit(solution)/shard_map/ppermute | solution.py:14
  154.7 5.3 %collective-permute-start.13 = (f32[232,128]{1,0:T(8,128)S(1)}, f32[232,128]{1,0:T(8,128)S(1)}, u32[]{:S(2)}, u32[]{:S(2)}) collective-permute-start(f32[232,128]{1,0:T(8,128)S(1)} %get-tuple-element.57), channel_id=1, source_target_pairs={{0,3},{1,2},{2,1},{3,0},{4,7},{5,6},{6,5},{7,4},{8,11},{9,10},{10,... | collective-permute-start | bytes 356360 | tf_op jit(solution)/shard_map/ppermute | solution.py:398
  155.7 6.8 %collective-permute-start.14 = (f32[232,128]{1,0:T(8,128)S(1)}, f32[232,128]{1,0:T(8,128)S(1)}, u32[]{:S(2)}, u32[]{:S(2)}) collective-permute-start(f32[232,128]{1,0:T(8,128)S(1)} %get-tuple-element.57), channel_id=1, source_target_pairs={{0,1},{1,0},{2,3},{3,2},{4,6},{5,7},{6,4},{7,5},{8,9},{9,8},{10,11... | collective-permute-start | bytes 356360 | tf_op jit(solution)/shard_map/ppermute | solution.py:398
  157.0 6.1 %collective-permute-start.15 = (f32[232,128]{1,0:T(8,128)S(1)}, f32[232,128]{1,0:T(8,128)S(1)}, u32[]{:S(2)}, u32[]{:S(2)}) collective-permute-start(f32[232,128]{1,0:T(8,128)S(1)} %get-tuple-element.57), channel_id=1, source_target_pairs={{0,2},{1,3},{2,0},{3,1},{4,5},{5,4},{6,7},{7,6},{8,10},{9,11},{10,... | collective-permute-start | bytes 356360 | tf_op jit(solution)/shard_map/ppermute | solution.py:398
  163.1 2.9 %collective-permute-start.16 = (f32[928,128]{1,0:T(8,128)S(1)}, f32[928,128]{1,0:T(8,128)S(1)}, u32[]{:S(2)}, u32[]{:S(2)}) collective-permute-start(f32[928,128]{1,0:T(8,128)S(1)} %bitcast.13), channel_id=1, source_target_pairs={{0,4},{4,0},{8,12},{12,8},{16,20},{20,16},{24,28},{28,24},{1,5},{5... | collective-permute-start | bytes 1425416 | tf_op jit(solution)/shard_map/ppermute | solution.py:14
  181.5 5.9 %collective-permute-start.17 = (f32[24,1024]{1,0:T(8,128)S(1)}, f32[24,1024]{1,0:T(8,128)S(1)}, u32[]{:S(2)}, u32[]{:S(2)}) collective-permute-start(f32[24,1024]{1,0:T(8,128)S(1)} %get-tuple-element.48), channel_id=1, source_target_pairs={{0,24},{4,28},{8,16},{12,20},{16,8},{20,12},{24,0},{28,4},{1,25},{... | collective-permute-start | bytes 294920 | tf_op jit(solution)/shard_map/ppermute | solution.py:14
  182.2 9.9 %collective-permute-start.18 = (f32[24,1024]{1,0:T(8,128)S(1)}, f32[24,1024]{1,0:T(8,128)S(1)}, u32[]{:S(2)}, u32[]{:S(2)}) collective-permute-start(f32[24,1024]{1,0:T(8,128)S(1)} %get-tuple-element.49), channel_id=1, source_target_pairs={{0,28},{4,24},{8,20},{12,16},{16,12},{20,8},{24,4},{28,0},{1,29},{... | collective-permute-start | bytes 294920 | tf_op jit(solution)/shard_map/ppermute | solution.py:14
  185.3 9.5 %collective-permute-start.19 = (f32[24,1024]{1,0:T(8,128)S(1)}, f32[24,1024]{1,0:T(8,128)S(1)}, u32[]{:S(2)}, u32[]{:S(2)}) collective-permute-start(f32[24,1024]{1,0:T(8,128)S(1)} %get-tuple-element.50), channel_id=1, source_target_pairs={{0,8},{4,12},{8,0},{12,4},{16,24},{20,28},{24,16},{28,20},{1,9},{5... | collective-permute-start | bytes 294920 | tf_op jit(solution)/shard_map/ppermute | solution.py:14
  185.3 12.0 %collective-permute-start.20 = (f32[24,1024]{1,0:T(8,128)S(1)}, f32[24,1024]{1,0:T(8,128)S(1)}, u32[]{:S(2)}, u32[]{:S(2)}) collective-permute-start(f32[24,1024]{1,0:T(8,128)S(1)} %get-tuple-element.51), channel_id=1, source_target_pairs={{0,12},{4,8},{8,4},{12,0},{16,28},{20,24},{24,20},{28,16},{1,13},{... | collective-permute-start | bytes 294920 | tf_op jit(solution)/shard_map/ppermute | solution.py:14
  186.8 10.5 %collective-permute-start.21 = (f32[24,1024]{1,0:T(8,128)S(1)}, f32[24,1024]{1,0:T(8,128)S(1)}, u32[]{:S(2)}, u32[]{:S(2)}) collective-permute-start(f32[24,1024]{1,0:T(8,128)S(1)} %get-tuple-element.52), channel_id=1, source_target_pairs={{0,16},{4,20},{8,24},{12,28},{16,0},{20,4},{24,8},{28,12},{1,17},{... | collective-permute-start | bytes 294920 | tf_op jit(solution)/shard_map/ppermute | solution.py:14
  187.4 12.6 %collective-permute-start.22 = (f32[24,1024]{1,0:T(8,128)S(1)}, f32[24,1024]{1,0:T(8,128)S(1)}, u32[]{:S(2)}, u32[]{:S(2)}) collective-permute-start(f32[24,1024]{1,0:T(8,128)S(1)} %get-tuple-element.53), channel_id=1, source_target_pairs={{0,20},{4,16},{8,28},{12,24},{16,4},{20,0},{24,12},{28,8},{1,21},{... | collective-permute-start | bytes 294920 | tf_op jit(solution)/shard_map/ppermute | solution.py:14
  192.1 7.9 %collective-permute-start.23 = (f32[24,1024]{1,0:T(8,128)S(1)}, f32[24,1024]{1,0:T(8,128)S(1)}, u32[]{:S(2)}, u32[]{:S(2)}) collective-permute-start(f32[24,1024]{1,0:T(8,128)S(1)} %get-tuple-element.54), channel_id=1, source_target_pairs={{0,4},{4,0},{8,12},{12,8},{16,20},{20,16},{24,28},{28,24},{1,5},{5... | collective-permute-start | bytes 294920 | tf_op jit(solution)/shard_map/ppermute | solution.py:14

commit v15 on v14

--- a/solution.py
+++ b/solution.py
@@ -461,8 +461,8 @@
         return lax.dynamic_slice(slab, (0, whose * half + (z ^ bits) * part + start), (rows, width))
 
     far = zs - 1
-    theirs, mine = cut(slab, 1 - core, far, 0, part), cut(slab, core, far, 0, part)
-    slab, theirs, mine = lax.optimization_barrier((slab, theirs, mine))
+    slab, theirs = lax.optimization_barrier((slab, cut(slab, 1 - core, far, 0, part)))
+    mine = cut(slab, core, far, 0, part)
     cuts = [(bits, 0, part) for bits in range(far - 1, -1, -1)]
     others = jnp.concatenate([cut(slab, 1 - core, *c) for c in cuts], 1)
     block = in_order(core, mine, swap(theirs, "fibre", fibre, 1), 0)

time: 202 us -> 202 us (level)
  transfers between devices with their start and end apart: 24 -> 24, of which waited for: 17 -> 16; matrix products, arithmetic and copies ran while one was open for 1% -> 1% of each run, Pallas kernels for 5% -> 5%
where the time goes in v15:
time: 202 us
  waiting for transfers between devices  101 us (50%)
  starting transfers between devices  61.7 us (31%)
  Pallas kernels  30.8 us (15%)
  local copies, waits for them, and re-layouts  6.45 us (3%)
    ppermute x18, waiting for transfers between devices, swap(): return lax.ppermute(x, axis, [(i, i ^ bits) for i in range(size)])  90.3 us
    ppermute x18, starting transfers between devices, swap(): return lax.ppermute(x, axis, [(i, i ^ bits) for i in range(size)])  56.1 us
    pallas_call x1, Pallas kernels, iterations(): pl.pallas_call(functools.partial(iterations_kernel, iters, zs), out_shape...  15.5 us
    ppermute x6, waiting for transfers between devices, swap_rest(): return lax.ppermute(x, ('fibre', 'rest'), pairs)  11 us
    pallas_call x2, Pallas kernels, gram_part(): pl.pallas_call(functools.partial(kernel, starts), out_shape=[*sums, *part...  9.29 us
    ppermute x6, starting transfers between devices, swap_rest(): return lax.ppermute(x, ('fibre', 'rest'), pairs)  5.61 us
    pallas_call x1, Pallas kernels, prepare(): pl.pallas_call(functools.partial(prepare_kernel, cuts, pieces), out_shape...  4.37 us
  transfers between devices with their start and end apart: 24, of which 16 were waited for; matrix products, arithmetic and copies ran while one was open for 1% of the time, Pallas kernels for 5%

profile of v15, /device:TPU:1, one launch (start us, length us, event | category | flops | bytes accessed | tf_op | source)
XLA Modules:
  0.0 201.6 jit_solution(7041092460263383505)
XLA Ops:
  2.0 2.0 constant_dynamic-slice_fusion.3
  4.8 4.4 %collective-permute-start.4 = (f32[168,2048]{1,0:T(8,128)S(1)}, f32[168,2048]{1,0:T(8,128)S(1)}, u32[]{:S(2)}, u32[]{:S(2)}) collective-permute-start(f32[168,2048]{1,0:T(8,128)S(1)} %maximum_select_fusion), channel_id=1, source_target_pairs={{0,24},{4,28},{8,16},{12,20},{16,8},{20,12},{24,0},{28,4},{1,25},{... | collective-permute-start | bytes 4128776 | tf_op jit(solution)/shard_map/ppermute | solution.py:14
  9.3 1.4 copy-done.4
  10.6 4.4 %prepare.1 = (f32[168,1536]{1,0:T(8,128)S(1)}, f32[168,512]{1,0:T(8,128)S(1)}, f32[168,2048]{1,0:T(8,128)S(1)}, f32[168,2048]{1,0:T(8,128)}) custom-call(s32[2]{0:T(128)S(1)} %pad_add_fusion.place_ref, f32[84,16384]{1,0:T(8,128)} %slab_ref, f32[84,6144]{1,0:T(8,128)} %copy-done.4), custom_call_target="tpu_custom_call" | custom-call | bytes 100000000 | tf_op jit(solution)/shard_map/prepare/pallas_call | solution.py:57
  15.0 2.1 %collective-permute-start.2 = (f32[168,2048]{1,0:T(8,128)S(1)}, f32[168,2048]{1,0:T(8,128)S(1)}, u32[]{:S(2)}, u32[]{:S(2)}) collective-permute-start(f32[168,2048]{1,0:T(8,128)S(1)} %get-tuple-element.32), channel_id=1, source_target_pairs={{0,8},{4,12},{8,0},{12,4},{16,24},{20,28},{24,16},{28,20},{1,9},{5... | collective-permute-start | bytes 4128776 | tf_op jit(solution)/shard_map/ppermute | solution.py:14
  17.2 2.3 %collective-permute-start.3 = (f32[168,1536]{1,0:T(8,128)S(1)}, f32[168,1536]{1,0:T(8,128)S(1)}, u32[]{:S(2)}, u32[]{:S(2)}) collective-permute-start(f32[168,1536]{1,0:T(8,128)S(1)} %get-tuple-element.33), channel_id=1, source_target_pairs={{0,16},{4,20},{8,24},{12,28},{16,0},{20,4},{24,8},{28,12},{1,17},{... | collective-permute-start | bytes 3096584 | tf_op jit(solution)/shard_map/ppermute | solution.py:14
  19.5 20.0 %collective-permute-done.4.refs_3_ = f32[168,2048]{1,0:T(8,128)S(1)} collective-permute-done((f32[168,2048]{1,0:T(8,128)S(1)}, f32[168,2048]{1,0:T(8,128)S(1)}, u32[]{:S(2)}, u32[]{:S(2)}) %collective-permute-start.4) | collective-permute-done | bytes 1376288 | tf_op jit(solution)/shard_map/ppermute | solution.py:14
  39.5 29.5 %collective-permute-start.5 = (f32[168,512]{1,0:T(8,128)S(1)}, f32[168,512]{1,0:T(8,128)S(1)}, u32[]{:S(2)}, u32[]{:S(2)}) collective-permute-start(f32[168,512]{1,0:T(8,128)S(1)} %get-tuple-element.38), channel_id=1, source_target_pairs={{0,16},{4,20},{8,24},{12,28},{16,0},{20,4},{24,8},{28,12},{1,17},{... | collective-permute-start | bytes 1032200 | tf_op jit(solution)/shard_map/ppermute | solution.py:14
  69.0 50.3 %collective-permute-done.3.refs_2_ = f32[168,1536]{1,0:T(8,128)S(1)} collective-permute-done((f32[168,1536]{1,0:T(8,128)S(1)}, f32[168,1536]{1,0:T(8,128)S(1)}, u32[]{:S(2)}, u32[]{:S(2)}) %collective-permute-start.3) | collective-permute-done | bytes 1032224 | tf_op jit(solution)/shard_map/ppermute | solution.py:14
  119.3 1.8 copy-done.1
  121.2 5.4 %gram_early.1 = (f32[1856,128]{1,0:T(8,128)S(1)}, bf16[672,1536]{1,0:T(8,128)(2,1)}, bf16[672,1536]{1,0:T(8,128)(2,1)}) custom-call(s32[2]{0:T(128)S(1)} %pad_add_fusion.place_ref, f32[168,2048]{1,0:T(8,128)S(1)} %copy-done.1, f32[168,2048]{1,0:T(8,128)S(1)} %collective-permute-done.2.refs_1_, f32[168,1536]{1,0:T(8,128)S(1)} %collective-permute-done.3.refs_2_, ...), custom_call_target="tpu_custom_call" | custom-call | flops 4161798144 | bytes 8257536 | tf_op jit(solution)/shard_map/gram_early/pallas_call | solution.py:229
  126.7 3.9 %gram_late.1 = (f32[928,128]{1,0:T(8,128)S(1)}, f32[928,128]{1,0:T(8,128)S(1)}, bf16[672,512]{1,0:T(8,128)(2,1)S(1)}, bf16[672,512]{1,0:T(8,128)(2,1)S(1)}) custom-call(s32[2]{0:T(128)S(1)} %pad_add_fusion.place_ref, f32[1856,128]{1,0:T(8,128)S(1)} %get-tuple-element.37.base_ref, f32[168,2048]{1,0:T(8,128)S(1)} %copy-done.1, f32[168,2048]{1,0:T(8,128)} %copy-done.2, ...), custom_call_target="tpu_custom_call" | custom-call | flops 1387266048 | bytes 2752512 | tf_op jit(solution)/shard_map/gram_late/pallas_call | solution.py:229
  130.6 2.1 %collective-permute-start.6 = (f32[928,128]{1,0:T(8,128)S(1)}, f32[928,128]{1,0:T(8,128)S(1)}, u32[]{:S(2)}, u32[]{:S(2)}) collective-permute-start(f32[928,128]{1,0:T(8,128)S(1)} %get-tuple-element.40), channel_id=1, source_target_pairs={{0,4},{4,0},{8,12},{12,8},{16,20},{20,16},{24,28},{28,24},{1,5},{5... | collective-permute-start | bytes 1425416 | tf_op jit(solution)/shard_map/ppermute | solution.py:14
  132.7 1.5 collective-permute-done.6
  134.3 2.2 %collective-permute-start.7 = (f32[232,128]{1,0:T(8,128)S(1)}, f32[232,128]{1,0:T(8,128)S(1)}, u32[]{:S(2)}, u32[]{:S(2)}) collective-permute-start(f32[232,128]{1,0:T(8,128)S(1)} %get-tuple-element.60), channel_id=1, source_target_pairs={{0,3},{1,2},{2,1},{3,0},{4,7},{5,6},{6,5},{7,4},{8,11},{9,10},{10,... | collective-permute-start | bytes 356360 | tf_op jit(solution)/shard_map/ppermute | solution.py:398
  137.0 2.7 %collective-permute-done.7 = f32[232,128]{1,0:T(8,128)S(1)} collective-permute-done((f32[232,128]{1,0:T(8,128)S(1)}, f32[232,128]{1,0:T(8,128)S(1)}, u32[]{:S(2)}, u32[]{:S(2)}) %collective-permute-start.7) | collective-permute-done | bytes 118816 | tf_op jit(solution)/shard_map/ppermute | solution.py:398
  139.7 2.9 %collective-permute-done.8 = f32[232,128]{1,0:T(8,128)S(1)} collective-permute-done((f32[232,128]{1,0:T(8,128)S(1)}, f32[232,128]{1,0:T(8,128)S(1)}, u32[]{:S(2)}, u32[]{:S(2)}) %collective-permute-start.8) | collective-permute-done | bytes 118816 | tf_op jit(solution)/shard_map/ppermute | solution.py:398
  142.6 2.3 %collective-permute-start.10 = (f32[232,128]{1,0:T(8,128)S(1)}, f32[232,128]{1,0:T(8,128)S(1)}, u32[]{:S(2)}, u32[]{:S(2)}) collective-permute-start(f32[232,128]{1,0:T(8,128)S(1)} %add_add_fusion.1), channel_id=1, source_target_pairs={{0,24},{4,28},{8,16},{12,20},{16,8},{20,12},{24,0},{28,4},{1,25},{... | collective-permute-start | bytes 356360 | tf_op jit(solution)/shard_map/ppermute | solution.py:14
  146.2 2.0 %collective-permute-done.10 = f32[232,128]{1,0:T(8,128)S(1)} collective-permute-done((f32[232,128]{1,0:T(8,128)S(1)}, f32[232,128]{1,0:T(8,128)S(1)}, u32[]{:S(2)}, u32[]{:S(2)}) %collective-permute-start.10) | collective-permute-done | bytes 118816 | tf_op jit(solution)/shard_map/ppermute | solution.py:14
  148.3 6.4 %collective-permute-done.11 = f32[232,128]{1,0:T(8,128)S(1)} collective-permute-done((f32[232,128]{1,0:T(8,128)S(1)}, f32[232,128]{1,0:T(8,128)S(1)}, u32[]{:S(2)}, u32[]{:S(2)}) %collective-permute-start.11) | collective-permute-done | bytes 118816 | tf_op jit(solution)/shard_map/ppermute | solution.py:14
  157.6 2.3 %collective-permute-done.13 = f32[232,128]{1,0:T(8,128)S(1)} collective-permute-done((f32[232,128]{1,0:T(8,128)S(1)}, f32[232,128]{1,0:T(8,128)S(1)}, u32[]{:S(2)}, u32[]{:S(2)}) %collective-permute-start.13) | collective-permute-done | bytes 118816 | tf_op jit(solution)/shard_map/ppermute | solution.py:398
  160.0 2.4 %collective-permute-done.14 = f32[232,128]{1,0:T(8,128)S(1)} collective-permute-done((f32[232,128]{1,0:T(8,128)S(1)}, f32[232,128]{1,0:T(8,128)S(1)}, u32[]{:S(2)}, u32[]{:S(2)}) %collective-permute-start.14) | collective-permute-done | bytes 118816 | tf_op jit(solution)/shard_map/ppermute | solution.py:398
  163.1 1.4 collective-permute-start.16
  164.5 1.5 collective-permute-done.16.other_ref
  166.0 15.5 %iterations.1 = (f32[96,672]{1,0:T(8,128)}, f32[24,1024]{1,0:T(8,128)S(1)}, f32[24,1024]{1,0:T(8,128)S(1)}, f32[24,1024]{1,0:T(8,128)S(1)}, f32[24,1024]{1,0:T(8...) custom-call(s32[2]{0:T(128)S(1)} %pad_add_fusion.place_ref, ...), custom_call_target="tpu_custom_call" | custom-call | tf_op jit(solution)/shard_map/iterations/pallas_call | solution.py:371
  182.1 3.2 %collective-permute-start.18 = (f32[24,1024]{1,0:T(8,128)S(1)}, f32[24,1024]{1,0:T(8,128)S(1)}, u32[]{:S(2)}, u32[]{:S(2)}) collective-permute-start(f32[24,1024]{1,0:T(8,128)S(1)} %get-tuple-element.47), channel_id=1, source_target_pairs={{0,28},{4,24},{8,20},{12,16},{16,12},{20,8},{24,4},{28,0},{1,29},{... | collective-permute-start | bytes 294920 | tf_op jit(solution)/shard_map/ppermute | solution.py:14
  185.3 1.5 collective-permute-start.20
  187.4 4.7 %collective-permute-start.22 = (f32[24,1024]{1,0:T(8,128)S(1)}, f32[24,1024]{1,0:T(8,128)S(1)}, u32[]{:S(2)}, u32[]{:S(2)}) collective-permute-start(f32[24,1024]{1,0:T(8,128)S(1)} %get-tuple-element.51), channel_id=1, source_target_pairs={{0,20},{4,16},{8,28},{12,24},{16,4},{20,0},{24,12},{28,8},{1,21},{... | collective-permute-start | bytes 294920 | tf_op jit(solution)/shard_map/ppermute | solution.py:14
  192.1 2.8 %collective-permute-done.19.refs_2_ = f32[24,1024]{1,0:T(8,128)S(1)} collective-permute-done((f32[24,1024]{1,0:T(8,128)S(1)}, f32[24,1024]{1,0:T(8,128)S(1)}, u32[]{:S(2)}, u32[]{:S(2)}) %collective-permute-start.19) | collective-permute-done | bytes 98336 | tf_op jit(solution)/shard_map/ppermute | solution.py:14
  194.9 2.4 %collective-permute-done.20.refs_3_ = f32[24,1024]{1,0:T(8,128)S(1)} collective-permute-done((f32[24,1024]{1,0:T(8,128)S(1)}, f32[24,1024]{1,0:T(8,128)S(1)}, u32[]{:S(2)}, u32[]{:S(2)}) %collective-permute-start.20) | collective-permute-done | bytes 98336 | tf_op jit(solution)/shard_map/ppermute | solution.py:14
  197.4 2.7 %collective-permute-done.22.refs_5_ = f32[24,1024]{1,0:T(8,128)S(1)} collective-permute-done((f32[24,1024]{1,0:T(8,128)S(1)}, f32[24,1024]{1,0:T(8,128)S(1)}, u32[]{:S(2)}, u32[]{:S(2)}) %collective-permute-start.22) | collective-permute-done | bytes 98336 | tf_op jit(solution)/shard_map/ppermute | solution.py:14
  200.0 1.6 assemble.1
  (44 shorter events, 9.2 us)
Async XLA Ops:
  1.8 2.3 %collective-permute-start = (f32[84,2048]{1,0:T(8,128)S(1)}, f32[84,2048]{1,0:T(8,128)S(1)}, u32[]{:S(2)}, u32[]{:S(2)}) collective-permute-start(f32[84,2048]{1,0:T(8,128)S(1)} %constant_dynamic-slice_fusion.7), channel_id=1, source_target_pairs={{0,4},{4,0},{8,12},{12,8},{16,20},{20,16},{24,28},{28,24},{1,5},{5... | collective-permute-start | bytes 2064392 | tf_op jit(solution)/shard_map/ppermute | solution.py:14
  4.3 5.0 %collective-permute-start.1 = (f32[84,6144]{1,0:T(8,128)S(1)}, f32[84,6144]{1,0:T(8,128)S(1)}, u32[]{:S(2)}, u32[]{:S(2)}) collective-permute-start(f32[84,6144]{1,0:T(8,128)S(1)} %pad_maximum_fusion), channel_id=1, source_target_pairs={{0,4},{4,0},{8,12},{12,8},{16,20},{20,16},{24,28},{28,24},{1,5},{5... | collective-permute-start | bytes 6193160 | tf_op jit(solution)/shard_map/ppermute | solution.py:14
  4.8 34.7 %collective-permute-start.4 = (f32[168,2048]{1,0:T(8,128)S(1)}, f32[168,2048]{1,0:T(8,128)S(1)}, u32[]{:S(2)}, u32[]{:S(2)}) collective-permute-start(f32[168,2048]{1,0:T(8,128)S(1)} %maximum_select_fusion), channel_id=1, source_target_pairs={{0,24},{4,28},{8,16},{12,20},{16,8},{20,12},{24,0},{28,4},{1,25},{... | collective-permute-start | bytes 4128776 | tf_op jit(solution)/shard_map/ppermute | solution.py:14
  9.3 1.4 copy-start.4
  15.0 104.3 %collective-permute-start.2 = (f32[168,2048]{1,0:T(8,128)S(1)}, f32[168,2048]{1,0:T(8,128)S(1)}, u32[]{:S(2)}, u32[]{:S(2)}) collective-permute-start(f32[168,2048]{1,0:T(8,128)S(1)} %get-tuple-element.32), channel_id=1, source_target_pairs={{0,8},{4,12},{8,0},{12,4},{16,24},{20,28},{24,16},{28,20},{1,9},{5... | collective-permute-start | bytes 4128776 | tf_op jit(solution)/shard_map/ppermute | solution.py:14
  17.2 102.2 %collective-permute-start.3 = (f32[168,1536]{1,0:T(8,128)S(1)}, f32[168,1536]{1,0:T(8,128)S(1)}, u32[]{:S(2)}, u32[]{:S(2)}) collective-permute-start(f32[168,1536]{1,0:T(8,128)S(1)} %get-tuple-element.33), channel_id=1, source_target_pairs={{0,16},{4,20},{8,24},{12,28},{16,0},{20,4},{24,8},{28,12},{1,17},{... | collective-permute-start | bytes 3096584 | tf_op jit(solution)/shard_map/ppermute | solution.py:14
  39.5 87.1 %copy-start = (f32[168,2048]{1,0:T(8,128)}, f32[168,2048]{1,0:T(8,128)S(1)}, u32[]{:S(2)}) copy-start(f32[168,2048]{1,0:T(8,128)S(1)} %collective-permute-done.4.refs_3_) | copy-start | bytes 4128772
  39.5 87.2 %collective-permute-start.5 = (f32[168,512]{1,0:T(8,128)S(1)}, f32[168,512]{1,0:T(8,128)S(1)}, u32[]{:S(2)}, u32[]{:S(2)}) collective-permute-start(f32[168,512]{1,0:T(8,128)S(1)} %get-tuple-element.38), channel_id=1, source_target_pairs={{0,16},{4,20},{8,24},{12,28},{16,0},{20,4},{24,8},{28,12},{1,17},{... | collective-permute-start | bytes 1032200 | tf_op jit(solution)/shard_map/ppermute | solution.py:14
  119.3 7.2 %copy-start.2 = (f32[168,2048]{1,0:T(8,128)}, f32[168,2048]{1,0:T(8,128)S(1)}, u32[]{:S(2)}) copy-start(f32[168,2048]{1,0:T(8,128)S(1)} %collective-permute-done.2.refs_1_) | copy-start | bytes 4128772
  119.3 1.8 copy-start.1
  130.6 3.5 %collective-permute-start.6 = (f32[928,128]{1,0:T(8,128)S(1)}, f32[928,128]{1,0:T(8,128)S(1)}, u32[]{:S(2)}, u32[]{:S(2)}) collective-permute-start(f32[928,128]{1,0:T(8,128)S(1)} %get-tuple-element.40), channel_id=1, source_target_pairs={{0,4},{4,0},{8,12},{12,8},{16,20},{20,16},{24,28},{28,24},{1,5},{5... | collective-permute-start | bytes 1425416 | tf_op jit(solution)/shard_map/ppermute | solution.py:14
  134.2 31.8 %copy-start.3 = (f32[672,96]{0,1:T(8,128)S(1)}, f32[672,96]{0,1:T(8,128)}, u32[]{:S(2)}) copy-start(f32[672,96]{0,1:T(8,128)} %param.3) | copy-start | bytes 774148
  134.3 5.4 %collective-permute-start.7 = (f32[232,128]{1,0:T(8,128)S(1)}, f32[232,128]{1,0:T(8,128)S(1)}, u32[]{:S(2)}, u32[]{:S(2)}) collective-permute-start(f32[232,128]{1,0:T(8,128)S(1)} %get-tuple-element.60), channel_id=1, source_target_pairs={{0,3},{1,2},{2,1},{3,0},{4,7},{5,6},{6,5},{7,4},{8,11},{9,10},{10,... | collective-permute-start | bytes 356360 | tf_op jit(solution)/shard_map/ppermute | solution.py:398
  136.5 6.1 %collective-permute-start.8 = (f32[232,128]{1,0:T(8,128)S(1)}, f32[232,128]{1,0:T(8,128)S(1)}, u32[]{:S(2)}, u32[]{:S(2)}) collective-permute-start(f32[232,128]{1,0:T(8,128)S(1)} %get-tuple-element.62), channel_id=1, source_target_pairs={{0,1},{1,0},{2,3},{3,2},{4,6},{5,7},{6,4},{7,5},{8,9},{9,8},{10,11... | collective-permute-start | bytes 356360 | tf_op jit(solution)/shard_map/ppermute | solution.py:398
  136.7 5.9 %collective-permute-start.9 = (f32[232,128]{1,0:T(8,128)S(1)}, f32[232,128]{1,0:T(8,128)S(1)}, u32[]{:S(2)}, u32[]{:S(2)}) collective-permute-start(f32[232,128]{1,0:T(8,128)S(1)} %get-tuple-element.61), channel_id=1, source_target_pairs={{0,2},{1,3},{2,0},{3,1},{4,5},{5,4},{6,7},{7,6},{8,10},{9,11},{10,... | collective-permute-start | bytes 356360 | tf_op jit(solution)/shard_map/ppermute | solution.py:398
  142.6 5.6 %collective-permute-start.10 = (f32[232,128]{1,0:T(8,128)S(1)}, f32[232,128]{1,0:T(8,128)S(1)}, u32[]{:S(2)}, u32[]{:S(2)}) collective-permute-start(f32[232,128]{1,0:T(8,128)S(1)} %add_add_fusion.1), channel_id=1, source_target_pairs={{0,24},{4,28},{8,16},{12,20},{16,8},{20,12},{24,0},{28,4},{1,25},{... | collective-permute-start | bytes 356360 | tf_op jit(solution)/shard_map/ppermute | solution.py:14
  144.9 9.8 %collective-permute-start.11 = (f32[232,128]{1,0:T(8,128)S(1)}, f32[232,128]{1,0:T(8,128)S(1)}, u32[]{:S(2)}, u32[]{:S(2)}) collective-permute-start(f32[232,128]{1,0:T(8,128)S(1)} %add_add_fusion.1), channel_id=1, source_target_pairs={{0,8},{4,12},{8,0},{12,4},{16,24},{20,28},{24,16},{28,20},{1,9},{5... | collective-permute-start | bytes 356360 | tf_op jit(solution)/shard_map/ppermute | solution.py:14
  144.9 9.8 %collective-permute-start.12 = (f32[232,128]{1,0:T(8,128)S(1)}, f32[232,128]{1,0:T(8,128)S(1)}, u32[]{:S(2)}, u32[]{:S(2)}) collective-permute-start(f32[232,128]{1,0:T(8,128)S(1)} %add_add_fusion.1), channel_id=1, source_target_pairs={{0,16},{4,20},{8,24},{12,28},{16,0},{20,4},{24,8},{28,12},{1,17},{... | collective-permute-start | bytes 356360 | tf_op jit(solution)/shard_map/ppermute | solution.py:14
  154.8 5.2 %collective-permute-start.13 = (f32[232,128]{1,0:T(8,128)S(1)}, f32[232,128]{1,0:T(8,128)S(1)}, u32[]{:S(2)}, u32[]{:S(2)}) collective-permute-start(f32[232,128]{1,0:T(8,128)S(1)} %get-tuple-element.55), channel_id=1, source_target_pairs={{0,3},{1,2},{2,1},{3,0},{4,7},{5,6},{6,5},{7,4},{8,11},{9,10},{10,... | collective-permute-start | bytes 356360 | tf_op jit(solution)/shard_map/ppermute | solution.py:398
  155.7 6.7 %collective-permute-start.14 = (f32[232,128]{1,0:T(8,128)S(1)}, f32[232,128]{1,0:T(8,128)S(1)}, u32[]{:S(2)}, u32[]{:S(2)}) collective-permute-start(f32[232,128]{1,0:T(8,128)S(1)} %get-tuple-element.55), channel_id=1, source_target_pairs={{0,1},{1,0},{2,3},{3,2},{4,6},{5,7},{6,4},{7,5},{8,9},{9,8},{10,11... | collective-permute-start | bytes 356360 | tf_op jit(solution)/shard_map/ppermute | solution.py:398
  157.0 6.1 %collective-permute-start.15 = (f32[232,128]{1,0:T(8,128)S(1)}, f32[232,128]{1,0:T(8,128)S(1)}, u32[]{:S(2)}, u32[]{:S(2)}) collective-permute-start(f32[232,128]{1,0:T(8,128)S(1)} %get-tuple-element.55), channel_id=1, source_target_pairs={{0,2},{1,3},{2,0},{3,1},{4,5},{5,4},{6,7},{7,6},{8,10},{9,11},{10,... | collective-permute-start | bytes 356360 | tf_op jit(solution)/shard_map/ppermute | solution.py:398
  163.1 2.9 %collective-permute-start.16 = (f32[928,128]{1,0:T(8,128)S(1)}, f32[928,128]{1,0:T(8,128)S(1)}, u32[]{:S(2)}, u32[]{:S(2)}) collective-permute-start(f32[928,128]{1,0:T(8,128)S(1)} %bitcast.13), channel_id=1, source_target_pairs={{0,4},{4,0},{8,12},{12,8},{16,20},{20,16},{24,28},{28,24},{1,5},{5... | collective-permute-start | bytes 1425416 | tf_op jit(solution)/shard_map/ppermute | solution.py:14
  181.5 5.9 %collective-permute-start.17 = (f32[24,1024]{1,0:T(8,128)S(1)}, f32[24,1024]{1,0:T(8,128)S(1)}, u32[]{:S(2)}, u32[]{:S(2)}) collective-permute-start(f32[24,1024]{1,0:T(8,128)S(1)} %get-tuple-element.46), channel_id=1, source_target_pairs={{0,24},{4,28},{8,16},{12,20},{16,8},{20,12},{24,0},{28,4},{1,25},{... | collective-permute-start | bytes 294920 | tf_op jit(solution)/shard_map/ppermute | solution.py:14
  182.1 10.0 %collective-permute-start.18 = (f32[24,1024]{1,0:T(8,128)S(1)}, f32[24,1024]{1,0:T(8,128)S(1)}, u32[]{:S(2)}, u32[]{:S(2)}) collective-permute-start(f32[24,1024]{1,0:T(8,128)S(1)} %get-tuple-element.47), channel_id=1, source_target_pairs={{0,28},{4,24},{8,20},{12,16},{16,12},{20,8},{24,4},{28,0},{1,29},{... | collective-permute-start | bytes 294920 | tf_op jit(solution)/shard_map/ppermute | solution.py:14
  185.3 9.6 %collective-permute-start.19 = (f32[24,1024]{1,0:T(8,128)S(1)}, f32[24,1024]{1,0:T(8,128)S(1)}, u32[]{:S(2)}, u32[]{:S(2)}) collective-permute-start(f32[24,1024]{1,0:T(8,128)S(1)} %get-tuple-element.48), channel_id=1, source_target_pairs={{0,8},{4,12},{8,0},{12,4},{16,24},{20,28},{24,16},{28,20},{1,9},{5... | collective-permute-start | bytes 294920 | tf_op jit(solution)/shard_map/ppermute | solution.py:14
  185.3 12.0 %collective-permute-start.20 = (f32[24,1024]{1,0:T(8,128)S(1)}, f32[24,1024]{1,0:T(8,128)S(1)}, u32[]{:S(2)}, u32[]{:S(2)}) collective-permute-start(f32[24,1024]{1,0:T(8,128)S(1)} %get-tuple-element.49), channel_id=1, source_target_pairs={{0,12},{4,8},{8,4},{12,0},{16,28},{20,24},{24,20},{28,16},{1,13},{... | collective-permute-start | bytes 294920 | tf_op jit(solution)/shard_map/ppermute | solution.py:14
  186.9 10.5 %collective-permute-start.21 = (f32[24,1024]{1,0:T(8,128)S(1)}, f32[24,1024]{1,0:T(8,128)S(1)}, u32[]{:S(2)}, u32[]{:S(2)}) collective-permute-start(f32[24,1024]{1,0:T(8,128)S(1)} %get-tuple-element.50), channel_id=1, source_target_pairs={{0,16},{4,20},{8,24},{12,28},{16,0},{20,4},{24,8},{28,12},{1,17},{... | collective-permute-start | bytes 294920 | tf_op jit(solution)/shard_map/ppermute | solution.py:14
  187.4 12.6 %collective-permute-start.22 = (f32[24,1024]{1,0:T(8,128)S(1)}, f32[24,1024]{1,0:T(8,128)S(1)}, u32[]{:S(2)}, u32[]{:S(2)}) collective-permute-start(f32[24,1024]{1,0:T(8,128)S(1)} %get-tuple-element.51), channel_id=1, source_target_pairs={{0,20},{4,16},{8,28},{12,24},{16,4},{20,0},{24,12},{28,8},{1,21},{... | collective-permute-start | bytes 294920 | tf_op jit(solution)/shard_map/ppermute | solution.py:14
  192.1 7.9 %collective-permute-start.23 = (f32[24,1024]{1,0:T(8,128)S(1)}, f32[24,1024]{1,0:T(8,128)S(1)}, u32[]{:S(2)}, u32[]{:S(2)}) collective-permute-start(f32[24,1024]{1,0:T(8,128)S(1)} %get-tuple-element.52), channel_id=1, source_target_pairs={{0,4},{4,0},{8,12},{12,8},{16,20},{20,16},{24,28},{28,24},{1,5},{5... | collective-permute-start | bytes 294920 | tf_op jit(solution)/shard_map/ppermute | solution.py:14
